TPU v7x, 32 devices: a whole 2x2x4 slice. The times are simulated.
32 devices in a mesh: dp: 8 (over z, y), mp: 4 (over x, core).
Axes of the slice: x: 2, y: 2, z: 4, core: 2. Of those that a mesh axis runs over, the one named last changes fastest.
Arguments:
- table: float32 [32768, 1024], P('dp', 'mp'), may hold values from -6 to 6
- q_weight: float32 [1024, 1024], P(None, 'mp'), may hold values from -0.1875 to 0.1875
- q_bias: float32 [1024], P('mp'), may hold values from -3 to 3
- w_weight: float32 [2048, 1024], P(None, 'mp'), may hold values from -0.125 to 0.125
- w_bias: float32 [1024], P('mp'), may hold values from -3 to 3
- neighbours: int32 [2048, 50], P('dp'), may hold values from 0 to 32767, as said below
- counts: int32 [2048], P('dp'), may hold values from 5 to 50
- importance: float32 [2048, 50], P('dp'), may hold values from 0.05 to 1
- cotangent: float32 [2048, 1024], P('dp', 'mp'), may hold values from -6 to 6
Outputs:
- embedding: float32 [2048, 1024], P('dp', 'mp')
- table_grad: float32 [32768, 1024], P('dp', 'mp')
- q_weight_grad: float32 [1024, 1024], P(None, 'mp')
- q_bias_grad: float32 [1024], P('mp')
- w_weight_grad: float32 [2048, 1024], P(None, 'mp')
- w_bias_grad: float32 [1024], P('mp')
- penalty: float32 [], replicated
Inputs may be any that keep to these rules, and one draw needn't show every extreme that they name: `neighbours`: table row r belongs to index r // 4096 of dp. Among the 12800 ids of one index's nodes (padded slots included) at most 2400 belong to any one index of dp, and this many is reached by some index of dp for every node block.
All inputs are finite; a program needn't handle non-finite values.
Results may differ from a plain program's by a relative error of at most 0.0074.
Values may be sent and summed in bfloat16 or wider, within the bound.
No kernel may reach another device: no remote copies, remote signals or barrier semaphores. Data moves between devices by JAX's collectives and lax.ppermute only.
A program may use at most 256 MiB of HBM per device.

v0:
```python
import jax
import jax.numpy as jnp
from jax import lax
from jax.sharding import PartitionSpec as P

epsilon = 1e-06
penalty_rate = 0.01


def gelu_slope(values):
    return jax.grad(lambda inner: jnp.sum(jax.nn.gelu(inner)))(values)


def shards(table, q_weight, q_bias, w_weight, w_bias, neighbours, counts, importance, cotangent):
    groups = lax.axis_size("dp")
    row_dev = table.shape[0]
    node_dev, slots_node = neighbours.shape
    slot_count = node_dev * slots_node
    width = q_weight.shape[0]
    capacity = 3 * slot_count // (2 * groups)
    flat_ids = neighbours.reshape(-1)
    owner_index = flat_ids // row_dev
    local_rows = flat_ids % row_dev
    order = jnp.argsort(owner_index, stable=True)
    sorted_owner = owner_index[order]
    starts = jnp.searchsorted(sorted_owner, jnp.arange(groups, dtype=jnp.int32))
    rank_sorted = jnp.arange(slot_count, dtype=jnp.int32) - starts[sorted_owner]
    slot_place = (
        jnp.zeros((slot_count,), jnp.int32).at[order].set(sorted_owner * capacity + rank_sorted)
    )
    request = (
        jnp.zeros((groups * capacity,), jnp.int32)
        .at[slot_place]
        .set(local_rows)
        .reshape(groups, capacity)
    )
    served_ids = lax.all_to_all(request, "dp", split_axis=0, concat_axis=0, tiled=True)
    table_low = table.astype(jnp.bfloat16)
    served_rows = table_low[served_ids]
    returned = lax.all_to_all(served_rows, "dp", split_axis=0, concat_axis=0, tiled=True)
    slot_rows = returned.reshape(groups * capacity, -1)[slot_place]
    q_low = q_weight.astype(jnp.bfloat16)
    w_low = w_weight.astype(jnp.bfloat16)
    whole_rows = lax.all_gather(slot_rows, "mp", axis=1, tiled=True)
    hidden_pre = jnp.dot(whole_rows, q_low, preferred_element_type=jnp.float32) + q_bias
    present = (jnp.arange(slots_node, dtype=jnp.int32)[None, :] < counts[:, None]).astype(
        jnp.float32
    )
    raw_weights = importance * present
    weights = raw_weights / jnp.sum(raw_weights, axis=1, keepdims=True)
    hidden = jax.nn.gelu(hidden_pre).reshape(node_dev, slots_node, -1)
    pooled = jnp.sum(weights[:, :, None] * hidden, axis=1)
    self_full, pooled_full = (
        lax.all_gather(table_low[:node_dev], "mp", axis=1, tiled=True),
        lax.all_gather(pooled.astype(jnp.bfloat16), "mp", axis=1, tiled=True),
    )
    joined = jnp.concatenate([self_full, pooled_full], axis=1)
    output_pre = jnp.dot(joined, w_low, preferred_element_type=jnp.float32) + w_bias
    activated = jax.nn.gelu(output_pre)
    squares, cross = lax.psum(
        (jnp.sum(activated * activated, axis=1), jnp.sum(activated * cotangent, axis=1)), "mp"
    )
    scale = lax.rsqrt(squares + epsilon)
    embedding = activated * scale[:, None]
    node_total = node_dev * groups
    grad_act = (
        cotangent * scale[:, None]
        - activated * (cross * scale * scale * scale)[:, None]
        + 2.0 * penalty_rate / node_total * activated
    )
    grad_out_pre = (grad_act * gelu_slope(output_pre)).astype(jnp.bfloat16)
    w_grad_local = lax.dot_general(
        joined, grad_out_pre, (((0,), (0,)), ((), ())), preferred_element_type=jnp.float32
    )
    wb_grad_local = jnp.sum(grad_out_pre.astype(jnp.float32), axis=0)
    grad_joined = lax.dot_general(
        grad_out_pre, w_low, (((1,), (1,)), ((), ())), preferred_element_type=jnp.float32
    )
    grad_self, grad_pooled = (
        lax.psum_scatter(grad_joined[:, :width], "mp", scatter_dimension=1, tiled=True),
        lax.psum_scatter(grad_joined[:, width:], "mp", scatter_dimension=1, tiled=True),
    )
    grad_hidden = (weights[:, :, None] * grad_pooled[:, None, :]).reshape(slot_count, -1)
    grad_hidden_pre = (grad_hidden * gelu_slope(hidden_pre)).astype(jnp.bfloat16)
    q_grad_local = lax.dot_general(
        whole_rows, grad_hidden_pre, (((0,), (0,)), ((), ())), preferred_element_type=jnp.float32
    )
    qb_grad_local = jnp.sum(grad_hidden_pre.astype(jnp.float32), axis=0)
    grad_rows = lax.psum_scatter(
        lax.dot_general(
            q_low, grad_hidden_pre, (((1,), (1,)), ((), ())), preferred_element_type=jnp.float32
        ).astype(jnp.bfloat16),
        "mp",
        scatter_dimension=0,
        tiled=True,
    ).astype(jnp.float32)
    outgoing = (
        jnp.zeros((grad_rows.shape[0], groups * capacity), jnp.float32)
        .at[:, slot_place]
        .set(grad_rows)
    )
    incoming = lax.all_to_all(
        outgoing.reshape(grad_rows.shape[0], groups, capacity).astype(jnp.bfloat16),
        "dp",
        split_axis=1,
        concat_axis=1,
        tiled=True,
    ).astype(jnp.float32)
    table_grad = (
        jnp.zeros((row_dev, grad_rows.shape[0]), jnp.float32)
        .at[served_ids.reshape(-1)]
        .add(incoming.reshape(grad_rows.shape[0], -1).T)
    )
    table_grad = table_grad.at[:node_dev].add(grad_self)
    q_weight_grad, q_bias_grad, w_weight_grad, w_bias_grad, square_total = lax.psum(
        (q_grad_local, qb_grad_local, w_grad_local, wb_grad_local, jnp.sum(squares)), "dp"
    )
    penalty = penalty_rate * square_total / node_total
    return (embedding, table_grad, q_weight_grad, q_bias_grad, w_weight_grad, w_bias_grad, penalty)


def solution(mesh):
    placed = (
        P("dp", "mp"),
        P(None, "mp"),
        P("mp"),
        P(None, "mp"),
        P("mp"),
        P("dp", None),
        P("dp"),
        P("dp", None),
        P("dp", "mp"),
    )
    return jax.shard_map(
        shards,
        mesh=mesh,
        in_specs=placed,
        out_specs=(
            P("dp", "mp"),
            P("dp", "mp"),
            P(None, "mp"),
            P("mp"),
            P(None, "mp"),
            P("mp"),
            P(),
        ),
        check_vma=False,
    )
```

profile of v0, /device:TPU:12, one launch (start us, length us, event | category | flops | bytes accessed | tf_op | source)
XLA Modules:
  0.0 1482.5 jit_solution(17926135389360252623)
XLA Ops:
  7.2 0.9 copy.21
  8.3 9.3 sort.17
  17.7 65.9 %gather_fusion.1 = s32[12800]{0:T(1024)S(1)} fusion(s32[12800]{0:T(1024)S(1)} %get-tuple-element.145, s32[13312]{0:T(1024)S(1)} %pad_clamp_fusion.3), kind=kCustom, calls=%fused_computation.1 | custom fusion | bytes 153600 | tf_op jit(solution)/shard_map/gather | solution.py:25
  83.8 9.7 while.25
  83.9 0.6 gather_fusion
  84.5 0.6 gather_fusion
  85.2 0.6 gather_fusion
  85.9 0.6 gather_fusion
  86.6 0.6 gather_fusion
  87.3 0.6 gather_fusion
  88.0 0.6 gather_fusion
  88.7 0.6 gather_fusion
  89.4 0.6 gather_fusion
  90.1 0.6 gather_fusion
  90.8 0.6 gather_fusion
  91.5 0.6 gather_fusion
  92.2 0.6 gather_fusion
  92.9 0.6 gather_fusion
  93.5 0.7 fusion.49
  94.2 4.9 fusion.37
  99.1 0.7 fusion.35
  99.8 47.3 %scatter_custom_fusion = s32[12800]{0:T(1024)S(1)} fusion(s32[12800]{0:T(1024)S(1)} %compare_select_fusion.10, s32[12800]{0:T(1024)S(1)} %fusion.35, s32[]{:T(128)} %constant.109.clone.1), kind=kCustom, calls=%fused_computation.95 | custom fusion | bytes 51204 | tf_op jit(solution)/shard_map/scatter | solution.py:29
  147.1 47.3 %scatter_custom_fusion.1 = s32[19200]{0:T(1024)S(1)} fusion(s32[12800]{0:T(1024)S(1)} %compare_select_fusion.9, s32[12800]{0:T(1024)S(1)} %get-tuple-element.144, s32[]{:T(128)} %constant.109.clone.1), kind=kCustom, calls=%fused_computation.92 | custom fusion | bytes 76804 | tf_op jit(solution)/shard_map/scatter | solution.py:34
  194.4 0.8 all_to_all.14
  195.2 6.2 all-to-all-start
  201.4 2.4 convert_element_type.51
  203.8 2.3 all-to-all-done
  206.1 0.2 fusion.32
  206.5 53.4 %gather_fusion.2 = bf16[19200,256]{1,0:T(8,128)(2,1)} fusion(bf16[4096,256]{1,0:T(8,128)(2,1)S(1)} %convert_element_type.51, s32[19456]{0:T(1024)S(1)} %pad_clamp_fusion.1), kind=kCustom, calls=%fused_computation.2 | custom fusion | bytes 19737600 | tf_op jit(solution)/shard_map/gather | solution.py:39
  259.9 7.2 all-to-all-start.1
  267.3 209.3 %all-to-all-done.1 = bf16[8,2400,256]{2,1,0:T(8,128)(2,1)} async-done(((bf16[8,2400,256]{2,1,0:T(8,128)(2,1)}), bf16[8,2400,256]{2,1,0:T(8,128)(2,1)}, u32[]{:S(2)}, u32[]{:S(2)}) %all-to-all-start.1) | async-done | bytes 9830432 | tf_op jit(solution)/shard_map/all_to_all | solution.py:40
  476.6 34.7 %gather_fusion.3 = bf16[12800,256]{1,0:T(8,128)(2,1)} fusion(bf16[19200,256]{1,0:T(8,128)(2,1)} %bitcast.10, s32[13312]{0:T(1024)S(1)} %pad_clamp_fusion.2), kind=kCustom, calls=%fused_computation.3 | custom fusion | bytes 13158400 | tf_op jit(solution)/shard_map/gather | solution.py:41
  511.8 7.2 all_gather.9
  519.0 158.6 %all-gather.3.cloned.1.call-done = bf16[12800,1024]{1,0:T(8,128)(2,1)} async-done(((bf16[12800,256]{1,0:T(8,128)(2,1)}), bf16[12800,1024]{1,0:T(8,128)(2,1)}) %all-gather.3.cloned.1.call-update) | async-done | bytes 26214416 | tf_op jit(solution)/shard_map/all_gather | solution.py:44
  677.6 19.5 %multiply_multiply_fusion.2 = (f32[12800,256]{1,0:T(8,128)}, f32[12800,256]{1,0:T(8,128)}) fusion(f32[256]{0:T(256)S(1)} %copy-done.12, bf16[12800,1024]{1,0:T(8,128)(2,1)} %all-gather.3.cloned.1.call-done, f32[1024,256]{1,0:T(8,128)} %param.14), kind=kOutput, calls=%fused_computation.35 | convolution fusion | flops 6740639744 | bytes 53478400 | tf_op jit(solution)/shard_map/dot_general | solution.py:45
  697.0 15.1 %reshape.145 = f32[256,50,256]{2,1,0:T(8,128)} reshape(f32[12800,256]{1,0:T(8,128)} %get-tuple-element.157) | data formatting | bytes 26214400 | tf_op jit(solution)/shard_map/reshape | solution.py:51
  712.1 6.7 multiply_reduce_fusion
  718.8 7.2 all_gather.11
  726.1 1.3 multiply_reduce_fusion.1
  727.4 6.1 all-reduce.2
  733.5 0.6 fusion.48
  734.1 1.9 convert_reduce_fusion.1
  736.0 0.7 copy-done.1
  736.7 0.5 fusion.18
  737.2 1.5 fusion.47
  738.6 0.3 reduce-scatter.6.cloned.1.call-start
  739.0 25.5 %reduce-scatter.4.cloned.1.call-done = f32[256,256]{1,0:T(8,128)} async-done(((f32[256,1024]{1,0:T(8,128)}), f32[256,256]{1,0:T(8,128)}) %reduce-scatter.4.cloned.1.call-update) | async-done | bytes 262160 | tf_op jit(solution)/shard_map/reduce_scatter | solution.py:81
  764.6 7.0 mul.203
  771.6 15.3 %mul.204 = f32[12800,256]{1,0:T(8,128)} reshape(f32[256,50,256]{2,1,0:T(8,128)} %mul.203) | data formatting | bytes 26214400 | tf_op jit(solution)/shard_map/mul | solution.py:83
  786.9 15.8 %convert_reduce_fusion = (f32[256]{0:T(256)S(1)}, bf16[12800,256]{1,0:T(8,128)(2,1)}) fusion(f32[12800,256]{1,0:T(8,128)} %get-tuple-element.158, f32[12800,256]{1,0:T(8,128)} %mul.204, f32[12800]{0:T(1024)S(1)} %mul.182), kind=kLoop, calls=%fused_computation.33 | loop fusion | flops 72089344 | bytes 32820224 | tf_op jit(solution)/shard_map/reduce_sum | solution.py:88
  802.7 15.2 %convert_bitcast_fusion = bf16[1024,12800]{0,1:T(8,128)(2,1)} fusion(bf16[12800,256]{1,0:T(8,128)(2,1)} %get-tuple-element.138, f32[1024,256]{1,0:T(8,128)S(1)} %copy-done.3), kind=kOutput, calls=%fused_computation.16 | convolution fusion | flops 6724255744 | bytes 33816576 | tf_op jit(solution)/shard_map/dot_general | solution.py:90
  817.9 187.4 %reduce-scatter.6.cloned.1.call-done = bf16[256,12800]{0,1:T(8,128)(2,1)} async-done(((bf16[1024,12800]{0,1:T(8,128)(2,1)}), bf16[256,12800]{0,1:T(8,128)(2,1)}) %reduce-scatter.6.cloned.1.call-update) | async-done | bytes 6553616 | tf_op jit(solution)/shard_map/reduce_scatter | solution.py:89
  1005.3 62.0 %scatter_custom_fusion.2 = f32[256,19200]{0,1:T(8,128)} fusion(s32[12800]{0:T(1024)} %copy-done.9, bf16[256,12800]{0,1:T(8,128)(2,1)} %reduce-scatter.6.cloned.1.call-done, f32[]{:T(128)} %constant.108.clone.1), kind=kCustom, calls=%fused_computation.31 | custom fusion | flops 3276800 | bytes 26214912 | tf_op jit(solution)/shard_map/scatter | solution.py:100
  1067.3 11.5 convert_element_type.61
  1078.8 6.2 all-to-all-start.2
  1085.0 0.6 reduce-scatter.8.cloned.1.call-update
  1085.6 1.8 fusion.51
  1087.4 15.3 %fusion.50 = f32[1024,256]{1,0:T(8,128)} fusion(bf16[12800,1024]{1,0:T(8,128)(2,1)} %all-gather.3.cloned.1.call-done, bf16[12800,256]{1,0:T(8,128)(2,1)} %get-tuple-element.138), kind=kOutput, calls=%fused_computation.104 | convolution fusion | flops 6710886400 | bytes 33816576 | tf_op jit(solution)/shard_map/dot_general | solution.py:85
  1103.3 0.8 copy.25
  1104.2 244.5 %all-reduce = (f32[256]{0:T(256)}, f32[256]{0:T(256)}, f32[]{:T(128)}) all-reduce(f32[256]{0:T(256)S(1)} %get-tuple-element.137, f32[256]{0:T(256)S(1)} %get-tuple-element.135, f32[]{:T(128)} %get-tuple-element.146), channel_id=1, replica_groups=mesh['dp'=8,'mp'=4] {'dp'}, use_global_device_ids=true, to_apply=%region_18.19 | all-reduce | flops 513 | bytes 4104 | tf_op jit(solution)/shard_map/psum | solution.py:115
  1349.3 118.0 %scatter_custom_fusion.3 = f32[4096,256]{1,0:T(8,128)} fusion(s32[19200]{0:T(1024)S(1)} %fusion.33, bf16[256,19200]{0,1:T(8,128)(2,1)} %bitcast.16, f32[]{:T(128)} %constant.108.clone.1), kind=kCustom, calls=%fused_computation.18 | custom fusion | flops 9830400 | bytes 14024708 | tf_op jit(solution)/shard_map/scatter-add | solution.py:112
  1467.3 1.8 fusion.29
  1469.0 2.3 copy.39
  1471.3 3.0 copy.40
  (102 shorter events, 2.4 us)
Async XLA Ops:
  147.1 120.2 %copy-start.9 = (s32[12800]{0:T(1024)}, s32[12800]{0:T(1024)S(1)}, u32[]{:S(2)}) copy-start(s32[12800]{0:T(1024)S(1)} %compare_select_fusion.9) | copy-start | bytes 153604
  195.2 11.0 all-to-all-start
  206.1 53.7 %copy-start.5 = (s32[8,1,2400]{2,1,0:T(1,128)}, s32[8,1,2400]{2,1,0:T(1,128)S(1)}, u32[]{:S(2)}) copy-start(s32[8,1,2400]{2,1,0:T(1,128)S(1)} %all-to-all-done) | copy-start | bytes 230404
  259.9 216.8 %all-to-all-start.1 = ((bf16[8,2400,256]{2,1,0:T(8,128)(2,1)}), bf16[8,2400,256]{2,1,0:T(8,128)(2,1)}, u32[]{:S(2)}, u32[]{:S(2)}) async-start(bf16[8,2400,256]{2,1,0:T(8,128)(2,1)} %bitcast.32), calls=%async_computation.1 | async-start | bytes 19660800 | tf_op jit(solution)/shard_map/all_to_all | solution.py:40
  267.1 410.5 %all-gather.3.cloned.1.call-start = ((), (), s32[]{:S(2)}) async-start(), calls=%async_computation.9 | async-start | bytes 32768000 | tf_op jit(solution)/shard_map/all_gather | solution.py:44
  476.6 34.8 %copy-start.7 = (f32[256,256]{1,0:T(8,128)S(1)}, f32[256,256]{1,0:T(8,128)}, u32[]{:S(2)}) copy-start(f32[256,256]{1,0:T(8,128)} %param.21) | copy-start | bytes 786436
  476.6 35.0 %copy-start.8 = (f32[256,50]{0,1:T(8,128)S(1)}, f32[256,50]{0,1:T(8,128)}, u32[]{:S(2)}) copy-start(f32[256,50]{0,1:T(8,128)} %param.20) | copy-start | bytes 153604
  476.6 35.0 %copy-start.10 = (s32[256]{0:T(256)S(1)}, s32[256]{0:T(256)}, u32[]{:S(2)}) copy-start(s32[256]{0:T(256)} %param.19) | copy-start | bytes 3076
  476.6 200.9 %copy-start.12 = (f32[256]{0:T(256)S(1)}, f32[256]{0:T(256)}, u32[]{:S(2)}) copy-start(f32[256]{0:T(256)} %param.15) | copy-start | bytes 3076
  511.4 253.2 %reduce-scatter.4.cloned.1.call-start = ((), (), s32[]{:S(2)}) async-start(), calls=%async_computation.6 | async-start | bytes 1310720 | tf_op jit(solution)/shard_map/reduce_scatter | solution.py:81
  712.1 14.0 copy-start
  712.1 14.0 copy-start.11
  736.0 0.7 copy-start.1
  738.6 266.7 %reduce-scatter.6.cloned.1.call-start = ((), (), s32[]{:S(2)}) async-start(), calls=%async_computation.7 | async-start | bytes 32768000 | tf_op jit(solution)/shard_map/reduce_scatter | solution.py:89
  786.9 15.8 %copy-start.3 = (f32[1024,256]{1,0:T(8,128)S(1)}, f32[1024,256]{1,0:T(8,128)}, u32[]{:S(2)}) copy-start(f32[1024,256]{1,0:T(8,128)} %param.14) | copy-start | bytes 3145732
  1078.8 6.8 copy-start.2
  1078.8 270.5 %all-to-all-start.2 = ((bf16[256,8,2400]{0,2,1:T(8,128)(2,1)}), bf16[256,8,2400]{0,2,1:T(8,128)(2,1)}, u32[]{:S(2)}, u32[]{:S(2)}) async-start(bf16[256,8,2400]{0,2,1:T(8,128)(2,1)} %bitcast.31), calls=%async_computation.4 | async-start | bytes 19660800 | tf_op jit(solution)/shard_map/all_to_all | solution.py:102
  1085.0 382.3 %reduce-scatter.8.cloned.1.call-start = ((), (), s32[]{:S(2)}) async-start(), calls=%async_computation.8 | async-start | bytes 1310720 | tf_op jit(solution)/shard_map/reduce_scatter | solution.py:80
  1085.5 383.5 %all-reduce.5.cloned.1.call-start = ((), (), s32[]{:S(2)}) async-start(), calls=%async_computation.10 | async-start | bytes 6291456 | tf_op jit(solution)/shard_map/psum | solution.py:115
  1087.4 15.3 %copy-start.6 = (s32[8,1,2400]{2,1,0:T(1,128)S(1)}, s32[8,1,2400]{2,1,0:T(1,128)}, u32[]{:S(2)}) copy-start(s32[8,1,2400]{2,1,0:T(1,128)} %copy-done.5) | copy-start | bytes 230404
  1087.4 15.9 %copy-start.4 = (f32[256,256]{0,1:T(8,128)S(1)}, f32[256,256]{0,1:T(8,128)}, u32[]{:S(2)}) copy-start(f32[256,256]{0,1:T(8,128)} %get-tuple-element.143) | copy-start | bytes 786436
Sparse Core Ops, SparseCore 0:
  511.5 166.0 all-gather.2
  738.8 25.7 reduce-scatter.3
  818.0 187.2 reduce-scatter.5
  1088.6 24.8 reduce-scatter.7
  1118.0 287.8 all-reduce.4
where the time goes:
time: 1500 us; the launch traced here: 1480 us
  waiting for transfers between devices  584 us (39%)
  local copies, waits for them, and re-layouts  306 us (20%)
  blocking collectives  265 us (18%)
  other arithmetic  237 us (16%)
  matrix products  53.5 us (4%)
  starting transfers between devices  20.1 us (1%)
  between operations  16.3 us (1%)
    psum x1, blocking collectives, shards(): lax.psum((q_grad_local, qb_grad_local, w_grad_local, wb_grad_local, jnp.s...  244 us
    all_to_all x1, waiting for transfers between devices, shards(): lax.all_to_all(served_rows, 'dp', split_axis=0, concat_axis=0, tiled=True)  209 us
    reduce_scatter x1, waiting for transfers between devices, shards(): lax.psum_scatter(lax.dot_general(q_low, grad_hidden_pre, (((1,), (1,)), (...  187 us
    all_gather x1, waiting for transfers between devices, shards(): whole_rows = lax.all_gather(slot_rows, 'mp', axis=1, tiled=True)  159 us
    scatter-add x1, other arithmetic, shards(): table_grad = jnp.zeros((row_dev, grad_rows.shape[0]), jnp.float32).at[ser...  118 us
    gather x1, local copies, waits for them, and re-layouts, shards(): sorted_owner = owner_index[order]  65.9 us
    scatter x1, other arithmetic, shards(): outgoing = jnp.zeros((grad_rows.shape[0], groups * capacity), jnp.float32...  62 us
    gather x1, local copies, waits for them, and re-layouts, shards(): served_rows = table_low[served_ids]  53.4 us
  transfers between devices with their start and end apart: 8, of which 5 were waited for; matrix products, arithmetic and copies ran while one was open for 10% of the time, Pallas kernels for 0%

commit v1 on v0

v1 whole, which is shorter than its diff:
```python
import functools

import jax
import jax.numpy as jnp
from jax import lax
from jax.experimental import pallas as pl
from jax.experimental.pallas import tpu as pltpu
from jax.sharding import PartitionSpec as P

epsilon = 1e-06
penalty_rate = 0.01
bf16, f32 = jnp.bfloat16, jnp.float32
bucket_rows = 256
lane_tile = 128


def dot(a, b, contract):
    return lax.dot_general(a, b, ((contract[:1], contract[1:]), ((), ())), preferred_element_type=f32)


def gelu_parts(values):
    c = 0.7978845608028654
    squared = values * values
    t = jnp.tanh(c * values * (1.0 + 0.044715 * squared))
    half = 0.5 * (1.0 + t)
    slope = half + 0.5 * values * (1.0 - t * t) * (c * (1.0 + 3 * 0.044715 * squared))
    return values * half, slope


def params(**kwargs):
    return pltpu.CompilerParams(vmem_limit_bytes=56 * 1024 * 1024, **kwargs)


def spread_kernel(row_dev, base_ref, slots_ref, out_ref):
    slots_node = slots_ref.shape[2]
    weight = slots_ref[0, 1]
    local = (slots_ref[0, 0] - base_ref[0].astype(f32)).astype(jnp.int32)
    owned = (local >= 0) & (local < row_dev) & (weight != 0.0)
    bucket = jnp.where(owned, local // bucket_rows, -1)
    within = (local - bucket * bucket_rows).astype(f32)
    index = lax.broadcasted_iota(jnp.int32, bucket.shape, 0)
    rank = jnp.zeros(bucket.shape, jnp.int32)
    for k in range(slots_node - 1):
        same = (bucket == bucket[k : k + 1, :]) & (index > k)
        rank = rank + jnp.where(same, 1, 0)
    code = jnp.where(owned, bucket * 64 + rank, -1)
    depth = jnp.max(jnp.where(owned, rank + 1, 0).astype(f32)).astype(jnp.int32)
    row_index = lax.broadcasted_iota(jnp.int32, (bucket_rows, lane_tile), 0).astype(f32)

    def one_bucket(b, carry):
        def body(j, total):
            hit = code == b * 64 + j
            row = jnp.sum(jnp.where(hit, within, 0.0), axis=0, keepdims=True)
            amount = jnp.sum(jnp.where(hit, weight, 0.0), axis=0, keepdims=True)
            return total + jnp.where(row_index == row, amount, 0.0)

        total = lax.fori_loop(0, depth, body, jnp.zeros((bucket_rows, lane_tile), f32))
        out_ref[pl.ds(pl.multiple_of(b * bucket_rows, bucket_rows), bucket_rows), :] = total.astype(bf16)
        return carry

    lax.fori_loop(0, row_dev // bucket_rows, one_bucket, 0)


def spread(base, slots, row_dev):
    groups, _, slots_node, node_dev = slots.shape
    tiles = node_dev // lane_tile
    return pl.pallas_call(
        functools.partial(spread_kernel, row_dev),
        grid=(groups, tiles),
        in_specs=[
            pl.BlockSpec(memory_space=pltpu.SMEM),
            pl.BlockSpec((1, 2, slots_node, lane_tile), lambda i, t: (i, 0, 0, t)),
        ],
        out_specs=pl.BlockSpec((row_dev, lane_tile), lambda i, t: (0, i * tiles + t)),
        out_shape=jax.ShapeDtypeStruct((row_dev, groups * node_dev), bf16),
        compiler_params=params(),
        name="spread",
    )(base, slots)


def pool_kernel(table_ref, q_ref, bias_ref, spread_ref, slope_ref, pooled_ref, total_ref):
    step = pl.program_id(0)
    width = table_ref.shape[2]
    pre = bias_ref[...]
    for m in range(table_ref.shape[0]):
        pre = pre + dot(table_ref[m], q_ref[m * width : (m + 1) * width, :], (1, 0))
    hidden, slope = gelu_parts(pre)
    slope_ref[...] = slope.astype(bf16)
    part = dot(hidden.astype(bf16), spread_ref[...], (0, 0))

    @pl.when(step == 0)
    def _():
        total_ref[...] = part

    @pl.when(step > 0)
    def _():
        total_ref[...] += part

    @pl.when(step == pl.num_programs(0) - 1)
    def _():
        groups, _, node_dev = pooled_ref.shape
        for g in range(groups):
            pooled_ref[g] = total_ref[:, g * node_dev : (g + 1) * node_dev].astype(bf16)


def pool(table4, q_low, bias, matrix, node_dev):
    sides, row_dev, width = table4.shape
    nodes = matrix.shape[1]
    columns = q_low.shape[1]
    block = min(row_dev, 512 * 2048 // nodes)
    groups = nodes // node_dev
    return pl.pallas_call(
        pool_kernel,
        grid=(row_dev // block,),
        in_specs=[
            pl.BlockSpec((sides, block, width), lambda i: (0, i, 0)),
            pl.BlockSpec(q_low.shape, lambda i: (0, 0)),
            pl.BlockSpec((1, columns), lambda i: (0, 0)),
            pl.BlockSpec((block, nodes), lambda i: (i, 0)),
        ],
        out_specs=(
            pl.BlockSpec((block, columns), lambda i: (i, 0)),
            pl.BlockSpec((groups, columns, node_dev), lambda i: (0, 0, 0)),
        ),
        out_shape=(
            jax.ShapeDtypeStruct((row_dev, columns), bf16),
            jax.ShapeDtypeStruct((groups, columns, node_dev), bf16),
        ),
        scratch_shapes=[pltpu.VMEM((columns, nodes), f32)],
        compiler_params=params(),
        name="pool",
    )(table4, q_low, bias.reshape(1, columns), matrix)


def combine_kernel(self_ref, pooled_ref, w_ref, bias_ref, cotangent_ref, pre_ref, sums_ref):
    sides, nodes, width = self_ref.shape
    pre = bias_ref[...]
    for m in range(sides):
        pre = pre + dot(self_ref[m], w_ref[m * width : (m + 1) * width, :], (1, 0))
    for m in range(sides):
        at = (sides + m) * width
        pre = pre + dot(pooled_ref[m], w_ref[at : at + width, :], (0, 0))
    pre_ref[...] = pre
    activated, _ = gelu_parts(pre)
    sums_ref[:, 0:1] = jnp.sum(activated * activated, axis=1, keepdims=True)
    sums_ref[:, 1:2] = jnp.sum(activated * cotangent_ref[...], axis=1, keepdims=True)


def combine(self4, pooled4, w_low, bias, cotangent):
    nodes, columns = cotangent.shape
    return pl.pallas_call(
        combine_kernel,
        out_shape=(
            jax.ShapeDtypeStruct((nodes, columns), f32),
            jax.ShapeDtypeStruct((nodes, 2), f32),
        ),
        compiler_params=params(),
        name="combine",
    )(self4, pooled4, w_low, bias.reshape(1, columns), cotangent)


def combine_back_kernel(
    node_total, pre_ref, sums_ref, cotangent_ref, self_ref, pooled_ref, w_ref, emb_ref, w_grad_ref, wb_grad_ref, joined_ref
):
    sides, nodes, width = self_ref.shape
    activated, slope = gelu_parts(pre_ref[...])
    scale = lax.rsqrt(sums_ref[:, 0:1] + epsilon)
    cross = sums_ref[:, 1:2]
    emb_ref[...] = activated * scale
    grad_act = (
        cotangent_ref[...] * scale
        - activated * (cross * scale * scale * scale)
        + (2.0 * penalty_rate / node_total) * activated
    )
    grad = (grad_act * slope).astype(bf16)
    wb_grad_ref[...] = jnp.sum(grad.astype(f32), axis=0, keepdims=True)
    for m in range(sides):
        at = m * width
        w_grad_ref[at : at + width, :] = dot(self_ref[m], grad, (0, 0)).astype(w_grad_ref.dtype)
        joined_ref[0, m] = dot(grad, w_ref[at : at + width, :], (1, 1)).astype(joined_ref.dtype)
    for m in range(sides):
        at = (sides + m) * width
        w_grad_ref[at : at + width, :] = dot(pooled_ref[m], grad, (1, 0)).astype(w_grad_ref.dtype)
        joined_ref[1, m] = dot(grad, w_ref[at : at + width, :], (1, 1)).astype(joined_ref.dtype)


def combine_back(node_total, pre, sums, cotangent, self4, pooled4, w_low):
    nodes, columns = cotangent.shape
    sides, _, width = self4.shape
    return pl.pallas_call(
        functools.partial(combine_back_kernel, node_total),
        out_shape=(
            jax.ShapeDtypeStruct((nodes, columns), f32),
            jax.ShapeDtypeStruct(w_low.shape, f32),
            jax.ShapeDtypeStruct((1, columns), f32),
            jax.ShapeDtypeStruct((2, sides, nodes, width), bf16),
        ),
        compiler_params=params(),
        name="combine_back",
    )(pre, sums, cotangent, self4, pooled4, w_low)


def rows_back_kernel(matrix_ref, pooled_ref, slope_ref, table_ref, grad_ref, q_grad_ref, qb_grad_ref, total_ref):
    step = pl.program_id(0)
    sides, _, width = table_ref.shape
    grad = dot(matrix_ref[...], pooled_ref[...], (1, 0)) * slope_ref[...].astype(f32)
    column_sums = jnp.sum(grad, axis=0, keepdims=True)
    grad = grad.astype(bf16)
    grad_ref[...] = grad

    @pl.when(step == 0)
    def _():
        qb_grad_ref[...] = column_sums
        total_ref[...] = jnp.zeros_like(total_ref)

    @pl.when(step > 0)
    def _():
        qb_grad_ref[...] += column_sums

    for m in range(sides):
        total_ref[:, m * width : (m + 1) * width] += dot(grad, table_ref[m], (0, 0))

    @pl.when(step == pl.num_programs(0) - 1)
    def _():
        q_grad_ref[...] = total_ref[...].T


def rows_back(matrix, grad_pooled, slope, table4):
    sides, row_dev, width = table4.shape
    nodes = matrix.shape[1]
    columns = slope.shape[1]
    block = min(row_dev, 512 * 2048 // nodes)
    return pl.pallas_call(
        rows_back_kernel,
        grid=(row_dev // block,),
        in_specs=[
            pl.BlockSpec((block, nodes), lambda i: (i, 0)),
            pl.BlockSpec(grad_pooled.shape, lambda i: (0, 0)),
            pl.BlockSpec((block, columns), lambda i: (i, 0)),
            pl.BlockSpec((sides, block, width), lambda i: (0, i, 0)),
        ],
        out_specs=(
            pl.BlockSpec((block, columns), lambda i: (i, 0)),
            pl.BlockSpec((sides * width, columns), lambda i: (0, 0)),
            pl.BlockSpec((1, columns), lambda i: (0, 0)),
        ),
        out_shape=(
            jax.ShapeDtypeStruct((row_dev, columns), bf16),
            jax.ShapeDtypeStruct((sides * width, columns), f32),
            jax.ShapeDtypeStruct((1, columns), f32),
        ),
        scratch_shapes=[pltpu.VMEM((columns, sides * width), f32)],
        compiler_params=params(),
        name="rows_back",
    )(matrix, grad_pooled, slope, table4)


def table_back_kernel(grad_ref, q_ref, self_ref, out_ref):
    total = dot(grad_ref[0], q_ref[0], (1, 1))
    for m in range(1, grad_ref.shape[0]):
        total = total + dot(grad_ref[m], q_ref[m], (1, 1))
    out_ref[...] = total

    @pl.when(pl.program_id(0) == 0)
    def _():
        out_ref[0 : self_ref.shape[0], :] += self_ref[...].astype(f32)


def table_back(grad4, q_rows, grad_self):
    sides, row_dev, columns = grad4.shape
    width = q_rows.shape[1]
    block = min(row_dev, 512)
    return pl.pallas_call(
        table_back_kernel,
        grid=(row_dev // block,),
        in_specs=[
            pl.BlockSpec((sides, block, columns), lambda i: (0, i, 0)),
            pl.BlockSpec(q_rows.shape, lambda i: (0, 0, 0)),
            pl.BlockSpec(grad_self.shape, lambda i: (0, 0)),
        ],
        out_specs=pl.BlockSpec((block, width), lambda i: (i, 0)),
        out_shape=jax.ShapeDtypeStruct((row_dev, width), f32),
        compiler_params=params(),
        name="table_back",
    )(grad4, q_rows, grad_self)


def shards(table, q_weight, q_bias, w_weight, w_bias, neighbours, counts, importance, cotangent):
    groups = lax.axis_size("dp")
    sides = lax.axis_size("mp")
    row_dev, width = table.shape
    node_dev, slots_node = neighbours.shape
    node_total = node_dev * groups
    columns = q_weight.shape[1]

    present = jnp.arange(slots_node, dtype=jnp.int32)[None, :] < counts[:, None]
    raw_weights = jnp.where(present, importance, 0.0)
    weights = raw_weights / jnp.sum(raw_weights, axis=1, keepdims=True)
    slots = lax.all_gather(jnp.stack([neighbours.astype(f32).T, weights.T]), "dp")
    table4 = lax.all_gather(table.astype(bf16), "mp")
    q_low = q_weight.astype(bf16)
    w_low = w_weight.astype(bf16)
    q_rows = lax.all_to_all(q_low.reshape(sides, width, columns), "mp", split_axis=0, concat_axis=0, tiled=True)

    base = (lax.axis_index("dp") * row_dev).astype(jnp.int32).reshape(1)
    matrix = spread(base, slots, row_dev)
    slope, pooled_part = pool(table4, q_low, q_bias, matrix, node_dev)
    pooled = lax.psum_scatter(pooled_part, "dp", scatter_dimension=0)
    pooled4 = lax.all_gather(pooled, "mp")
    self4 = table4[:, :node_dev]
    pre, sums = combine(self4, pooled4, w_low, w_bias, cotangent)
    sums = lax.psum(sums, "mp")
    embedding, w_grad, wb_grad, joined_part = combine_back(node_total, pre, sums, cotangent, self4, pooled4, w_low)
    grad_pooled = lax.psum_scatter(joined_part[1], "mp", scatter_dimension=0)
    grad_self = lax.psum_scatter(joined_part[0], "mp", scatter_dimension=0)
    grad_pooled = lax.all_gather(grad_pooled, "dp", axis=0, tiled=True)
    grad, q_grad, qb_grad = rows_back(matrix, grad_pooled, slope, table4)
    grad4 = lax.all_gather(grad, "mp")
    table_grad = table_back(grad4, q_rows, grad_self)
    q_grad, qb_grad, w_grad, wb_grad, square_total = lax.psum(
        (q_grad, qb_grad[0], w_grad, wb_grad[0], jnp.sum(sums[:, 0])), "dp"
    )
    penalty = penalty_rate * square_total / node_total
    return (embedding, table_grad, q_grad, qb_grad, w_grad, wb_grad, penalty)


def solution(mesh):
    placed = (
        P("dp", "mp"),
        P(None, "mp"),
        P("mp"),
        P(None, "mp"),
        P("mp"),
        P("dp", None),
        P("dp"),
        P("dp", None),
        P("dp", "mp"),
    )
    return jax.shard_map(
        shards,
        mesh=mesh,
        in_specs=placed,
        out_specs=(
            P("dp", "mp"),
            P("dp", "mp"),
            P(None, "mp"),
            P("mp"),
            P(None, "mp"),
            P("mp"),
            P(),
        ),
        check_vma=False,
    )
```

time: 1500 us -> 502 us (0.33)
  local copies, waits for them, and re-layouts: 306 us -> 9.02 us
  waiting for transfers between devices: 584 us -> 289 us
  other arithmetic: 237 us -> 6.34 us
  blocking collectives: 265 us -> 71.8 us
  Pallas kernels: 0 us -> 100 us
  matrix products: 53.5 us -> 0 us
  starting transfers between devices: 20.1 us -> 3.76 us
    psum x2, blocking collectives: 251 us -> 30.6 us  [the longest x1 17.5 us: shards(): lax.psum((q_grad, qb_grad[0], w_grad, wb_grad[0], jnp.sum(sums[:, 0])), '...]
    all_to_all x3 -> x1, waiting for transfers between devices: 212 us -> 0.01 us  [shards(): lax.all_to_all(q_low.reshape(sides, width, columns), 'mp', split_axis=0,...]
    gather x18 -> x0, local copies, waits for them, and re-layouts: 164 us -> none  [the longest x1 65.9 us: shards(): sorted_owner = owner_index[order]]
    reduce_scatter x3, waiting for transfers between devices: 213 us -> 81.7 us  [the longest x1 60.9 us: shards(): pooled = lax.psum_scatter(pooled_part, 'dp', scatter_dimension=0)]
    psum x1, waiting for transfers between devices: 0.01 us -> 123 us  [shards(): lax.psum((q_grad, qb_grad[0], w_grad, wb_grad[0], jnp.sum(sums[:, 0])), '...]
    scatter-add x2 -> x0, other arithmetic: 120 us -> none  [the longest x1 118 us: shards(): table_grad = jnp.zeros((row_dev, grad_rows.shape[0]), jnp.float32).at[ser...]
    pallas_call x0 -> x6, Pallas kernels: none -> 100 us  [the longest x1 45.4 us: spread(): pl.pallas_call(functools.partial(spread_kernel, row_dev), grid=(groups, t...]
    scatter x2 -> x0, local copies, waits for them, and re-layouts: 94.6 us -> none  [the longest x1 47.3 us: shards(): jnp.zeros((slot_count,), jnp.int32).at[order]]
  transfers between devices with their start and end apart: 8 -> 8, of which waited for: 5 -> 5; matrix products, arithmetic and copies ran while one was open for 10% -> 1% of each run, Pallas kernels for 0% -> 15%
where the time goes in v1:
time: 502 us; the launch traced here: 497 us
  waiting for transfers between devices  289 us (58%)
  Pallas kernels  100 us (20%)
  blocking collectives  71.8 us (14%)
  between operations  16 us (3%)
  local copies, waits for them, and re-layouts  9.02 us (2%)
  other arithmetic  6.34 us (1%)
    psum x1, waiting for transfers between devices, shards(): lax.psum((q_grad, qb_grad[0], w_grad, wb_grad[0], jnp.sum(sums[:, 0])), '...  123 us
    reduce_scatter x1, waiting for transfers between devices, shards(): pooled = lax.psum_scatter(pooled_part, 'dp', scatter_dimension=0)  60.9 us
    pallas_call x1, Pallas kernels, spread(): pl.pallas_call(functools.partial(spread_kernel, row_dev), grid=(groups, t...  45.4 us
    all_gather x1, waiting for transfers between devices, shards(): grad4 = lax.all_gather(grad, 'mp')  43.3 us
    all_gather x1, waiting for transfers between devices, shards(): grad_pooled = lax.all_gather(grad_pooled, 'dp', axis=0, tiled=True)  39.6 us
    all_gather x1, blocking collectives, shards(): lax.all_gather(jnp.stack([neighbours.astype(f32).T, weights.T]), 'dp')  33.2 us
    reduce_scatter x1, waiting for transfers between devices, shards(): grad_pooled = lax.psum_scatter(joined_part[1], 'mp', scatter_dimension=0)  20.7 us
    pallas_call x1, Pallas kernels, pool(): pl.pallas_call(pool_kernel, grid=(row_dev // block,), in_specs=[pl.BlockS...  19.9 us
  transfers between devices with their start and end apart: 8, of which 5 were waited for; matrix products, arithmetic and copies ran while one was open for 1% of the time, Pallas kernels for 15%

profile of v1, /device:TPU:12, one launch (start us, length us, event | category | flops | bytes accessed | tf_op | source)
XLA Modules:
  0.0 496.6 jit_solution(14218764724512389667)
XLA Ops:
  7.2 0.0 all-gather.8.cloned.1.call-start
  7.2 3.7 convert_element_type.12
  10.9 0.0 copy-start.4
  10.9 0.0 copy-start.5
  10.9 0.0 copy-start.7
  10.9 0.0 copy-start.6
  10.9 0.0 all-gather.8.cloned.1.call-update
  11.0 0.0 reduce-scatter.4.cloned.1.call-start
  11.0 1.1 copy-done.4
  12.1 0.9 convert_element_type.13.q_ref
  13.0 0.0 copy-done.5
  13.0 0.0 copy-done.7
  13.0 0.0 copy-done.6
  13.1 33.2 %all-gather.1 = f32[16,50,256]{2,1,0:T(8,128)} all-gather(f32[2,50,256]{2,1,0:T(8,128)S(1)} %pad_maximum_fusion), channel_id=3, replica_groups=mesh['dp'=8,'mp'=4] {'dp'}, dimensions={0}, use_global_device_ids=true | all-gather | bytes 921600 | tf_op jit(solution)/shard_map/all_gather | solution.py:299
  46.3 45.4 %spread.1.spread_ref.matrix_ref = bf16[4096,2048]{1,0:T(8,128)(2,1)} custom-call(s32[1]{0:T(128)} %bitcast.2.base_ref, f32[8,2,50,256]{3,2,1,0:T(8,128)} %bitcast.27), custom_call_target="tpu_custom_call" | custom-call | tf_op jit(solution)/shard_map/spread/pallas_call | solution.py:67
  91.7 0.0 all-gather.8.cloned.1.call-done
  91.7 0.0 copy-start.1
  91.7 19.9 %pool.1 = (bf16[4096,256]{1,0:T(8,128)(2,1)}, bf16[8,256,256]{2,1,0:T(8,128)(2,1)}) custom-call(bf16[4,4096,256]{2,1,0:T(8,128)(2,1)} %bitcast.23, bf16[1024,256]{1,0:T(8,128)(2,1)} %convert_element_type.13.q_ref, f32[1,256]{1,0:T(1,128)} %bitcast.30, bf16[4096,2048]{1,0:T(8,128)(2,1)} %spread.1.spread_ref.matrix_ref), custom_call_target="tpu_custom_call" | custom-call | tf_op jit(solution)/shard_map/pool/pallas_call | solution.py:112
  111.5 0.0 reduce-scatter.4.cloned.1.call-update
  111.5 0.0 reduce-scatter.6.cloned.1.call-start
  111.6 0.0 copy-done.1
  111.6 1.1 convert_element_type.15.w_ref
  112.7 1.9 slice.16.self_ref
  114.6 60.9 %reduce-scatter.4.cloned.1.call-done = bf16[1,256,256]{2,1,0:T(8,128)(2,1)} async-done(((bf16[8,256,256]{2,1,0:T(8,128)(2,1)}), bf16[1,256,256]{2,1,0:T(8,128)(2,1)}) %reduce-scatter.4.cloned.1.call-update) | async-done | bytes 131088 | tf_op jit(solution)/shard_map/reduce_scatter | solution.py:308
  175.5 8.1 %all_gather.28.pooled_ref = bf16[4,256,256]{2,1,0:T(8,128)(2,1)} all-gather(bf16[1,256,256]{2,1,0:T(8,128)(2,1)} %reduce-scatter.4.cloned.1.call-done), channel_id=1, replica_groups=mesh['dp'=8,'mp'=4] {'mp'}, dimensions={0}, use_global_device_ids=true | all-gather | bytes 655360 | tf_op jit(solution)/shard_map/all_gather | solution.py:309
  183.6 2.8 combine.1
  186.4 13.1 %psum.42.sums_ref = f32[256,2]{1,0:T(8,128)} all-reduce(f32[256,2]{1,0:T(8,128)} %get-tuple-element.20), channel_id=1, replica_groups=mesh['dp'=8,'mp'=4] {'mp'}, use_global_device_ids=true, to_apply=%region_2.3 | all-reduce | flops 512 | bytes 4096 | tf_op jit(solution)/shard_map/psum | solution.py:312
  199.5 4.4 combine_back.1
  203.9 2.2 slice_bitcast_fusion
  206.1 0.0 reduce-scatter.6.cloned.1.call-update
  206.2 0.0 all-gather.10.cloned.1.call-start
  206.2 20.7 %reduce-scatter.6.cloned.1.call-done = bf16[1,256,256]{2,1,0:T(8,128)(2,1)} async-done(((bf16[4,256,256]{2,1,0:T(8,128)(2,1)}), bf16[1,256,256]{2,1,0:T(8,128)(2,1)}) %reduce-scatter.6.cloned.1.call-update) | async-done | bytes 131088 | tf_op jit(solution)/shard_map/reduce_scatter | solution.py:314
  226.9 0.0 all-gather.10.cloned.1.call-update
  227.0 0.0 reduce-scatter.8.cloned.1.call-start
  227.0 0.5 reduce-scatter.8.cloned.1.call-update
  227.6 0.0 all-gather.12.cloned.1.call-start
  227.6 39.6 %all-gather.10.cloned.1.call-done = bf16[1,2048,256]{2,1,0:T(8,128)(2,1)} async-done(((bf16[1,256,256]{2,1,0:T(8,128)(2,1)}), bf16[1,2048,256]{2,1,0:T(8,128)(2,1)}) %all-gather.10.cloned.1.call-update) | async-done | bytes 1048592 | tf_op jit(solution)/shard_map/all_gather | solution.py:316
  267.2 18.6 %rows_back.1 = (bf16[4096,256]{1,0:T(8,128)(2,1)}, f32[1024,256]{1,0:T(8,128)}, f32[1,256]{1,0:T(1,128)}) custom-call(bf16[4096,2048]{1,0:T(8,128)(2,1)} %spread.1.spread_ref.matrix_ref, bf16[2048,256]{1,0:T(8,128)(2,1)} %bitcast.28, bf16[4096,256]{1,0:T(8,128)(2,1)} %get-tuple-element.23.slope_ref, bf16[4,4096,256]{2,1,0:T(8,128)(2,1)} %bitcast.25), custom_call_target="tpu_custom_call" | custom-call | tf_op jit(solution)/shard_map/rows_back/pallas_call | solution.py:233
  285.9 0.0 all-gather.12.cloned.1.call-update
  285.9 0.0 all-reduce.4.cloned.1.call-start
  285.9 0.0 copy-start.3
  286.0 0.0 copy-start.8
  286.0 0.0 copy-start.9
  286.0 0.7 all-reduce.4.cloned.1.call-update
  286.6 3.5 all-to-all-start
  290.1 0.0 copy-done.3
  290.1 0.6 slice_reduce_fusion
  290.8 0.0 copy-done.8
  290.8 0.0 copy-done.9
  290.8 17.5 %all-reduce = (f32[256]{0:T(256)}, f32[256]{0:T(256)}, f32[]{:T(128)}) all-reduce(f32[256]{0:T(256)S(1)} %bitcast.33, f32[256]{0:T(256)S(1)} %bitcast.32, f32[]{:T(128)} %slice_reduce_fusion), channel_id=1, replica_groups=mesh['dp'=8,'mp'=4] {'dp'}, use_global_device_ids=true, to_apply=%region_6.7 | all-reduce | flops 513 | bytes 4104 | tf_op jit(solution)/shard_map/psum | solution.py:320
  308.9 0.0 all-to-all-done.q_ref
  308.9 0.0 copy-start
  308.9 0.0 reduce-scatter.8.cloned.1.call-done
  309.0 43.3 %all-gather.12.cloned.1.call-done = bf16[16384,256]{1,0:T(8,128)(2,1)} async-done(((bf16[4096,256]{1,0:T(8,128)(2,1)}), bf16[16384,256]{1,0:T(8,128)(2,1)}) %all-gather.12.cloned.1.call-update) | async-done | bytes 8388624 | tf_op jit(solution)/shard_map/all_gather | solution.py:318
  352.3 0.0 copy-done
  352.3 9.2 %table_back.1 = f32[4096,256]{1,0:T(8,128)} custom-call(bf16[4,4096,256]{2,1,0:T(8,128)(2,1)} %bitcast.26, bf16[4,256,256]{2,1,0:T(8,128)(2,1)} %copy-done, bf16[256,256]{1,0:T(8,128)(2,1)} %bitcast.29), custom_call_target="tpu_custom_call" | custom-call | tf_op jit(solution)/shard_map/table_back/pallas_call | solution.py:273
  361.4 123.5 %all-reduce.4.cloned.1.call-done = (f32[1024,256]{1,0:T(8,128)}, f32[2048,256]{1,0:T(8,128)}) async-done(((f32[1024,256]{1,0:T(8,128)}, f32[2048,256]{1,0:T(8,128)}), (f32[1024,256]{1,0:T(8,128)}, f32[2048,256]{1,0:T(8,128)})) %all-reduce.4.cloned.1.call-update) | async-done | bytes 3145744 | tf_op jit(solution)/shard_map/psum | solution.py:320
  484.9 0.0 copy-start.2
  484.9 2.4 copy.18
  487.3 0.0 copy-done.2
  487.3 1.3 copy.19
  (4 shorter events, 0.1 us)
Async XLA Ops:
  7.2 84.5 %all-gather.8.cloned.1.call-start = ((), (), s32[]{:S(2)}) async-start(), calls=%async_computation.7 | async-start | bytes 10485760 | tf_op jit(solution)/shard_map/all_gather | solution.py:300
  10.9 1.2 copy-start.4
  10.9 2.1 copy-start.5
  10.9 2.1 copy-start.7
  10.9 2.1 copy-start.6
  11.0 164.5 %reduce-scatter.4.cloned.1.call-start = ((), (), s32[]{:S(2)}) async-start(), calls=%async_computation.4 | async-start | bytes 1179648 | tf_op jit(solution)/shard_map/reduce_scatter | solution.py:308
  91.7 19.9 %copy-start.1 = (f32[2048,256]{1,0:T(8,128)S(1)}, f32[2048,256]{1,0:T(8,128)}, u32[]{:S(2)}) copy-start(f32[2048,256]{1,0:T(8,128)} %param.12) | copy-start | bytes 6291460
  111.5 115.4 %reduce-scatter.6.cloned.1.call-start = ((), (), s32[]{:S(2)}) async-start(), calls=%async_computation.5 | async-start | bytes 655360 | tf_op jit(solution)/shard_map/reduce_scatter | solution.py:314
  206.2 61.1 %all-gather.10.cloned.1.call-start = ((), (), s32[]{:S(2)}) async-start(), calls=%async_computation.8 | async-start | bytes 1179648 | tf_op jit(solution)/shard_map/all_gather | solution.py:316
  227.0 82.0 %reduce-scatter.8.cloned.1.call-start = ((), (), s32[]{:S(2)}) async-start(), calls=%async_computation.6 | async-start | bytes 655360 | tf_op jit(solution)/shard_map/reduce_scatter | solution.py:315
  227.6 124.7 %all-gather.12.cloned.1.call-start = ((), (), s32[]{:S(2)}) async-start(), calls=%async_computation.9 | async-start | bytes 10485760 | tf_op jit(solution)/shard_map/all_gather | solution.py:318
  285.9 199.0 %all-reduce.4.cloned.1.call-start = ((), (), s32[]{:S(2)}) async-start(), calls=%async_computation.10 | async-start | bytes 6291456 | tf_op jit(solution)/shard_map/psum | solution.py:320
  285.9 4.2 copy-start.3
  286.0 4.8 copy-start.8
  286.0 4.8 copy-start.9
  286.6 22.3 %all-to-all-start = ((bf16[4,256,256]{2,1,0:T(8,128)(2,1)}), bf16[4,256,256]{2,1,0:T(8,128)(2,1)S(1)}, u32[]{:S(2)}, u32[]{:S(2)}) async-start(bf16[4,256,256]{2,1,0:T(8,128)(2,1)} %bitcast.12), calls=%async_computation.2 | async-start | bytes 1048576 | tf_op jit(solution)/shard_map/all_to_all | solution.py:303
  308.9 43.4 %copy-start = (bf16[4,256,256]{2,1,0:T(8,128)(2,1)}, bf16[4,256,256]{2,1,0:T(8,128)(2,1)S(1)}, u32[]{:S(2)}) copy-start(bf16[4,256,256]{2,1,0:T(8,128)(2,1)S(1)} %all-to-all-done.q_ref) | copy-start | bytes 1572868
  484.9 2.4 copy-start.2
Sparse Core Ops, SparseCore 0:
  11.1 59.3 all-gather.7
  111.7 63.7 reduce-scatter.3
  206.3 20.6 reduce-scatter.5
  228.9 38.2 all-gather.9
  269.6 22.2 reduce-scatter.7
  294.0 58.2 all-gather.11
  356.9 127.9 all-reduce.3

commit v2 on v0

v2 whole, which is shorter than its diff:
```python
import functools

import jax
import jax.numpy as jnp
from jax import lax
from jax.experimental import pallas as pl
from jax.experimental.pallas import tpu as pltpu
from jax.sharding import PartitionSpec as P

epsilon = 1e-06
penalty_rate = 0.01
bf16, f32, i32, i16 = jnp.bfloat16, jnp.float32, jnp.int32, jnp.int16
bucket_rows = 256
lane_tile = 128
weight_unit = 32767.0
code_step = 64
extra_rows = 16
mib = 1024 * 1024
expected_us = dict(
    slots=3,
    low=4,
    spread=20,
    hidden_both=1,
    hidden_slope=5,
    pool=5,
    self_half=3,
    combine=4,
    w_back=4,
    add=2,
    add_pairs=2,
    collect=2,
    stack=1,
    widen=2,
    rows_back_q=13,
    rows_back=9,
    table_back=8,
)


def dot(a, b, contract):
    return lax.dot_general(a, b, ((contract[:1], contract[1:]), ((), ())), preferred_element_type=f32)


def gelu_parts(values):
    c = 0.7978845608028654
    squared = values * values
    t = jnp.tanh(c * values * (1.0 + 0.044715 * squared))
    half = 0.5 * (1.0 + t)
    slope = half + 0.5 * values * (1.0 - t * t) * (c * (1.0 + 3 * 0.044715 * squared))
    return values * half, slope


def size(dims, dtype):
    rows = dims[-2] if len(dims) > 1 else 1
    rest = 1
    for d in dims[:-2]:
        rest *= d
    return rest * (-(-rows // 16) * 16) * (-(-dims[-1] // 128) * 128) * jnp.dtype(dtype).itemsize


def far(array):
    return pltpu.with_memory_space_constraint(array, pltpu.HBM)


def far_shape(dims, dtype):
    return pltpu.HBM(dims, dtype)


def call(kernel, name, operands, outs, grid=(1,), scratch=(), after=(), spare=8):
    specs, arrays, need = [], [], 0
    for operand in operands:
        array, spec = operand if isinstance(operand, tuple) else (operand, whole(operand))
        specs.append(spec)
        arrays.append(array)
        if spec is not smem:
            need += (2 if isinstance(operand, tuple) else 1) * size(spec.block_shape, array.dtype)
    for spec, out in outs:
        need += 2 * size(spec.block_shape, out.dtype)
    for item in scratch:
        need += size(item.shape, item.dtype)
    count = len(arrays)
    inner = lambda *refs: kernel(*refs[:count], *refs[count + len(after) :])
    return pl.pallas_call(
        inner,
        grid=grid,
        in_specs=specs + [pl.BlockSpec(memory_space=pl.ANY)] * len(after),
        out_specs=[o[0] for o in outs],
        out_shape=[o[1] for o in outs],
        scratch_shapes=list(scratch),
        compiler_params=pltpu.CompilerParams(vmem_limit_bytes=need + spare * mib),
        cost_estimate=pl.CostEstimate(
            flops=int(expected_us[name] * 1.15e9), bytes_accessed=int(expected_us[name] * 3.69e6), transcendentals=0
        ),
        name=name,
    )(*arrays, *after)


def full(dims, dtype, kind=jax.ShapeDtypeStruct):
    return whole(shape(dims, dtype)), kind(dims, dtype)


def shape(dims, dtype):
    return jax.ShapeDtypeStruct(dims, dtype)


def whole(array):
    return pl.BlockSpec(array.shape, lambda *_: (0,) * array.ndim)


smem = pl.BlockSpec(memory_space=pltpu.SMEM)


def swap(array, axis, bits):
    size = lax.axis_size(axis)
    return lax.ppermute(array, axis, [(i, i ^ bits) for i in range(size)])


def halves(values):
    high = values.astype(bf16)
    return high, (values - high.astype(f32)).astype(bf16)


def exchange(array, axes):
    return lax.all_to_all(array, axes, split_axis=0, concat_axis=0, tiled=True)


def rows_at(ref, start, size):
    return ref.at[pl.ds(pl.multiple_of(start, size), size)]


def row_blocks(block, columns):
    return pl.BlockSpec((block, columns), lambda i: (i, 0))


def chunk_spec(block, columns, first, count):
    return pl.BlockSpec((block, columns), lambda i: (jnp.clip(i - first, 0, count - 1), 0))


def chunk_specs(chunks, block):
    specs, first = [], 0
    for a in chunks:
        count = a.shape[0] // block
        specs.append(chunk_spec(block, a.shape[1], first, count))
        first += count
    return specs


def low_kernel(first, table_ref, q_ref, w_ref, a_ref, b_ref, q_low_ref, self_ref, pooled_ref):
    step = pl.program_id(0)
    low = table_ref[...].astype(bf16)
    q_low_ref[...] = q_ref[...].astype(bf16)
    w_low = w_ref[...].astype(bf16)

    @pl.when(step < first)
    def _():
        a_ref[...] = low

    @pl.when(step >= first)
    def _():
        b_ref[...] = low

    @pl.when(step < 2)
    def _():
        self_ref[...] = w_low

    @pl.when(step >= 2)
    def _():
        pooled_ref[...] = w_low


def low_all(table, q_weight, w_weight, cut):
    rows, columns = table.shape
    block = rows // 4
    first = cut // block
    q_rows, w_rows = q_weight.shape[0], w_weight.shape[0]
    return call(
        functools.partial(low_kernel, first),
        "low",
        [
            (far(table), row_blocks(block, columns)),
            (far(q_weight), row_blocks(q_rows // 4, columns)),
            (far(w_weight), row_blocks(w_rows // 4, columns)),
        ],
        [
            (chunk_spec(block, columns, 0, first), far_shape((cut, columns), bf16)),
            (chunk_spec(block, columns, first, 4 - first), far_shape((rows - cut, columns), bf16)),
            (row_blocks(q_rows // 4, columns), far_shape((q_rows, columns), bf16)),
            (chunk_spec(w_rows // 4, columns, 0, 2), far_shape((w_rows // 2, columns), bf16)),
            (chunk_spec(w_rows // 4, columns, 2, 2), far_shape((w_rows // 2, columns), bf16)),
        ],
        grid=(4,),
    )


def gate_kernel(*refs):
    del refs


def gate(array, after):
    return pl.pallas_call(
        gate_kernel,
        in_specs=[pl.BlockSpec(memory_space=pl.ANY)] * (1 + len(after)),
        out_specs=pl.BlockSpec(memory_space=pl.ANY),
        out_shape=shape(array.shape, array.dtype),
        input_output_aliases={0: 0},
        compiler_params=pltpu.CompilerParams(vmem_limit_bytes=mib),
        cost_estimate=pl.CostEstimate(flops=1, bytes_accessed=1, transcendentals=0),
        name="gate",
    )(far(array), *map(far, after))


def slots_kernel(row_dev, place_ref, ids_ref, counts_ref, importance_ref, out_ref):
    del place_ref
    ids = ids_ref[...]
    index = lax.broadcasted_iota(i32, ids.shape, 0)
    raw = jnp.where(index < counts_ref[...], importance_ref[...], 0.0)
    weight = raw / jnp.sum(raw, axis=0, keepdims=True)
    bucket = jnp.where(weight > 0.0, ids // bucket_rows, -1)
    within = ids - (ids // bucket_rows) * bucket_rows
    merged = jnp.zeros_like(weight)
    rank = jnp.zeros_like(bucket)
    for k in range(ids.shape[0]):
        merged = merged + jnp.where(ids == ids[k : k + 1, :], weight[k : k + 1, :], 0.0)
        rank = rank + jnp.where((bucket == bucket[k : k + 1, :]) & (index > k), 1, 0)
    amount = jnp.round(merged * weight_unit).astype(i32)
    per = row_dev // bucket_rows
    for d in range(out_ref.shape[0]):
        mine = (bucket >= d * per) & (bucket < (d + 1) * per)
        out_ref[d, 0] = jnp.where(mine, (bucket - d * per) * code_step + rank, -1).astype(i16)
        out_ref[d, 1] = within.astype(i16)
        out_ref[d, 2] = amount.astype(i16)


def make_slots(place, neighbours, counts, importance, row_dev, groups, after=()):
    node_dev, slots_node = neighbours.shape
    return call(
        functools.partial(slots_kernel, row_dev),
        "slots",
        [(place, smem), far(neighbours.T), far(counts.reshape(1, node_dev)), far(importance.T)],
        [full((groups, 3, slots_node, node_dev), i16)],
        after=after,
    )[0]


def spread_kernel(slots_ref, out_ref, all_ref, row_ref, amount_ref):
    _, _, slots_node, lanes = slots_ref.shape
    buckets = out_ref.shape[1] // bucket_rows
    tiles = lanes // lane_tile
    codes = slots_ref[0, 0].astype(i32)
    depth = jnp.max(jnp.where(codes >= 0, (codes & (code_step - 1)) + 1, 0).astype(f32)).astype(i32)
    for t in range(tiles):
        at = slice(t * lane_tile, (t + 1) * lane_tile)
        all_ref[t, 0] = codes[:, at].astype(f32)
        all_ref[t, 1] = slots_ref[0, 1, :, at].astype(i32).astype(f32)
        all_ref[t, 2] = slots_ref[0, 2, :, at].astype(i32).astype(f32) * (1.0 / weight_unit)
    eight = lax.broadcasted_iota(i32, (8, lane_tile), 0).astype(f32)

    def extract(t, first):
        target = eight + first
        for start in range(0, buckets, 8):
            some = range(start, min(start + 8, buckets))
            rows = [jnp.full((8, lane_tile), -1.0, f32) for _ in some]
            amounts = [jnp.zeros((8, lane_tile), f32) for _ in some]
            for k in range(slots_node):
                code = jnp.broadcast_to(all_ref[t, 0, k : k + 1, :], (8, lane_tile))
                row = jnp.broadcast_to(all_ref[t, 1, k : k + 1, :], (8, lane_tile))
                amount = jnp.broadcast_to(all_ref[t, 2, k : k + 1, :], (8, lane_tile))
                for i, b in enumerate(some):
                    hit = code == target + float(b * code_step)
                    rows[i] = jnp.where(hit, row, rows[i])
                    amounts[i] = jnp.where(hit, amount, amounts[i])
            for i, b in enumerate(some):
                row_ref[t, b] = rows[i]
                amount_ref[t, b] = amounts[i]

    tall = (bucket_rows // 16, 16, lane_tile)
    row_index = (lax.broadcasted_iota(i32, tall, 0) * 16 + lax.broadcasted_iota(i32, tall, 1)).astype(f32).astype(bf16)

    def place_all(count, add):
        def one(b, carry):
            at = pl.ds(pl.multiple_of(b * bucket_rows, bucket_rows), bucket_rows)
            for t in range(tiles):
                lane = slice(t * lane_tile, (t + 1) * lane_tile)
                total = out_ref[0, at, lane].reshape(tall) if add else jnp.zeros(tall, bf16)
                for j in range(count):
                    row = jnp.broadcast_to(row_ref[t, b, j : j + 1, :], tall[1:]).astype(bf16)
                    amount = jnp.broadcast_to(amount_ref[t, b, j : j + 1, :], tall[1:]).astype(bf16)
                    total = jnp.where(row_index == row[None], amount[None], total)
                out_ref[0, at, lane] = total.reshape(bucket_rows, lane_tile)
            return carry

        lax.fori_loop(0, buckets, one, 0)

    for t in range(tiles):
        extract(t, 0.0)
    for low, high in ((0, 3), (4, 4), (5, 5), (6, 6), (7, slots_node)):

        @pl.when((depth >= low) & (depth <= high))
        def _():
            place_all(min(high, 8), False)

    def more(p, carry):
        for t in range(tiles):
            extract(t, (p * 8).astype(f32))
        place_all(8, True)
        return carry

    lax.fori_loop(1, (depth + 7) // 8, more, 0)


def spread(slots, row_dev):
    groups, _, slots_node, node_dev = slots.shape
    tiles = node_dev // lane_tile
    buckets = row_dev // bucket_rows
    return call(
        spread_kernel,
        "spread",
        [(slots, pl.BlockSpec((1, 3, slots_node, node_dev), lambda i: (i, 0, 0, 0)))],
        [(pl.BlockSpec((1, row_dev, node_dev), lambda i: (i, 0, 0)), shape((groups, row_dev, node_dev), bf16))],
        grid=(groups,),
        scratch=[
            pltpu.VMEM((tiles, 3, slots_node, lane_tile), f32),
            pltpu.VMEM((tiles, buckets, 8, lane_tile), f32),
            pltpu.VMEM((tiles, buckets, 8, lane_tile), f32),
        ],
    )[0]


def hidden_kernel(sides, want, place_ref, *refs):
    table, q_ref, bias_ref, outs = refs[:sides], refs[sides], refs[sides + 1], refs[sides + 2 :]
    width = table[0].shape[1]
    pre = bias_ref[...]
    for j in range(sides):
        pre = pre + dot(table[j][...], rows_at(q_ref, (place_ref[1] ^ j) * width, width)[...], (1, 0))
    value, slope = gelu_parts(pre)
    if want == "both":
        outs[0][...] = value.astype(bf16).T
    outs[-1][...] = slope.astype(bf16)


def hidden(place, table, q_low, bias, want, after=()):
    rows, width = table[0].shape
    columns = q_low.shape[1]
    sides = len(table)
    block = min(rows, 512)
    outs = [(row_blocks(block, columns), far_shape((rows, columns), bf16))]
    if want == "both":
        outs.insert(0, (pl.BlockSpec((columns, block), lambda i: (0, i)), shape((columns, rows), bf16)))
    return call(
        functools.partial(hidden_kernel, sides, want),
        "hidden_" + want,
        [(place, smem)]
        + [(far(a), row_blocks(block, width)) for a in table]
        + [far(q_low), far(bias.reshape(1, columns))],
        outs,
        grid=(rows // block,),
        after=after,
    )


def pool_kernel(last, hidden_ref, matrix_ref, *refs):
    for g in range(matrix_ref.shape[0]):
        total = dot(hidden_ref[...], matrix_ref[g], (1, 0))
        nodes = total.shape[1]
        at = slice(g * nodes, (g + 1) * nodes)
        if last:
            refs[1][at, :] = (refs[0][:, at] + total).T.astype(bf16)
        else:
            refs[0][:, at] = total


def pool(hidden_t, matrix, first, so_far, after=()):
    columns, rows = hidden_t.shape
    groups, _, node_dev = matrix.shape
    nodes = groups * node_dev
    last = so_far is not None
    total_block = pl.BlockSpec((columns, 2 * node_dev), lambda i: (0, i))
    return call(
        functools.partial(pool_kernel, last),
        "pool",
        [hidden_t, (matrix, pl.BlockSpec((2, rows, node_dev), lambda i: (i, first // rows, 0)))]
        + ([(so_far, total_block)] if last else []),
        [
            (row_blocks(2 * node_dev, columns), shape((nodes, columns), bf16))
            if last
            else (total_block, shape((columns, nodes), f32))
        ],
        grid=(groups // 2,),
        after=after,
    )[0]


def first_rows(table, nodes):
    return [(far(a), pl.BlockSpec((nodes, a.shape[1]), lambda *_: (0, 0))) for a in table]


def self_kernel(sides, place_ref, *refs):
    own, (w_ref, bias_ref, cotangent_ref), outs = refs[:sides], refs[sides : sides + 3], refs[sides + 3 : -1]
    pre_ref = refs[-1]
    width = own[0].shape[1]
    pre = bias_ref[...]
    for j in range(sides):
        pre = pre + dot(own[j][...], rows_at(w_ref, (place_ref[1] ^ j) * width, width)[...], (1, 0))
    pre_ref[...] = pre
    few, columns = outs[0].shape[0], pre.shape[1]
    for j in range(sides):
        at = (place_ref[1] ^ j) * few
        outs[j][:, 0:columns] = rows_at(pre_ref, at, few)[...]
        outs[j][:, columns:] = rows_at(cotangent_ref, at, few)[...]


def self_half(place, table, w_self, bias, cotangent, after=()):
    nodes, columns = cotangent.shape
    sides = len(table)
    return call(
        functools.partial(self_kernel, sides),
        "self_half",
        [(place, smem)] + first_rows(table, nodes) + [far(w_self), far(bias.reshape(1, columns)), far(cotangent)],
        [full((nodes // sides, 2 * columns), f32, far_shape)] * sides,
        scratch=[pltpu.VMEM((nodes, columns), f32)],
        after=after,
    )


def combine_kernel(node_total, sides, parts_ref, *refs):
    early, w_refs = refs[:sides], refs[sides : 2 * sides]
    grad_ref, late = refs[2 * sides], refs[2 * sides + 1 :]
    groups, _, few, columns = parts_ref.shape
    pooled = []
    for m in range(sides):
        total = parts_ref[0, m].astype(f32)
        for g in range(1, groups):
            total = total + parts_ref[g, m].astype(f32)
        pooled.append(total.astype(bf16))
    pooled = jnp.concatenate(pooled, axis=1)
    activated, slope, squares, cross = [], [], 0.0, 0.0
    for j in range(sides):
        pre = early[j][:, 0:columns] + dot(pooled, w_refs[j][...], (1, 0))
        a, s = gelu_parts(pre)
        activated.append(a)
        slope.append(s)
        squares = squares + jnp.sum(a * a, axis=1, keepdims=True)
        cross = cross + jnp.sum(a * early[j][:, columns:], axis=1, keepdims=True)
    scale = lax.rsqrt(squares + epsilon)
    pull = cross * scale * scale * scale
    grad_pooled = 0.0
    square_high, square_low = halves(jnp.sum(squares, axis=0, keepdims=True))
    index = lax.broadcasted_iota(i32, (extra_rows, late[0].shape[1]), 0)
    extra = jnp.where(
        index == 0, square_high.astype(f32), jnp.where(index == 1, square_low.astype(f32), 0.0)
    ).astype(bf16)
    for j in range(sides):
        grad_act = early[j][:, columns:] * scale - activated[j] * pull + (2.0 * penalty_rate / node_total) * activated[j]
        grad = (grad_act * slope[j]).astype(bf16)
        grad_pooled = grad_pooled + dot(grad, w_refs[j][...], (1, 1))
        high, low = halves(activated[j] * scale)
        late[j][0:few, 0:columns] = high
        late[j][0:few, columns : 2 * columns] = low
        late[j][0:few, 2 * columns : 3 * columns] = grad
        late[j][0:few, 3 * columns :] = pooled
        late[j][few:, :] = extra
    for m in range(sides):
        part = grad_pooled[:, m * columns : (m + 1) * columns].astype(bf16)
        for g in range(groups):
            grad_ref[g, m] = part


def combine(node_total, parts, early, w_pooled, after=()):
    groups, sides, few, columns = parts.shape
    return call(
        functools.partial(combine_kernel, node_total, sides),
        "combine",
        [parts, *map(far, early), *map(far, w_pooled)],
        [full(parts.shape, bf16)] + [full((few + extra_rows, (3 + sides) * columns), bf16, far_shape)] * sides,
        after=after,
    )


def w_back_kernel(sides, groups, place_ref, *refs):
    own, late, (w_ref, emb_ref, even_ref, odd_ref, *self_refs), scratch = (
        refs[:sides],
        refs[sides : 2 * sides],
        refs[2 * sides : -3],
        refs[-3:],
    )
    grad_ref, pooled_ref, total_ref = scratch
    nodes, columns = emb_ref.shape
    few = nodes // sides
    squares = 0.0
    for j in range(sides):
        at = (place_ref[1] ^ j) * few
        rows_at(emb_ref, at, few)[...] = late[j][0:few, 0:columns].astype(f32) + late[j][
            0:few, columns : 2 * columns
        ].astype(f32)
        rows_at(grad_ref, at, few)[...] = late[j][0:few, 2 * columns : 3 * columns]
        rows_at(pooled_ref, at, few)[...] = late[j][0:few, 3 * columns :]
        squares = squares + late[j][few : few + 1, 0:columns].astype(f32)
        squares = squares + late[j][few + 1 : few + 2, 0:columns].astype(f32)
    grad = grad_ref[...]
    for j in range(sides):
        side = place_ref[1] ^ j
        rows_at(total_ref, side * columns, columns)[...] = dot(own[j][...], grad, (0, 0))
        self_refs[j][...] = dot(grad, rows_at(w_ref, side * columns, columns)[...], (1, 1)).astype(bf16)
    total_ref[sides * columns :, :] = dot(pooled_ref[...], grad, (0, 0))
    bias_high, bias_low = halves(jnp.sum(grad.astype(f32), axis=0, keepdims=True))
    square_high, square_low = halves(squares)
    piece = total_ref.shape[0] // groups
    index = lax.broadcasted_iota(i32, (extra_rows, columns), 0)
    extra = jnp.zeros(index.shape, f32)
    for i, row in enumerate((bias_high, bias_low, square_high, square_low)):
        extra = jnp.where(index == i, row.astype(f32), extra)
    extra = extra.astype(bf16)
    for s in range(groups):
        part = (odd_ref if s % 2 else even_ref).at[s // 2]
        part[0:piece, :] = rows_at(total_ref, (place_ref[0] ^ s) * piece, piece)[...].astype(bf16)
        part[piece:, :] = extra


def w_back(place, table, late, w_self, node_dev, groups, after=()):
    sides = len(table)
    rows, columns = 2 * w_self.shape[0], w_self.shape[1]
    half = full((groups // 2, rows // groups + extra_rows, columns), bf16, far_shape)
    return call(
        functools.partial(w_back_kernel, sides, groups),
        "w_back",
        [(place, smem)] + first_rows(table, node_dev) + [*map(far, late), far(w_self)],
        [full((node_dev, columns), f32, far_shape), half, half]
        + [full((node_dev, columns), bf16, far_shape)] * sides,
        scratch=[
            pltpu.VMEM((node_dev, columns), bf16),
            pltpu.VMEM((node_dev, sides * columns), bf16),
            pltpu.VMEM((rows, columns), f32),
        ],
        after=after,
    )


def split_extra(total):
    index = lax.broadcasted_iota(i32, total.shape, 0)
    extra = jnp.zeros(total.shape, f32)
    for i in (0, 2):
        high, low = halves(total[i : i + 1, :] + total[i + 1 : i + 2, :])
        extra = jnp.where(index == i, high.astype(f32), jnp.where(index == i + 1, low.astype(f32), extra))
    return extra


def add_kernel(copies, scale, count, *refs):
    parts, (piece_ref, bias_ref, scalar_ref) = refs[:count], refs[count:]
    terms = []
    for part in parts:
        terms += [part] if len(part.shape) == 2 else [part.at[i] for i in range(part.shape[0])]
    total = terms[0][...].astype(f32)
    for part in terms[1:]:
        total = total + part[...].astype(f32)
    piece = total.shape[0] - extra_rows
    low = total[0:piece, :].astype(bf16)
    if copies:
        for i in range(copies):
            piece_ref[i] = low
    else:
        piece_ref[...] = low
    bias_ref[...] = total[piece : piece + 1, :] + total[piece + 1 : piece + 2, :]
    scalar_ref[...] = scale * (total[piece + 2 : piece + 3, 0:1] + total[piece + 3 : piece + 4, 0:1])


def add(parts, copies, scale):
    rows, columns = parts[0].shape[-2:]
    piece = (rows - extra_rows, columns)
    return call(
        functools.partial(add_kernel, copies, scale, len(parts)),
        "add",
        parts,
        [full((copies, *piece) if copies else piece, bf16), full((1, columns), f32), full((1, 1), f32)],
    )


def add_pairs_kernel(own_ref, other_ref, *outs):
    for i, out in enumerate(outs):
        total = own_ref[i].astype(f32) + other_ref[i].astype(f32)
        piece = total.shape[0] - extra_rows
        out[0:piece, :] = total[0:piece, :].astype(bf16)
        out[piece:, :] = split_extra(total[piece:, :]).astype(bf16)


def add_pairs(own, other, after=()):
    count, rows, columns = own.shape
    return call(add_pairs_kernel, "add_pairs", [far(own), far(other)], [full((rows, columns), bf16, far_shape)] * count, after=after)


def stack_kernel(*refs):
    for i, ref in enumerate(refs[:-1]):
        refs[-1][i] = ref[...]


def stack(arrays):
    return call(stack_kernel, "stack", arrays, [full((len(arrays), *arrays[0].shape), bf16)])[0]


def collect_kernel(place_ref, own_ref, other_ref, out_ref):
    count, piece, _ = other_ref.shape
    for s in range(count):
        rows_at(out_ref, (place_ref[0] ^ (2 * s)) * piece, piece)[...] = own_ref[s].astype(f32)
        rows_at(out_ref, (place_ref[0] ^ (2 * s + 1)) * piece, piece)[...] = other_ref[s].astype(f32)


def collect(place, own, other):
    count, piece, columns = own.shape
    return call(
        collect_kernel, "collect", [(place, smem), own, other], [full((2 * count * piece, columns), f32)]
    )[0]


def widen_kernel(low_ref, out_ref):
    out_ref[...] = low_ref[...].astype(f32)


def widen(low):
    rows, columns = low.shape
    block = rows // 2
    return call(
        widen_kernel,
        "widen",
        [(low, row_blocks(block, columns))],
        [(row_blocks(block, columns), shape((rows, columns), f32))],
        grid=(2,),
    )[0]


def total_direct(parts, scale=0.0):
    groups, rows, columns = parts.shape
    pieces, *sums = add([exchange(parts, "dp")], groups, scale)
    return widen(exchange(pieces, "dp").reshape(-1, columns)), *sums


def total_in_steps(place, parts, scale, after=()):
    count = parts[0].shape[0]
    mine = add_pairs(parts[0], swap(parts[1], "dp", 1), after=after)
    piece, *sums = add([mine[0]] + [swap(mine[s], "dp", 2 * s) for s in range(1, count)], 0, scale)
    pieces = stack([piece] + [swap(piece, "dp", 2 * s) for s in range(1, count)])
    return collect(place, pieces, swap(pieces, "dp", 1)), *sums


def rows_back_kernel(chunk_counts, sides, place_ref, *refs):
    chunks = len(chunk_counts)
    matrix_ref, pooled_ref, slopes = refs[0], refs[1], refs[2 : 2 + chunks]
    table = refs[2 + chunks : 2 + chunks + chunks * sides]
    grad_ref, rest = refs[2 + chunks + chunks * sides], refs[3 + chunks + chunks * sides :]
    step = pl.program_id(0)
    matrix = jnp.concatenate([matrix_ref[g] for g in range(matrix_ref.shape[0])], axis=1)
    summed = dot(matrix, pooled_ref[...], (1, 0))
    slope = slopes[0][...]
    first = chunk_counts[0]
    for k in range(1, chunks):
        slope = jnp.where(step >= first, slopes[k][...], slope)
        first += chunk_counts[k]
    grad = summed * slope.astype(f32)
    column_sums = jnp.sum(grad, axis=0, keepdims=True)
    grad = grad.astype(bf16)
    grad_ref[...] = grad
    if not sides:
        return
    q_ref, total_ref, bias_ref = rest
    width = table[0].shape[1]

    @pl.when(step == 0)
    def _():
        bias_ref[...] = jnp.zeros_like(bias_ref)
        total_ref[...] = jnp.zeros_like(total_ref)

    bias_ref[...] += column_sums
    first = 0
    for k in range(chunks):

        @pl.when((step >= first) & (step < first + chunk_counts[k]))
        def _():
            for j in range(sides):
                total_ref[j] += dot(grad, table[k * sides + j][...], (0, 0))

        first += chunk_counts[k]

    @pl.when(step == pl.num_programs(0) - 1)
    def _():
        high, low = halves(bias_ref[...])
        groups, rows, columns = q_ref.shape
        index = lax.broadcasted_iota(i32, (extra_rows, columns), 0)
        extra = jnp.where(index == 0, high.astype(f32), jnp.where(index == 1, low.astype(f32), 0.0)).astype(bf16)
        piece = rows - extra_rows
        per = width // piece
        for g in range(groups):
            q_ref[g, piece:, :] = extra
        for j in range(sides):
            flat = total_ref[j].T.astype(bf16)
            for part in range(per):
                q_ref[(place_ref[1] ^ j) * per + part, 0:piece, :] = flat[part * piece : (part + 1) * piece, :]


def rows_back(place, matrix, pooled, slopes, table, after=()):
    sides = len(table[0]) if table else 0
    groups, row_dev, node_dev = matrix.shape
    columns = pooled.shape[1]
    block = min(slopes[-1].shape[0], 512 * 2048 // (groups * node_dev))
    counts = [a.shape[0] // block for a in slopes]
    operands = [(place, smem), (far(matrix), pl.BlockSpec((groups, block, node_dev), lambda i: (0, i, 0))), pooled]
    operands += list(zip(map(far, slopes), chunk_specs(slopes, block)))
    outs = [(row_blocks(block, columns), far_shape((row_dev, columns), bf16))]
    scratch = []
    if sides:
        width = table[0][0].shape[1]
        by_side = [chunk_specs([part[j] for part in table], block) for j in range(sides)]
        operands += [(far(table[k][j]), by_side[j][k]) for k in range(len(table)) for j in range(sides)]
        outs.append(full((groups, sides * width // groups + extra_rows, columns), bf16))
        scratch = [pltpu.VMEM((sides, columns, width), f32), pltpu.VMEM((1, columns), f32)]
    return call(
        functools.partial(rows_back_kernel, counts, sides),
        "rows_back_q" if sides else "rows_back",
        operands,
        outs,
        grid=(row_dev // block,),
        scratch=scratch,
        after=after,
    )


def table_back_kernel(sides, place_ref, *refs):
    grads, qs, self_refs, out_ref = refs[:sides], refs[sides : 2 * sides], refs[2 * sides : 3 * sides], refs[-1]
    width = out_ref.shape[1]
    at = place_ref[1] * width
    total = dot(grads[0][...], rows_at(qs[0], at, width)[...], (1, 1))
    for j in range(1, sides):
        total = total + dot(grads[j][...], rows_at(qs[j], at, width)[...], (1, 1))
    out_ref[...] = total

    @pl.when(pl.program_id(0) == 0)
    def _():
        nodes = self_refs[0].shape[0]
        own = self_refs[0][...].astype(f32)
        for ref in self_refs[1:]:
            own = own + ref[...].astype(f32)
        out_ref[0:nodes, :] += own


def table_back(place, grads, qs, grad_self):
    sides = len(grads)
    row_dev, columns = grads[0].shape
    width = grad_self[0].shape[1]
    block = min(row_dev, 512)
    return call(
        functools.partial(table_back_kernel, sides),
        "table_back",
        [(place, smem)] + [(far(a), row_blocks(block, columns)) for a in grads] + [*map(far, qs), *map(far, grad_self)],
        [(row_blocks(block, width), far_shape((row_dev, width), f32))],
        grid=(row_dev // block,),
    )[0]


def all_sides(array):
    across = swap(array, "mp", 2)
    return [array, swap(array, "mp", 1), across, swap(across, "mp", 1)]


def shards(table, q_weight, q_bias, w_weight, w_bias, neighbours, counts, importance, cotangent):
    groups = lax.axis_size("dp")
    sides = lax.axis_size("mp")
    row_dev, width = table.shape
    node_dev, _ = neighbours.shape
    node_total = node_dev * groups
    columns = q_weight.shape[1]
    few = node_dev // sides
    place = jnp.stack([lax.axis_index("dp"), lax.axis_index("mp")]).astype(i32)

    cut = row_dev * 3 // 4
    low_a, low_b, q_low, w_self, w_pooled = low_all(table, q_weight, w_weight, cut)
    slots = make_slots(place, neighbours, counts, importance, row_dev, groups, after=[low_a])
    slots = exchange(slots, "dp")
    across_a, across_b = swap(low_a, "mp", 2), swap(low_b, "mp", 2)
    beside_a, beside_b = swap(low_a, "mp", 1), swap(low_b, "mp", 1)

    matrix = spread(slots, row_dev)
    across_a = gate(across_a, [matrix])
    part_a = [low_a, beside_a, across_a, swap(across_a, "mp", 1)]
    hidden_a, slope_a = hidden(place, part_a, q_low, q_bias, "both")
    so_far = pool(hidden_a, matrix, 0, None)
    across_b = gate(across_b, [hidden_a])
    part_b = [low_b, beside_b, across_b, swap(across_b, "mp", 1)]
    parts = [part_a, part_b]
    early = self_half(place, part_a, w_self, w_bias, cotangent)
    early = [early[0]] + [swap(early[j], "mp", j) for j in range(1, sides)]
    hidden_b, slope_b = hidden(place, part_b, q_low, q_bias, "both", after=[so_far])
    pooled = pool(hidden_b, matrix, cut, so_far, after=early)
    slope = [slope_a, slope_b]
    pooled = exchange(pooled.reshape(groups * sides, few, columns), ("dp", "mp"))

    w_pooled = all_sides(gate(w_pooled, [hidden_b]))
    q_all = all_sides(gate(q_low, [hidden_b]))
    q_bias_x = swap(q_bias, "mp", 2)
    slope_x = [hidden(place, part, q_all[2], q_bias_x, "slope")[0] for part in parts]

    grad_pooled, *late = combine(
        node_total, pooled.reshape(groups, sides, few, columns), early, w_pooled, after=slope_x
    )
    grad_pooled = exchange(grad_pooled.reshape(groups * sides, few, columns), ("dp", "mp")).reshape(node_total, columns)
    late = [late[0]] + [swap(late[j], "mp", j) for j in range(1, sides)]
    embedding, *w_parts = w_back(place, part_a, late, w_self, node_dev, groups)
    w_parts, grad_self = w_parts[:2], w_parts[2:]
    grad_self = [grad_self[0]] + [swap(grad_self[j], "mp", j) for j in range(1, sides)]

    grad_pooled_x = swap(grad_pooled, "mp", 2)
    grad, q_parts = rows_back(place, matrix, grad_pooled, slope, parts, after=[embedding])
    grad_x = rows_back(place, matrix, grad_pooled_x, slope_x, [], after=[grad])[0]
    grads = [grad, swap(grad, "mp", 1), grad_x, swap(grad_x, "mp", 1)]
    table_grad = table_back(place, grads, q_all, grad_self)
    q_grad, q_bias_grad, _ = total_direct(q_parts)
    scale = penalty_rate / node_total
    if groups <= 8:
        w_grad, w_bias_grad, penalty = total_in_steps(place, w_parts, scale, after=[grad])
    else:
        order = place[0] ^ jnp.arange(groups, dtype=i32)
        w_grad, w_bias_grad, penalty = total_direct(jnp.stack(w_parts)[order % 2, order // 2], scale)
    return (
        embedding,
        table_grad,
        q_grad,
        q_bias_grad.reshape(columns),
        w_grad,
        w_bias_grad.reshape(columns),
        penalty.reshape(()),
    )


def solution(mesh):
    placed = (
        P("dp", "mp"),
        P(None, "mp"),
        P("mp"),
        P(None, "mp"),
        P("mp"),
        P("dp", None),
        P("dp"),
        P("dp", None),
        P("dp", "mp"),
    )
    return jax.shard_map(
        shards,
        mesh=mesh,
        in_specs=placed,
        out_specs=(
            P("dp", "mp"),
            P("dp", "mp"),
            P(None, "mp"),
            P("mp"),
            P(None, "mp"),
            P("mp"),
            P(),
        ),
        check_vma=False,
    )
```

time: 1500 us -> 300 us (0.20)
  waiting for transfers between devices: 584 us -> 116 us
  local copies, waits for them, and re-layouts: 306 us -> 20.3 us
  blocking collectives: 265 us -> 0 us
  other arithmetic: 237 us -> 0.08 us
  Pallas kernels: 0 us -> 106 us
  matrix products: 53.5 us -> 0 us
  starting transfers between devices: 20.1 us -> 51.9 us
  between operations: 16.3 us -> 1.04 us
    psum x2 -> x0, blocking collectives: 251 us -> none  [the longest x1 244 us: shards(): lax.psum((q_grad_local, qb_grad_local, w_grad_local, wb_grad_local, jnp.s...]
    reduce_scatter x3 -> x0, waiting for transfers between devices: 213 us -> none  [the longest x1 187 us: shards(): lax.psum_scatter(lax.dot_general(q_low, grad_hidden_pre, (((1,), (1,)), (...]
    all_to_all x3 -> x5, waiting for transfers between devices: 212 us -> 13.2 us  [exchange(): return lax.all_to_all(array, axes, split_axis=0, concat_axis=0, tiled=True)]
    gather x18 -> x0, local copies, waits for them, and re-layouts: 164 us -> none  [the longest x1 65.9 us: shards(): sorted_owner = owner_index[order]]
    all_gather x1 -> x0, waiting for transfers between devices: 159 us -> none  [shards(): whole_rows = lax.all_gather(slot_rows, 'mp', axis=1, tiled=True)]
    scatter-add x2 -> x0, other arithmetic: 120 us -> none  [the longest x1 118 us: shards(): table_grad = jnp.zeros((row_dev, grad_rows.shape[0]), jnp.float32).at[ser...]
    pallas_call x0 -> x25, Pallas kernels: none -> 106 us  [the longest x21 106 us: call(): pl.pallas_call(inner, grid=grid, in_specs=specs + [pl.BlockSpec(memory_sp...]
    ppermute x0 -> x33, waiting for transfers between devices: none -> 102 us  [swap(): return lax.ppermute(array, axis, [(i, i ^ bits) for i in range(size)])]
  transfers between devices with their start and end apart: 8 -> 38, of which waited for: 5 -> 17; matrix products, arithmetic and copies ran while one was open for 10% -> 0% of each run, Pallas kernels for 0% -> 27%
where the time goes in v2:
time: 300 us; the launch traced here: 295 us
  waiting for transfers between devices  116 us (39%)
  Pallas kernels  106 us (35%)
  starting transfers between devices  51.9 us (17%)
  local copies, waits for them, and re-layouts  20.3 us (7%)
    pallas_call x21, Pallas kernels, call(): pl.pallas_call(inner, grid=grid, in_specs=specs + [pl.BlockSpec(memory_sp...  106 us
    ppermute x33, waiting for transfers between devices, swap(): return lax.ppermute(array, axis, [(i, i ^ bits) for i in range(size)])  102 us
    all_to_all x5, starting transfers between devices, exchange(): return lax.all_to_all(array, axes, split_axis=0, concat_axis=0, tiled=True)  28.9 us
    ppermute x33, starting transfers between devices, swap(): return lax.ppermute(array, axis, [(i, i ^ bits) for i in range(size)])  23 us
    unnamed x92, local copies, waits for them, and re-layouts  20.3 us
    all_to_all x5, waiting for transfers between devices, exchange(): return lax.all_to_all(array, axes, split_axis=0, concat_axis=0, tiled=True)  13.2 us
  transfers between devices with their start and end apart: 38, of which 17 were waited for; matrix products, arithmetic and copies ran while one was open for 0% of the time, Pallas kernels for 27%

profile of v2, /device:TPU:12, one launch (start us, length us, event | category | flops | bytes accessed | tf_op | source)
XLA Modules:
  0.0 294.9 jit_solution(9616127636820199402)
XLA Ops:
  0.7 5.6 %low.1 = (bf16[3072,256]{1,0:T(8,128)(2,1)}, bf16[1024,256]{1,0:T(8,128)(2,1)}, bf16[1024,256]{1,0:T(8,128)(2,1)}, bf16[1024,256]{1,0:T(8,128)(2,1)}, bf16[1024,256]{1,0:T(8,128)(2,1)}) custom-call(f32[4096,256]{1,0:T(8,128)} %refs_0_.1, f32[1024,256]{1,0:T(8,128)} %refs_1_.1, f32[2048,256]{1,0:T(8,128)} %refs_2_.1), custom_call_target="tpu_custom_call" | custom-call | flops 4600000000 | bytes 14760000 | tf_op jit(solution)/shard_map/low/pallas_call | solution.py:83
  6.4 1.4 copy-done.4
  7.8 2.5 slots.1
  10.3 6.2 %all-to-all-start = ((s16[8,3,50,256]{3,2,1,0:T(8,128)(2,1)}), s16[8,3,50,256]{3,2,1,0:T(8,128)(2,1)S(1)}, u32[]{:S(2)}, u32[]{:S(2)}) async-start(s16[8,3,50,256]{3,2,1,0:T(8,128)(2,1)} %slots.1), calls=%async_computation | async-start | bytes 1376256 | tf_op jit(solution)/shard_map/all_to_all | solution.py:124
  16.5 1.6 collective-permute-start.1
  18.1 13.2 %all-to-all-done.refs_0_ = s16[8,3,50,256]{3,2,1,0:T(8,128)(2,1)S(1)} async-done(((s16[8,3,50,256]{3,2,1,0:T(8,128)(2,1)}), s16[8,3,50,256]{3,2,1,0:T(8,128)(2,1)S(1)}, u32[]{:S(2)}, u32[]{:S(2)}) %all-to-all-start) | async-done | bytes 614432 | tf_op jit(solution)/shard_map/all_to_all | solution.py:124
  31.2 12.1 %spread.1.refs_1_ = bf16[8,4096,256]{2,1,0:T(8,128)(2,1)S(1)} custom-call(s16[8,3,50,256]{3,2,1,0:T(8,128)(2,1)S(1)} %all-to-all-done.refs_0_), custom_call_target="tpu_custom_call" | custom-call | flops 23000000512 | bytes 73800000 | tf_op jit(solution)/shard_map/spread/pallas_call | solution.py:83
  43.4 5.8 %copy-done = bf16[8,4096,256]{2,1,0:T(8,128)(2,1)} copy-done((bf16[8,4096,256]{2,1,0:T(8,128)(2,1)}, bf16[8,4096,256]{2,1,0:T(8,128)(2,1)S(1)}, u32[]{:S(2)}) %copy-start) | copy-done | bytes 16777240
  49.2 4.2 %collective-permute-done.1.refs_0_ = bf16[3072,256]{1,0:T(8,128)(2,1)} collective-permute-done((bf16[3072,256]{1,0:T(8,128)(2,1)S(1)}, bf16[3072,256]{1,0:T(8,128)(2,1)}, u32[]{:S(2)}, u32[]{:S(2)}) %collective-permute-start.1) | collective-permute-done | bytes 1572896 | tf_op jit(solution)/shard_map/ppermute | solution.py:115
  53.5 1.6 collective-permute-start.4
  55.2 1.9 collective-permute-done.2.refs_4_.refs_8_
  57.1 1.1 copy-done.17
  58.2 8.1 %hidden_both.2 = (bf16[256,3072]{1,0:T(8,128)(2,1)S(1)}, bf16[3072,256]{1,0:T(8,128)(2,1)}) custom-call(s32[2]{0:T(128)S(1)} %pad_add_fusion.refs_0_, bf16[3072,256]{1,0:T(8,128)(2,1)} %get-tuple-element.43.refs_4_.refs_1_.refs_5_, bf16[3072,256]{1,0:T(8,128)(2,1)} %collective-permute-done.refs_2_.refs_6_, bf16[3072,256]{1,0:T(8,128)(2,1)} %gate.4.refs_3_.refs_7_, ...), custom_call_target="tpu_custom_call" | custom-call | flops 1150000000 | bytes 3690000 | tf_op jit(solution)/shard_map/hidden_both/pallas_call | solution.py:83
  66.3 1.2 copy-done.2
  67.8 0.8 copy-done.16
  68.6 2.6 self_half.1
  71.8 1.5 collective-permute-start.7
  73.3 5.0 %pool.2.refs_7_.refs_2_ = f32[256,2048]{1,0:T(8,128)S(1)} custom-call(bf16[256,3072]{1,0:T(8,128)(2,1)S(1)} %copy-done.3, bf16[8,4096,256]{2,1,0:T(8,128)(2,1)S(1)} %bitcast.17), custom_call_target="tpu_custom_call" | custom-call | flops 5750000128 | bytes 18450000 | tf_op jit(solution)/shard_map/pool/pallas_call | solution.py:83
  78.4 0.8 copy-done.19
  79.2 0.8 copy-done.20
  80.0 3.7 %hidden_both.3 = (bf16[256,1024]{1,0:T(8,128)(2,1)S(1)}, bf16[1024,256]{1,0:T(8,128)(2,1)}) custom-call(s32[2]{0:T(128)S(1)} %pad_add_fusion.refs_0_, bf16[1024,256]{1,0:T(8,128)(2,1)} %get-tuple-element.44.refs_1_.refs_9_, bf16[1024,256]{1,0:T(8,128)(2,1)} %copy-done.19, bf16[1024,256]{1,0:T(8,128)(2,1)} %gate.5.refs_3_.refs_11_, ...), custom_call_target="tpu_custom_call" | custom-call | flops 1150000000 | bytes 3690000 | tf_op jit(solution)/shard_map/hidden_both/pallas_call | solution.py:83
  83.8 3.4 %pool.3 = bf16[2048,256]{1,0:T(8,128)(2,1)} custom-call(bf16[256,1024]{1,0:T(8,128)(2,1)S(1)} %get-tuple-element.47.refs_0_.refs_1_, bf16[8,4096,256]{2,1,0:T(8,128)(2,1)S(1)} %bitcast.17, f32[256,2048]{1,0:T(8,128)S(1)} %pool.2.refs_7_.refs_2_, f32[64,512]{1,0:T(8,128)S(1)} %copy-done.11, f32[64,512]{1,0:T(8,128)S(1)} %collective-permute-done.6.refs_4_.refs_2_, ...), custom_call_target="tpu_custom_call" | custom-call | flops 5750000128 | bytes 18450000 | tf_op jit(solution)/shard_map/pool/pallas_call | solution.py:83
  87.2 6.0 %all-to-all-start.1 = ((bf16[32,64,256]{2,1,0:T(8,128)(2,1)}), bf16[32,64,256]{2,1,0:T(8,128)(2,1)S(1)}, u32[]{:S(2)}, u32[]{:S(2)}) async-start(bf16[32,64,256]{2,1,0:T(8,128)(2,1)} %bitcast.7), calls=%async_computation.1 | async-start | bytes 2097152 | tf_op jit(solution)/shard_map/all_to_all | solution.py:124
  93.3 1.5 collective-permute-start.10
  95.4 1.5 collective-permute-start.13
  96.8 21.9 %collective-permute-done.10.refs_7_ = bf16[1024,256]{1,0:T(8,128)(2,1)S(1)} collective-permute-done((bf16[1024,256]{1,0:T(8,128)(2,1)}, bf16[1024,256]{1,0:T(8,128)(2,1)S(1)}, u32[]{:S(2)}, u32[]{:S(2)}) %collective-permute-start.10) | collective-permute-done | bytes 524320 | tf_op jit(solution)/shard_map/ppermute | solution.py:115
  118.8 10.8 %collective-permute-done.13 = f32[256]{0:T(256)S(1)} collective-permute-done((f32[256]{0:T(256)S(1)}, f32[256]{0:T(256)S(1)}, u32[]{:S(2)}, u32[]{:S(2)}) %collective-permute-start.13) | collective-permute-done | bytes 1056 | tf_op jit(solution)/shard_map/ppermute | solution.py:115
  130.4 7.6 %hidden_slope.2.refs_9_.refs_3_ = bf16[3072,256]{1,0:T(8,128)(2,1)} custom-call(s32[2]{0:T(128)S(1)} %pad_add_fusion.refs_0_, bf16[3072,256]{1,0:T(8,128)(2,1)} %get-tuple-element.43.refs_4_.refs_1_.refs_5_, bf16[3072,256]{1,0:T(8,128)(2,1)} %collective-permute-done.refs_2_.refs_6_, bf16[3072,256]{1,0:T(8,128)(2,1)} %gate.4.refs_3_.refs_7_, ...), custom_call_target="tpu_custom_call" | custom-call | flops 5750000128 | bytes 18450000 | tf_op jit(solution)/shard_map/hidden_slope/pallas_call | solution.py:83
  137.9 3.7 %hidden_slope.3.refs_10_.refs_4_ = bf16[1024,256]{1,0:T(8,128)(2,1)} custom-call(s32[2]{0:T(128)S(1)} %pad_add_fusion.refs_0_, bf16[1024,256]{1,0:T(8,128)(2,1)} %get-tuple-element.44.refs_1_.refs_9_, bf16[1024,256]{1,0:T(8,128)(2,1)} %copy-done.19, bf16[1024,256]{1,0:T(8,128)(2,1)} %gate.5.refs_3_.refs_11_, bf16[1024,256]{1,0:T(8,128)(2,1)} %copy-done.20, ...), custom_call_target="tpu_custom_call" | custom-call | flops 5750000128 | bytes 18450000 | tf_op jit(solution)/shard_map/hidden_slope/pallas_call | solution.py:83
  141.6 0.8 copy-done.28
  142.4 1.0 copy-done.14
  143.5 4.1 %combine.1 = (bf16[8,4,64,256]{3,2,1,0:T(8,128)(2,1)}, bf16[80,1792]{1,0:T(8,128)(2,1)}, bf16[80,1792]{1,0:T(8,128)(2,1)}, bf16[80,1792]{1,0:T(8,128)(2,1)}, bf16[80,1792]{1,0:T(8,128)(2,1)}) custom-call(bf16[8,4,64,256]{3,2,1,0:T(8,128)(2,1)S(1)} %bitcast.20, f32[64,512]{1,0:T(8,128)} %get-tuple-element.49.refs_3_.refs_1_, f32[64,512]{1,0:T(8,128)} %copy-done.7, ...), custom_call_target="tpu_custom_call" | custom-call | flops 4600000000 | bytes 14760000 | tf_op jit(solution)/shard_map/combine/pallas_call | solution.py:83
  147.5 4.9 %all-to-all-start.2 = ((bf16[32,64,256]{2,1,0:T(8,128)(2,1)}), bf16[32,64,256]{2,1,0:T(8,128)(2,1)S(1)}, u32[]{:S(2)}, u32[]{:S(2)}) async-start(bf16[32,64,256]{2,1,0:T(8,128)(2,1)} %bitcast.10), calls=%async_computation.2 | async-start | bytes 2097152 | tf_op jit(solution)/shard_map/all_to_all | solution.py:124
  152.6 1.5 collective-permute-start.15
  154.4 16.8 %collective-permute-done.15.refs_7_ = bf16[80,1792]{1,0:T(8,128)(2,1)S(1)} collective-permute-done((bf16[80,1792]{1,0:T(8,128)(2,1)S(1)}, bf16[80,1792]{1,0:T(8,128)(2,1)S(1)}, u32[]{:S(2)}, u32[]{:S(2)}) %collective-permute-start.15) | collective-permute-done | bytes 286752 | tf_op jit(solution)/shard_map/ppermute | solution.py:115
  171.2 6.8 %collective-permute-done.16.refs_8_ = bf16[80,1792]{1,0:T(8,128)(2,1)S(1)} collective-permute-done((bf16[80,1792]{1,0:T(8,128)(2,1)S(1)}, bf16[80,1792]{1,0:T(8,128)(2,1)S(1)}, u32[]{:S(2)}, u32[]{:S(2)}) %collective-permute-start.16) | collective-permute-done | bytes 286752 | tf_op jit(solution)/shard_map/ppermute | solution.py:115
  178.7 3.4 %w_back.1 = (f32[256,256]{1,0:T(8,128)}, bf16[4,272,256]{2,1,0:T(8,128)(2,1)}, bf16[4,272,256]{2,1,0:T(8,128)(2,1)}, bf16[256,256]{1,0:T(8,128)(2,1)}, bf16[256,...) custom-call(s32[2]{0:T(128)S(1)} %pad_add_fusion.refs_0_, ...), custom_call_target="tpu_custom_call" | custom-call | flops 4600000000 | bytes 14760000 | tf_op jit(solution)/shard_map/w_back/pallas_call | solution.py:83
  183.3 0.9 copy-done.10
  184.2 16.0 %rows_back_q.1 = (bf16[4096,256]{1,0:T(8,128)(2,1)}, bf16[8,144,256]{2,1,0:T(8,128)(2,1)}) custom-call(s32[2]{0:T(128)S(1)} %pad_add_fusion.refs_0_, bf16[8,4096,256]{2,1,0:T(8,128)(2,1)} %copy-done, bf16[2048,256]{1,0:T(8,128)(2,1)S(1)} %bitcast.19, bf16[3072,256]{1,0:T(8,128)(2,1)} %get-tuple-element.60.refs_3_, ...), custom_call_target="tpu_custom_call" | custom-call | flops 14949999616 | bytes 47970000 | tf_op jit(solution)/shard_map/rows_back_q/pallas_call | solution.py:83
  200.3 6.3 %all-to-all-start.3 = ((bf16[8,144,256]{2,1,0:T(8,128)(2,1)}), bf16[8,144,256]{2,1,0:T(8,128)(2,1)S(1)}, u32[]{:S(2)}, u32[]{:S(2)}) async-start(bf16[8,144,256]{2,1,0:T(8,128)(2,1)} %get-tuple-element.67), calls=%async_computation.3 | async-start | bytes 1179648 | tf_op jit(solution)/shard_map/all_to_all | solution.py:124
  206.6 1.2 collective-permute-done.18.refs_2_
  207.8 1.6 copy-done.6
  209.4 11.7 %rows_back.1.refs_3_ = bf16[4096,256]{1,0:T(8,128)(2,1)} custom-call(s32[2]{0:T(128)S(1)} %pad_add_fusion.refs_0_, bf16[8,4096,256]{2,1,0:T(8,128)(2,1)} %copy-done, bf16[2048,256]{1,0:T(8,128)(2,1)S(1)} %collective-permute-done.18.refs_2_, bf16[3072,256]{1,0:T(8,128)(2,1)} %hidden_slope.2.refs_9_.refs_3_, bf16[1024,256]{1,0:T(8,128)(2,1)} %hidden_slope.3.refs_10_.refs_4_, ...), custom_call_target="tpu_custom_call" | custom-call | flops 10350000128 | bytes 33210000 | tf_op jit(solution)/shard_map/rows_back/pallas_call | solution.py:83
  221.1 0.8 copy-done.22
  221.9 2.1 add_pairs.1
  224.7 2.2 collective-permute-start.27
  227.5 3.7 %collective-permute-done.26.refs_1_ = bf16[272,256]{1,0:T(8,128)(2,1)S(1)} collective-permute-done((bf16[272,256]{1,0:T(8,128)(2,1)}, bf16[272,256]{1,0:T(8,128)(2,1)S(1)}, u32[]{:S(2)}, u32[]{:S(2)}) %collective-permute-start.26) | collective-permute-done | bytes 139296 | tf_op jit(solution)/shard_map/ppermute | solution.py:115
  231.1 6.1 %collective-permute-done.27.refs_2_ = bf16[272,256]{1,0:T(8,128)(2,1)S(1)} collective-permute-done((bf16[272,256]{1,0:T(8,128)(2,1)}, bf16[272,256]{1,0:T(8,128)(2,1)S(1)}, u32[]{:S(2)}, u32[]{:S(2)}) %collective-permute-start.27) | collective-permute-done | bytes 139296 | tf_op jit(solution)/shard_map/ppermute | solution.py:115
  237.2 3.2 %collective-permute-done.28.refs_3_ = bf16[272,256]{1,0:T(8,128)(2,1)S(1)} collective-permute-done((bf16[272,256]{1,0:T(8,128)(2,1)}, bf16[272,256]{1,0:T(8,128)(2,1)S(1)}, u32[]{:S(2)}, u32[]{:S(2)}) %collective-permute-start.28) | collective-permute-done | bytes 139296 | tf_op jit(solution)/shard_map/ppermute | solution.py:115
  240.4 0.9 copy-done.13
  241.9 2.9 collective-permute-start.30
  245.4 0.9 add.4
  246.3 5.5 %all-to-all-start.4 = ((bf16[8,128,256]{2,1,0:T(8,128)(2,1)}), bf16[8,128,256]{2,1,0:T(8,128)(2,1)S(1)}, u32[]{:S(2)}, u32[]{:S(2)}) async-start(bf16[8,128,256]{2,1,0:T(8,128)(2,1)} %get-tuple-element.68), calls=%async_computation.4 | async-start | bytes 1048576 | tf_op jit(solution)/shard_map/all_to_all | solution.py:124
  251.8 5.2 %collective-permute-done.30.refs_2_ = bf16[256,256]{1,0:T(8,128)(2,1)S(1)} collective-permute-done((bf16[256,256]{1,0:T(8,128)(2,1)S(1)}, bf16[256,256]{1,0:T(8,128)(2,1)S(1)}, u32[]{:S(2)}, u32[]{:S(2)}) %collective-permute-start.30) | collective-permute-done | bytes 131104 | tf_op jit(solution)/shard_map/ppermute | solution.py:115
  256.9 6.4 %collective-permute-done.31.refs_3_ = bf16[256,256]{1,0:T(8,128)(2,1)S(1)} collective-permute-done((bf16[256,256]{1,0:T(8,128)(2,1)S(1)}, bf16[256,256]{1,0:T(8,128)(2,1)S(1)}, u32[]{:S(2)}, u32[]{:S(2)}) %collective-permute-start.31) | collective-permute-done | bytes 131104 | tf_op jit(solution)/shard_map/ppermute | solution.py:115
  263.4 1.5 collective-permute-start.32
  265.5 8.5 %collective-permute-done.32.refs_2_ = bf16[4,256,256]{2,1,0:T(8,128)(2,1)S(1)} collective-permute-done((bf16[4,256,256]{2,1,0:T(8,128)(2,1)S(1)}, bf16[4,256,256]{2,1,0:T(8,128)(2,1)S(1)}, u32[]{:S(2)}, u32[]{:S(2)}) %collective-permute-start.32) | collective-permute-done | bytes 524320 | tf_op jit(solution)/shard_map/ppermute | solution.py:115
  274.0 2.0 collect.1
  276.0 0.8 collective-permute-start.23
  276.8 1.2 collective-permute-start.24
  278.0 1.0 widen.1
  279.0 3.3 %collective-permute-done.23.refs_11_ = bf16[256,256]{1,0:T(8,128)(2,1)S(1)} collective-permute-done((bf16[256,256]{1,0:T(8,128)(2,1)S(1)}, bf16[256,256]{1,0:T(8,128)(2,1)S(1)}, u32[]{:S(2)}, u32[]{:S(2)}) %collective-permute-start.23) | collective-permute-done | bytes 131104 | tf_op jit(solution)/shard_map/ppermute | solution.py:115
  282.4 2.0 collective-permute-done.24.refs_12_
  285.1 9.8 %table_back.1 = f32[4096,256]{1,0:T(8,128)} custom-call(s32[2]{0:T(128)S(1)} %pad_add_fusion.refs_0_, bf16[4096,256]{1,0:T(8,128)(2,1)} %get-tuple-element.62.refs_5_.refs_1_.refs_2_, bf16[4096,256]{1,0:T(8,128)(2,1)} %collective-permute-done.17.refs_2_, bf16[4096,256]{1,0:T(8,128)(2,1)} %rows_back.1.refs_3_, ...), custom_call_target="tpu_custom_call" | custom-call | flops 9200000000 | bytes 29520000 | tf_op jit(solution)/shard_map/table_back/pallas_call | solution.py:83
  (131 shorter events, 8.6 us)
Async XLA Ops:
  7.8 8.8 %copy-start.5 = (bf16[3072,256]{1,0:T(8,128)(2,1)S(1)}, bf16[3072,256]{1,0:T(8,128)(2,1)}, u32[]{:S(2)}) copy-start(bf16[3072,256]{1,0:T(8,128)(2,1)} %get-tuple-element.43.refs_4_.refs_1_.refs_5_) | copy-start | bytes 4718596
  10.3 20.9 %all-to-all-start = ((s16[8,3,50,256]{3,2,1,0:T(8,128)(2,1)}), s16[8,3,50,256]{3,2,1,0:T(8,128)(2,1)S(1)}, u32[]{:S(2)}, u32[]{:S(2)}) async-start(s16[8,3,50,256]{3,2,1,0:T(8,128)(2,1)} %slots.1), calls=%async_computation | async-start | bytes 1376256 | tf_op jit(solution)/shard_map/all_to_all | solution.py:124
  16.5 38.7 %collective-permute-start = (bf16[3072,256]{1,0:T(8,128)(2,1)S(1)}, bf16[3072,256]{1,0:T(8,128)(2,1)}, u32[]{:S(2)}, u32[]{:S(2)}) collective-permute-start(bf16[3072,256]{1,0:T(8,128)(2,1)S(1)} %copy-done.5), channel_id=1, source_target_pairs={{0,1},{1,0},{2,3},{3,2},{4,5},{5,4},{6,7},{7,6},{8,9},{9,8},{10,11... | collective-permute-start | bytes 4718600 | tf_op jit(solution)/shard_map/ppermute | solution.py:115
  16.5 36.9 %collective-permute-start.1 = (bf16[3072,256]{1,0:T(8,128)(2,1)S(1)}, bf16[3072,256]{1,0:T(8,128)(2,1)}, u32[]{:S(2)}, u32[]{:S(2)}) collective-permute-start(bf16[3072,256]{1,0:T(8,128)(2,1)S(1)} %copy-done.5), channel_id=1, source_target_pairs={{0,2},{1,3},{2,0},{3,1},{4,6},{5,7},{6,4},{7,5},{8,10},{9,11},{10,... | collective-permute-start | bytes 4718600 | tf_op jit(solution)/shard_map/ppermute | solution.py:115
  43.4 5.8 %copy-start = (bf16[8,4096,256]{2,1,0:T(8,128)(2,1)}, bf16[8,4096,256]{2,1,0:T(8,128)(2,1)S(1)}, u32[]{:S(2)}) copy-start(bf16[8,4096,256]{2,1,0:T(8,128)(2,1)S(1)} %spread.1.refs_1_) | copy-start | bytes 50331652
  49.2 4.2 %copy-start.18 = (bf16[1024,256]{1,0:T(8,128)(2,1)S(1)}, bf16[1024,256]{1,0:T(8,128)(2,1)}, u32[]{:S(2)}) copy-start(bf16[1024,256]{1,0:T(8,128)(2,1)} %get-tuple-element.44.refs_1_.refs_9_) | copy-start | bytes 1572868
  53.4 19.9 %slice-start = ((s8[16777216]{0:T(1024)(128)(4,1)}), s8[4194304]{0:T(1024)(128)(4,1)S(1)}, s32[]{:S(2)}) async-start(s8[16777216]{0:T(1024)(128)(4,1)} %bitcast.16), calls=%async_computation.5 | async-start | bytes 8388608
  53.4 19.9 %slice-start.1 = ((s8[16777216]{0:T(1024)(128)(4,1)}), s8[4194304]{0:T(1024)(128)(4,1)S(1)}, s32[]{:S(2)}) async-start(s8[16777216]{0:T(1024)(128)(4,1)} %bitcast.16), calls=%async_computation.6 | async-start | bytes 8388608
  53.4 3.6 %collective-permute-start.2 = (bf16[3072,256]{1,0:T(8,128)(2,1)}, bf16[3072,256]{1,0:T(8,128)(2,1)S(1)}, u32[]{:S(2)}, u32[]{:S(2)}) collective-permute-start(bf16[3072,256]{1,0:T(8,128)(2,1)} %gate.4.refs_3_.refs_7_), channel_id=1, source_target_pairs={{0,1},{1,0},{2,3},{3,2},{4,5},{5,4},{6,7},{7,6},{8,9},{9,8},{10,11... | collective-permute-start | bytes 4718600 | tf_op jit(solution)/shard_map/ppermute | solution.py:115
  53.5 14.3 %collective-permute-start.4 = (bf16[1024,256]{1,0:T(8,128)(2,1)S(1)}, bf16[1024,256]{1,0:T(8,128)(2,1)S(1)}, u32[]{:S(2)}, u32[]{:S(2)}) collective-permute-start(bf16[1024,256]{1,0:T(8,128)(2,1)S(1)} %copy-done.18), channel_id=1, source_target_pairs={{0,2},{1,3},{2,0},{3,1},{4,6},{5,7},{6,4},{7,5},{8,10},{9,11},{10,... | collective-permute-start | bytes 1572872 | tf_op jit(solution)/shard_map/ppermute | solution.py:115
  55.0 23.4 %collective-permute-start.3 = (bf16[1024,256]{1,0:T(8,128)(2,1)S(1)}, bf16[1024,256]{1,0:T(8,128)(2,1)S(1)}, u32[]{:S(2)}, u32[]{:S(2)}) collective-permute-start(bf16[1024,256]{1,0:T(8,128)(2,1)S(1)} %copy-done.18), channel_id=1, source_target_pairs={{0,1},{1,0},{2,3},{3,2},{4,5},{5,4},{6,7},{7,6},{8,9},{9,8},{10,11... | collective-permute-start | bytes 1572872 | tf_op jit(solution)/shard_map/ppermute | solution.py:115
  58.2 15.1 %slice-start.2 = ((s8[16777216]{0:T(1024)(128)(4,1)}), s8[4194304]{0:T(1024)(128)(4,1)S(1)}, s32[]{:S(2)}) async-start(s8[16777216]{0:T(1024)(128)(4,1)} %bitcast.16), calls=%async_computation.7 | async-start | bytes 8388608
  68.6 9.8 %collective-permute-start.5 = (bf16[1024,256]{1,0:T(8,128)(2,1)}, bf16[1024,256]{1,0:T(8,128)(2,1)S(1)}, u32[]{:S(2)}, u32[]{:S(2)}) collective-permute-start(bf16[1024,256]{1,0:T(8,128)(2,1)} %gate.5.refs_3_.refs_11_), channel_id=1, source_target_pairs={{0,1},{1,0},{2,3},{3,2},{4,5},{5,4},{6,7},{7,6},{8,9},{9,8},{10,11... | collective-permute-start | bytes 1572872 | tf_op jit(solution)/shard_map/ppermute | solution.py:115
  68.6 4.7 %slice-start.3 = ((s8[16777216]{0:T(1024)(128)(4,1)}), s8[4194304]{0:T(1024)(128)(4,1)S(1)}, s32[]{:S(2)}) async-start(s8[16777216]{0:T(1024)(128)(4,1)} %bitcast.16), calls=%async_computation.8 | async-start | bytes 8388608
  68.6 4.7 %copy-start.3 = (bf16[256,3072]{1,0:T(8,128)(2,1)S(1)}, bf16[256,3072]{1,0:T(8,128)(2,1)}, u32[]{:S(2)}) copy-start(bf16[256,3072]{1,0:T(8,128)(2,1)} %copy-done.2) | copy-start | bytes 4718596
  71.3 12.4 %collective-permute-start.6 = (f32[64,512]{1,0:T(8,128)}, f32[64,512]{1,0:T(8,128)S(1)}, u32[]{:S(2)}, u32[]{:S(2)}) collective-permute-start(f32[64,512]{1,0:T(8,128)} %get-tuple-element.50), channel_id=1, source_target_pairs={{0,1},{1,0},{2,3},{3,2},{4,5},{5,4},{6,7},{7,6},{8,9},{9,8},{10,11... | collective-permute-start | bytes 393224 | tf_op jit(solution)/shard_map/ppermute | solution.py:115
  71.8 11.9 %collective-permute-start.7 = (f32[64,512]{1,0:T(8,128)}, f32[64,512]{1,0:T(8,128)S(1)}, u32[]{:S(2)}, u32[]{:S(2)}) collective-permute-start(f32[64,512]{1,0:T(8,128)} %get-tuple-element.51), channel_id=1, source_target_pairs={{0,2},{1,3},{2,0},{3,1},{4,6},{5,7},{6,4},{7,5},{8,10},{9,11},{10,... | collective-permute-start | bytes 393224 | tf_op jit(solution)/shard_map/ppermute | solution.py:115
  73.3 10.5 %collective-permute-start.8 = (f32[64,512]{1,0:T(8,128)}, f32[64,512]{1,0:T(8,128)S(1)}, u32[]{:S(2)}, u32[]{:S(2)}) collective-permute-start(f32[64,512]{1,0:T(8,128)} %get-tuple-element.52), channel_id=1, source_target_pairs={{0,3},{1,2},{2,1},{3,0},{4,7},{5,6},{6,5},{7,4},{8,11},{9,10},{10,... | collective-permute-start | bytes 393224 | tf_op jit(solution)/shard_map/ppermute | solution.py:115
  78.4 5.4 %copy-start.11 = (f32[64,512]{1,0:T(8,128)S(1)}, f32[64,512]{1,0:T(8,128)}, u32[]{:S(2)}) copy-start(f32[64,512]{1,0:T(8,128)} %get-tuple-element.49.refs_3_.refs_1_) | copy-start | bytes 393220
  83.7 3.5 %copy-start.1 = (bf16[256,1024]{1,0:T(8,128)(2,1)}, bf16[256,1024]{1,0:T(8,128)(2,1)S(1)}, u32[]{:S(2)}) copy-start(bf16[256,1024]{1,0:T(8,128)(2,1)S(1)} %get-tuple-element.47.refs_0_.refs_1_) | copy-start | bytes 1572868
  83.7 3.5 %copy-start.7 = (f32[64,512]{1,0:T(8,128)}, f32[64,512]{1,0:T(8,128)S(1)}, u32[]{:S(2)}) copy-start(f32[64,512]{1,0:T(8,128)S(1)} %collective-permute-done.6.refs_4_.refs_2_) | copy-start | bytes 393220
  83.8 3.5 %copy-start.8 = (f32[64,512]{1,0:T(8,128)}, f32[64,512]{1,0:T(8,128)S(1)}, u32[]{:S(2)}) copy-start(f32[64,512]{1,0:T(8,128)S(1)} %collective-permute-done.7.refs_5_.refs_3_) | copy-start | bytes 393220
  83.8 3.4 %copy-start.9 = (f32[64,512]{1,0:T(8,128)}, f32[64,512]{1,0:T(8,128)S(1)}, u32[]{:S(2)}) copy-start(f32[64,512]{1,0:T(8,128)S(1)} %collective-permute-done.8.refs_6_.refs_4_) | copy-start | bytes 393220
  87.2 55.2 %all-to-all-start.1 = ((bf16[32,64,256]{2,1,0:T(8,128)(2,1)}), bf16[32,64,256]{2,1,0:T(8,128)(2,1)S(1)}, u32[]{:S(2)}, u32[]{:S(2)}) async-start(bf16[32,64,256]{2,1,0:T(8,128)(2,1)} %bitcast.7), calls=%async_computation.1 | async-start | bytes 2097152 | tf_op jit(solution)/shard_map/all_to_all | solution.py:124
  93.3 25.5 %collective-permute-start.10 = (bf16[1024,256]{1,0:T(8,128)(2,1)}, bf16[1024,256]{1,0:T(8,128)(2,1)S(1)}, u32[]{:S(2)}, u32[]{:S(2)}) collective-permute-start(bf16[1024,256]{1,0:T(8,128)(2,1)} %gate.6.refs_5_), channel_id=1, source_target_pairs={{0,2},{1,3},{2,0},{3,1},{4,6},{5,7},{6,4},{7,5},{8,10},{9,11},{10,... | collective-permute-start | bytes 1572872 | tf_op jit(solution)/shard_map/ppermute | solution.py:115
  94.8 34.8 %collective-permute-start.12 = (bf16[1024,256]{1,0:T(8,128)(2,1)}, bf16[1024,256]{1,0:T(8,128)(2,1)S(1)}, u32[]{:S(2)}, u32[]{:S(2)}) collective-permute-start(bf16[1024,256]{1,0:T(8,128)(2,1)} %gate.7.refs_5_), channel_id=1, source_target_pairs={{0,2},{1,3},{2,0},{3,1},{4,6},{5,7},{6,4},{7,5},{8,10},{9,11},{10,... | collective-permute-start | bytes 1572872 | tf_op jit(solution)/shard_map/ppermute | solution.py:115
  95.4 34.2 %collective-permute-start.13 = (f32[256]{0:T(256)S(1)}, f32[256]{0:T(256)S(1)}, u32[]{:S(2)}, u32[]{:S(2)}) collective-permute-start(f32[256]{0:T(256)S(1)} %copy-done.21), channel_id=1, source_target_pairs={{0,2},{1,3},{2,0},{3,1},{4,6},{5,7},{6,4},{7,5},{8,10},{9,11},{10,... | collective-permute-start | bytes 3080 | tf_op jit(solution)/shard_map/ppermute | solution.py:115
  96.8 44.8 %collective-permute-start.9 = (bf16[1024,256]{1,0:T(8,128)(2,1)}, bf16[1024,256]{1,0:T(8,128)(2,1)S(1)}, u32[]{:S(2)}, u32[]{:S(2)}) collective-permute-start(bf16[1024,256]{1,0:T(8,128)(2,1)} %gate.6.refs_5_), channel_id=1, source_target_pairs={{0,1},{1,0},{2,3},{3,2},{4,5},{5,4},{6,7},{7,6},{8,9},{9,8},{10,11... | collective-permute-start | bytes 1572872 | tf_op jit(solution)/shard_map/ppermute | solution.py:115
  118.8 19.2 %copy-start.27 = (bf16[1024,256]{1,0:T(8,128)(2,1)}, bf16[1024,256]{1,0:T(8,128)(2,1)S(1)}, u32[]{:S(2)}) copy-start(bf16[1024,256]{1,0:T(8,128)(2,1)S(1)} %collective-permute-done.10.refs_7_) | copy-start | bytes 1572868
  118.8 23.6 %collective-permute-start.11 = (bf16[1024,256]{1,0:T(8,128)(2,1)S(1)}, bf16[1024,256]{1,0:T(8,128)(2,1)}, u32[]{:S(2)}, u32[]{:S(2)}) collective-permute-start(bf16[1024,256]{1,0:T(8,128)(2,1)S(1)} %collective-permute-done.10.refs_7_), channel_id=1, source_target_pairs={{0,1},{1,0},{2,3},{3,2},{4,5},{5,4},{6,7},{7,6},{8,9},{9,8},{10,11... | collective-permute-start | bytes 1572872 | tf_op jit(solution)/shard_map/ppermute | solution.py:115
  137.9 4.5 %copy-start.12 = (bf16[3072,256]{1,0:T(8,128)(2,1)S(1)}, bf16[3072,256]{1,0:T(8,128)(2,1)}, u32[]{:S(2)}) copy-start(bf16[3072,256]{1,0:T(8,128)(2,1)} %hidden_slope.2.refs_9_.refs_3_) | copy-start | bytes 4718596
  147.5 4.9 %copy-start.31 = (bf16[80,1792]{1,0:T(8,128)(2,1)S(1)}, bf16[80,1792]{1,0:T(8,128)(2,1)}, u32[]{:S(2)}) copy-start(bf16[80,1792]{1,0:T(8,128)(2,1)} %get-tuple-element.55) | copy-start | bytes 860164
  147.5 5.1 %copy-start.30 = (bf16[80,1792]{1,0:T(8,128)(2,1)S(1)}, bf16[80,1792]{1,0:T(8,128)(2,1)}, u32[]{:S(2)}) copy-start(bf16[80,1792]{1,0:T(8,128)(2,1)} %get-tuple-element.56) | copy-start | bytes 860164
  147.5 6.6 %copy-start.29 = (bf16[80,1792]{1,0:T(8,128)(2,1)S(1)}, bf16[80,1792]{1,0:T(8,128)(2,1)}, u32[]{:S(2)}) copy-start(bf16[80,1792]{1,0:T(8,128)(2,1)} %get-tuple-element.57) | copy-start | bytes 860164
  147.5 35.2 %all-to-all-start.2 = ((bf16[32,64,256]{2,1,0:T(8,128)(2,1)}), bf16[32,64,256]{2,1,0:T(8,128)(2,1)S(1)}, u32[]{:S(2)}, u32[]{:S(2)}) async-start(bf16[32,64,256]{2,1,0:T(8,128)(2,1)} %bitcast.10), calls=%async_computation.2 | async-start | bytes 2097152 | tf_op jit(solution)/shard_map/all_to_all | solution.py:124
  152.4 1.9 collective-permute-start.14
  152.6 18.6 %collective-permute-start.15 = (bf16[80,1792]{1,0:T(8,128)(2,1)S(1)}, bf16[80,1792]{1,0:T(8,128)(2,1)S(1)}, u32[]{:S(2)}, u32[]{:S(2)}) collective-permute-start(bf16[80,1792]{1,0:T(8,128)(2,1)S(1)} %copy-done.30), channel_id=1, source_target_pairs={{0,2},{1,3},{2,0},{3,1},{4,6},{5,7},{6,4},{7,5},{8,10},{9,11},{10,... | collective-permute-start | bytes 860168 | tf_op jit(solution)/shard_map/ppermute | solution.py:115
  154.1 23.9 %collective-permute-start.16 = (bf16[80,1792]{1,0:T(8,128)(2,1)S(1)}, bf16[80,1792]{1,0:T(8,128)(2,1)S(1)}, u32[]{:S(2)}, u32[]{:S(2)}) collective-permute-start(bf16[80,1792]{1,0:T(8,128)(2,1)S(1)} %copy-done.29), channel_id=1, source_target_pairs={{0,3},{1,2},{2,1},{3,0},{4,7},{5,6},{6,5},{7,4},{8,11},{9,10},{10,... | collective-permute-start | bytes 860168 | tf_op jit(solution)/shard_map/ppermute | solution.py:115
  154.4 23.6 %copy-start.32 = (bf16[80,1792]{1,0:T(8,128)(2,1)}, bf16[80,1792]{1,0:T(8,128)(2,1)S(1)}, u32[]{:S(2)}) copy-start(bf16[80,1792]{1,0:T(8,128)(2,1)S(1)} %collective-permute-done.14.refs_6_) | copy-start | bytes 860164
  171.2 6.8 %copy-start.33 = (bf16[80,1792]{1,0:T(8,128)(2,1)}, bf16[80,1792]{1,0:T(8,128)(2,1)S(1)}, u32[]{:S(2)}) copy-start(bf16[80,1792]{1,0:T(8,128)(2,1)S(1)} %collective-permute-done.15.refs_7_) | copy-start | bytes 860164
  182.1 39.0 %collective-permute-start.25 = (bf16[4,272,256]{2,1,0:T(8,128)(2,1)}, bf16[4,272,256]{2,1,0:T(8,128)(2,1)S(1)}, u32[]{:S(2)}, u32[]{:S(2)}) collective-permute-start(bf16[4,272,256]{2,1,0:T(8,128)(2,1)} %get-tuple-element.71), channel_id=1, source_target_pairs={{0,4},{4,0},{8,12},{12,8},{16,20},{20,16},{24,28},{28,24},{1,5},{5... | collective-permute-start | bytes 1671176 | tf_op jit(solution)/shard_map/ppermute | solution.py:115
  182.7 25.1 %collective-permute-start.18 = (bf16[2048,256]{1,0:T(8,128)(2,1)S(1)}, bf16[2048,256]{1,0:T(8,128)(2,1)S(1)}, u32[]{:S(2)}, u32[]{:S(2)}) collective-permute-start(bf16[2048,256]{1,0:T(8,128)(2,1)S(1)} %bitcast.18), channel_id=1, source_target_pairs={{0,2},{1,3},{2,0},{3,1},{4,6},{5,7},{6,4},{7,5},{8,10},{9,11},{10,... | collective-permute-start | bytes 3145736 | tf_op jit(solution)/shard_map/ppermute | solution.py:115
  200.2 84.2 %collective-permute-start.17 = (bf16[4096,256]{1,0:T(8,128)(2,1)}, bf16[4096,256]{1,0:T(8,128)(2,1)}, u32[]{:S(2)}, u32[]{:S(2)}) collective-permute-start(bf16[4096,256]{1,0:T(8,128)(2,1)} %get-tuple-element.62.refs_5_.refs_1_.refs_2_), channel_id=1, source_target_pairs={{0,1},{1,0},{2,3},{3,2},{4,5},{5,4},{6,7},{7,6},{8,9},{9,8},{10,11... | collective-permute-start | bytes 6291464 | tf_op jit(solution)/shard_map/ppermute | solution.py:115
  200.3 45.1 %all-to-all-start.3 = ((bf16[8,144,256]{2,1,0:T(8,128)(2,1)}), bf16[8,144,256]{2,1,0:T(8,128)(2,1)S(1)}, u32[]{:S(2)}, u32[]{:S(2)}) async-start(bf16[8,144,256]{2,1,0:T(8,128)(2,1)} %get-tuple-element.67), calls=%async_computation.3 | async-start | bytes 1179648 | tf_op jit(solution)/shard_map/all_to_all | solution.py:124
  221.1 63.3 %collective-permute-start.19 = (bf16[4096,256]{1,0:T(8,128)(2,1)}, bf16[4096,256]{1,0:T(8,128)(2,1)}, u32[]{:S(2)}, u32[]{:S(2)}) collective-permute-start(bf16[4096,256]{1,0:T(8,128)(2,1)} %rows_back.1.refs_3_), channel_id=1, source_target_pairs={{0,1},{1,0},{2,3},{3,2},{4,5},{5,4},{6,7},{7,6},{8,9},{9,8},{10,11... | collective-permute-start | bytes 6291464 | tf_op jit(solution)/shard_map/ppermute | solution.py:115
  224.0 7.2 %collective-permute-start.26 = (bf16[272,256]{1,0:T(8,128)(2,1)}, bf16[272,256]{1,0:T(8,128)(2,1)S(1)}, u32[]{:S(2)}, u32[]{:S(2)}) collective-permute-start(bf16[272,256]{1,0:T(8,128)(2,1)} %get-tuple-element.73), channel_id=1, source_target_pairs={{0,8},{4,12},{8,0},{12,4},{16,24},{20,28},{24,16},{28,20},{1,9},{5... | collective-permute-start | bytes 417800 | tf_op jit(solution)/shard_map/ppermute | solution.py:115
  224.7 12.6 %collective-permute-start.27 = (bf16[272,256]{1,0:T(8,128)(2,1)}, bf16[272,256]{1,0:T(8,128)(2,1)S(1)}, u32[]{:S(2)}, u32[]{:S(2)}) collective-permute-start(bf16[272,256]{1,0:T(8,128)(2,1)} %get-tuple-element.74), channel_id=1, source_target_pairs={{0,16},{4,20},{8,24},{12,28},{16,0},{20,4},{24,8},{28,12},{1,17},{... | collective-permute-start | bytes 417800 | tf_op jit(solution)/shard_map/ppermute | solution.py:115
  226.9 13.5 %collective-permute-start.28 = (bf16[272,256]{1,0:T(8,128)(2,1)}, bf16[272,256]{1,0:T(8,128)(2,1)S(1)}, u32[]{:S(2)}, u32[]{:S(2)}) collective-permute-start(bf16[272,256]{1,0:T(8,128)(2,1)} %get-tuple-element.75), channel_id=1, source_target_pairs={{0,24},{4,28},{8,16},{12,20},{16,8},{20,12},{24,0},{28,4},{1,25},{... | collective-permute-start | bytes 417800 | tf_op jit(solution)/shard_map/ppermute | solution.py:115
  241.9 9.8 %collective-permute-start.29 = (bf16[256,256]{1,0:T(8,128)(2,1)S(1)}, bf16[256,256]{1,0:T(8,128)(2,1)S(1)}, u32[]{:S(2)}, u32[]{:S(2)}) collective-permute-start(bf16[256,256]{1,0:T(8,128)(2,1)S(1)} %get-tuple-element.76.refs_0_), channel_id=1, source_target_pairs={{0,8},{4,12},{8,0},{12,4},{16,24},{20,28},{24,16},{28,20},{1,9},{5... | collective-permute-start | bytes 393224 | tf_op jit(solution)/shard_map/ppermute | solution.py:115
  241.9 15.0 %collective-permute-start.30 = (bf16[256,256]{1,0:T(8,128)(2,1)S(1)}, bf16[256,256]{1,0:T(8,128)(2,1)S(1)}, u32[]{:S(2)}, u32[]{:S(2)}) collective-permute-start(bf16[256,256]{1,0:T(8,128)(2,1)S(1)} %get-tuple-element.76.refs_0_), channel_id=1, source_target_pairs={{0,16},{4,20},{8,24},{12,28},{16,0},{20,4},{24,8},{28,12},{1,17},{... | collective-permute-start | bytes 393224 | tf_op jit(solution)/shard_map/ppermute | solution.py:115
  244.8 18.5 %collective-permute-start.31 = (bf16[256,256]{1,0:T(8,128)(2,1)S(1)}, bf16[256,256]{1,0:T(8,128)(2,1)S(1)}, u32[]{:S(2)}, u32[]{:S(2)}) collective-permute-start(bf16[256,256]{1,0:T(8,128)(2,1)S(1)} %get-tuple-element.76.refs_0_), channel_id=1, source_target_pairs={{0,24},{4,28},{8,16},{12,20},{16,8},{20,12},{24,0},{28,4},{1,25},{... | collective-permute-start | bytes 393224 | tf_op jit(solution)/shard_map/ppermute | solution.py:115
  246.3 31.7 %all-to-all-start.4 = ((bf16[8,128,256]{2,1,0:T(8,128)(2,1)}), bf16[8,128,256]{2,1,0:T(8,128)(2,1)S(1)}, u32[]{:S(2)}, u32[]{:S(2)}) async-start(bf16[8,128,256]{2,1,0:T(8,128)(2,1)} %get-tuple-element.68), calls=%async_computation.4 | async-start | bytes 1048576 | tf_op jit(solution)/shard_map/all_to_all | solution.py:124
  251.8 13.2 %copy-start.15 = (bf16[1024,256]{1,0:T(8,128)(2,1)S(1)}, bf16[1024,256]{1,0:T(8,128)(2,1)}, u32[]{:S(2)}) copy-start(bf16[1024,256]{1,0:T(8,128)(2,1)} %gate.7.refs_5_) | copy-start | bytes 1572868
  251.8 13.2 %copy-start.24 = (bf16[1024,256]{1,0:T(8,128)(2,1)S(1)}, bf16[1024,256]{1,0:T(8,128)(2,1)}, u32[]{:S(2)}) copy-start(bf16[1024,256]{1,0:T(8,128)(2,1)} %copy-done.23) | copy-start | bytes 1572868
  251.8 22.2 %copy-start.37 = (bf16[256,256]{1,0:T(8,128)(2,1)S(1)}, bf16[256,256]{1,0:T(8,128)(2,1)}, u32[]{:S(2)}) copy-start(bf16[256,256]{1,0:T(8,128)(2,1)} %get-tuple-element.64) | copy-start | bytes 393220
  263.4 10.6 %collective-permute-start.32 = (bf16[4,256,256]{2,1,0:T(8,128)(2,1)S(1)}, bf16[4,256,256]{2,1,0:T(8,128)(2,1)S(1)}, u32[]{:S(2)}, u32[]{:S(2)}) collective-permute-start(bf16[4,256,256]{2,1,0:T(8,128)(2,1)S(1)} %stack.13.refs_1_), channel_id=1, source_target_pairs={{0,4},{4,0},{8,12},{12,8},{16,20},{20,16},{24,28},{28,24},{1,5},{5... | collective-permute-start | bytes 1572872 | tf_op jit(solution)/shard_map/ppermute | solution.py:115
  265.0 11.1 %collective-permute-start.20 = (bf16[1024,256]{1,0:T(8,128)(2,1)S(1)}, bf16[1024,256]{1,0:T(8,128)(2,1)S(1)}, u32[]{:S(2)}, u32[]{:S(2)}) collective-permute-start(bf16[1024,256]{1,0:T(8,128)(2,1)S(1)} %copy-done.15), channel_id=1, source_target_pairs={{0,1},{1,0},{2,3},{3,2},{4,5},{5,4},{6,7},{7,6},{8,9},{9,8},{10,11... | collective-permute-start | bytes 1572872 | tf_op jit(solution)/shard_map/ppermute | solution.py:115
  265.0 11.8 %collective-permute-start.21 = (bf16[1024,256]{1,0:T(8,128)(2,1)S(1)}, bf16[1024,256]{1,0:T(8,128)(2,1)S(1)}, u32[]{:S(2)}, u32[]{:S(2)}) collective-permute-start(bf16[1024,256]{1,0:T(8,128)(2,1)S(1)} %copy-done.24), channel_id=1, source_target_pairs={{0,1},{1,0},{2,3},{3,2},{4,5},{5,4},{6,7},{7,6},{8,9},{9,8},{10,11... | collective-permute-start | bytes 1572872 | tf_op jit(solution)/shard_map/ppermute | solution.py:115
  274.0 2.8 copy-start.35
  274.0 5.0 %collective-permute-start.22 = (bf16[256,256]{1,0:T(8,128)(2,1)S(1)}, bf16[256,256]{1,0:T(8,128)(2,1)S(1)}, u32[]{:S(2)}, u32[]{:S(2)}) collective-permute-start(bf16[256,256]{1,0:T(8,128)(2,1)S(1)} %copy-done.37), channel_id=1, source_target_pairs={{0,1},{1,0},{2,3},{3,2},{4,5},{5,4},{6,7},{7,6},{8,9},{9,8},{10,11... | collective-permute-start | bytes 393224 | tf_op jit(solution)/shard_map/ppermute | solution.py:115
  276.0 3.0 %copy-start.25 = (bf16[1024,256]{1,0:T(8,128)(2,1)}, bf16[1024,256]{1,0:T(8,128)(2,1)S(1)}, u32[]{:S(2)}) copy-start(bf16[1024,256]{1,0:T(8,128)(2,1)S(1)} %collective-permute-done.20.refs_6_) | copy-start | bytes 1572868
  276.0 6.4 %collective-permute-start.23 = (bf16[256,256]{1,0:T(8,128)(2,1)S(1)}, bf16[256,256]{1,0:T(8,128)(2,1)S(1)}, u32[]{:S(2)}, u32[]{:S(2)}) collective-permute-start(bf16[256,256]{1,0:T(8,128)(2,1)S(1)} %copy-done.36), channel_id=1, source_target_pairs={{0,2},{1,3},{2,0},{3,1},{4,6},{5,7},{6,4},{7,5},{8,10},{9,11},{10,... | collective-permute-start | bytes 393224 | tf_op jit(solution)/shard_map/ppermute | solution.py:115
  276.8 7.6 %collective-permute-start.24 = (bf16[256,256]{1,0:T(8,128)(2,1)S(1)}, bf16[256,256]{1,0:T(8,128)(2,1)S(1)}, u32[]{:S(2)}, u32[]{:S(2)}) collective-permute-start(bf16[256,256]{1,0:T(8,128)(2,1)S(1)} %copy-done.35), channel_id=1, source_target_pairs={{0,3},{1,2},{2,1},{3,0},{4,7},{5,6},{6,5},{7,4},{8,11},{9,10},{10,... | collective-permute-start | bytes 393224 | tf_op jit(solution)/shard_map/ppermute | solution.py:115
  279.0 5.4 %copy-start.38 = (bf16[256,256]{1,0:T(8,128)(2,1)}, bf16[256,256]{1,0:T(8,128)(2,1)S(1)}, u32[]{:S(2)}) copy-start(bf16[256,256]{1,0:T(8,128)(2,1)S(1)} %collective-permute-done.22.refs_10_) | copy-start | bytes 393220
  (20 other events, 23.4 us)

commit v3 on v2

--- a/solution.py
+++ b/solution.py
@@ -1,3 +1,4 @@
+import collections
 import functools
 
 import jax
@@ -16,24 +17,20 @@
 code_step = 64
 extra_rows = 16
 mib = 1024 * 1024
-expected_us = dict(
-    slots=3,
-    low=4,
-    spread=20,
-    hidden_both=1,
+expected_us = collections.defaultdict(
+    lambda: 0.001,
     hidden_slope=5,
-    pool=5,
     self_half=3,
     combine=4,
     w_back=4,
-    add=2,
+    rows_back=16,
+    add=20,
+    add_some=1,
     add_pairs=2,
+    table_back=20,
+    cut=1,
     collect=2,
-    stack=1,
-    widen=2,
-    rows_back_q=13,
-    rows_back=9,
-    table_back=8,
+    widen=1,
 )
 
 
@@ -66,7 +63,7 @@
     return pltpu.HBM(dims, dtype)
 
 
-def call(kernel, name, operands, outs, grid=(1,), scratch=(), after=(), spare=8):
+def call(kernel, name, operands, outs, grid=(1,), scratch=(), after=(), aliases={}, spare=8):
     specs, arrays, need = [], [], 0
     for operand in operands:
         array, spec = operand if isinstance(operand, tuple) else (operand, whole(operand))
@@ -87,6 +84,7 @@
         out_specs=[o[0] for o in outs],
         out_shape=[o[1] for o in outs],
         scratch_shapes=list(scratch),
+        input_output_aliases=dict(aliases),
         compiler_params=pltpu.CompilerParams(vmem_limit_bytes=need + spare * mib),
         cost_estimate=pl.CostEstimate(
             flops=int(expected_us[name] * 1.15e9), bytes_accessed=int(expected_us[name] * 3.69e6), transcendentals=0
@@ -145,51 +143,21 @@
     return specs
 
 
-def low_kernel(first, table_ref, q_ref, w_ref, a_ref, b_ref, q_low_ref, self_ref, pooled_ref):
-    step = pl.program_id(0)
-    low = table_ref[...].astype(bf16)
-    q_low_ref[...] = q_ref[...].astype(bf16)
-    w_low = w_ref[...].astype(bf16)
-
-    @pl.when(step < first)
-    def _():
-        a_ref[...] = low
-
-    @pl.when(step >= first)
-    def _():
-        b_ref[...] = low
-
-    @pl.when(step < 2)
-    def _():
-        self_ref[...] = w_low
-
-    @pl.when(step >= 2)
-    def _():
-        pooled_ref[...] = w_low
-
-
-def low_all(table, q_weight, w_weight, cut):
-    rows, columns = table.shape
-    block = rows // 4
-    first = cut // block
-    q_rows, w_rows = q_weight.shape[0], w_weight.shape[0]
-    return call(
-        functools.partial(low_kernel, first),
-        "low",
-        [
-            (far(table), row_blocks(block, columns)),
-            (far(q_weight), row_blocks(q_rows // 4, columns)),
-            (far(w_weight), row_blocks(w_rows // 4, columns)),
-        ],
-        [
-            (chunk_spec(block, columns, 0, first), far_shape((cut, columns), bf16)),
-            (chunk_spec(block, columns, first, 4 - first), far_shape((rows - cut, columns), bf16)),
-            (row_blocks(q_rows // 4, columns), far_shape((q_rows, columns), bf16)),
-            (chunk_spec(w_rows // 4, columns, 0, 2), far_shape((w_rows // 2, columns), bf16)),
-            (chunk_spec(w_rows // 4, columns, 2, 2), far_shape((w_rows // 2, columns), bf16)),
-        ],
-        grid=(4,),
-    )
+def low_kernel(count, *refs):
+    for i in range(count):
+        refs[count + i][...] = refs[i][...].astype(bf16)
+
+
+def low(pieces, after=()):
+    steps = 4
+    operands, outs = [], []
+    for array, first, rows in pieces:
+        block, columns = rows // steps, array.shape[1]
+        operands.append(
+            (far(array), pl.BlockSpec((block, columns), functools.partial(lambda f, i: (f + i, 0), first // block)))
+        )
+        outs.append((row_blocks(block, columns), far_shape((rows, columns), bf16)))
+    return call(functools.partial(low_kernel, len(pieces)), "low", operands, outs, grid=(steps,), after=after)
 
 
 def gate_kernel(*refs):
@@ -206,7 +174,7 @@
         compiler_params=pltpu.CompilerParams(vmem_limit_bytes=mib),
         cost_estimate=pl.CostEstimate(flops=1, bytes_accessed=1, transcendentals=0),
         name="gate",
-    )(far(array), *map(far, after))
+    )(array, *after)
 
 
 def slots_kernel(row_dev, place_ref, ids_ref, counts_ref, importance_ref, out_ref):
@@ -308,7 +276,7 @@
     lax.fori_loop(1, (depth + 7) // 8, more, 0)
 
 
-def spread(slots, row_dev):
+def spread(slots, row_dev, after=()):
     groups, _, slots_node, node_dev = slots.shape
     tiles = node_dev // lane_tile
     buckets = row_dev // bucket_rows
@@ -323,6 +291,7 @@
             pltpu.VMEM((tiles, buckets, 8, lane_tile), f32),
             pltpu.VMEM((tiles, buckets, 8, lane_tile), f32),
         ],
+        after=after,
     )[0]
 
 
@@ -333,9 +302,10 @@
     for j in range(sides):
         pre = pre + dot(table[j][...], rows_at(q_ref, (place_ref[1] ^ j) * width, width)[...], (1, 0))
     value, slope = gelu_parts(pre)
-    if want == "both":
+    if want == "value":
         outs[0][...] = value.astype(bf16).T
-    outs[-1][...] = slope.astype(bf16)
+    else:
+        outs[0][...] = slope.astype(bf16)
 
 
 def hidden(place, table, q_low, bias, want, after=()):
@@ -343,19 +313,20 @@
     columns = q_low.shape[1]
     sides = len(table)
     block = min(rows, 512)
-    outs = [(row_blocks(block, columns), far_shape((rows, columns), bf16))]
-    if want == "both":
-        outs.insert(0, (pl.BlockSpec((columns, block), lambda i: (0, i)), shape((columns, rows), bf16)))
+    if want == "value":
+        out = (pl.BlockSpec((columns, block), lambda i: (0, i)), shape((columns, rows), bf16))
+    else:
+        out = (row_blocks(block, columns), far_shape((rows, columns), bf16))
     return call(
         functools.partial(hidden_kernel, sides, want),
         "hidden_" + want,
         [(place, smem)]
-        + [(far(a), row_blocks(block, width)) for a in table]
+        + [(a if want == "value" else far(a), row_blocks(block, width)) for a in table]
         + [far(q_low), far(bias.reshape(1, columns))],
-        outs,
+        [out],
         grid=(rows // block,),
         after=after,
-    )
+    )[0]
 
 
 def pool_kernel(last, hidden_ref, matrix_ref, *refs):
@@ -424,7 +395,7 @@
 
 def combine_kernel(node_total, sides, parts_ref, *refs):
     early, w_refs = refs[:sides], refs[sides : 2 * sides]
-    grad_ref, late = refs[2 * sides], refs[2 * sides + 1 :]
+    grad_ref, pooled_ref, late = refs[2 * sides], refs[2 * sides + 1], refs[2 * sides + 2 :]
     groups, _, few, columns = parts_ref.shape
     pooled = []
     for m in range(sides):
@@ -433,6 +404,7 @@
             total = total + parts_ref[g, m].astype(f32)
         pooled.append(total.astype(bf16))
     pooled = jnp.concatenate(pooled, axis=1)
+    pooled_ref[...] = pooled
     activated, slope, squares, cross = [], [], 0.0, 0.0
     for j in range(sides):
         pre = early[j][:, 0:columns] + dot(pooled, w_refs[j][...], (1, 0))
@@ -453,11 +425,8 @@
         grad_act = early[j][:, columns:] * scale - activated[j] * pull + (2.0 * penalty_rate / node_total) * activated[j]
         grad = (grad_act * slope[j]).astype(bf16)
         grad_pooled = grad_pooled + dot(grad, w_refs[j][...], (1, 1))
-        high, low = halves(activated[j] * scale)
-        late[j][0:few, 0:columns] = high
-        late[j][0:few, columns : 2 * columns] = low
-        late[j][0:few, 2 * columns : 3 * columns] = grad
-        late[j][0:few, 3 * columns :] = pooled
+        late[j][0:few, 0:columns] = (activated[j] * scale).astype(bf16)
+        late[j][0:few, columns:] = grad
         late[j][few:, :] = extra
     for m in range(sides):
         part = grad_pooled[:, m * columns : (m + 1) * columns].astype(bf16)
@@ -471,29 +440,24 @@
         functools.partial(combine_kernel, node_total, sides),
         "combine",
         [parts, *map(far, early), *map(far, w_pooled)],
-        [full(parts.shape, bf16)] + [full((few + extra_rows, (3 + sides) * columns), bf16, far_shape)] * sides,
-        after=after,
-    )
-
-
-def w_back_kernel(sides, groups, place_ref, *refs):
-    own, late, (w_ref, emb_ref, even_ref, odd_ref, *self_refs), scratch = (
-        refs[:sides],
-        refs[sides : 2 * sides],
-        refs[2 * sides : -3],
-        refs[-3:],
-    )
+        [full(parts.shape, bf16), full((few, sides * columns), bf16, far_shape)]
+        + [full((few + extra_rows, 2 * columns), bf16, far_shape)] * sides,
+        after=after,
+    )
+
+
+def w_back_kernel(sides, place_ref, *refs):
+    own, late, pooled = refs[:sides], refs[sides : 2 * sides], refs[2 * sides : 3 * sides]
+    (w_ref, emb_ref, even_ref, odd_ref, extra_ref, *self_refs), scratch = refs[3 * sides : -3], refs[-3:]
     grad_ref, pooled_ref, total_ref = scratch
     nodes, columns = emb_ref.shape
     few = nodes // sides
     squares = 0.0
     for j in range(sides):
         at = (place_ref[1] ^ j) * few
-        rows_at(emb_ref, at, few)[...] = late[j][0:few, 0:columns].astype(f32) + late[j][
-            0:few, columns : 2 * columns
-        ].astype(f32)
-        rows_at(grad_ref, at, few)[...] = late[j][0:few, 2 * columns : 3 * columns]
-        rows_at(pooled_ref, at, few)[...] = late[j][0:few, 3 * columns :]
+        rows_at(emb_ref, at, few)[...] = late[j][0:few, 0:columns].astype(f32)
+        rows_at(grad_ref, at, few)[...] = late[j][0:few, columns:]
+        rows_at(pooled_ref, at, few)[...] = pooled[j][...]
         squares = squares + late[j][few : few + 1, 0:columns].astype(f32)
         squares = squares + late[j][few + 1 : few + 2, 0:columns].astype(f32)
     grad = grad_ref[...]
@@ -504,27 +468,27 @@
     total_ref[sides * columns :, :] = dot(pooled_ref[...], grad, (0, 0))
     bias_high, bias_low = halves(jnp.sum(grad.astype(f32), axis=0, keepdims=True))
     square_high, square_low = halves(squares)
-    piece = total_ref.shape[0] // groups
     index = lax.broadcasted_iota(i32, (extra_rows, columns), 0)
     extra = jnp.zeros(index.shape, f32)
     for i, row in enumerate((bias_high, bias_low, square_high, square_low)):
-        extra = jnp.where(index == i, row.astype(f32), extra)
-    extra = extra.astype(bf16)
-    for s in range(groups):
-        part = (odd_ref if s % 2 else even_ref).at[s // 2]
-        part[0:piece, :] = rows_at(total_ref, (place_ref[0] ^ s) * piece, piece)[...].astype(bf16)
-        part[piece:, :] = extra
-
-
-def w_back(place, table, late, w_self, node_dev, groups, after=()):
+        extra = jnp.where(index == 2 + i, row.astype(f32), extra)
+    extra_ref[...] = extra.astype(bf16)
+    count, piece, _ = even_ref.shape
+    for s in range(count):
+        even_ref[s] = rows_at(total_ref, (place_ref[0] ^ (2 * s)) * piece, piece)[...].astype(bf16)
+        odd_ref[s] = rows_at(total_ref, (place_ref[0] ^ (2 * s + 1)) * piece, piece)[...].astype(bf16)
+
+
+def w_back(place, table, late, pooled, w_self, node_dev, groups, after=()):
     sides = len(table)
     rows, columns = 2 * w_self.shape[0], w_self.shape[1]
-    half = full((groups // 2, rows // groups + extra_rows, columns), bf16, far_shape)
-    return call(
-        functools.partial(w_back_kernel, sides, groups),
+    half = full((groups // 2, rows // groups, columns), bf16, far_shape)
+    return call(
+        functools.partial(w_back_kernel, sides),
         "w_back",
-        [(place, smem)] + first_rows(table, node_dev) + [*map(far, late), far(w_self)],
+        [(place, smem)] + first_rows(table, node_dev) + [*map(far, late), *map(far, pooled), far(w_self)],
         [full((node_dev, columns), f32, far_shape), half, half]
+        + [full((extra_rows, columns), bf16, far_shape)]
         + [full((node_dev, columns), bf16, far_shape)] * sides,
         scratch=[
             pltpu.VMEM((node_dev, columns), bf16),
@@ -535,131 +499,100 @@
     )
 
 
-def split_extra(total):
-    index = lax.broadcasted_iota(i32, total.shape, 0)
-    extra = jnp.zeros(total.shape, f32)
-    for i in (0, 2):
-        high, low = halves(total[i : i + 1, :] + total[i + 1 : i + 2, :])
-        extra = jnp.where(index == i, high.astype(f32), jnp.where(index == i + 1, low.astype(f32), extra))
-    return extra
-
-
-def add_kernel(copies, scale, count, *refs):
-    parts, (piece_ref, bias_ref, scalar_ref) = refs[:count], refs[count:]
-    terms = []
-    for part in parts:
-        terms += [part] if len(part.shape) == 2 else [part.at[i] for i in range(part.shape[0])]
-    total = terms[0][...].astype(f32)
-    for part in terms[1:]:
-        total = total + part[...].astype(f32)
-    piece = total.shape[0] - extra_rows
-    low = total[0:piece, :].astype(bf16)
-    if copies:
-        for i in range(copies):
-            piece_ref[i] = low
-    else:
-        piece_ref[...] = low
-    bias_ref[...] = total[piece : piece + 1, :] + total[piece + 1 : piece + 2, :]
-    scalar_ref[...] = scale * (total[piece + 2 : piece + 3, 0:1] + total[piece + 3 : piece + 4, 0:1])
-
-
-def add(parts, copies, scale):
-    rows, columns = parts[0].shape[-2:]
-    piece = (rows - extra_rows, columns)
-    return call(
-        functools.partial(add_kernel, copies, scale, len(parts)),
-        "add",
-        parts,
-        [full((copies, *piece) if copies else piece, bf16), full((1, columns), f32), full((1, 1), f32)],
-    )
-
-
 def add_pairs_kernel(own_ref, other_ref, *outs):
     for i, out in enumerate(outs):
-        total = own_ref[i].astype(f32) + other_ref[i].astype(f32)
-        piece = total.shape[0] - extra_rows
-        out[0:piece, :] = total[0:piece, :].astype(bf16)
-        out[piece:, :] = split_extra(total[piece:, :]).astype(bf16)
+        out[...] = (own_ref[i].astype(f32) + other_ref[i].astype(f32)).astype(bf16)
 
 
 def add_pairs(own, other, after=()):
     count, rows, columns = own.shape
-    return call(add_pairs_kernel, "add_pairs", [far(own), far(other)], [full((rows, columns), bf16, far_shape)] * count, after=after)
-
-
-def stack_kernel(*refs):
-    for i, ref in enumerate(refs[:-1]):
-        refs[-1][i] = ref[...]
-
-
-def stack(arrays):
-    return call(stack_kernel, "stack", arrays, [full((len(arrays), *arrays[0].shape), bf16)])[0]
-
-
-def collect_kernel(place_ref, own_ref, other_ref, out_ref):
-    count, piece, _ = other_ref.shape
-    for s in range(count):
-        rows_at(out_ref, (place_ref[0] ^ (2 * s)) * piece, piece)[...] = own_ref[s].astype(f32)
-        rows_at(out_ref, (place_ref[0] ^ (2 * s + 1)) * piece, piece)[...] = other_ref[s].astype(f32)
-
-
-def collect(place, own, other):
-    count, piece, columns = own.shape
-    return call(
-        collect_kernel, "collect", [(place, smem), own, other], [full((2 * count * piece, columns), f32)]
+    return call(
+        add_pairs_kernel, "add_pairs", [far(own), far(other)], [full((rows, columns), bf16, far_shape)] * count, after=after
+    )
+
+
+def add_some_kernel(count, *refs):
+    total = refs[0][...].astype(f32)
+    for ref in refs[1:count]:
+        total = total + ref[...].astype(f32)
+    refs[count][...] = total.astype(bf16)
+
+
+def add_some(parts, after=()):
+    return call(
+        functools.partial(add_some_kernel, len(parts)), "add_some", parts, [full(parts[0].shape, bf16, far_shape)], after=after
     )[0]
+
+
+def collect_kernel(count, place_ref, *refs):
+    piece = refs[0].shape[0]
+    for i in range(count):
+        rows_at(refs[count], (place_ref[0] ^ i) * piece, piece)[...] = refs[i][...].astype(f32)
+
+
+def collect(place, pieces, after=()):
+    rows, columns = pieces[0].shape
+    return call(
+        functools.partial(collect_kernel, len(pieces)),
+        "collect",
+        [(place, smem), *pieces],
+        [full((len(pieces) * rows, columns), f32, far_shape)],
+        after=after,
+    )[0]
+
+
+def add_kernel(scale, parts_ref, piece_ref, q_bias_ref, w_bias_ref, scalar_ref):
+    groups, rows, _ = parts_ref.shape
+    total = parts_ref[0].astype(f32)
+    for g in range(1, groups):
+        total = total + parts_ref[g].astype(f32)
+    piece = rows - extra_rows
+    low = total[0:piece, :].astype(bf16)
+    for g in range(groups):
+        piece_ref[g] = low
+    pairs = [total[piece + 2 * i : piece + 2 * i + 1, :] + total[piece + 2 * i + 1 : piece + 2 * i + 2, :] for i in range(3)]
+    q_bias_ref[...] = pairs[0]
+    w_bias_ref[...] = pairs[1]
+    scalar_ref[...] = scale * pairs[2][:, 0:1]
+
+
+def add(parts, scale, after=()):
+    groups, rows, columns = parts.shape
+    return call(
+        functools.partial(add_kernel, scale),
+        "add",
+        [parts],
+        [full((groups, rows - extra_rows, columns), bf16), full((1, columns), f32), full((1, columns), f32), full((1, 1), f32)],
+        after=after,
+    )
 
 
 def widen_kernel(low_ref, out_ref):
     out_ref[...] = low_ref[...].astype(f32)
 
 
-def widen(low):
+def widen(low, after=()):
     rows, columns = low.shape
     block = rows // 2
     return call(
         widen_kernel,
         "widen",
         [(low, row_blocks(block, columns))],
-        [(row_blocks(block, columns), shape((rows, columns), f32))],
+        [(row_blocks(block, columns), far_shape((rows, columns), f32))],
         grid=(2,),
+        after=after,
     )[0]
-
-
-def total_direct(parts, scale=0.0):
-    groups, rows, columns = parts.shape
-    pieces, *sums = add([exchange(parts, "dp")], groups, scale)
-    return widen(exchange(pieces, "dp").reshape(-1, columns)), *sums
-
-
-def total_in_steps(place, parts, scale, after=()):
-    count = parts[0].shape[0]
-    mine = add_pairs(parts[0], swap(parts[1], "dp", 1), after=after)
-    piece, *sums = add([mine[0]] + [swap(mine[s], "dp", 2 * s) for s in range(1, count)], 0, scale)
-    pieces = stack([piece] + [swap(piece, "dp", 2 * s) for s in range(1, count)])
-    return collect(place, pieces, swap(pieces, "dp", 1)), *sums
 
 
 def rows_back_kernel(chunk_counts, sides, place_ref, *refs):
     chunks = len(chunk_counts)
     matrix_ref, pooled_ref, slopes = refs[0], refs[1], refs[2 : 2 + chunks]
     table = refs[2 + chunks : 2 + chunks + chunks * sides]
-    grad_ref, rest = refs[2 + chunks + chunks * sides], refs[3 + chunks + chunks * sides :]
+    rest = refs[2 + chunks + chunks * sides :]
+    extra_ref, grad_refs, (q_ref, total_ref, bias_ref) = rest[0], rest[1 : 1 + chunks], rest[1 + chunks :]
     step = pl.program_id(0)
     matrix = jnp.concatenate([matrix_ref[g] for g in range(matrix_ref.shape[0])], axis=1)
     summed = dot(matrix, pooled_ref[...], (1, 0))
-    slope = slopes[0][...]
-    first = chunk_counts[0]
-    for k in range(1, chunks):
-        slope = jnp.where(step >= first, slopes[k][...], slope)
-        first += chunk_counts[k]
-    grad = summed * slope.astype(f32)
-    column_sums = jnp.sum(grad, axis=0, keepdims=True)
-    grad = grad.astype(bf16)
-    grad_ref[...] = grad
-    if not sides:
-        return
-    q_ref, total_ref, bias_ref = rest
     width = table[0].shape[1]
 
     @pl.when(step == 0)
@@ -667,12 +600,15 @@
         bias_ref[...] = jnp.zeros_like(bias_ref)
         total_ref[...] = jnp.zeros_like(total_ref)
 
-    bias_ref[...] += column_sums
     first = 0
     for k in range(chunks):
 
         @pl.when((step >= first) & (step < first + chunk_counts[k]))
         def _():
+            grad = summed * slopes[k][...].astype(f32)
+            bias_ref[...] += jnp.sum(grad, axis=0, keepdims=True)
+            grad = grad.astype(bf16)
+            grad_refs[k][...] = grad
             for j in range(sides):
                 total_ref[j] += dot(grad, table[k * sides + j][...], (0, 0))
 
@@ -683,7 +619,8 @@
         high, low = halves(bias_ref[...])
         groups, rows, columns = q_ref.shape
         index = lax.broadcasted_iota(i32, (extra_rows, columns), 0)
-        extra = jnp.where(index == 0, high.astype(f32), jnp.where(index == 1, low.astype(f32), 0.0)).astype(bf16)
+        extra = extra_ref[...].astype(f32)
+        extra = jnp.where(index == 0, high.astype(f32), jnp.where(index == 1, low.astype(f32), extra)).astype(bf16)
         piece = rows - extra_rows
         per = width // piece
         for g in range(groups):
@@ -694,63 +631,78 @@
                 q_ref[(place_ref[1] ^ j) * per + part, 0:piece, :] = flat[part * piece : (part + 1) * piece, :]
 
 
-def rows_back(place, matrix, pooled, slopes, table, after=()):
-    sides = len(table[0]) if table else 0
+def rows_back(place, matrix, pooled, slopes, table, extra, after=()):
+    sides = len(table[0])
     groups, row_dev, node_dev = matrix.shape
-    columns = pooled.shape[1]
+    columns, width = pooled.shape[1], table[0][0].shape[1]
     block = min(slopes[-1].shape[0], 512 * 2048 // (groups * node_dev))
-    counts = [a.shape[0] // block for a in slopes]
-    operands = [(place, smem), (far(matrix), pl.BlockSpec((groups, block, node_dev), lambda i: (0, i, 0))), pooled]
-    operands += list(zip(map(far, slopes), chunk_specs(slopes, block)))
-    outs = [(row_blocks(block, columns), far_shape((row_dev, columns), bf16))]
-    scratch = []
-    if sides:
-        width = table[0][0].shape[1]
-        by_side = [chunk_specs([part[j] for part in table], block) for j in range(sides)]
-        operands += [(far(table[k][j]), by_side[j][k]) for k in range(len(table)) for j in range(sides)]
-        outs.append(full((groups, sides * width // groups + extra_rows, columns), bf16))
-        scratch = [pltpu.VMEM((sides, columns, width), f32), pltpu.VMEM((1, columns), f32)]
-    return call(
-        functools.partial(rows_back_kernel, counts, sides),
-        "rows_back_q" if sides else "rows_back",
-        operands,
-        outs,
+    specs = chunk_specs(slopes, block)
+    by_side = [chunk_specs([part[j] for part in table], block) for j in range(sides)]
+    return call(
+        functools.partial(rows_back_kernel, [a.shape[0] // block for a in slopes], sides),
+        "rows_back",
+        [(place, smem), (far(matrix), pl.BlockSpec((groups, block, node_dev), lambda i: (0, i, 0))), pooled]
+        + list(zip(map(far, slopes), specs))
+        + [(far(table[k][j]), by_side[j][k]) for k in range(len(table)) for j in range(sides)]
+        + [far(extra)],
+        [(spec, far_shape(a.shape, bf16)) for spec, a in zip(specs, slopes)]
+        + [full((groups, sides * width // groups + extra_rows, columns), bf16)],
         grid=(row_dev // block,),
-        scratch=scratch,
-        after=after,
-    )
-
-
-def table_back_kernel(sides, place_ref, *refs):
-    grads, qs, self_refs, out_ref = refs[:sides], refs[sides : 2 * sides], refs[2 * sides : 3 * sides], refs[-1]
+        scratch=[pltpu.VMEM((sides, columns, width), f32), pltpu.VMEM((1, columns), f32)],
+        after=after,
+    )
+
+
+def table_back_kernel(sides, nodes, with_self, place_ref, *refs):
+    grads, qs, self_refs, out_ref = refs[:sides], refs[sides : 2 * sides], refs[2 * sides : -1], refs[-1]
     width = out_ref.shape[1]
-    at = place_ref[1] * width
-    total = dot(grads[0][...], rows_at(qs[0], at, width)[...], (1, 1))
+    total = dot(grads[0][...], qs[0][...], (1, 1))
     for j in range(1, sides):
-        total = total + dot(grads[j][...], rows_at(qs[j], at, width)[...], (1, 1))
+        total = total + dot(grads[j][...], qs[j][...], (1, 1))
     out_ref[...] = total
+    if not with_self:
+        return
 
     @pl.when(pl.program_id(0) == 0)
     def _():
-        nodes = self_refs[0].shape[0]
         own = self_refs[0][...].astype(f32)
-        for ref in self_refs[1:]:
+        for ref in self_refs[1:sides]:
             own = own + ref[...].astype(f32)
         out_ref[0:nodes, :] += own
 
 
-def table_back(place, grads, qs, grad_self):
+def table_back(place, grads, qs, grad_self, first, row_dev, so_far=None, after=()):
     sides = len(grads)
-    row_dev, columns = grads[0].shape
-    width = grad_self[0].shape[1]
-    block = min(row_dev, 512)
-    return call(
-        functools.partial(table_back_kernel, sides),
+    rows, columns = grads[0].shape
+    nodes, width = grad_self[0].shape
+    block = min(rows, 512)
+    operands = [(place, smem)] + [(far(a), row_blocks(block, columns)) for a in grads] + [*map(far, qs), *map(far, grad_self)]
+    return call(
+        functools.partial(table_back_kernel, sides, nodes, first == 0),
         "table_back",
-        [(place, smem)] + [(far(a), row_blocks(block, columns)) for a in grads] + [*map(far, qs), *map(far, grad_self)],
-        [(row_blocks(block, width), far_shape((row_dev, width), f32))],
-        grid=(row_dev // block,),
+        operands,
+        [(pl.BlockSpec((block, width), lambda i: (first // block + i, 0)), far_shape((row_dev, width), f32))],
+        grid=(rows // block,),
+        after=after if so_far is None else [so_far, *after],
+        aliases={} if so_far is None else {len(operands): 0},
     )[0]
+
+
+def cut_kernel(sides, place_ref, q_ref, *outs):
+    width = outs[0].shape[0]
+    for j in range(sides):
+        outs[j][...] = rows_at(q_ref, (place_ref[1] ^ j) * width, width)[...]
+
+
+def cut_rows(place, q_low, sides, after=()):
+    rows, columns = q_low.shape
+    return call(
+        functools.partial(cut_kernel, sides),
+        "cut",
+        [(place, smem), far(q_low)],
+        [full((rows // sides, columns), bf16, far_shape)] * sides,
+        after=after,
+    )
 
 
 def all_sides(array):
@@ -769,53 +721,64 @@
     place = jnp.stack([lax.axis_index("dp"), lax.axis_index("mp")]).astype(i32)
 
     cut = row_dev * 3 // 4
-    low_a, low_b, q_low, w_self, w_pooled = low_all(table, q_weight, w_weight, cut)
+    (low_a,) = low([(table, 0, cut)])
+    across_a, beside_a = swap(low_a, "mp", 2), swap(low_a, "mp", 1)
     slots = make_slots(place, neighbours, counts, importance, row_dev, groups, after=[low_a])
+    half = sides * width
+    low_b, q_low, w_self, w_pooled = low(
+        [(table, cut, row_dev - cut), (q_weight, 0, half), (w_weight, 0, half), (w_weight, half, half)], after=[slots]
+    )
     slots = exchange(slots, "dp")
-    across_a, across_b = swap(low_a, "mp", 2), swap(low_b, "mp", 2)
-    beside_a, beside_b = swap(low_a, "mp", 1), swap(low_b, "mp", 1)
-
-    matrix = spread(slots, row_dev)
+    across_b, beside_b = swap(low_b, "mp", 2), swap(low_b, "mp", 1)
+
+    matrix = spread(slots, row_dev, after=[low_b])
     across_a = gate(across_a, [matrix])
     part_a = [low_a, beside_a, across_a, swap(across_a, "mp", 1)]
-    hidden_a, slope_a = hidden(place, part_a, q_low, q_bias, "both")
+    hidden_a = hidden(place, part_a, q_low, q_bias, "value")
     so_far = pool(hidden_a, matrix, 0, None)
+    w_pooled = all_sides(gate(w_pooled, [hidden_a]))
     across_b = gate(across_b, [hidden_a])
     part_b = [low_b, beside_b, across_b, swap(across_b, "mp", 1)]
     parts = [part_a, part_b]
-    early = self_half(place, part_a, w_self, w_bias, cotangent)
+    hidden_b = hidden(place, part_b, q_low, q_bias, "value", after=[so_far])
+    part_sums = pool(hidden_b, matrix, cut, so_far, after=[w_pooled[2]])
+    pooled = exchange(part_sums.reshape(groups * sides, few, columns), ("dp", "mp"))
+
+    early = self_half(place, part_a, w_self, w_bias, cotangent, after=[part_sums])
     early = [early[0]] + [swap(early[j], "mp", j) for j in range(1, sides)]
-    hidden_b, slope_b = hidden(place, part_b, q_low, q_bias, "both", after=[so_far])
-    pooled = pool(hidden_b, matrix, cut, so_far, after=early)
-    slope = [slope_a, slope_b]
-    pooled = exchange(pooled.reshape(groups * sides, few, columns), ("dp", "mp"))
-
-    w_pooled = all_sides(gate(w_pooled, [hidden_b]))
-    q_all = all_sides(gate(q_low, [hidden_b]))
-    q_bias_x = swap(q_bias, "mp", 2)
-    slope_x = [hidden(place, part, q_all[2], q_bias_x, "slope")[0] for part in parts]
-
-    grad_pooled, *late = combine(
-        node_total, pooled.reshape(groups, sides, few, columns), early, w_pooled, after=slope_x
+    slope = [hidden(place, part, q_low, q_bias, "slope", after=[early[0]]) for part in parts]
+
+    grad_pooled, pooled, *late = combine(
+        node_total, pooled.reshape(groups, sides, few, columns), early, w_pooled, after=slope
     )
     grad_pooled = exchange(grad_pooled.reshape(groups * sides, few, columns), ("dp", "mp")).reshape(node_total, columns)
     late = [late[0]] + [swap(late[j], "mp", j) for j in range(1, sides)]
-    embedding, *w_parts = w_back(place, part_a, late, w_self, node_dev, groups)
-    w_parts, grad_self = w_parts[:2], w_parts[2:]
+    embedding, even, odd, extra, *grad_self = w_back(
+        place, part_a, late, all_sides(pooled), w_self, node_dev, groups
+    )
+    q_cut = cut_rows(place, q_low, sides, after=[late[0]])
+    q_cut = [q_cut[0]] + [swap(q_cut[j], "mp", j) for j in range(1, sides)]
     grad_self = [grad_self[0]] + [swap(grad_self[j], "mp", j) for j in range(1, sides)]
 
-    grad_pooled_x = swap(grad_pooled, "mp", 2)
-    grad, q_parts = rows_back(place, matrix, grad_pooled, slope, parts, after=[embedding])
-    grad_x = rows_back(place, matrix, grad_pooled_x, slope_x, [], after=[grad])[0]
-    grads = [grad, swap(grad, "mp", 1), grad_x, swap(grad_x, "mp", 1)]
-    table_grad = table_back(place, grads, q_all, grad_self)
-    q_grad, q_bias_grad, _ = total_direct(q_parts)
-    scale = penalty_rate / node_total
-    if groups <= 8:
-        w_grad, w_bias_grad, penalty = total_in_steps(place, w_parts, scale, after=[grad])
-    else:
-        order = place[0] ^ jnp.arange(groups, dtype=i32)
-        w_grad, w_bias_grad, penalty = total_direct(jnp.stack(w_parts)[order % 2, order // 2], scale)
+    grad_a, grad_b, q_parts = rows_back(place, matrix, grad_pooled, slope, parts, extra, after=[q_cut[2]])
+    pairs = add_pairs(even, swap(odd, "dp", 1), after=[grad_a])
+    count = groups // 2
+    pairs = [pairs[0]] + [swap(pairs[s], "dp", 2 * s) for s in range(1, count)]
+    grad_a = gate(grad_a, [pairs[0]])
+    across_a = swap(grad_a, "mp", 2)
+    piece = add_some(pairs)
+    pieces = [piece] + [swap(piece, "dp", 2 * s) for s in range(1, count)]
+    q_pieces, q_bias_grad, w_bias_grad, penalty = add(
+        exchange(q_parts, "dp"), penalty_rate / node_total, after=[piece]
+    )
+    pieces = [p for own in pieces for p in (own, swap(own, "dp", 1))]
+    grads = [grad_a, swap(grad_a, "mp", 1), across_a, swap(across_a, "mp", 1)]
+    table_grad = table_back(place, grads, q_cut, grad_self, 0, row_dev, after=[pieces[2], pieces[4], pieces[6]])
+    across_b = swap(grad_b, "mp", 2)
+    grads = [grad_b, swap(grad_b, "mp", 1), across_b, swap(across_b, "mp", 1)]
+    table_grad = table_back(place, grads, q_cut, grad_self, grad_a.shape[0], row_dev, table_grad)
+    q_grad = widen(exchange(q_pieces, "dp").reshape(-1, columns), after=[table_grad])
+    w_grad = collect(place, pieces, after=[table_grad])
     return (
         embedding,
         table_grad,

time: 300 us -> 249 us (0.83)
  waiting for transfers between devices: 116 us -> 69.4 us
  starting transfers between devices: 51.9 us -> 63.3 us
  Pallas kernels: 106 us -> 97.1 us
  local copies, waits for them, and re-layouts: 20.3 us -> 15 us
    ppermute x33 -> x41, waiting for transfers between devices: 102 us -> 53.4 us  [swap(): return lax.ppermute(array, axis, [(i, i ^ bits) for i in range(size)])]
    ppermute x33 -> x41, starting transfers between devices: 23 us -> 31.9 us  [swap(): return lax.ppermute(array, axis, [(i, i ^ bits) for i in range(size)])]
    pallas_call x21 -> x22, Pallas kernels: 106 us -> 97.1 us  [call(): pl.pallas_call(inner, grid=grid, in_specs=specs + [pl.BlockSpec(memory_sp...]
    unnamed x92 -> x110, local copies, waits for them, and re-layouts: 20.3 us -> 15 us
  transfers between devices with their start and end apart: 38 -> 46, of which waited for: 17 -> 14; matrix products, arithmetic and copies ran while one was open for 0% -> 0% of each run, Pallas kernels for 27% -> 33%
where the time goes in v3:
time: 249 us; the launch traced here: 246 us
  Pallas kernels  97.1 us (39%)
  waiting for transfers between devices  69.4 us (28%)
  starting transfers between devices  63.3 us (25%)
  local copies, waits for them, and re-layouts  15 us (6%)
    pallas_call x22, Pallas kernels, call(): pl.pallas_call(inner, grid=grid, in_specs=specs + [pl.BlockSpec(memory_sp...  97.1 us
    ppermute x41, waiting for transfers between devices, swap(): return lax.ppermute(array, axis, [(i, i ^ bits) for i in range(size)])  53.4 us
    ppermute x41, starting transfers between devices, swap(): return lax.ppermute(array, axis, [(i, i ^ bits) for i in range(size)])  31.9 us
    all_to_all x5, starting transfers between devices, exchange(): return lax.all_to_all(array, axes, split_axis=0, concat_axis=0, tiled=True)  31.4 us
    all_to_all x5, waiting for transfers between devices, exchange(): return lax.all_to_all(array, axes, split_axis=0, concat_axis=0, tiled=True)  16 us
    unnamed x110, local copies, waits for them, and re-layouts  15 us
  transfers between devices with their start and end apart: 46, of which 14 were waited for; matrix products, arithmetic and copies ran while one was open for 0% of the time, Pallas kernels for 33%

profile of v3, /device:TPU:12, one launch (start us, length us, event | category | flops | bytes accessed | tf_op | source)
XLA Modules:
  0.0 246.0 jit_solution(8679870164118119702)
XLA Ops:
  0.6 3.9 %low.2.refs_4_.refs_1_.refs_5_ = bf16[3072,256]{1,0:T(8,128)(2,1)} custom-call(f32[4096,256]{1,0:T(8,128)} %refs_0_.3), custom_call_target="tpu_custom_call" | custom-call | flops 1150000 | bytes 3690 | tf_op jit(solution)/shard_map/low/pallas_call | solution.py:80
  4.5 1.5 collective-permute-start.1
  6.1 1.4 copy-done.1
  7.5 1.7 slots.1.refs_4_
  9.2 0.8 copy-done.4
  10.1 6.2 %all-to-all-start = ((s16[8,3,50,256]{3,2,1,0:T(8,128)(2,1)}), s16[8,3,50,256]{3,2,1,0:T(8,128)(2,1)}, u32[]{:S(2)}, u32[]{:S(2)}) async-start(s16[8,3,50,256]{3,2,1,0:T(8,128)(2,1)} %copy-done.4), calls=%async_computation | async-start | bytes 1376256 | tf_op jit(solution)/shard_map/all_to_all | solution.py:122
  16.3 1.1 copy-done.5
  17.4 4.2 %low.3 = (bf16[1024,256]{1,0:T(8,128)(2,1)}, bf16[1024,256]{1,0:T(8,128)(2,1)}, bf16[1024,256]{1,0:T(8,128)(2,1)}, bf16[1024,256]{1,0:T(8,128)(2,1)}) custom-call(f32[4096,256]{1,0:T(8,128)} %refs_0_.3, f32[1024,256]{1,0:T(8,128)} %refs_1_.1, f32[2048,256]{1,0:T(8,128)} %refs_3_.1, f32[2048,256]{1,0:T(8,128)} %refs_3_.1, s16[8,3,50,256]{3,2,1,0:T(8,128)(2,1)S(1)} %copy-done.5), custom_call_target="tpu_custom_call" | custom-call | flops 1150000 | bytes 3690 | tf_op jit(solution)/shard_map/low/pallas_call | solution.py:80
  21.6 9.1 %all-to-all-done.refs_0_ = s16[8,3,50,256]{3,2,1,0:T(8,128)(2,1)} async-done(((s16[8,3,50,256]{3,2,1,0:T(8,128)(2,1)}), s16[8,3,50,256]{3,2,1,0:T(8,128)(2,1)}, u32[]{:S(2)}, u32[]{:S(2)}) %all-to-all-start) | async-done | bytes 614432 | tf_op jit(solution)/shard_map/all_to_all | solution.py:122
  30.7 13.5 %spread.1.refs_1_ = bf16[8,4096,256]{2,1,0:T(8,128)(2,1)S(1)} custom-call(s16[8,3,50,256]{3,2,1,0:T(8,128)(2,1)} %all-to-all-done.refs_0_, bf16[1024,256]{1,0:T(8,128)(2,1)} %get-tuple-element.44.refs_1_.refs_9_), custom_call_target="tpu_custom_call" | custom-call | flops 1150000 | bytes 3690 | tf_op jit(solution)/shard_map/spread/pallas_call | solution.py:80
  45.1 2.6 %collective-permute-done.2.refs_4_.refs_8_ = bf16[3072,256]{1,0:T(8,128)(2,1)S(1)} collective-permute-done((bf16[3072,256]{1,0:T(8,128)(2,1)S(1)}, bf16[3072,256]{1,0:T(8,128)(2,1)S(1)}, u32[]{:S(2)}, u32[]{:S(2)}) %collective-permute-start.2) | collective-permute-done | bytes 1572896 | tf_op jit(solution)/shard_map/ppermute | solution.py:113
  47.8 6.3 %hidden_value.2.refs_1_.refs_0_ = bf16[256,3072]{1,0:T(8,128)(2,1)S(1)} custom-call(s32[2]{0:T(128)S(1)} %pad_add_fusion.refs_0_, bf16[3072,256]{1,0:T(8,128)(2,1)S(1)} %copy-done.2, bf16[3072,256]{1,0:T(8,128)(2,1)} %collective-permute-done.refs_2_.refs_6_, bf16[3072,256]{1,0:T(8,128)(2,1)S(1)} %gate.4.refs_3_.refs_7_, ...), custom_call_target="tpu_custom_call" | custom-call | flops 1150000 | bytes 3690 | tf_op jit(solution)/shard_map/hidden_value/pallas_call | solution.py:80
  54.1 4.8 %collective-permute-done.4.refs_0_ = bf16[1024,256]{1,0:T(8,128)(2,1)S(1)} collective-permute-done((bf16[1024,256]{1,0:T(8,128)(2,1)}, bf16[1024,256]{1,0:T(8,128)(2,1)S(1)}, u32[]{:S(2)}, u32[]{:S(2)}) %collective-permute-start.4) | collective-permute-done | bytes 524320 | tf_op jit(solution)/shard_map/ppermute | solution.py:113
  59.5 4.9 %pool.2.refs_7_.refs_2_ = f32[256,2048]{1,0:T(8,128)S(1)} custom-call(bf16[256,3072]{1,0:T(8,128)(2,1)S(1)} %hidden_value.2.refs_1_.refs_0_, bf16[8,4096,256]{2,1,0:T(8,128)(2,1)S(1)} %spread.1.refs_1_), custom_call_target="tpu_custom_call" | custom-call | flops 1150000 | bytes 3690 | tf_op jit(solution)/shard_map/pool/pallas_call | solution.py:80
  64.5 2.7 %hidden_value.3.refs_0_ = bf16[256,1024]{1,0:T(8,128)(2,1)S(1)} custom-call(s32[2]{0:T(128)S(1)} %pad_add_fusion.refs_0_, bf16[1024,256]{1,0:T(8,128)(2,1)} %get-tuple-element.44.refs_1_.refs_9_, bf16[1024,256]{1,0:T(8,128)(2,1)S(1)} %collective-permute-done.3.refs_2_.refs_10_, bf16[1024,256]{1,0:T(8,128)(2,1)S(1)} %gate.5.refs_3_.refs_11_, ...), custom_call_target="tpu_custom_call" | custom-call | flops 1150000 | bytes 3690 | tf_op jit(solution)/shard_map/hidden_value/pallas_call | solution.py:80
  67.3 6.0 %collective-permute-done.6.refs_3_.refs_7_ = bf16[1024,256]{1,0:T(8,128)(2,1)S(1)} collective-permute-done((bf16[1024,256]{1,0:T(8,128)(2,1)S(1)}, bf16[1024,256]{1,0:T(8,128)(2,1)S(1)}, u32[]{:S(2)}, u32[]{:S(2)}) %collective-permute-start.6) | collective-permute-done | bytes 524320 | tf_op jit(solution)/shard_map/ppermute | solution.py:113
  73.3 3.4 %pool.3.refs_8_ = bf16[2048,256]{1,0:T(8,128)(2,1)} custom-call(bf16[256,1024]{1,0:T(8,128)(2,1)S(1)} %hidden_value.3.refs_0_, bf16[8,4096,256]{2,1,0:T(8,128)(2,1)S(1)} %spread.1.refs_1_, f32[256,2048]{1,0:T(8,128)S(1)} %pool.2.refs_7_.refs_2_, bf16[1024,256]{1,0:T(8,128)(2,1)S(1)} %collective-permute-done.6.refs_3_.refs_7_), custom_call_target="tpu_custom_call" | custom-call | flops 1150000 | bytes 3690 | tf_op jit(solution)/shard_map/pool/pallas_call | solution.py:80
  76.7 5.5 %all-to-all-start.1 = ((bf16[32,64,256]{2,1,0:T(8,128)(2,1)}), bf16[32,64,256]{2,1,0:T(8,128)(2,1)S(1)}, u32[]{:S(2)}, u32[]{:S(2)}) async-start(bf16[32,64,256]{2,1,0:T(8,128)(2,1)} %bitcast.6), calls=%async_computation.1 | async-start | bytes 2097152 | tf_op jit(solution)/shard_map/all_to_all | solution.py:122
  82.4 2.5 %self_half.1 = (f32[64,512]{1,0:T(8,128)}, f32[64,512]{1,0:T(8,128)}, f32[64,512]{1,0:T(8,128)}, f32[64,512]{1,0:T(8,128)}) custom-call(s32[2]{0:T(128)S(1)} %pad_add_fusion.refs_0_, bf16[3072,256]{1,0:T(8,128)(2,1)} %low.2.refs_4_.refs_1_.refs_5_, bf16[3072,256]{1,0:T(8,128)(2,1)} %collective-permute-done.refs_2_.refs_6_, bf16[3072,256]{1,0:T(8,128)(2,1)} %copy-done.3, ...), custom_call_target="tpu_custom_call" | custom-call | flops 3449999872 | bytes 11070000 | tf_op jit(solution)/shard_map/self_half/pallas_call | solution.py:80
  85.3 1.5 collective-permute-start.8
  87.4 0.9 copy-done.22
  88.3 3.5 %hidden_slope.3.refs_10_.refs_4_ = bf16[1024,256]{1,0:T(8,128)(2,1)} custom-call(s32[2]{0:T(128)S(1)} %pad_add_fusion.refs_0_, bf16[1024,256]{1,0:T(8,128)(2,1)} %get-tuple-element.44.refs_1_.refs_9_, bf16[1024,256]{1,0:T(8,128)(2,1)} %copy-done.10, bf16[1024,256]{1,0:T(8,128)(2,1)} %copy-done.8, bf16[1024,256]{1,0:T(8,128)(2,1)} %copy-done.11, ...), custom_call_target="tpu_custom_call" | custom-call | flops 5750000128 | bytes 18450000 | tf_op jit(solution)/shard_map/hidden_slope/pallas_call | solution.py:80
  91.8 7.6 %hidden_slope.2.refs_9_.refs_3_ = bf16[3072,256]{1,0:T(8,128)(2,1)} custom-call(s32[2]{0:T(128)S(1)} %pad_add_fusion.refs_0_, bf16[3072,256]{1,0:T(8,128)(2,1)} %low.2.refs_4_.refs_1_.refs_5_, bf16[3072,256]{1,0:T(8,128)(2,1)} %collective-permute-done.refs_2_.refs_6_, bf16[3072,256]{1,0:T(8,128)(2,1)} %copy-done.3, bf16[3072,256]{1,0:T(8,128)(2,1)} %copy-done.9, ...), custom_call_target="tpu_custom_call" | custom-call | flops 5750000128 | bytes 18450000 | tf_op jit(solution)/shard_map/hidden_slope/pallas_call | solution.py:80
  100.3 6.9 %all-to-all-done.1 = bf16[32,64,256]{2,1,0:T(8,128)(2,1)S(1)} async-done(((bf16[32,64,256]{2,1,0:T(8,128)(2,1)}), bf16[32,64,256]{2,1,0:T(8,128)(2,1)S(1)}, u32[]{:S(2)}, u32[]{:S(2)}) %all-to-all-start.1) | async-done | bytes 1048608 | tf_op jit(solution)/shard_map/all_to_all | solution.py:122
  107.2 1.4 copy-done.20
  108.6 4.0 %combine.1 = (bf16[8,4,64,256]{3,2,1,0:T(8,128)(2,1)}, bf16[64,1024]{1,0:T(8,128)(2,1)}, bf16[80,512]{1,0:T(8,128)(2,1)}, bf16[80,512]{1,0:T(8,128)(2,1)}, bf16[...) custom-call(bf16[8,4,64,256]{3,2,1,0:T(8,128)(2,1)S(1)} %bitcast.17, f32[64,512]{1,0:T(8,128)} %get-tuple-element.48.refs_7_.refs_1_, ...), custom_call_target="tpu_custom_call" | custom-call | flops 4600000000 | bytes 14760000 | tf_op jit(solution)/shard_map/combine/pallas_call | solution.py:80
  112.7 4.9 %all-to-all-start.2 = ((bf16[32,64,256]{2,1,0:T(8,128)(2,1)}), bf16[32,64,256]{2,1,0:T(8,128)(2,1)S(1)}, u32[]{:S(2)}, u32[]{:S(2)}) async-start(bf16[32,64,256]{2,1,0:T(8,128)(2,1)} %bitcast.9), calls=%async_computation.2 | async-start | bytes 2097152 | tf_op jit(solution)/shard_map/all_to_all | solution.py:122
  117.6 1.5 collective-permute-start.16
  119.1 10.4 %collective-permute-done.16.refs_11_ = bf16[64,1024]{1,0:T(8,128)(2,1)S(1)} collective-permute-done((bf16[64,1024]{1,0:T(8,128)(2,1)S(1)}, bf16[64,1024]{1,0:T(8,128)(2,1)S(1)}, u32[]{:S(2)}, u32[]{:S(2)}) %collective-permute-start.16) | collective-permute-done | bytes 131104 | tf_op jit(solution)/shard_map/ppermute | solution.py:113
  130.0 0.9 collective-permute-start.13
  131.4 1.9 cut.1
  133.3 1.0 collective-permute-start.18
  134.3 1.4 collective-permute-done.13.refs_7_
  135.7 1.3 collective-permute-done.14.refs_8_
  138.4 3.4 %w_back.1 = (f32[256,256]{1,0:T(8,128)}, bf16[4,256,256]{2,1,0:T(8,128)(2,1)}, bf16[4,256,256]{2,1,0:T(8,128)(2,1)}, bf16[16,256]{1,0:T(8,128)(2,1)}, bf16[256,2...) custom-call(s32[2]{0:T(128)S(1)} %pad_add_fusion.refs_0_, ...), custom_call_target="tpu_custom_call" | custom-call | flops 4600000000 | bytes 14760000 | tf_op jit(solution)/shard_map/w_back/pallas_call | solution.py:80
  141.8 0.8 collective-permute-start.27
  142.6 16.0 %rows_back.1 = (bf16[3072,256]{1,0:T(8,128)(2,1)}, bf16[1024,256]{1,0:T(8,128)(2,1)}, bf16[8,144,256]{2,1,0:T(8,128)(2,1)}) custom-call(s32[2]{0:T(128)S(1)} %pad_add_fusion.refs_0_, bf16[8,4096,256]{2,1,0:T(8,128)(2,1)} %copy-done, bf16[2048,256]{1,0:T(8,128)(2,1)S(1)} %bitcast.16, bf16[3072,256]{1,0:T(8,128)(2,1)} %hidden_slope.2.refs_9_.refs_3_, ...), custom_call_target="tpu_custom_call" | custom-call | flops 18400000000 | bytes 59040000 | tf_op jit(solution)/shard_map/rows_back/pallas_call | solution.py:80
  159.5 2.0 add_pairs.1
  161.5 0.9 copy-done.15
  162.4 1.4 collective-permute-start.29
  163.8 6.6 %all-to-all-start.3 = ((bf16[8,144,256]{2,1,0:T(8,128)(2,1)}), bf16[8,144,256]{2,1,0:T(8,128)(2,1)S(1)}, u32[]{:S(2)}, u32[]{:S(2)}) async-start(bf16[8,144,256]{2,1,0:T(8,128)(2,1)} %get-tuple-element.76), calls=%async_computation.3 | async-start | bytes 1179648 | tf_op jit(solution)/shard_map/all_to_all | solution.py:122
  171.0 2.4 collective-permute-start.32
  173.9 11.1 %collective-permute-done.31.refs_1_ = bf16[256,256]{1,0:T(8,128)(2,1)S(1)} collective-permute-done((bf16[256,256]{1,0:T(8,128)(2,1)S(1)}, bf16[256,256]{1,0:T(8,128)(2,1)S(1)}, u32[]{:S(2)}, u32[]{:S(2)}) %collective-permute-start.31) | collective-permute-done | bytes 131104 | tf_op jit(solution)/shard_map/ppermute | solution.py:113
  185.0 7.0 %collective-permute-done.32.refs_2_ = bf16[256,256]{1,0:T(8,128)(2,1)S(1)} collective-permute-done((bf16[256,256]{1,0:T(8,128)(2,1)S(1)}, bf16[256,256]{1,0:T(8,128)(2,1)S(1)}, u32[]{:S(2)}, u32[]{:S(2)}) %collective-permute-start.32) | collective-permute-done | bytes 131104 | tf_op jit(solution)/shard_map/ppermute | solution.py:113
  192.0 4.7 %collective-permute-done.33.refs_3_ = bf16[256,256]{1,0:T(8,128)(2,1)S(1)} collective-permute-done((bf16[256,256]{1,0:T(8,128)(2,1)S(1)}, bf16[256,256]{1,0:T(8,128)(2,1)S(1)}, u32[]{:S(2)}, u32[]{:S(2)}) %collective-permute-start.33) | collective-permute-done | bytes 131104 | tf_op jit(solution)/shard_map/ppermute | solution.py:113
  196.7 1.6 collective-permute-start.25
  199.1 2.5 %collective-permute-done.23.refs_8_ = bf16[256,256]{1,0:T(8,128)(2,1)S(1)} collective-permute-done((bf16[256,256]{1,0:T(8,128)(2,1)S(1)}, bf16[256,256]{1,0:T(8,128)(2,1)S(1)}, u32[]{:S(2)}, u32[]{:S(2)}) %collective-permute-start.23) | collective-permute-done | bytes 131104 | tf_op jit(solution)/shard_map/ppermute | solution.py:113
  201.6 3.9 %collective-permute-start.36 = (bf16[256,256]{1,0:T(8,128)(2,1)}, bf16[256,256]{1,0:T(8,128)(2,1)S(1)}, u32[]{:S(2)}, u32[]{:S(2)}) collective-permute-start(bf16[256,256]{1,0:T(8,128)(2,1)} %add_some.1.refs_1_), channel_id=1, source_target_pairs={{0,24},{4,28},{8,16},{12,20},{16,8},{20,12},{24,0},{28,4},{1,25},{... | collective-permute-start | bytes 393224 | tf_op jit(solution)/shard_map/ppermute | solution.py:113
  205.5 1.0 collective-permute-start.28
  207.1 4.2 %collective-permute-start.35 = (bf16[256,256]{1,0:T(8,128)(2,1)}, bf16[256,256]{1,0:T(8,128)(2,1)S(1)}, u32[]{:S(2)}, u32[]{:S(2)}) collective-permute-start(bf16[256,256]{1,0:T(8,128)(2,1)} %add_some.1.refs_1_), channel_id=1, source_target_pairs={{0,16},{4,20},{8,24},{12,28},{16,0},{20,4},{24,8},{28,12},{1,17},{... | collective-permute-start | bytes 393224 | tf_op jit(solution)/shard_map/ppermute | solution.py:113
  211.4 1.2 collective-permute-done.36.refs_15_.refs_7_
  212.6 0.8 collective-permute-start.30
  213.4 0.9 copy-done.18
  214.3 0.9 add.3
  215.2 8.1 %all-to-all-start.4 = ((bf16[8,128,256]{2,1,0:T(8,128)(2,1)}), bf16[8,128,256]{2,1,0:T(8,128)(2,1)S(1)}, u32[]{:S(2)}, u32[]{:S(2)}) async-start(bf16[8,128,256]{2,1,0:T(8,128)(2,1)} %get-tuple-element.77), calls=%async_computation.4 | async-start | bytes 1048576 | tf_op jit(solution)/shard_map/all_to_all | solution.py:122
  224.0 1.5 collective-permute-start.40
  226.1 7.4 %table_back.2.refs_13_ = f32[4096,256]{1,0:T(8,128)} custom-call(s32[2]{0:T(128)S(1)} %pad_add_fusion.refs_0_, bf16[3072,256]{1,0:T(8,128)(2,1)} %gate.7.refs_1_, bf16[3072,256]{1,0:T(8,128)(2,1)} %collective-permute-done.28.refs_2_, bf16[3072,256]{1,0:T(8,128)(2,1)} %copy-done.24, bf16[3072,256]{1,0:T(8,128)(2,1)} %collective-permute-done.30.refs_4_, ...), custom_call_target="tpu_custom_call" | custom-call | flops 23000000512 | bytes 73800000 | tf_op jit(solution)/shard_map/table_back/pallas_call | solution.py:80
  233.5 1.5 collective-permute-start.38
  235.0 0.8 copy-done.28
  235.8 3.5 %table_back.3.refs_1_.refs_9_ = f32[4096,256]{1,0:T(8,128)} custom-call(s32[2]{0:T(128)S(1)} %pad_add_fusion.refs_0_, bf16[1024,256]{1,0:T(8,128)(2,1)} %get-tuple-element.61.refs_1_, bf16[1024,256]{1,0:T(8,128)(2,1)} %copy-done.26, bf16[1024,256]{1,0:T(8,128)(2,1)} %collective-permute-done.20.refs_3_, ...), custom_call_target="tpu_custom_call", output_to_operand_aliasing={{}: (13, {})} | custom-call | flops 23000000512 | bytes 73800000 | tf_op jit(solution)/shard_map/table_back/pallas_call | solution.py:80
  239.3 2.2 copy-done.6
  241.5 1.0 widen.1
  242.5 1.5 copy-done.7
  244.0 2.0 collect.1
  (165 shorter events, 10.8 us)
Async XLA Ops:
  4.5 39.7 %collective-permute-start.1 = (bf16[3072,256]{1,0:T(8,128)(2,1)}, bf16[3072,256]{1,0:T(8,128)(2,1)S(1)}, u32[]{:S(2)}, u32[]{:S(2)}) collective-permute-start(bf16[3072,256]{1,0:T(8,128)(2,1)} %low.2.refs_4_.refs_1_.refs_5_), channel_id=1, source_target_pairs={{0,2},{1,3},{2,0},{3,1},{4,6},{5,7},{6,4},{7,5},{8,10},{9,11},{10,... | collective-permute-start | bytes 4718600 | tf_op jit(solution)/shard_map/ppermute | solution.py:113
  10.1 20.7 %all-to-all-start = ((s16[8,3,50,256]{3,2,1,0:T(8,128)(2,1)}), s16[8,3,50,256]{3,2,1,0:T(8,128)(2,1)}, u32[]{:S(2)}, u32[]{:S(2)}) async-start(s16[8,3,50,256]{3,2,1,0:T(8,128)(2,1)} %copy-done.4), calls=%async_computation | async-start | bytes 1376256 | tf_op jit(solution)/shard_map/all_to_all | solution.py:122
  16.3 28.9 %collective-permute-start = (bf16[3072,256]{1,0:T(8,128)(2,1)S(1)}, bf16[3072,256]{1,0:T(8,128)(2,1)}, u32[]{:S(2)}, u32[]{:S(2)}) collective-permute-start(bf16[3072,256]{1,0:T(8,128)(2,1)S(1)} %copy-done.2), channel_id=1, source_target_pairs={{0,1},{1,0},{2,3},{3,2},{4,5},{5,4},{6,7},{7,6},{8,9},{9,8},{10,11... | collective-permute-start | bytes 4718600 | tf_op jit(solution)/shard_map/ppermute | solution.py:113
  44.2 29.0 %copy-start = (bf16[8,4096,256]{2,1,0:T(8,128)(2,1)}, bf16[8,4096,256]{2,1,0:T(8,128)(2,1)S(1)}, u32[]{:S(2)}) copy-start(bf16[8,4096,256]{2,1,0:T(8,128)(2,1)S(1)} %spread.1.refs_1_) | copy-start | bytes 50331652
  44.3 9.8 %copy-start.3 = (bf16[3072,256]{1,0:T(8,128)(2,1)}, bf16[3072,256]{1,0:T(8,128)(2,1)S(1)}, u32[]{:S(2)}) copy-start(bf16[3072,256]{1,0:T(8,128)(2,1)S(1)} %gate.4.refs_3_.refs_7_) | copy-start | bytes 4718596
  44.3 3.5 %collective-permute-start.2 = (bf16[3072,256]{1,0:T(8,128)(2,1)S(1)}, bf16[3072,256]{1,0:T(8,128)(2,1)S(1)}, u32[]{:S(2)}, u32[]{:S(2)}) collective-permute-start(bf16[3072,256]{1,0:T(8,128)(2,1)S(1)} %gate.4.refs_3_.refs_7_), channel_id=1, source_target_pairs={{0,1},{1,0},{2,3},{3,2},{4,5},{5,4},{6,7},{7,6},{8,9},{9,8},{10,11... | collective-permute-start | bytes 4718600 | tf_op jit(solution)/shard_map/ppermute | solution.py:113
  44.4 14.5 %collective-permute-start.4 = (bf16[1024,256]{1,0:T(8,128)(2,1)}, bf16[1024,256]{1,0:T(8,128)(2,1)S(1)}, u32[]{:S(2)}, u32[]{:S(2)}) collective-permute-start(bf16[1024,256]{1,0:T(8,128)(2,1)} %get-tuple-element.44.refs_1_.refs_9_), channel_id=1, source_target_pairs={{0,2},{1,3},{2,0},{3,1},{4,6},{5,7},{6,4},{7,5},{8,10},{9,11},{10,... | collective-permute-start | bytes 1572872 | tf_op jit(solution)/shard_map/ppermute | solution.py:113
  45.0 19.5 %collective-permute-start.3 = (bf16[1024,256]{1,0:T(8,128)(2,1)}, bf16[1024,256]{1,0:T(8,128)(2,1)S(1)}, u32[]{:S(2)}, u32[]{:S(2)}) collective-permute-start(bf16[1024,256]{1,0:T(8,128)(2,1)} %get-tuple-element.44.refs_1_.refs_9_), channel_id=1, source_target_pairs={{0,1},{1,0},{2,3},{3,2},{4,5},{5,4},{6,7},{7,6},{8,9},{9,8},{10,11... | collective-permute-start | bytes 1572872 | tf_op jit(solution)/shard_map/ppermute | solution.py:113
  58.9 5.6 %collective-permute-start.5 = (bf16[1024,256]{1,0:T(8,128)(2,1)S(1)}, bf16[1024,256]{1,0:T(8,128)(2,1)S(1)}, u32[]{:S(2)}, u32[]{:S(2)}) collective-permute-start(bf16[1024,256]{1,0:T(8,128)(2,1)S(1)} %gate.5.refs_3_.refs_11_), channel_id=1, source_target_pairs={{0,1},{1,0},{2,3},{3,2},{4,5},{5,4},{6,7},{7,6},{8,9},{9,8},{10,11... | collective-permute-start | bytes 1572872 | tf_op jit(solution)/shard_map/ppermute | solution.py:113
  58.9 23.2 %copy-start.14 = (bf16[1024,256]{1,0:T(8,128)(2,1)}, bf16[1024,256]{1,0:T(8,128)(2,1)S(1)}, u32[]{:S(2)}) copy-start(bf16[1024,256]{1,0:T(8,128)(2,1)S(1)} %gate.6.refs_5_) | copy-start | bytes 1572868
  58.9 14.3 %collective-permute-start.6 = (bf16[1024,256]{1,0:T(8,128)(2,1)S(1)}, bf16[1024,256]{1,0:T(8,128)(2,1)S(1)}, u32[]{:S(2)}, u32[]{:S(2)}) collective-permute-start(bf16[1024,256]{1,0:T(8,128)(2,1)S(1)} %gate.6.refs_5_), channel_id=1, source_target_pairs={{0,2},{1,3},{2,0},{3,1},{4,6},{5,7},{6,4},{7,5},{8,10},{9,11},{10,... | collective-permute-start | bytes 1572872 | tf_op jit(solution)/shard_map/ppermute | solution.py:113
  73.3 13.5 %copy-start.12 = (bf16[1024,256]{1,0:T(8,128)(2,1)}, bf16[1024,256]{1,0:T(8,128)(2,1)S(1)}, u32[]{:S(2)}) copy-start(bf16[1024,256]{1,0:T(8,128)(2,1)S(1)} %collective-permute-done.6.refs_3_.refs_7_) | copy-start | bytes 1572868
  76.7 30.5 %all-to-all-start.1 = ((bf16[32,64,256]{2,1,0:T(8,128)(2,1)}), bf16[32,64,256]{2,1,0:T(8,128)(2,1)S(1)}, u32[]{:S(2)}, u32[]{:S(2)}) async-start(bf16[32,64,256]{2,1,0:T(8,128)(2,1)} %bitcast.6), calls=%async_computation.1 | async-start | bytes 2097152 | tf_op jit(solution)/shard_map/all_to_all | solution.py:122
  82.2 17.3 %collective-permute-start.10 = (bf16[1024,256]{1,0:T(8,128)(2,1)S(1)}, bf16[1024,256]{1,0:T(8,128)(2,1)S(1)}, u32[]{:S(2)}, u32[]{:S(2)}) collective-permute-start(bf16[1024,256]{1,0:T(8,128)(2,1)S(1)} %gate.6.refs_5_), channel_id=1, source_target_pairs={{0,1},{1,0},{2,3},{3,2},{4,5},{5,4},{6,7},{7,6},{8,9},{9,8},{10,11... | collective-permute-start | bytes 1572872 | tf_op jit(solution)/shard_map/ppermute | solution.py:113
  84.9 14.6 %collective-permute-start.7 = (f32[64,512]{1,0:T(8,128)}, f32[64,512]{1,0:T(8,128)S(1)}, u32[]{:S(2)}, u32[]{:S(2)}) collective-permute-start(f32[64,512]{1,0:T(8,128)} %get-tuple-element.49), channel_id=1, source_target_pairs={{0,1},{1,0},{2,3},{3,2},{4,5},{5,4},{6,7},{7,6},{8,9},{9,8},{10,11... | collective-permute-start | bytes 393224 | tf_op jit(solution)/shard_map/ppermute | solution.py:113
  85.3 14.2 %collective-permute-start.8 = (f32[64,512]{1,0:T(8,128)}, f32[64,512]{1,0:T(8,128)S(1)}, u32[]{:S(2)}, u32[]{:S(2)}) collective-permute-start(f32[64,512]{1,0:T(8,128)} %get-tuple-element.50), channel_id=1, source_target_pairs={{0,2},{1,3},{2,0},{3,1},{4,6},{5,7},{6,4},{7,5},{8,10},{9,11},{10,... | collective-permute-start | bytes 393224 | tf_op jit(solution)/shard_map/ppermute | solution.py:113
  86.7 12.8 %collective-permute-start.9 = (f32[64,512]{1,0:T(8,128)}, f32[64,512]{1,0:T(8,128)S(1)}, u32[]{:S(2)}, u32[]{:S(2)}) collective-permute-start(f32[64,512]{1,0:T(8,128)} %get-tuple-element.51), channel_id=1, source_target_pairs={{0,3},{1,2},{2,1},{3,0},{4,7},{5,6},{6,5},{7,4},{8,11},{9,10},{10,... | collective-permute-start | bytes 393224 | tf_op jit(solution)/shard_map/ppermute | solution.py:113
  86.8 13.5 %collective-permute-start.11 = (bf16[1024,256]{1,0:T(8,128)(2,1)S(1)}, bf16[1024,256]{1,0:T(8,128)(2,1)}, u32[]{:S(2)}, u32[]{:S(2)}) collective-permute-start(bf16[1024,256]{1,0:T(8,128)(2,1)S(1)} %collective-permute-done.6.refs_3_.refs_7_), channel_id=1, source_target_pairs={{0,1},{1,0},{2,3},{3,2},{4,5},{5,4},{6,7},{7,6},{8,9},{9,8},{10,11... | collective-permute-start | bytes 1572872 | tf_op jit(solution)/shard_map/ppermute | solution.py:113
  91.8 15.3 %copy-start.23 = (bf16[1024,256]{1,0:T(8,128)(2,1)S(1)}, bf16[1024,256]{1,0:T(8,128)(2,1)}, u32[]{:S(2)}) copy-start(bf16[1024,256]{1,0:T(8,128)(2,1)} %hidden_slope.3.refs_10_.refs_4_) | copy-start | bytes 1572868
  112.6 16.9 %copy-start.51 = (bf16[80,512]{1,0:T(8,128)(2,1)S(1)}, bf16[80,512]{1,0:T(8,128)(2,1)}, u32[]{:S(2)}) copy-start(bf16[80,512]{1,0:T(8,128)(2,1)} %get-tuple-element.53) | copy-start | bytes 245764
  112.7 17.4 %copy-start.50 = (bf16[80,512]{1,0:T(8,128)(2,1)S(1)}, bf16[80,512]{1,0:T(8,128)(2,1)}, u32[]{:S(2)}) copy-start(bf16[80,512]{1,0:T(8,128)(2,1)} %get-tuple-element.54) | copy-start | bytes 245764
  112.7 18.3 %copy-start.49 = (bf16[80,512]{1,0:T(8,128)(2,1)S(1)}, bf16[80,512]{1,0:T(8,128)(2,1)}, u32[]{:S(2)}) copy-start(bf16[80,512]{1,0:T(8,128)(2,1)} %get-tuple-element.55) | copy-start | bytes 245764
  112.7 18.8 %copy-start.21 = (bf16[80,512]{1,0:T(8,128)(2,1)S(1)}, bf16[80,512]{1,0:T(8,128)(2,1)}, u32[]{:S(2)}) copy-start(bf16[80,512]{1,0:T(8,128)(2,1)} %get-tuple-element.52.refs_5_.refs_2_) | copy-start | bytes 245764
  112.7 29.9 %all-to-all-start.2 = ((bf16[32,64,256]{2,1,0:T(8,128)(2,1)}), bf16[32,64,256]{2,1,0:T(8,128)(2,1)S(1)}, u32[]{:S(2)}, u32[]{:S(2)}) async-start(bf16[32,64,256]{2,1,0:T(8,128)(2,1)} %bitcast.9), calls=%async_computation.2 | async-start | bytes 2097152 | tf_op jit(solution)/shard_map/all_to_all | solution.py:122
  117.6 11.9 %collective-permute-start.16 = (bf16[64,1024]{1,0:T(8,128)(2,1)S(1)}, bf16[64,1024]{1,0:T(8,128)(2,1)S(1)}, u32[]{:S(2)}, u32[]{:S(2)}) collective-permute-start(bf16[64,1024]{1,0:T(8,128)(2,1)S(1)} %copy-done.39), channel_id=1, source_target_pairs={{0,2},{1,3},{2,0},{3,1},{4,6},{5,7},{6,4},{7,5},{8,10},{9,11},{10,... | collective-permute-start | bytes 393224 | tf_op jit(solution)/shard_map/ppermute | solution.py:113
  119.1 18.0 %collective-permute-start.15 = (bf16[64,1024]{1,0:T(8,128)(2,1)S(1)}, bf16[64,1024]{1,0:T(8,128)(2,1)S(1)}, u32[]{:S(2)}, u32[]{:S(2)}) collective-permute-start(bf16[64,1024]{1,0:T(8,128)(2,1)S(1)} %copy-done.39), channel_id=1, source_target_pairs={{0,1},{1,0},{2,3},{3,2},{4,5},{5,4},{6,7},{7,6},{8,9},{9,8},{10,11... | collective-permute-start | bytes 393224 | tf_op jit(solution)/shard_map/ppermute | solution.py:113
  129.5 7.6 %collective-permute-start.17 = (bf16[64,1024]{1,0:T(8,128)(2,1)S(1)}, bf16[64,1024]{1,0:T(8,128)(2,1)S(1)}, u32[]{:S(2)}, u32[]{:S(2)}) collective-permute-start(bf16[64,1024]{1,0:T(8,128)(2,1)S(1)} %collective-permute-done.16.refs_11_), channel_id=1, source_target_pairs={{0,1},{1,0},{2,3},{3,2},{4,5},{5,4},{6,7},{7,6},{8,9},{9,8},{10,11... | collective-permute-start | bytes 393224 | tf_op jit(solution)/shard_map/ppermute | solution.py:113
  129.5 3.8 %collective-permute-start.12 = (bf16[80,512]{1,0:T(8,128)(2,1)S(1)}, bf16[80,512]{1,0:T(8,128)(2,1)S(1)}, u32[]{:S(2)}, u32[]{:S(2)}) collective-permute-start(bf16[80,512]{1,0:T(8,128)(2,1)S(1)} %copy-done.51), channel_id=1, source_target_pairs={{0,1},{1,0},{2,3},{3,2},{4,5},{5,4},{6,7},{7,6},{8,9},{9,8},{10,11... | collective-permute-start | bytes 245768 | tf_op jit(solution)/shard_map/ppermute | solution.py:113
  130.0 5.7 %collective-permute-start.13 = (bf16[80,512]{1,0:T(8,128)(2,1)S(1)}, bf16[80,512]{1,0:T(8,128)(2,1)S(1)}, u32[]{:S(2)}, u32[]{:S(2)}) collective-permute-start(bf16[80,512]{1,0:T(8,128)(2,1)S(1)} %copy-done.50), channel_id=1, source_target_pairs={{0,2},{1,3},{2,0},{3,1},{4,6},{5,7},{6,4},{7,5},{8,10},{9,11},{10,... | collective-permute-start | bytes 245768 | tf_op jit(solution)/shard_map/ppermute | solution.py:113
  130.9 6.1 %collective-permute-start.14 = (bf16[80,512]{1,0:T(8,128)(2,1)S(1)}, bf16[80,512]{1,0:T(8,128)(2,1)S(1)}, u32[]{:S(2)}, u32[]{:S(2)}) collective-permute-start(bf16[80,512]{1,0:T(8,128)(2,1)S(1)} %copy-done.49), channel_id=1, source_target_pairs={{0,3},{1,2},{2,1},{3,0},{4,7},{5,6},{6,5},{7,4},{8,11},{9,10},{10,... | collective-permute-start | bytes 245768 | tf_op jit(solution)/shard_map/ppermute | solution.py:113
  133.3 9.3 %collective-permute-start.18 = (bf16[256,256]{1,0:T(8,128)(2,1)}, bf16[256,256]{1,0:T(8,128)(2,1)S(1)}, u32[]{:S(2)}, u32[]{:S(2)}) collective-permute-start(bf16[256,256]{1,0:T(8,128)(2,1)} %get-tuple-element.60), channel_id=1, source_target_pairs={{0,2},{1,3},{2,0},{3,1},{4,6},{5,7},{6,4},{7,5},{8,10},{9,11},{10,... | collective-permute-start | bytes 393224 | tf_op jit(solution)/shard_map/ppermute | solution.py:113
  141.8 16.9 %collective-permute-start.27 = (bf16[4,256,256]{2,1,0:T(8,128)(2,1)}, bf16[4,256,256]{2,1,0:T(8,128)(2,1)S(1)}, u32[]{:S(2)}, u32[]{:S(2)}) collective-permute-start(bf16[4,256,256]{2,1,0:T(8,128)(2,1)} %get-tuple-element.71), channel_id=1, source_target_pairs={{0,4},{4,0},{8,12},{12,8},{16,20},{20,16},{24,28},{28,24},{1,5},{5... | collective-permute-start | bytes 1572872 | tf_op jit(solution)/shard_map/ppermute | solution.py:113
  142.6 16.0 %copy-start.17 = (bf16[256,256]{1,0:T(8,128)(2,1)}, bf16[256,256]{1,0:T(8,128)(2,1)S(1)}, u32[]{:S(2)}) copy-start(bf16[256,256]{1,0:T(8,128)(2,1)S(1)} %collective-permute-done.18.refs_14_.refs_7_) | copy-start | bytes 393220
  162.4 11.0 %copy-start.45 = (bf16[256,256]{1,0:T(8,128)(2,1)S(1)}, bf16[256,256]{1,0:T(8,128)(2,1)}, u32[]{:S(2)}) copy-start(bf16[256,256]{1,0:T(8,128)(2,1)} %get-tuple-element.75) | copy-start | bytes 393220
  162.4 11.5 %copy-start.33 = (bf16[256,256]{1,0:T(8,128)(2,1)S(1)}, bf16[256,256]{1,0:T(8,128)(2,1)}, u32[]{:S(2)}) copy-start(bf16[256,256]{1,0:T(8,128)(2,1)} %get-tuple-element.63) | copy-start | bytes 393220
  162.4 22.6 %copy-start.30 = (bf16[256,256]{1,0:T(8,128)(2,1)S(1)}, bf16[256,256]{1,0:T(8,128)(2,1)}, u32[]{:S(2)}) copy-start(bf16[256,256]{1,0:T(8,128)(2,1)} %get-tuple-element.64) | copy-start | bytes 393220
  162.4 29.6 %copy-start.37 = (bf16[256,256]{1,0:T(8,128)(2,1)S(1)}, bf16[256,256]{1,0:T(8,128)(2,1)}, u32[]{:S(2)}) copy-start(bf16[256,256]{1,0:T(8,128)(2,1)} %get-tuple-element.66) | copy-start | bytes 393220
  162.4 34.3 %copy-start.35 = (bf16[256,256]{1,0:T(8,128)(2,1)S(1)}, bf16[256,256]{1,0:T(8,128)(2,1)}, u32[]{:S(2)}) copy-start(bf16[256,256]{1,0:T(8,128)(2,1)} %get-tuple-element.67) | copy-start | bytes 393220
  162.4 35.8 %copy-start.16 = (bf16[256,256]{1,0:T(8,128)(2,1)S(1)}, bf16[256,256]{1,0:T(8,128)(2,1)}, u32[]{:S(2)}) copy-start(bf16[256,256]{1,0:T(8,128)(2,1)} %get-tuple-element.72.refs_1_.refs_0_) | copy-start | bytes 393220
  162.4 50.1 %collective-permute-start.29 = (bf16[3072,256]{1,0:T(8,128)(2,1)}, bf16[3072,256]{1,0:T(8,128)(2,1)S(1)}, u32[]{:S(2)}, u32[]{:S(2)}) collective-permute-start(bf16[3072,256]{1,0:T(8,128)(2,1)} %gate.7.refs_1_), channel_id=1, source_target_pairs={{0,2},{1,3},{2,0},{3,1},{4,6},{5,7},{6,4},{7,5},{8,10},{9,11},{10,... | collective-permute-start | bytes 4718600 | tf_op jit(solution)/shard_map/ppermute | solution.py:113
  163.8 49.5 %all-to-all-start.3 = ((bf16[8,144,256]{2,1,0:T(8,128)(2,1)}), bf16[8,144,256]{2,1,0:T(8,128)(2,1)S(1)}, u32[]{:S(2)}, u32[]{:S(2)}) async-start(bf16[8,144,256]{2,1,0:T(8,128)(2,1)} %get-tuple-element.76), calls=%async_computation.3 | async-start | bytes 1179648 | tf_op jit(solution)/shard_map/all_to_all | solution.py:122
  170.4 14.6 %collective-permute-start.31 = (bf16[256,256]{1,0:T(8,128)(2,1)S(1)}, bf16[256,256]{1,0:T(8,128)(2,1)S(1)}, u32[]{:S(2)}, u32[]{:S(2)}) collective-permute-start(bf16[256,256]{1,0:T(8,128)(2,1)S(1)} %copy-done.48), channel_id=1, source_target_pairs={{0,8},{4,12},{8,0},{12,4},{16,24},{20,28},{24,16},{28,20},{1,9},{5... | collective-permute-start | bytes 393224 | tf_op jit(solution)/shard_map/ppermute | solution.py:113
  171.0 21.0 %collective-permute-start.32 = (bf16[256,256]{1,0:T(8,128)(2,1)S(1)}, bf16[256,256]{1,0:T(8,128)(2,1)S(1)}, u32[]{:S(2)}, u32[]{:S(2)}) collective-permute-start(bf16[256,256]{1,0:T(8,128)(2,1)S(1)} %copy-done.47), channel_id=1, source_target_pairs={{0,16},{4,20},{8,24},{12,28},{16,0},{20,4},{24,8},{28,12},{1,17},{... | collective-permute-start | bytes 393224 | tf_op jit(solution)/shard_map/ppermute | solution.py:113
  173.4 23.3 %collective-permute-start.33 = (bf16[256,256]{1,0:T(8,128)(2,1)S(1)}, bf16[256,256]{1,0:T(8,128)(2,1)S(1)}, u32[]{:S(2)}, u32[]{:S(2)}) collective-permute-start(bf16[256,256]{1,0:T(8,128)(2,1)S(1)} %copy-done.45), channel_id=1, source_target_pairs={{0,24},{4,28},{8,16},{12,20},{16,8},{20,12},{24,0},{28,4},{1,25},{... | collective-permute-start | bytes 393224 | tf_op jit(solution)/shard_map/ppermute | solution.py:113
  173.9 25.0 %collective-permute-start.22 = (bf16[256,256]{1,0:T(8,128)(2,1)S(1)}, bf16[256,256]{1,0:T(8,128)(2,1)S(1)}, u32[]{:S(2)}, u32[]{:S(2)}) collective-permute-start(bf16[256,256]{1,0:T(8,128)(2,1)S(1)} %copy-done.33), channel_id=1, source_target_pairs={{0,1},{1,0},{2,3},{3,2},{4,5},{5,4},{6,7},{7,6},{8,9},{9,8},{10,11... | collective-permute-start | bytes 393224 | tf_op jit(solution)/shard_map/ppermute | solution.py:113
  185.0 16.5 %collective-permute-start.23 = (bf16[256,256]{1,0:T(8,128)(2,1)S(1)}, bf16[256,256]{1,0:T(8,128)(2,1)S(1)}, u32[]{:S(2)}, u32[]{:S(2)}) collective-permute-start(bf16[256,256]{1,0:T(8,128)(2,1)S(1)} %copy-done.30), channel_id=1, source_target_pairs={{0,3},{1,2},{2,1},{3,0},{4,7},{5,6},{6,5},{7,4},{8,11},{9,10},{10,... | collective-permute-start | bytes 393224 | tf_op jit(solution)/shard_map/ppermute | solution.py:113
  192.0 13.4 %collective-permute-start.24 = (bf16[256,256]{1,0:T(8,128)(2,1)S(1)}, bf16[256,256]{1,0:T(8,128)(2,1)S(1)}, u32[]{:S(2)}, u32[]{:S(2)}) collective-permute-start(bf16[256,256]{1,0:T(8,128)(2,1)S(1)} %copy-done.37), channel_id=1, source_target_pairs={{0,1},{1,0},{2,3},{3,2},{4,5},{5,4},{6,7},{7,6},{8,9},{9,8},{10,11... | collective-permute-start | bytes 393224 | tf_op jit(solution)/shard_map/ppermute | solution.py:113
  196.7 9.7 %collective-permute-start.25 = (bf16[256,256]{1,0:T(8,128)(2,1)S(1)}, bf16[256,256]{1,0:T(8,128)(2,1)S(1)}, u32[]{:S(2)}, u32[]{:S(2)}) collective-permute-start(bf16[256,256]{1,0:T(8,128)(2,1)S(1)} %copy-done.35), channel_id=1, source_target_pairs={{0,2},{1,3},{2,0},{3,1},{4,6},{5,7},{6,4},{7,5},{8,10},{9,11},{10,... | collective-permute-start | bytes 393224 | tf_op jit(solution)/shard_map/ppermute | solution.py:113
  199.0 16.2 %copy-start.29 = (bf16[256,256]{1,0:T(8,128)(2,1)}, bf16[256,256]{1,0:T(8,128)(2,1)S(1)}, u32[]{:S(2)}) copy-start(bf16[256,256]{1,0:T(8,128)(2,1)S(1)} %collective-permute-done.22.refs_6_) | copy-start | bytes 393220
  199.0 8.2 %collective-permute-start.26 = (bf16[256,256]{1,0:T(8,128)(2,1)S(1)}, bf16[256,256]{1,0:T(8,128)(2,1)S(1)}, u32[]{:S(2)}, u32[]{:S(2)}) collective-permute-start(bf16[256,256]{1,0:T(8,128)(2,1)S(1)} %copy-done.32), channel_id=1, source_target_pairs={{0,3},{1,2},{2,1},{3,0},{4,7},{5,6},{6,5},{7,4},{8,11},{9,10},{10,... | collective-permute-start | bytes 393224 | tf_op jit(solution)/shard_map/ppermute | solution.py:113
  201.6 13.6 %copy-start.31 = (bf16[256,256]{1,0:T(8,128)(2,1)}, bf16[256,256]{1,0:T(8,128)(2,1)S(1)}, u32[]{:S(2)}) copy-start(bf16[256,256]{1,0:T(8,128)(2,1)S(1)} %collective-permute-done.23.refs_8_) | copy-start | bytes 393220
  201.6 11.0 %collective-permute-start.36 = (bf16[256,256]{1,0:T(8,128)(2,1)}, bf16[256,256]{1,0:T(8,128)(2,1)S(1)}, u32[]{:S(2)}, u32[]{:S(2)}) collective-permute-start(bf16[256,256]{1,0:T(8,128)(2,1)} %add_some.1.refs_1_), channel_id=1, source_target_pairs={{0,24},{4,28},{8,16},{12,20},{16,8},{20,12},{24,0},{28,4},{1,25},{... | collective-permute-start | bytes 393224 | tf_op jit(solution)/shard_map/ppermute | solution.py:113
  205.5 20.0 %collective-permute-start.28 = (bf16[3072,256]{1,0:T(8,128)(2,1)}, bf16[3072,256]{1,0:T(8,128)(2,1)}, u32[]{:S(2)}, u32[]{:S(2)}) collective-permute-start(bf16[3072,256]{1,0:T(8,128)(2,1)} %gate.7.refs_1_), channel_id=1, source_target_pairs={{0,1},{1,0},{2,3},{3,2},{4,5},{5,4},{6,7},{7,6},{8,9},{9,8},{10,11... | collective-permute-start | bytes 4718600 | tf_op jit(solution)/shard_map/ppermute | solution.py:113
  206.4 17.6 %collective-permute-start.20 = (bf16[1024,256]{1,0:T(8,128)(2,1)}, bf16[1024,256]{1,0:T(8,128)(2,1)}, u32[]{:S(2)}, u32[]{:S(2)}) collective-permute-start(bf16[1024,256]{1,0:T(8,128)(2,1)} %get-tuple-element.61.refs_1_), channel_id=1, source_target_pairs={{0,2},{1,3},{2,0},{3,1},{4,6},{5,7},{6,4},{7,5},{8,10},{9,11},{10,... | collective-permute-start | bytes 1572872 | tf_op jit(solution)/shard_map/ppermute | solution.py:113
  207.1 16.2 %collective-permute-start.35 = (bf16[256,256]{1,0:T(8,128)(2,1)}, bf16[256,256]{1,0:T(8,128)(2,1)S(1)}, u32[]{:S(2)}, u32[]{:S(2)}) collective-permute-start(bf16[256,256]{1,0:T(8,128)(2,1)} %add_some.1.refs_1_), channel_id=1, source_target_pairs={{0,16},{4,20},{8,24},{12,28},{16,0},{20,4},{24,8},{28,12},{1,17},{... | collective-permute-start | bytes 393224 | tf_op jit(solution)/shard_map/ppermute | solution.py:113
  212.6 10.9 %collective-permute-start.34 = (bf16[256,256]{1,0:T(8,128)(2,1)}, bf16[256,256]{1,0:T(8,128)(2,1)S(1)}, u32[]{:S(2)}, u32[]{:S(2)}) collective-permute-start(bf16[256,256]{1,0:T(8,128)(2,1)} %add_some.1.refs_1_), channel_id=1, source_target_pairs={{0,8},{4,12},{8,0},{12,4},{16,24},{20,28},{24,16},{28,20},{1,9},{5... | collective-permute-start | bytes 393224 | tf_op jit(solution)/shard_map/ppermute | solution.py:113
  212.6 13.5 %collective-permute-start.30 = (bf16[3072,256]{1,0:T(8,128)(2,1)S(1)}, bf16[3072,256]{1,0:T(8,128)(2,1)}, u32[]{:S(2)}, u32[]{:S(2)}) collective-permute-start(bf16[3072,256]{1,0:T(8,128)(2,1)S(1)} %collective-permute-done.29.refs_3_), channel_id=1, source_target_pairs={{0,1},{1,0},{2,3},{3,2},{4,5},{5,4},{6,7},{7,6},{8,9},{9,8},{10,11... | collective-permute-start | bytes 4718600 | tf_op jit(solution)/shard_map/ppermute | solution.py:113
  215.2 24.1 %all-to-all-start.4 = ((bf16[8,128,256]{2,1,0:T(8,128)(2,1)}), bf16[8,128,256]{2,1,0:T(8,128)(2,1)S(1)}, u32[]{:S(2)}, u32[]{:S(2)}) async-start(bf16[8,128,256]{2,1,0:T(8,128)(2,1)} %get-tuple-element.77), calls=%async_computation.4 | async-start | bytes 1048576 | tf_op jit(solution)/shard_map/all_to_all | solution.py:122
  223.4 10.1 %collective-permute-start.19 = (bf16[1024,256]{1,0:T(8,128)(2,1)}, bf16[1024,256]{1,0:T(8,128)(2,1)S(1)}, u32[]{:S(2)}, u32[]{:S(2)}) collective-permute-start(bf16[1024,256]{1,0:T(8,128)(2,1)} %get-tuple-element.61.refs_1_), channel_id=1, source_target_pairs={{0,1},{1,0},{2,3},{3,2},{4,5},{5,4},{6,7},{7,6},{8,9},{9,8},{10,11... | collective-permute-start | bytes 1572872 | tf_op jit(solution)/shard_map/ppermute | solution.py:113
  223.4 19.1 %collective-permute-start.37 = (bf16[256,256]{1,0:T(8,128)(2,1)S(1)}, bf16[256,256]{1,0:T(8,128)(2,1)S(1)}, u32[]{:S(2)}, u32[]{:S(2)}) collective-permute-start(bf16[256,256]{1,0:T(8,128)(2,1)S(1)} %copy-done.19), channel_id=1, source_target_pairs={{0,4},{4,0},{8,12},{12,8},{16,20},{20,16},{24,28},{28,24},{1,5},{5... | collective-permute-start | bytes 393224 | tf_op jit(solution)/shard_map/ppermute | solution.py:113
  224.0 18.5 %collective-permute-start.40 = (bf16[256,256]{1,0:T(8,128)(2,1)S(1)}, bf16[256,256]{1,0:T(8,128)(2,1)S(1)}, u32[]{:S(2)}, u32[]{:S(2)}) collective-permute-start(bf16[256,256]{1,0:T(8,128)(2,1)S(1)} %collective-permute-done.36.refs_15_.refs_7_), channel_id=1, source_target_pairs={{0,4},{4,0},{8,12},{12,8},{16,20},{20,16},{24,28},{28,24},{1,5},{5... | collective-permute-start | bytes 393224 | tf_op jit(solution)/shard_map/ppermute | solution.py:113
  225.5 17.0 %collective-permute-start.39 = (bf16[256,256]{1,0:T(8,128)(2,1)S(1)}, bf16[256,256]{1,0:T(8,128)(2,1)S(1)}, u32[]{:S(2)}, u32[]{:S(2)}) collective-permute-start(bf16[256,256]{1,0:T(8,128)(2,1)S(1)} %collective-permute-done.35.refs_14_.refs_5_), channel_id=1, source_target_pairs={{0,4},{4,0},{8,12},{12,8},{16,20},{20,16},{24,28},{28,24},{1,5},{5... | collective-permute-start | bytes 393224 | tf_op jit(solution)/shard_map/ppermute | solution.py:113
  226.1 9.0 %collective-permute-start.21 = (bf16[1024,256]{1,0:T(8,128)(2,1)}, bf16[1024,256]{1,0:T(8,128)(2,1)S(1)}, u32[]{:S(2)}, u32[]{:S(2)}) collective-permute-start(bf16[1024,256]{1,0:T(8,128)(2,1)} %collective-permute-done.20.refs_3_), channel_id=1, source_target_pairs={{0,1},{1,0},{2,3},{3,2},{4,5},{5,4},{6,7},{7,6},{8,9},{9,8},{10,11... | collective-permute-start | bytes 1572872 | tf_op jit(solution)/shard_map/ppermute | solution.py:113
  233.5 9.0 %collective-permute-start.38 = (bf16[256,256]{1,0:T(8,128)(2,1)S(1)}, bf16[256,256]{1,0:T(8,128)(2,1)S(1)}, u32[]{:S(2)}, u32[]{:S(2)}) collective-permute-start(bf16[256,256]{1,0:T(8,128)(2,1)S(1)} %collective-permute-done.34.refs_13_.refs_3_), channel_id=1, source_target_pairs={{0,4},{4,0},{8,12},{12,8},{16,20},{20,16},{24,28},{28,24},{1,5},{5... | collective-permute-start | bytes 393224 | tf_op jit(solution)/shard_map/ppermute | solution.py:113
  (37 other events, 140.8 us)

commit v4 on v3

--- a/solution.py
+++ b/solution.py
@@ -17,6 +17,7 @@
 code_step = 64
 extra_rows = 16
 mib = 1024 * 1024
+step_rows = 1024
 expected_us = collections.defaultdict(
     lambda: 0.001,
     hidden_slope=5,
@@ -63,7 +64,8 @@
     return pltpu.HBM(dims, dtype)
 
 
-def call(kernel, name, operands, outs, grid=(1,), scratch=(), after=(), aliases={}, spare=8):
+def call(kernel, name, operands, outs, grid=(1,), scratch=(), after=(), near=(), aliases={}, spare=8):
+    after = (*map(far, after), *near)
     specs, arrays, need = [], [], 0
     for operand in operands:
         array, spec = operand if isinstance(operand, tuple) else (operand, whole(operand))
@@ -148,8 +150,7 @@
         refs[count + i][...] = refs[i][...].astype(bf16)
 
 
-def low(pieces, after=()):
-    steps = 4
+def low(pieces, steps, after=(), near=()):
     operands, outs = [], []
     for array, first, rows in pieces:
         block, columns = rows // steps, array.shape[1]
@@ -157,7 +158,7 @@
             (far(array), pl.BlockSpec((block, columns), functools.partial(lambda f, i: (f + i, 0), first // block)))
         )
         outs.append((row_blocks(block, columns), far_shape((rows, columns), bf16)))
-    return call(functools.partial(low_kernel, len(pieces)), "low", operands, outs, grid=(steps,), after=after)
+    return call(functools.partial(low_kernel, len(pieces)), "low", operands, outs, grid=(steps,), after=after, near=near)
 
 
 def gate_kernel(*refs):
@@ -276,7 +277,7 @@
     lax.fori_loop(1, (depth + 7) // 8, more, 0)
 
 
-def spread(slots, row_dev, after=()):
+def spread(slots, row_dev, near=()):
     groups, _, slots_node, node_dev = slots.shape
     tiles = node_dev // lane_tile
     buckets = row_dev // bucket_rows
@@ -291,7 +292,7 @@
             pltpu.VMEM((tiles, buckets, 8, lane_tile), f32),
             pltpu.VMEM((tiles, buckets, 8, lane_tile), f32),
         ],
-        after=after,
+        near=near,
     )[0]
 
 
@@ -308,7 +309,7 @@
         outs[0][...] = slope.astype(bf16)
 
 
-def hidden(place, table, q_low, bias, want, after=()):
+def hidden(place, table, q_low, bias, want, after=(), near=()):
     rows, width = table[0].shape
     columns = q_low.shape[1]
     sides = len(table)
@@ -326,38 +327,46 @@
         [out],
         grid=(rows // block,),
         after=after,
+        near=near,
     )[0]
 
 
-def pool_kernel(last, hidden_ref, matrix_ref, *refs):
-    for g in range(matrix_ref.shape[0]):
-        total = dot(hidden_ref[...], matrix_ref[g], (1, 0))
+def pool_kernel(last, views, hidden_ref, *refs):
+    matrix, refs = refs[:views], refs[views:]
+    rows = matrix[0].shape[1]
+    for g in range(matrix[0].shape[0]):
+        total = dot(hidden_ref[:, 0:rows], matrix[0][g], (1, 0))
+        for v in range(1, views):
+            total = total + dot(hidden_ref[:, v * rows : (v + 1) * rows], matrix[v][g], (1, 0))
         nodes = total.shape[1]
         at = slice(g * nodes, (g + 1) * nodes)
+        if len(refs) > 1:
+            total = total + refs[0][:, at]
         if last:
-            refs[1][at, :] = (refs[0][:, at] + total).T.astype(bf16)
+            refs[-1][at, :] = total.T.astype(bf16)
         else:
-            refs[0][:, at] = total
-
-
-def pool(hidden_t, matrix, first, so_far, after=()):
+            refs[-1][:, at] = total
+
+
+def pool(hidden_t, matrix, first, so_far, step_rows, last, near=()):
     columns, rows = hidden_t.shape
     groups, _, node_dev = matrix.shape
     nodes = groups * node_dev
-    last = so_far is not None
+    views = rows // step_rows
     total_block = pl.BlockSpec((columns, 2 * node_dev), lambda i: (0, i))
-    return call(
-        functools.partial(pool_kernel, last),
+    block = (2, step_rows, node_dev)
+    view = [pl.BlockSpec(block, functools.partial(lambda v, i: (i, v, 0), first // step_rows + v)) for v in range(views)]
+    return call(
+        functools.partial(pool_kernel, last, views),
         "pool",
-        [hidden_t, (matrix, pl.BlockSpec((2, rows, node_dev), lambda i: (i, first // rows, 0)))]
-        + ([(so_far, total_block)] if last else []),
+        [hidden_t] + [(matrix, spec) for spec in view] + ([] if so_far is None else [(so_far, total_block)]),
         [
             (row_blocks(2 * node_dev, columns), shape((nodes, columns), bf16))
             if last
             else (total_block, shape((columns, nodes), f32))
         ],
         grid=(groups // 2,),
-        after=after,
+        near=near,
     )[0]
 
 
@@ -380,7 +389,7 @@
         outs[j][:, columns:] = rows_at(cotangent_ref, at, few)[...]
 
 
-def self_half(place, table, w_self, bias, cotangent, after=()):
+def self_half(place, table, w_self, bias, cotangent, near=()):
     nodes, columns = cotangent.shape
     sides = len(table)
     return call(
@@ -389,7 +398,7 @@
         [(place, smem)] + first_rows(table, nodes) + [far(w_self), far(bias.reshape(1, columns)), far(cotangent)],
         [full((nodes // sides, 2 * columns), f32, far_shape)] * sides,
         scratch=[pltpu.VMEM((nodes, columns), f32)],
-        after=after,
+        near=near,
     )
 
 
@@ -486,7 +495,7 @@
     return call(
         functools.partial(w_back_kernel, sides),
         "w_back",
-        [(place, smem)] + first_rows(table, node_dev) + [*map(far, late), *map(far, pooled), far(w_self)],
+        [(place, smem)] + first_rows(table, node_dev) + [*late, *pooled, far(w_self)],
         [full((node_dev, columns), f32, far_shape), half, half]
         + [full((extra_rows, columns), bf16, far_shape)]
         + [full((node_dev, columns), bf16, far_shape)] * sides,
@@ -504,10 +513,10 @@
         out[...] = (own_ref[i].astype(f32) + other_ref[i].astype(f32)).astype(bf16)
 
 
-def add_pairs(own, other, after=()):
+def add_pairs(own, other, after=(), near=()):
     count, rows, columns = own.shape
     return call(
-        add_pairs_kernel, "add_pairs", [far(own), far(other)], [full((rows, columns), bf16, far_shape)] * count, after=after
+        add_pairs_kernel, "add_pairs", [far(own), other], [full((rows, columns), bf16, far_shape)] * count, after=after, near=near
     )
 
 
@@ -584,12 +593,19 @@
     )[0]
 
 
-def rows_back_kernel(chunk_counts, sides, place_ref, *refs):
+def each_chunk(step, counts, run):
+    first = 0
+    for k, count in enumerate(counts):
+        pl.when((step >= first) & (step < first + count))(functools.partial(run, k))
+        first += count
+
+
+def rows_back_kernel(chunk_counts, grad_counts, sides, place_ref, *refs):
     chunks = len(chunk_counts)
     matrix_ref, pooled_ref, slopes = refs[0], refs[1], refs[2 : 2 + chunks]
     table = refs[2 + chunks : 2 + chunks + chunks * sides]
-    rest = refs[2 + chunks + chunks * sides :]
-    extra_ref, grad_refs, (q_ref, total_ref, bias_ref) = rest[0], rest[1 : 1 + chunks], rest[1 + chunks :]
+    extra_ref, rest = refs[2 + chunks + chunks * sides], refs[3 + chunks + chunks * sides :]
+    grad_refs, (q_ref, total_ref, bias_ref, low_ref) = rest[: len(grad_counts)], rest[len(grad_counts) :]
     step = pl.program_id(0)
     matrix = jnp.concatenate([matrix_ref[g] for g in range(matrix_ref.shape[0])], axis=1)
     summed = dot(matrix, pooled_ref[...], (1, 0))
@@ -600,19 +616,19 @@
         bias_ref[...] = jnp.zeros_like(bias_ref)
         total_ref[...] = jnp.zeros_like(total_ref)
 
-    first = 0
-    for k in range(chunks):
-
-        @pl.when((step >= first) & (step < first + chunk_counts[k]))
-        def _():
-            grad = summed * slopes[k][...].astype(f32)
-            bias_ref[...] += jnp.sum(grad, axis=0, keepdims=True)
-            grad = grad.astype(bf16)
-            grad_refs[k][...] = grad
-            for j in range(sides):
-                total_ref[j] += dot(grad, table[k * sides + j][...], (0, 0))
-
-        first += chunk_counts[k]
+    def in_chunk(k):
+        grad = summed * slopes[k][...].astype(f32)
+        bias_ref[...] += jnp.sum(grad, axis=0, keepdims=True)
+        grad = grad.astype(bf16)
+        low_ref[...] = grad
+        for j in range(sides):
+            total_ref[j] += dot(grad, table[k * sides + j][...], (0, 0))
+
+    def put(k):
+        grad_refs[k][...] = low_ref[...]
+
+    each_chunk(step, chunk_counts, in_chunk)
+    each_chunk(step, grad_counts, put)
 
     @pl.when(step == pl.num_programs(0) - 1)
     def _():
@@ -631,25 +647,29 @@
                 q_ref[(place_ref[1] ^ j) * per + part, 0:piece, :] = flat[part * piece : (part + 1) * piece, :]
 
 
-def rows_back(place, matrix, pooled, slopes, table, extra, after=()):
+def rows_back(place, matrix, pooled, slopes, table, extra, grad_rows, near=()):
     sides = len(table[0])
     groups, row_dev, node_dev = matrix.shape
     columns, width = pooled.shape[1], table[0][0].shape[1]
-    block = min(slopes[-1].shape[0], 512 * 2048 // (groups * node_dev))
-    specs = chunk_specs(slopes, block)
+    block = min(min(a.shape[0] for a in slopes), step_rows * 2048 // (groups * node_dev))
     by_side = [chunk_specs([part[j] for part in table], block) for j in range(sides)]
-    return call(
-        functools.partial(rows_back_kernel, [a.shape[0] // block for a in slopes], sides),
+    grads = [shape((rows, columns), bf16) for rows in grad_rows]
+    return call(
+        functools.partial(rows_back_kernel, [a.shape[0] // block for a in slopes], [r // block for r in grad_rows], sides),
         "rows_back",
         [(place, smem), (far(matrix), pl.BlockSpec((groups, block, node_dev), lambda i: (0, i, 0))), pooled]
-        + list(zip(map(far, slopes), specs))
+        + list(zip(map(far, slopes), chunk_specs(slopes, block)))
         + [(far(table[k][j]), by_side[j][k]) for k in range(len(table)) for j in range(sides)]
         + [far(extra)],
-        [(spec, far_shape(a.shape, bf16)) for spec, a in zip(specs, slopes)]
+        [(spec, far_shape(a.shape, bf16)) for spec, a in zip(chunk_specs(grads, block), grads)]
         + [full((groups, sides * width // groups + extra_rows, columns), bf16)],
         grid=(row_dev // block,),
-        scratch=[pltpu.VMEM((sides, columns, width), f32), pltpu.VMEM((1, columns), f32)],
-        after=after,
+        scratch=[
+            pltpu.VMEM((sides, columns, width), f32),
+            pltpu.VMEM((1, columns), f32),
+            pltpu.VMEM((block, columns), bf16),
+        ],
+        near=near,
     )
 
 
@@ -671,7 +691,7 @@
         out_ref[0:nodes, :] += own
 
 
-def table_back(place, grads, qs, grad_self, first, row_dev, so_far=None, after=()):
+def table_back(place, grads, qs, grad_self, first, row_dev, so_far=None, near=()):
     sides = len(grads)
     rows, columns = grads[0].shape
     nodes, width = grad_self[0].shape
@@ -683,7 +703,8 @@
         operands,
         [(pl.BlockSpec((block, width), lambda i: (first // block + i, 0)), far_shape((row_dev, width), f32))],
         grid=(rows // block,),
-        after=after if so_far is None else [so_far, *after],
+        after=() if so_far is None else [so_far],
+        near=near,
         aliases={} if so_far is None else {len(operands): 0},
     )[0]
 
@@ -720,31 +741,36 @@
     few = node_dev // sides
     place = jnp.stack([lax.axis_index("dp"), lax.axis_index("mp")]).astype(i32)
 
-    cut = row_dev * 3 // 4
-    (low_a,) = low([(table, 0, cut)])
+    unit = row_dev // 4
+    (low_a,) = low([(table, 0, unit)], 1)
+    low_b, low_c = low([(table, unit, 2 * unit), (table, 3 * unit, unit)], 2, after=[low_a])
     across_a, beside_a = swap(low_a, "mp", 2), swap(low_a, "mp", 1)
-    slots = make_slots(place, neighbours, counts, importance, row_dev, groups, after=[low_a])
+    slots = make_slots(place, neighbours, counts, importance, row_dev, groups, after=[low_b])
     half = sides * width
-    low_b, q_low, w_self, w_pooled = low(
-        [(table, cut, row_dev - cut), (q_weight, 0, half), (w_weight, 0, half), (w_weight, half, half)], after=[slots]
-    )
+    q_low, w_self, w_pooled = low([(q_weight, 0, half), (w_weight, 0, half), (w_weight, half, half)], 4, near=[slots])
+    low_b = gate(low_b, [across_a])
+    across_b, beside_b = swap(low_b, "mp", 2), swap(low_b, "mp", 1)
     slots = exchange(slots, "dp")
-    across_b, beside_b = swap(low_b, "mp", 2), swap(low_b, "mp", 1)
-
-    matrix = spread(slots, row_dev, after=[low_b])
-    across_a = gate(across_a, [matrix])
+
     part_a = [low_a, beside_a, across_a, swap(across_a, "mp", 1)]
     hidden_a = hidden(place, part_a, q_low, q_bias, "value")
-    so_far = pool(hidden_a, matrix, 0, None)
-    w_pooled = all_sides(gate(w_pooled, [hidden_a]))
-    across_b = gate(across_b, [hidden_a])
+    matrix = spread(slots, row_dev, near=[hidden_a])
+    so_far = pool(hidden_a, matrix, 0, None, unit, False)
+    low_c = gate(low_c, [across_b])
+    across_c, beside_c = swap(low_c, "mp", 2), swap(low_c, "mp", 1)
+    across_b = gate(across_b, [matrix])
     part_b = [low_b, beside_b, across_b, swap(across_b, "mp", 1)]
-    parts = [part_a, part_b]
-    hidden_b = hidden(place, part_b, q_low, q_bias, "value", after=[so_far])
-    part_sums = pool(hidden_b, matrix, cut, so_far, after=[w_pooled[2]])
+    hidden_b = hidden(place, part_b, q_low, q_bias, "value", near=[so_far])
+    so_far = pool(hidden_b, matrix, unit, so_far, unit, False)
+    across_c = gate(across_c, [hidden_b])
+    part_c = [low_c, beside_c, across_c, swap(across_c, "mp", 1)]
+    parts = [part_a, part_b, part_c]
+    hidden_c = hidden(place, part_c, q_low, q_bias, "value", near=[so_far])
+    w_pooled = all_sides(gate(w_pooled, [matrix]))
+    part_sums = pool(hidden_c, matrix, 3 * unit, so_far, unit, True)
     pooled = exchange(part_sums.reshape(groups * sides, few, columns), ("dp", "mp"))
 
-    early = self_half(place, part_a, w_self, w_bias, cotangent, after=[part_sums])
+    early = self_half(place, part_a, w_self, w_bias, cotangent, near=[part_sums, w_pooled[2]])
     early = [early[0]] + [swap(early[j], "mp", j) for j in range(1, sides)]
     slope = [hidden(place, part, q_low, q_bias, "slope", after=[early[0]]) for part in parts]
 
@@ -760,23 +786,23 @@
     q_cut = [q_cut[0]] + [swap(q_cut[j], "mp", j) for j in range(1, sides)]
     grad_self = [grad_self[0]] + [swap(grad_self[j], "mp", j) for j in range(1, sides)]
 
-    grad_a, grad_b, q_parts = rows_back(place, matrix, grad_pooled, slope, parts, extra, after=[q_cut[2]])
-    pairs = add_pairs(even, swap(odd, "dp", 1), after=[grad_a])
+    grad_a, grad_b, q_parts = rows_back(place, matrix, grad_pooled, slope, parts, extra, [unit, 3 * unit], near=[q_cut[2]])
+    pairs = add_pairs(even, swap(odd, "dp", 1), after=[grad_a], near=[grad_self[2], grad_self[3]])
     count = groups // 2
     pairs = [pairs[0]] + [swap(pairs[s], "dp", 2 * s) for s in range(1, count)]
-    grad_a = gate(grad_a, [pairs[0]])
-    across_a = swap(grad_a, "mp", 2)
+    grad_b = gate(grad_b, [pairs[0]])
+    across_b = swap(grad_b, "mp", 2)
     piece = add_some(pairs)
     pieces = [piece] + [swap(piece, "dp", 2 * s) for s in range(1, count)]
     q_pieces, q_bias_grad, w_bias_grad, penalty = add(
         exchange(q_parts, "dp"), penalty_rate / node_total, after=[piece]
     )
     pieces = [p for own in pieces for p in (own, swap(own, "dp", 1))]
+    grads = [grad_b, swap(grad_b, "mp", 1), across_b, swap(across_b, "mp", 1)]
+    table_grad = table_back(place, grads, q_cut, grad_self, unit, row_dev, near=[pieces[2], pieces[4], pieces[6]])
+    across_a = swap(grad_a, "mp", 2)
     grads = [grad_a, swap(grad_a, "mp", 1), across_a, swap(across_a, "mp", 1)]
-    table_grad = table_back(place, grads, q_cut, grad_self, 0, row_dev, after=[pieces[2], pieces[4], pieces[6]])
-    across_b = swap(grad_b, "mp", 2)
-    grads = [grad_b, swap(grad_b, "mp", 1), across_b, swap(across_b, "mp", 1)]
-    table_grad = table_back(place, grads, q_cut, grad_self, grad_a.shape[0], row_dev, table_grad)
+    table_grad = table_back(place, grads, q_cut, grad_self, 0, row_dev, table_grad)
     q_grad = widen(exchange(q_pieces, "dp").reshape(-1, columns), after=[table_grad])
     w_grad = collect(place, pieces, after=[table_grad])
     return (

time: 249 us -> 229 us (0.920)
  waiting for transfers between devices: 69.4 us -> 57.3 us
  local copies, waits for them, and re-layouts: 15 us -> 4.48 us
    unnamed x110 -> x94, local copies, waits for them, and re-layouts: 15 us -> 4.48 us
    ppermute x41 -> x44, waiting for transfers between devices: 53.4 us -> 47 us  [swap(): return lax.ppermute(array, axis, [(i, i ^ bits) for i in range(size)])]
    all_to_all x5, waiting for transfers between devices: 16 us -> 10.3 us  [exchange(): return lax.all_to_all(array, axes, split_axis=0, concat_axis=0, tiled=True)]
    pallas_call x22 -> x26, Pallas kernels: 97.1 us -> 99 us  [call(): pl.pallas_call(inner, grid=grid, in_specs=specs + [pl.BlockSpec(memory_sp...]
    ppermute x41 -> x44, starting transfers between devices: 31.9 us -> 32.6 us  [swap(): return lax.ppermute(array, axis, [(i, i ^ bits) for i in range(size)])]
  transfers between devices with their start and end apart: 46 -> 49, of which waited for: 14 -> 14; matrix products, arithmetic and copies ran while one was open for 0% -> 0% of each run, Pallas kernels for 33% -> 39%
where the time goes in v4:
time: 229 us; the launch traced here: 225 us
  Pallas kernels  99 us (43%)
  starting transfers between devices  63.2 us (28%)
  waiting for transfers between devices  57.3 us (25%)
  local copies, waits for them, and re-layouts  4.48 us (2%)
    pallas_call x26, Pallas kernels, call(): pl.pallas_call(inner, grid=grid, in_specs=specs + [pl.BlockSpec(memory_sp...  99 us
    ppermute x44, waiting for transfers between devices, swap(): return lax.ppermute(array, axis, [(i, i ^ bits) for i in range(size)])  47 us
    ppermute x44, starting transfers between devices, swap(): return lax.ppermute(array, axis, [(i, i ^ bits) for i in range(size)])  32.6 us
    all_to_all x5, starting transfers between devices, exchange(): return lax.all_to_all(array, axes, split_axis=0, concat_axis=0, tiled=True)  30.7 us
    all_to_all x5, waiting for transfers between devices, exchange(): return lax.all_to_all(array, axes, split_axis=0, concat_axis=0, tiled=True)  10.3 us
  transfers between devices with their start and end apart: 49, of which 14 were waited for; matrix products, arithmetic and copies ran while one was open for 0% of the time, Pallas kernels for 39%

profile of v4, /device:TPU:12, one launch (start us, length us, event | category | flops | bytes accessed | tf_op | source)
XLA Modules:
  0.0 225.4 jit_solution(12210957766309680691)
XLA Ops:
  0.6 2.1 low.3.refs_2_.refs_1_.refs_6_
  2.7 1.5 collective-permute-start.1
  4.2 2.8 %low.4 = (bf16[2048,256]{1,0:T(8,128)(2,1)}, bf16[1024,256]{1,0:T(8,128)(2,1)}) custom-call(f32[4096,256]{1,0:T(8,128)} %refs_1_.2, f32[4096,256]{1,0:T(8,128)} %refs_1_.2, bf16[1024,256]{1,0:T(8,128)(2,1)} %low.3.refs_2_.refs_1_.refs_6_), custom_call_target="tpu_custom_call" | custom-call | flops 1150000 | bytes 3690 | tf_op jit(solution)/shard_map/low/pallas_call | solution.py:82
  7.1 2.5 %slots.1.refs_3_ = s16[8,3,50,256]{3,2,1,0:T(8,128)(2,1)} custom-call(s32[2]{0:T(128)S(1)} %pad_add_fusion.refs_0_, s32[50,256]{1,0:T(8,128)} %bitcast.18, s32[1,256]{1,0:T(1,128)} %bitcast.26, f32[50,256]{1,0:T(8,128)} %bitcast.19, bf16[2048,256]{1,0:T(8,128)(2,1)} %get-tuple-element.46.refs_0_.refs_4_), custom_call_target="tpu_custom_call" | custom-call | flops 1150000 | bytes 3690 | tf_op jit(solution)/shard_map/slots/pallas_call | solution.py:82
  9.5 6.4 %all-to-all-start = ((s16[8,3,50,256]{3,2,1,0:T(8,128)(2,1)}), s16[8,3,50,256]{3,2,1,0:T(8,128)(2,1)}, u32[]{:S(2)}, u32[]{:S(2)}) async-start(s16[8,3,50,256]{3,2,1,0:T(8,128)(2,1)} %slots.1.refs_3_), calls=%async_computation | async-start | bytes 1376256 | tf_op jit(solution)/shard_map/all_to_all | solution.py:124
  16.6 1.6 collective-permute-start.3
  18.7 3.8 %low.5 = (bf16[1024,256]{1,0:T(8,128)(2,1)}, bf16[1024,256]{1,0:T(8,128)(2,1)}, bf16[1024,256]{1,0:T(8,128)(2,1)}) custom-call(f32[1024,256]{1,0:T(8,128)} %refs_0_.5, f32[2048,256]{1,0:T(8,128)} %refs_2_.1, f32[2048,256]{1,0:T(8,128)} %refs_2_.1, s16[8,3,50,256]{3,2,1,0:T(8,128)(2,1)} %slots.1.refs_3_), custom_call_target="tpu_custom_call" | custom-call | flops 1150000 | bytes 3690 | tf_op jit(solution)/shard_map/low/pallas_call | solution.py:82
  22.5 1.0 copy-done.6
  23.6 2.3 %hidden_value.3.refs_1_.refs_0_ = bf16[256,1024]{1,0:T(8,128)(2,1)S(1)} custom-call(s32[2]{0:T(128)S(1)} %pad_add_fusion.refs_0_, bf16[1024,256]{1,0:T(8,128)(2,1)S(1)} %copy-done.4, bf16[1024,256]{1,0:T(8,128)(2,1)S(1)} %collective-permute-done.refs_2_.refs_7_, bf16[1024,256]{1,0:T(8,128)(2,1)S(1)} %copy-done.6, ...), custom_call_target="tpu_custom_call" | custom-call | flops 1150000 | bytes 3690 | tf_op jit(solution)/shard_map/hidden_value/pallas_call | solution.py:82
  25.8 0.8 copy-done.14
  26.6 0.8 copy-done.15
  27.4 2.9 %all-to-all-done.refs_0_ = s16[8,3,50,256]{3,2,1,0:T(8,128)(2,1)} async-done(((s16[8,3,50,256]{3,2,1,0:T(8,128)(2,1)}), s16[8,3,50,256]{3,2,1,0:T(8,128)(2,1)}, u32[]{:S(2)}, u32[]{:S(2)}) %all-to-all-start) | async-done | bytes 614432 | tf_op jit(solution)/shard_map/all_to_all | solution.py:124
  30.3 13.2 %spread.1.refs_1_.refs_2_ = bf16[8,4096,256]{2,1,0:T(8,128)(2,1)S(1)} custom-call(s16[8,3,50,256]{3,2,1,0:T(8,128)(2,1)} %all-to-all-done.refs_0_, bf16[256,1024]{1,0:T(8,128)(2,1)S(1)} %hidden_value.3.refs_1_.refs_0_), custom_call_target="tpu_custom_call" | custom-call | flops 1150000 | bytes 3690 | tf_op jit(solution)/shard_map/spread/pallas_call | solution.py:82
  44.7 2.2 pool.3.refs_7_.refs_3_
  47.0 0.8 collective-permute-done.7.refs_4_.refs_13_
  47.8 3.9 %hidden_value.4.refs_1_.refs_0_ = bf16[256,2048]{1,0:T(8,128)(2,1)S(1)} custom-call(s32[2]{0:T(128)S(1)} %pad_add_fusion.refs_0_, bf16[2048,256]{1,0:T(8,128)(2,1)S(1)} %gate.6.refs_1_.refs_10_, bf16[2048,256]{1,0:T(8,128)(2,1)S(1)} %collective-permute-done.6.refs_2_.refs_11_, bf16[2048,256]{1,0:T(8,128)(2,1)S(1)} %gate.8.refs_3_.refs_12_, ...), custom_call_target="tpu_custom_call" | custom-call | flops 1150000 | bytes 3690 | tf_op jit(solution)/shard_map/hidden_value/pallas_call | solution.py:82
  51.8 6.4 %collective-permute-done.5.refs_0_ = bf16[1024,256]{1,0:T(8,128)(2,1)S(1)} collective-permute-done((bf16[1024,256]{1,0:T(8,128)(2,1)S(1)}, bf16[1024,256]{1,0:T(8,128)(2,1)S(1)}, u32[]{:S(2)}, u32[]{:S(2)}) %collective-permute-start.5) | collective-permute-done | bytes 524320 | tf_op jit(solution)/shard_map/ppermute | solution.py:115
  58.7 3.7 %pool.4.refs_7_.refs_2_ = f32[256,2048]{1,0:T(8,128)S(1)} custom-call(bf16[256,2048]{1,0:T(8,128)(2,1)S(1)} %hidden_value.4.refs_1_.refs_0_, bf16[8,4096,256]{2,1,0:T(8,128)(2,1)S(1)} %spread.1.refs_1_.refs_2_, bf16[8,4096,256]{2,1,0:T(8,128)(2,1)S(1)} %spread.1.refs_1_.refs_2_, f32[256,2048]{1,0:T(8,128)S(1)} %pool.3.refs_7_.refs_3_), custom_call_target="tpu_custom_call" | custom-call | flops 1150000 | bytes 3690 | tf_op jit(solution)/shard_map/pool/pallas_call | solution.py:82
  62.5 2.6 %hidden_value.5.refs_0_ = bf16[256,1024]{1,0:T(8,128)(2,1)S(1)} custom-call(s32[2]{0:T(128)S(1)} %pad_add_fusion.refs_0_, bf16[1024,256]{1,0:T(8,128)(2,1)S(1)} %gate.7.refs_1_.refs_14_, bf16[1024,256]{1,0:T(8,128)(2,1)S(1)} %collective-permute-done.4.refs_2_.refs_15_, bf16[1024,256]{1,0:T(8,128)(2,1)S(1)} %gate.9.refs_3_.refs_16_, ...), custom_call_target="tpu_custom_call" | custom-call | flops 1150000 | bytes 3690 | tf_op jit(solution)/shard_map/hidden_value/pallas_call | solution.py:82
  65.2 3.4 %pool.5.refs_8_ = bf16[2048,256]{1,0:T(8,128)(2,1)} custom-call(bf16[256,1024]{1,0:T(8,128)(2,1)S(1)} %hidden_value.5.refs_0_, bf16[8,4096,256]{2,1,0:T(8,128)(2,1)S(1)} %spread.1.refs_1_.refs_2_, f32[256,2048]{1,0:T(8,128)S(1)} %pool.4.refs_7_.refs_2_), custom_call_target="tpu_custom_call" | custom-call | flops 1150000 | bytes 3690 | tf_op jit(solution)/shard_map/pool/pallas_call | solution.py:82
  68.6 7.2 %all-to-all-start.1 = ((bf16[32,64,256]{2,1,0:T(8,128)(2,1)}), bf16[32,64,256]{2,1,0:T(8,128)(2,1)S(1)}, u32[]{:S(2)}, u32[]{:S(2)}) async-start(bf16[32,64,256]{2,1,0:T(8,128)(2,1)} %bitcast.6), calls=%async_computation.1 | async-start | bytes 2097152 | tf_op jit(solution)/shard_map/all_to_all | solution.py:124
  76.4 2.5 %self_half.1 = (f32[64,512]{1,0:T(8,128)}, f32[64,512]{1,0:T(8,128)}, f32[64,512]{1,0:T(8,128)}, f32[64,512]{1,0:T(8,128)}) custom-call(s32[2]{0:T(128)S(1)} %pad_add_fusion.refs_0_, bf16[1024,256]{1,0:T(8,128)(2,1)} %low.3.refs_2_.refs_1_.refs_6_, bf16[1024,256]{1,0:T(8,128)(2,1)} %copy-done.14, bf16[1024,256]{1,0:T(8,128)(2,1)} %copy-done.5, ...), custom_call_target="tpu_custom_call" | custom-call | flops 3449999872 | bytes 11070000 | tf_op jit(solution)/shard_map/self_half/pallas_call | solution.py:82
  79.0 1.5 collective-permute-start.11
  80.7 3.5 %hidden_slope.5.refs_11_.refs_5_ = bf16[1024,256]{1,0:T(8,128)(2,1)} custom-call(s32[2]{0:T(128)S(1)} %pad_add_fusion.refs_0_, bf16[1024,256]{1,0:T(8,128)(2,1)} %copy-done.8, bf16[1024,256]{1,0:T(8,128)(2,1)} %copy-done.16, bf16[1024,256]{1,0:T(8,128)(2,1)} %copy-done.9, bf16[1024,256]{1,0:T(8,128)(2,1)} %copy-done.17, ...), custom_call_target="tpu_custom_call" | custom-call | flops 5750000128 | bytes 18450000 | tf_op jit(solution)/shard_map/hidden_slope/pallas_call | solution.py:82
  84.2 3.5 %hidden_slope.3.refs_9_.refs_3_ = bf16[1024,256]{1,0:T(8,128)(2,1)} custom-call(s32[2]{0:T(128)S(1)} %pad_add_fusion.refs_0_, bf16[1024,256]{1,0:T(8,128)(2,1)} %low.3.refs_2_.refs_1_.refs_6_, bf16[1024,256]{1,0:T(8,128)(2,1)} %copy-done.14, bf16[1024,256]{1,0:T(8,128)(2,1)} %copy-done.5, bf16[1024,256]{1,0:T(8,128)(2,1)} %copy-done.15, ...), custom_call_target="tpu_custom_call" | custom-call | flops 5750000128 | bytes 18450000 | tf_op jit(solution)/shard_map/hidden_slope/pallas_call | solution.py:82
  87.7 5.6 %hidden_slope.4.refs_10_.refs_4_ = bf16[2048,256]{1,0:T(8,128)(2,1)} custom-call(s32[2]{0:T(128)S(1)} %pad_add_fusion.refs_0_, bf16[2048,256]{1,0:T(8,128)(2,1)} %copy-done.3, bf16[2048,256]{1,0:T(8,128)(2,1)} %copy-done.12, bf16[2048,256]{1,0:T(8,128)(2,1)} %copy-done.1, bf16[2048,256]{1,0:T(8,128)(2,1)} %copy-done.13, ...), custom_call_target="tpu_custom_call" | custom-call | flops 5750000128 | bytes 18450000 | tf_op jit(solution)/shard_map/hidden_slope/pallas_call | solution.py:82
  93.4 7.4 %all-to-all-done.1 = bf16[32,64,256]{2,1,0:T(8,128)(2,1)S(1)} async-done(((bf16[32,64,256]{2,1,0:T(8,128)(2,1)}), bf16[32,64,256]{2,1,0:T(8,128)(2,1)S(1)}, u32[]{:S(2)}, u32[]{:S(2)}) %all-to-all-start.1) | async-done | bytes 1048608 | tf_op jit(solution)/shard_map/all_to_all | solution.py:124
  100.8 4.0 %combine.1 = (bf16[8,4,64,256]{3,2,1,0:T(8,128)(2,1)}, bf16[64,1024]{1,0:T(8,128)(2,1)}, bf16[80,512]{1,0:T(8,128)(2,1)}, bf16[80,512]{1,0:T(8,128)(2,1)}, bf16[...) custom-call(bf16[8,4,64,256]{3,2,1,0:T(8,128)(2,1)S(1)} %bitcast.17, f32[64,512]{1,0:T(8,128)} %get-tuple-element.50.refs_7_.refs_1_, ...), custom_call_target="tpu_custom_call" | custom-call | flops 4600000000 | bytes 14760000 | tf_op jit(solution)/shard_map/combine/pallas_call | solution.py:82
  104.9 4.9 %all-to-all-start.2 = ((bf16[32,64,256]{2,1,0:T(8,128)(2,1)}), bf16[32,64,256]{2,1,0:T(8,128)(2,1)S(1)}, u32[]{:S(2)}, u32[]{:S(2)}) async-start(bf16[32,64,256]{2,1,0:T(8,128)(2,1)} %bitcast.9), calls=%async_computation.2 | async-start | bytes 2097152 | tf_op jit(solution)/shard_map/all_to_all | solution.py:124
  109.8 1.5 collective-permute-start.19
  111.3 10.4 %collective-permute-done.19.refs_11_ = bf16[64,1024]{1,0:T(8,128)(2,1)S(1)} collective-permute-done((bf16[64,1024]{1,0:T(8,128)(2,1)S(1)}, bf16[64,1024]{1,0:T(8,128)(2,1)S(1)}, u32[]{:S(2)}, u32[]{:S(2)}) %collective-permute-start.19) | collective-permute-done | bytes 131104 | tf_op jit(solution)/shard_map/ppermute | solution.py:115
  122.2 0.9 collective-permute-start.16
  123.7 1.9 cut.1
  125.6 0.9 collective-permute-start.21
  126.5 1.5 collective-permute-done.16.refs_7_
  128.0 1.3 collective-permute-done.17.refs_8_
  129.3 3.1 %w_back.1 = (f32[256,256]{1,0:T(8,128)}, bf16[4,256,256]{2,1,0:T(8,128)(2,1)}, bf16[4,256,256]{2,1,0:T(8,128)(2,1)}, bf16[16,256]{1,0:T(8,128)(2,1)}, bf16[256,2...) custom-call(s32[2]{0:T(128)S(1)} %pad_add_fusion.refs_0_, ...), custom_call_target="tpu_custom_call" | custom-call | flops 4600000000 | bytes 14760000 | tf_op jit(solution)/shard_map/w_back/pallas_call | solution.py:82
  133.0 1.6 collective-permute-start.29
  135.1 15.1 %rows_back.1 = (bf16[1024,256]{1,0:T(8,128)(2,1)}, bf16[3072,256]{1,0:T(8,128)(2,1)}, bf16[8,144,256]{2,1,0:T(8,128)(2,1)}) custom-call(s32[2]{0:T(128)S(1)} %pad_add_fusion.refs_0_, bf16[8,4096,256]{2,1,0:T(8,128)(2,1)} %copy-done, bf16[2048,256]{1,0:T(8,128)(2,1)S(1)} %bitcast.16, bf16[1024,256]{1,0:T(8,128)(2,1)} %hidden_slope.3.refs_9_.refs_3_, ...), custom_call_target="tpu_custom_call" | custom-call | flops 18400000000 | bytes 59040000 | tf_op jit(solution)/shard_map/rows_back/pallas_call | solution.py:82
  150.3 2.0 add_pairs.1
  152.3 0.9 copy-done.20
  153.3 1.3 collective-permute-start.32
  154.6 7.1 %all-to-all-start.3 = ((bf16[8,144,256]{2,1,0:T(8,128)(2,1)}), bf16[8,144,256]{2,1,0:T(8,128)(2,1)S(1)}, u32[]{:S(2)}, u32[]{:S(2)}) async-start(bf16[8,144,256]{2,1,0:T(8,128)(2,1)} %get-tuple-element.78), calls=%async_computation.3 | async-start | bytes 1179648 | tf_op jit(solution)/shard_map/all_to_all | solution.py:124
  162.2 2.4 %collective-permute-start.35 = (bf16[256,256]{1,0:T(8,128)(2,1)S(1)}, bf16[256,256]{1,0:T(8,128)(2,1)S(1)}, u32[]{:S(2)}, u32[]{:S(2)}) collective-permute-start(bf16[256,256]{1,0:T(8,128)(2,1)S(1)} %copy-done.42), channel_id=1, source_target_pairs={{0,16},{4,20},{8,24},{12,28},{16,0},{20,4},{24,8},{28,12},{1,17},{... | collective-permute-start | bytes 393224 | tf_op jit(solution)/shard_map/ppermute | solution.py:115
  165.2 11.2 %collective-permute-done.34.refs_1_ = bf16[256,256]{1,0:T(8,128)(2,1)S(1)} collective-permute-done((bf16[256,256]{1,0:T(8,128)(2,1)S(1)}, bf16[256,256]{1,0:T(8,128)(2,1)S(1)}, u32[]{:S(2)}, u32[]{:S(2)}) %collective-permute-start.34) | collective-permute-done | bytes 131104 | tf_op jit(solution)/shard_map/ppermute | solution.py:115
  176.4 6.1 %collective-permute-done.35.refs_2_ = bf16[256,256]{1,0:T(8,128)(2,1)S(1)} collective-permute-done((bf16[256,256]{1,0:T(8,128)(2,1)S(1)}, bf16[256,256]{1,0:T(8,128)(2,1)S(1)}, u32[]{:S(2)}, u32[]{:S(2)}) %collective-permute-start.35) | collective-permute-done | bytes 131104 | tf_op jit(solution)/shard_map/ppermute | solution.py:115
  182.5 4.6 %collective-permute-done.36.refs_3_ = bf16[256,256]{1,0:T(8,128)(2,1)S(1)} collective-permute-done((bf16[256,256]{1,0:T(8,128)(2,1)S(1)}, bf16[256,256]{1,0:T(8,128)(2,1)S(1)}, u32[]{:S(2)}, u32[]{:S(2)}) %collective-permute-start.36) | collective-permute-done | bytes 131104 | tf_op jit(solution)/shard_map/ppermute | solution.py:115
  188.4 1.5 collective-permute-start.23
  189.9 2.3 %collective-permute-done.26.refs_8_ = bf16[256,256]{1,0:T(8,128)(2,1)S(1)} collective-permute-done((bf16[256,256]{1,0:T(8,128)(2,1)S(1)}, bf16[256,256]{1,0:T(8,128)(2,1)S(1)}, u32[]{:S(2)}, u32[]{:S(2)}) %collective-permute-start.26) | collective-permute-done | bytes 131104 | tf_op jit(solution)/shard_map/ppermute | solution.py:115
  192.2 1.3 collective-permute-start.31
  193.5 3.9 %collective-permute-start.38 = (bf16[256,256]{1,0:T(8,128)(2,1)}, bf16[256,256]{1,0:T(8,128)(2,1)S(1)}, u32[]{:S(2)}, u32[]{:S(2)}) collective-permute-start(bf16[256,256]{1,0:T(8,128)(2,1)} %add_some.1.refs_1_), channel_id=1, source_target_pairs={{0,16},{4,20},{8,24},{12,28},{16,0},{20,4},{24,8},{28,12},{1,17},{... | collective-permute-start | bytes 393224 | tf_op jit(solution)/shard_map/ppermute | solution.py:115
  197.4 1.3 collective-permute-start.37
  198.7 0.9 add.3
  199.6 5.1 %all-to-all-start.4 = ((bf16[8,128,256]{2,1,0:T(8,128)(2,1)}), bf16[8,128,256]{2,1,0:T(8,128)(2,1)S(1)}, u32[]{:S(2)}, u32[]{:S(2)}) async-start(bf16[8,128,256]{2,1,0:T(8,128)(2,1)} %get-tuple-element.79), calls=%async_computation.4 | async-start | bytes 1048576 | tf_op jit(solution)/shard_map/all_to_all | solution.py:124
  205.3 0.8 collective-permute-start.40
  206.1 1.2 collective-permute-start.43
  207.3 0.8 collective-permute-start.42
  208.1 7.3 %table_back.2.refs_13_ = f32[4096,256]{1,0:T(8,128)} custom-call(s32[2]{0:T(128)S(1)} %pad_add_fusion.refs_0_, bf16[3072,256]{1,0:T(8,128)(2,1)} %copy-done.11, bf16[3072,256]{1,0:T(8,128)(2,1)} %collective-permute-done.31.refs_2_, bf16[3072,256]{1,0:T(8,128)(2,1)} %collective-permute-done.32.refs_3_, bf16[3072,256]{1,0:T(8,128)(2,1)} %collective-permute-done.33.refs_4_, ...), custom_call_target="tpu_custom_call" | custom-call | flops 23000000512 | bytes 73800000 | tf_op jit(solution)/shard_map/table_back/pallas_call | solution.py:82
  215.5 1.2 collective-permute-start.41
  216.8 0.8 copy-done.31
  217.6 3.5 %table_back.3.refs_1_.refs_9_ = f32[4096,256]{1,0:T(8,128)} custom-call(s32[2]{0:T(128)S(1)} %pad_add_fusion.refs_0_, bf16[1024,256]{1,0:T(8,128)(2,1)} %get-tuple-element.63.refs_2_.refs_1_, bf16[1024,256]{1,0:T(8,128)(2,1)} %copy-done.30, bf16[1024,256]{1,0:T(8,128)(2,1)} %collective-permute-done.23.refs_3_, ...), custom_call_target="tpu_custom_call", output_to_operand_aliasing={{}: (13, {})} | custom-call | flops 23000000512 | bytes 73800000 | tf_op jit(solution)/shard_map/table_back/pallas_call | solution.py:82
  221.0 1.0 widen.1
  222.1 1.4 collective-permute-done.41.refs_4_
  223.4 2.0 collect.1
  (161 shorter events, 9.3 us)
Async XLA Ops:
  2.7 13.9 %collective-permute-start.1 = (bf16[1024,256]{1,0:T(8,128)(2,1)}, bf16[1024,256]{1,0:T(8,128)(2,1)S(1)}, u32[]{:S(2)}, u32[]{:S(2)}) collective-permute-start(bf16[1024,256]{1,0:T(8,128)(2,1)} %low.3.refs_2_.refs_1_.refs_6_), channel_id=1, source_target_pairs={{0,2},{1,3},{2,0},{3,1},{4,6},{5,7},{6,4},{7,5},{8,10},{9,11},{10,... | collective-permute-start | bytes 1572872 | tf_op jit(solution)/shard_map/ppermute | solution.py:115
  9.5 20.8 %all-to-all-start = ((s16[8,3,50,256]{3,2,1,0:T(8,128)(2,1)}), s16[8,3,50,256]{3,2,1,0:T(8,128)(2,1)}, u32[]{:S(2)}, u32[]{:S(2)}) async-start(s16[8,3,50,256]{3,2,1,0:T(8,128)(2,1)} %slots.1.refs_3_), calls=%async_computation | async-start | bytes 1376256 | tf_op jit(solution)/shard_map/all_to_all | solution.py:124
  16.6 31.2 %copy-start.3 = (bf16[2048,256]{1,0:T(8,128)(2,1)}, bf16[2048,256]{1,0:T(8,128)(2,1)S(1)}, u32[]{:S(2)}) copy-start(bf16[2048,256]{1,0:T(8,128)(2,1)S(1)} %gate.6.refs_1_.refs_10_) | copy-start | bytes 3145732
  16.6 27.0 %collective-permute-start.3 = (bf16[2048,256]{1,0:T(8,128)(2,1)S(1)}, bf16[2048,256]{1,0:T(8,128)(2,1)S(1)}, u32[]{:S(2)}, u32[]{:S(2)}) collective-permute-start(bf16[2048,256]{1,0:T(8,128)(2,1)S(1)} %gate.6.refs_1_.refs_10_), channel_id=1, source_target_pairs={{0,2},{1,3},{2,0},{3,1},{4,6},{5,7},{6,4},{7,5},{8,10},{9,11},{10,... | collective-permute-start | bytes 3145736 | tf_op jit(solution)/shard_map/ppermute | solution.py:115
  18.1 4.3 %collective-permute-start = (bf16[1024,256]{1,0:T(8,128)(2,1)S(1)}, bf16[1024,256]{1,0:T(8,128)(2,1)S(1)}, u32[]{:S(2)}, u32[]{:S(2)}) collective-permute-start(bf16[1024,256]{1,0:T(8,128)(2,1)S(1)} %copy-done.4), channel_id=1, source_target_pairs={{0,1},{1,0},{2,3},{3,2},{4,5},{5,4},{6,7},{7,6},{8,9},{9,8},{10,11... | collective-permute-start | bytes 1572872 | tf_op jit(solution)/shard_map/ppermute | solution.py:115
  18.2 4.3 %collective-permute-start.2 = (bf16[1024,256]{1,0:T(8,128)(2,1)S(1)}, bf16[1024,256]{1,0:T(8,128)(2,1)S(1)}, u32[]{:S(2)}, u32[]{:S(2)}) collective-permute-start(bf16[1024,256]{1,0:T(8,128)(2,1)S(1)} %collective-permute-done.1.refs_1_.refs_3_.refs_8_), channel_id=1, source_target_pairs={{0,1},{1,0},{2,3},{3,2},{4,5},{5,4},{6,7},{7,6},{8,9},{9,8},{10,11... | collective-permute-start | bytes 1572872 | tf_op jit(solution)/shard_map/ppermute | solution.py:115
  27.4 16.2 %copy-start.7 = (bf16[1024,256]{1,0:T(8,128)(2,1)S(1)}, bf16[1024,256]{1,0:T(8,128)(2,1)}, u32[]{:S(2)}) copy-start(bf16[1024,256]{1,0:T(8,128)(2,1)} %get-tuple-element.45.refs_0_) | copy-start | bytes 1572868
  43.6 21.6 %copy-start = (bf16[8,4096,256]{2,1,0:T(8,128)(2,1)}, bf16[8,4096,256]{2,1,0:T(8,128)(2,1)S(1)}, u32[]{:S(2)}) copy-start(bf16[8,4096,256]{2,1,0:T(8,128)(2,1)S(1)} %spread.1.refs_1_.refs_2_) | copy-start | bytes 50331652
  43.6 18.9 %copy-start.8 = (bf16[1024,256]{1,0:T(8,128)(2,1)}, bf16[1024,256]{1,0:T(8,128)(2,1)S(1)}, u32[]{:S(2)}) copy-start(bf16[1024,256]{1,0:T(8,128)(2,1)S(1)} %gate.7.refs_1_.refs_14_) | copy-start | bytes 1572868
  43.6 3.4 %collective-permute-start.6 = (bf16[2048,256]{1,0:T(8,128)(2,1)S(1)}, bf16[2048,256]{1,0:T(8,128)(2,1)S(1)}, u32[]{:S(2)}, u32[]{:S(2)}) collective-permute-start(bf16[2048,256]{1,0:T(8,128)(2,1)S(1)} %gate.6.refs_1_.refs_10_), channel_id=1, source_target_pairs={{0,1},{1,0},{2,3},{3,2},{4,5},{5,4},{6,7},{7,6},{8,9},{9,8},{10,11... | collective-permute-start | bytes 3145736 | tf_op jit(solution)/shard_map/ppermute | solution.py:115
  43.7 4.1 %collective-permute-start.7 = (bf16[2048,256]{1,0:T(8,128)(2,1)S(1)}, bf16[2048,256]{1,0:T(8,128)(2,1)S(1)}, u32[]{:S(2)}, u32[]{:S(2)}) collective-permute-start(bf16[2048,256]{1,0:T(8,128)(2,1)S(1)} %gate.8.refs_3_.refs_12_), channel_id=1, source_target_pairs={{0,1},{1,0},{2,3},{3,2},{4,5},{5,4},{6,7},{7,6},{8,9},{9,8},{10,11... | collective-permute-start | bytes 3145736 | tf_op jit(solution)/shard_map/ppermute | solution.py:115
  44.2 13.9 %collective-permute-start.5 = (bf16[1024,256]{1,0:T(8,128)(2,1)S(1)}, bf16[1024,256]{1,0:T(8,128)(2,1)S(1)}, u32[]{:S(2)}, u32[]{:S(2)}) collective-permute-start(bf16[1024,256]{1,0:T(8,128)(2,1)S(1)} %gate.7.refs_1_.refs_14_), channel_id=1, source_target_pairs={{0,2},{1,3},{2,0},{3,1},{4,6},{5,7},{6,4},{7,5},{8,10},{9,11},{10,... | collective-permute-start | bytes 1572872 | tf_op jit(solution)/shard_map/ppermute | solution.py:115
  46.9 15.5 %collective-permute-start.4 = (bf16[1024,256]{1,0:T(8,128)(2,1)S(1)}, bf16[1024,256]{1,0:T(8,128)(2,1)S(1)}, u32[]{:S(2)}, u32[]{:S(2)}) collective-permute-start(bf16[1024,256]{1,0:T(8,128)(2,1)S(1)} %gate.7.refs_1_.refs_14_), channel_id=1, source_target_pairs={{0,1},{1,0},{2,3},{3,2},{4,5},{5,4},{6,7},{7,6},{8,9},{9,8},{10,11... | collective-permute-start | bytes 1572872 | tf_op jit(solution)/shard_map/ppermute | solution.py:115
  58.1 4.4 %collective-permute-start.8 = (bf16[1024,256]{1,0:T(8,128)(2,1)S(1)}, bf16[1024,256]{1,0:T(8,128)(2,1)S(1)}, u32[]{:S(2)}, u32[]{:S(2)}) collective-permute-start(bf16[1024,256]{1,0:T(8,128)(2,1)S(1)} %gate.9.refs_3_.refs_16_), channel_id=1, source_target_pairs={{0,1},{1,0},{2,3},{3,2},{4,5},{5,4},{6,7},{7,6},{8,9},{9,8},{10,11... | collective-permute-start | bytes 1572872 | tf_op jit(solution)/shard_map/ppermute | solution.py:115
  58.1 17.7 %copy-start.19 = (bf16[1024,256]{1,0:T(8,128)(2,1)}, bf16[1024,256]{1,0:T(8,128)(2,1)S(1)}, u32[]{:S(2)}) copy-start(bf16[1024,256]{1,0:T(8,128)(2,1)S(1)} %gate.10.refs_5_) | copy-start | bytes 1572868
  58.1 17.9 %collective-permute-start.9 = (bf16[1024,256]{1,0:T(8,128)(2,1)S(1)}, bf16[1024,256]{1,0:T(8,128)(2,1)}, u32[]{:S(2)}, u32[]{:S(2)}) collective-permute-start(bf16[1024,256]{1,0:T(8,128)(2,1)S(1)} %gate.10.refs_5_), channel_id=1, source_target_pairs={{0,2},{1,3},{2,0},{3,1},{4,6},{5,7},{6,4},{7,5},{8,10},{9,11},{10,... | collective-permute-start | bytes 1572872 | tf_op jit(solution)/shard_map/ppermute | solution.py:115
  68.6 32.2 %all-to-all-start.1 = ((bf16[32,64,256]{2,1,0:T(8,128)(2,1)}), bf16[32,64,256]{2,1,0:T(8,128)(2,1)S(1)}, u32[]{:S(2)}, u32[]{:S(2)}) async-start(bf16[32,64,256]{2,1,0:T(8,128)(2,1)} %bitcast.6), calls=%async_computation.1 | async-start | bytes 2097152 | tf_op jit(solution)/shard_map/all_to_all | solution.py:124
  75.8 17.5 %collective-permute-start.13 = (bf16[1024,256]{1,0:T(8,128)(2,1)S(1)}, bf16[1024,256]{1,0:T(8,128)(2,1)S(1)}, u32[]{:S(2)}, u32[]{:S(2)}) collective-permute-start(bf16[1024,256]{1,0:T(8,128)(2,1)S(1)} %gate.10.refs_5_), channel_id=1, source_target_pairs={{0,1},{1,0},{2,3},{3,2},{4,5},{5,4},{6,7},{7,6},{8,9},{9,8},{10,11... | collective-permute-start | bytes 1572872 | tf_op jit(solution)/shard_map/ppermute | solution.py:115
  76.0 17.3 %collective-permute-start.14 = (bf16[1024,256]{1,0:T(8,128)(2,1)}, bf16[1024,256]{1,0:T(8,128)(2,1)S(1)}, u32[]{:S(2)}, u32[]{:S(2)}) collective-permute-start(bf16[1024,256]{1,0:T(8,128)(2,1)} %collective-permute-done.9.refs_9_.refs_7_), channel_id=1, source_target_pairs={{0,1},{1,0},{2,3},{3,2},{4,5},{5,4},{6,7},{7,6},{8,9},{9,8},{10,11... | collective-permute-start | bytes 1572872 | tf_op jit(solution)/shard_map/ppermute | solution.py:115
  78.9 14.5 %collective-permute-start.10 = (f32[64,512]{1,0:T(8,128)}, f32[64,512]{1,0:T(8,128)S(1)}, u32[]{:S(2)}, u32[]{:S(2)}) collective-permute-start(f32[64,512]{1,0:T(8,128)} %get-tuple-element.51), channel_id=1, source_target_pairs={{0,1},{1,0},{2,3},{3,2},{4,5},{5,4},{6,7},{7,6},{8,9},{9,8},{10,11... | collective-permute-start | bytes 393224 | tf_op jit(solution)/shard_map/ppermute | solution.py:115
  79.0 14.3 %collective-permute-start.11 = (f32[64,512]{1,0:T(8,128)}, f32[64,512]{1,0:T(8,128)S(1)}, u32[]{:S(2)}, u32[]{:S(2)}) collective-permute-start(f32[64,512]{1,0:T(8,128)} %get-tuple-element.52), channel_id=1, source_target_pairs={{0,2},{1,3},{2,0},{3,1},{4,6},{5,7},{6,4},{7,5},{8,10},{9,11},{10,... | collective-permute-start | bytes 393224 | tf_op jit(solution)/shard_map/ppermute | solution.py:115
  80.5 12.9 %collective-permute-start.12 = (f32[64,512]{1,0:T(8,128)}, f32[64,512]{1,0:T(8,128)S(1)}, u32[]{:S(2)}, u32[]{:S(2)}) collective-permute-start(f32[64,512]{1,0:T(8,128)} %get-tuple-element.53), channel_id=1, source_target_pairs={{0,3},{1,2},{2,1},{3,0},{4,7},{5,6},{6,5},{7,4},{8,11},{9,10},{10,... | collective-permute-start | bytes 393224 | tf_op jit(solution)/shard_map/ppermute | solution.py:115
  104.9 16.9 %copy-start.46 = (bf16[80,512]{1,0:T(8,128)(2,1)S(1)}, bf16[80,512]{1,0:T(8,128)(2,1)}, u32[]{:S(2)}) copy-start(bf16[80,512]{1,0:T(8,128)(2,1)} %get-tuple-element.55) | copy-start | bytes 245764
  104.9 17.4 %copy-start.45 = (bf16[80,512]{1,0:T(8,128)(2,1)S(1)}, bf16[80,512]{1,0:T(8,128)(2,1)}, u32[]{:S(2)}) copy-start(bf16[80,512]{1,0:T(8,128)(2,1)} %get-tuple-element.56) | copy-start | bytes 245764
  104.9 18.3 %copy-start.44 = (bf16[80,512]{1,0:T(8,128)(2,1)S(1)}, bf16[80,512]{1,0:T(8,128)(2,1)}, u32[]{:S(2)}) copy-start(bf16[80,512]{1,0:T(8,128)(2,1)} %get-tuple-element.57) | copy-start | bytes 245764
  104.9 30.2 %all-to-all-start.2 = ((bf16[32,64,256]{2,1,0:T(8,128)(2,1)}), bf16[32,64,256]{2,1,0:T(8,128)(2,1)S(1)}, u32[]{:S(2)}, u32[]{:S(2)}) async-start(bf16[32,64,256]{2,1,0:T(8,128)(2,1)} %bitcast.9), calls=%async_computation.2 | async-start | bytes 2097152 | tf_op jit(solution)/shard_map/all_to_all | solution.py:124
  109.8 11.9 %collective-permute-start.19 = (bf16[64,1024]{1,0:T(8,128)(2,1)S(1)}, bf16[64,1024]{1,0:T(8,128)(2,1)S(1)}, u32[]{:S(2)}, u32[]{:S(2)}) collective-permute-start(bf16[64,1024]{1,0:T(8,128)(2,1)S(1)} %copy-done.26), channel_id=1, source_target_pairs={{0,2},{1,3},{2,0},{3,1},{4,6},{5,7},{6,4},{7,5},{8,10},{9,11},{10,... | collective-permute-start | bytes 393224 | tf_op jit(solution)/shard_map/ppermute | solution.py:115
  111.3 18.0 %collective-permute-start.18 = (bf16[64,1024]{1,0:T(8,128)(2,1)S(1)}, bf16[64,1024]{1,0:T(8,128)(2,1)S(1)}, u32[]{:S(2)}, u32[]{:S(2)}) collective-permute-start(bf16[64,1024]{1,0:T(8,128)(2,1)S(1)} %copy-done.26), channel_id=1, source_target_pairs={{0,1},{1,0},{2,3},{3,2},{4,5},{5,4},{6,7},{7,6},{8,9},{9,8},{10,11... | collective-permute-start | bytes 393224 | tf_op jit(solution)/shard_map/ppermute | solution.py:115
  121.7 7.6 %collective-permute-start.20 = (bf16[64,1024]{1,0:T(8,128)(2,1)S(1)}, bf16[64,1024]{1,0:T(8,128)(2,1)S(1)}, u32[]{:S(2)}, u32[]{:S(2)}) collective-permute-start(bf16[64,1024]{1,0:T(8,128)(2,1)S(1)} %collective-permute-done.19.refs_11_), channel_id=1, source_target_pairs={{0,1},{1,0},{2,3},{3,2},{4,5},{5,4},{6,7},{7,6},{8,9},{9,8},{10,11... | collective-permute-start | bytes 393224 | tf_op jit(solution)/shard_map/ppermute | solution.py:115
  121.7 3.8 %collective-permute-start.15 = (bf16[80,512]{1,0:T(8,128)(2,1)S(1)}, bf16[80,512]{1,0:T(8,128)(2,1)S(1)}, u32[]{:S(2)}, u32[]{:S(2)}) collective-permute-start(bf16[80,512]{1,0:T(8,128)(2,1)S(1)} %copy-done.46), channel_id=1, source_target_pairs={{0,1},{1,0},{2,3},{3,2},{4,5},{5,4},{6,7},{7,6},{8,9},{9,8},{10,11... | collective-permute-start | bytes 245768 | tf_op jit(solution)/shard_map/ppermute | solution.py:115
  122.2 5.7 %collective-permute-start.16 = (bf16[80,512]{1,0:T(8,128)(2,1)S(1)}, bf16[80,512]{1,0:T(8,128)(2,1)S(1)}, u32[]{:S(2)}, u32[]{:S(2)}) collective-permute-start(bf16[80,512]{1,0:T(8,128)(2,1)S(1)} %copy-done.45), channel_id=1, source_target_pairs={{0,2},{1,3},{2,0},{3,1},{4,6},{5,7},{6,4},{7,5},{8,10},{9,11},{10,... | collective-permute-start | bytes 245768 | tf_op jit(solution)/shard_map/ppermute | solution.py:115
  123.2 6.1 %collective-permute-start.17 = (bf16[80,512]{1,0:T(8,128)(2,1)S(1)}, bf16[80,512]{1,0:T(8,128)(2,1)S(1)}, u32[]{:S(2)}, u32[]{:S(2)}) collective-permute-start(bf16[80,512]{1,0:T(8,128)(2,1)S(1)} %copy-done.44), channel_id=1, source_target_pairs={{0,3},{1,2},{2,1},{3,0},{4,7},{5,6},{6,5},{7,4},{8,11},{9,10},{10,... | collective-permute-start | bytes 245768 | tf_op jit(solution)/shard_map/ppermute | solution.py:115
  125.6 9.5 %collective-permute-start.21 = (bf16[256,256]{1,0:T(8,128)(2,1)}, bf16[256,256]{1,0:T(8,128)(2,1)S(1)}, u32[]{:S(2)}, u32[]{:S(2)}) collective-permute-start(bf16[256,256]{1,0:T(8,128)(2,1)} %get-tuple-element.62), channel_id=1, source_target_pairs={{0,2},{1,3},{2,0},{3,1},{4,6},{5,7},{6,4},{7,5},{8,10},{9,11},{10,... | collective-permute-start | bytes 393224 | tf_op jit(solution)/shard_map/ppermute | solution.py:115
  132.4 17.9 %collective-permute-start.28 = (bf16[256,256]{1,0:T(8,128)(2,1)}, bf16[256,256]{1,0:T(8,128)(2,1)S(1)}, u32[]{:S(2)}, u32[]{:S(2)}) collective-permute-start(bf16[256,256]{1,0:T(8,128)(2,1)} %get-tuple-element.69), channel_id=1, source_target_pairs={{0,2},{1,3},{2,0},{3,1},{4,6},{5,7},{6,4},{7,5},{8,10},{9,11},{10,... | collective-permute-start | bytes 393224 | tf_op jit(solution)/shard_map/ppermute | solution.py:115
  133.0 17.3 %collective-permute-start.29 = (bf16[256,256]{1,0:T(8,128)(2,1)}, bf16[256,256]{1,0:T(8,128)(2,1)S(1)}, u32[]{:S(2)}, u32[]{:S(2)}) collective-permute-start(bf16[256,256]{1,0:T(8,128)(2,1)} %get-tuple-element.70), channel_id=1, source_target_pairs={{0,3},{1,2},{2,1},{3,0},{4,7},{5,6},{6,5},{7,4},{8,11},{9,10},{10,... | collective-permute-start | bytes 393224 | tf_op jit(solution)/shard_map/ppermute | solution.py:115
  134.6 15.7 %collective-permute-start.30 = (bf16[4,256,256]{2,1,0:T(8,128)(2,1)}, bf16[4,256,256]{2,1,0:T(8,128)(2,1)S(1)}, u32[]{:S(2)}, u32[]{:S(2)}) collective-permute-start(bf16[4,256,256]{2,1,0:T(8,128)(2,1)} %get-tuple-element.73), channel_id=1, source_target_pairs={{0,4},{4,0},{8,12},{12,8},{16,20},{20,16},{24,28},{28,24},{1,5},{5... | collective-permute-start | bytes 1572872 | tf_op jit(solution)/shard_map/ppermute | solution.py:115
  135.1 15.2 %copy-start.22 = (bf16[256,256]{1,0:T(8,128)(2,1)}, bf16[256,256]{1,0:T(8,128)(2,1)S(1)}, u32[]{:S(2)}) copy-start(bf16[256,256]{1,0:T(8,128)(2,1)S(1)} %collective-permute-done.21.refs_19_.refs_7_) | copy-start | bytes 393220
  153.2 12.0 %copy-start.33 = (bf16[256,256]{1,0:T(8,128)(2,1)S(1)}, bf16[256,256]{1,0:T(8,128)(2,1)}, u32[]{:S(2)}) copy-start(bf16[256,256]{1,0:T(8,128)(2,1)} %get-tuple-element.65) | copy-start | bytes 393220
  153.2 23.2 %copy-start.32 = (bf16[256,256]{1,0:T(8,128)(2,1)S(1)}, bf16[256,256]{1,0:T(8,128)(2,1)}, u32[]{:S(2)}) copy-start(bf16[256,256]{1,0:T(8,128)(2,1)} %get-tuple-element.66) | copy-start | bytes 393220
  153.2 29.3 %copy-start.34 = (bf16[256,256]{1,0:T(8,128)(2,1)S(1)}, bf16[256,256]{1,0:T(8,128)(2,1)}, u32[]{:S(2)}) copy-start(bf16[256,256]{1,0:T(8,128)(2,1)} %get-tuple-element.68) | copy-start | bytes 393220
  153.2 33.9 %copy-start.21 = (bf16[256,256]{1,0:T(8,128)(2,1)S(1)}, bf16[256,256]{1,0:T(8,128)(2,1)}, u32[]{:S(2)}) copy-start(bf16[256,256]{1,0:T(8,128)(2,1)} %get-tuple-element.74.refs_1_.refs_0_) | copy-start | bytes 393220
  153.2 38.9 %copy-start.11 = (bf16[3072,256]{1,0:T(8,128)(2,1)}, bf16[3072,256]{1,0:T(8,128)(2,1)S(1)}, u32[]{:S(2)}) copy-start(bf16[3072,256]{1,0:T(8,128)(2,1)S(1)} %gate.11.refs_1_) | copy-start | bytes 4718596
  153.3 45.5 %collective-permute-start.32 = (bf16[3072,256]{1,0:T(8,128)(2,1)S(1)}, bf16[3072,256]{1,0:T(8,128)(2,1)}, u32[]{:S(2)}, u32[]{:S(2)}) collective-permute-start(bf16[3072,256]{1,0:T(8,128)(2,1)S(1)} %gate.11.refs_1_), channel_id=1, source_target_pairs={{0,2},{1,3},{2,0},{3,1},{4,6},{5,7},{6,4},{7,5},{8,10},{9,11},{10,... | collective-permute-start | bytes 4718600 | tf_op jit(solution)/shard_map/ppermute | solution.py:115
  154.6 44.2 %all-to-all-start.3 = ((bf16[8,144,256]{2,1,0:T(8,128)(2,1)}), bf16[8,144,256]{2,1,0:T(8,128)(2,1)S(1)}, u32[]{:S(2)}, u32[]{:S(2)}) async-start(bf16[8,144,256]{2,1,0:T(8,128)(2,1)} %get-tuple-element.78), calls=%async_computation.3 | async-start | bytes 1179648 | tf_op jit(solution)/shard_map/all_to_all | solution.py:124
  161.7 14.7 %collective-permute-start.34 = (bf16[256,256]{1,0:T(8,128)(2,1)S(1)}, bf16[256,256]{1,0:T(8,128)(2,1)S(1)}, u32[]{:S(2)}, u32[]{:S(2)}) collective-permute-start(bf16[256,256]{1,0:T(8,128)(2,1)S(1)} %copy-done.43), channel_id=1, source_target_pairs={{0,8},{4,12},{8,0},{12,4},{16,24},{20,28},{24,16},{28,20},{1,9},{5... | collective-permute-start | bytes 393224 | tf_op jit(solution)/shard_map/ppermute | solution.py:115
  162.2 20.3 %collective-permute-start.35 = (bf16[256,256]{1,0:T(8,128)(2,1)S(1)}, bf16[256,256]{1,0:T(8,128)(2,1)S(1)}, u32[]{:S(2)}, u32[]{:S(2)}) collective-permute-start(bf16[256,256]{1,0:T(8,128)(2,1)S(1)} %copy-done.42), channel_id=1, source_target_pairs={{0,16},{4,20},{8,24},{12,28},{16,0},{20,4},{24,8},{28,12},{1,17},{... | collective-permute-start | bytes 393224 | tf_op jit(solution)/shard_map/ppermute | solution.py:115
  164.6 22.5 %collective-permute-start.36 = (bf16[256,256]{1,0:T(8,128)(2,1)S(1)}, bf16[256,256]{1,0:T(8,128)(2,1)S(1)}, u32[]{:S(2)}, u32[]{:S(2)}) collective-permute-start(bf16[256,256]{1,0:T(8,128)(2,1)S(1)} %copy-done.39), channel_id=1, source_target_pairs={{0,24},{4,28},{8,16},{12,20},{16,8},{20,12},{24,0},{28,4},{1,25},{... | collective-permute-start | bytes 393224 | tf_op jit(solution)/shard_map/ppermute | solution.py:115
  165.2 23.3 %collective-permute-start.25 = (bf16[256,256]{1,0:T(8,128)(2,1)S(1)}, bf16[256,256]{1,0:T(8,128)(2,1)S(1)}, u32[]{:S(2)}, u32[]{:S(2)}) collective-permute-start(bf16[256,256]{1,0:T(8,128)(2,1)S(1)} %copy-done.33), channel_id=1, source_target_pairs={{0,1},{1,0},{2,3},{3,2},{4,5},{5,4},{6,7},{7,6},{8,9},{9,8},{10,11... | collective-permute-start | bytes 393224 | tf_op jit(solution)/shard_map/ppermute | solution.py:115
  176.4 15.8 %collective-permute-start.26 = (bf16[256,256]{1,0:T(8,128)(2,1)S(1)}, bf16[256,256]{1,0:T(8,128)(2,1)S(1)}, u32[]{:S(2)}, u32[]{:S(2)}) collective-permute-start(bf16[256,256]{1,0:T(8,128)(2,1)S(1)} %copy-done.32), channel_id=1, source_target_pairs={{0,3},{1,2},{2,1},{3,0},{4,7},{5,6},{6,5},{7,4},{8,11},{9,10},{10,... | collective-permute-start | bytes 393224 | tf_op jit(solution)/shard_map/ppermute | solution.py:115
  182.5 11.0 %collective-permute-start.27 = (bf16[256,256]{1,0:T(8,128)(2,1)S(1)}, bf16[256,256]{1,0:T(8,128)(2,1)S(1)}, u32[]{:S(2)}, u32[]{:S(2)}) collective-permute-start(bf16[256,256]{1,0:T(8,128)(2,1)S(1)} %copy-done.34), channel_id=1, source_target_pairs={{0,1},{1,0},{2,3},{3,2},{4,5},{5,4},{6,7},{7,6},{8,9},{9,8},{10,11... | collective-permute-start | bytes 393224 | tf_op jit(solution)/shard_map/ppermute | solution.py:115
  187.9 17.4 %copy-start.25 = (bf16[256,256]{1,0:T(8,128)(2,1)S(1)}, bf16[256,256]{1,0:T(8,128)(2,1)}, u32[]{:S(2)}) copy-start(bf16[256,256]{1,0:T(8,128)(2,1)} %add_some.1.refs_1_) | copy-start | bytes 393220
  187.9 9.6 %collective-permute-start.39 = (bf16[256,256]{1,0:T(8,128)(2,1)}, bf16[256,256]{1,0:T(8,128)(2,1)S(1)}, u32[]{:S(2)}, u32[]{:S(2)}) collective-permute-start(bf16[256,256]{1,0:T(8,128)(2,1)} %add_some.1.refs_1_), channel_id=1, source_target_pairs={{0,24},{4,28},{8,16},{12,20},{16,8},{20,12},{24,0},{28,4},{1,25},{... | collective-permute-start | bytes 393224 | tf_op jit(solution)/shard_map/ppermute | solution.py:115
  188.4 17.7 %collective-permute-start.23 = (bf16[1024,256]{1,0:T(8,128)(2,1)}, bf16[1024,256]{1,0:T(8,128)(2,1)}, u32[]{:S(2)}, u32[]{:S(2)}) collective-permute-start(bf16[1024,256]{1,0:T(8,128)(2,1)} %get-tuple-element.63.refs_2_.refs_1_), channel_id=1, source_target_pairs={{0,2},{1,3},{2,0},{3,1},{4,6},{5,7},{6,4},{7,5},{8,10},{9,11},{10,... | collective-permute-start | bytes 1572872 | tf_op jit(solution)/shard_map/ppermute | solution.py:115
  192.2 15.1 %collective-permute-start.31 = (bf16[3072,256]{1,0:T(8,128)(2,1)S(1)}, bf16[3072,256]{1,0:T(8,128)(2,1)}, u32[]{:S(2)}, u32[]{:S(2)}) collective-permute-start(bf16[3072,256]{1,0:T(8,128)(2,1)S(1)} %gate.11.refs_1_), channel_id=1, source_target_pairs={{0,1},{1,0},{2,3},{3,2},{4,5},{5,4},{6,7},{7,6},{8,9},{9,8},{10,11... | collective-permute-start | bytes 4718600 | tf_op jit(solution)/shard_map/ppermute | solution.py:115
  193.5 11.2 %collective-permute-start.38 = (bf16[256,256]{1,0:T(8,128)(2,1)}, bf16[256,256]{1,0:T(8,128)(2,1)S(1)}, u32[]{:S(2)}, u32[]{:S(2)}) collective-permute-start(bf16[256,256]{1,0:T(8,128)(2,1)} %add_some.1.refs_1_), channel_id=1, source_target_pairs={{0,16},{4,20},{8,24},{12,28},{16,0},{20,4},{24,8},{28,12},{1,17},{... | collective-permute-start | bytes 393224 | tf_op jit(solution)/shard_map/ppermute | solution.py:115
  197.4 7.9 %collective-permute-start.37 = (bf16[256,256]{1,0:T(8,128)(2,1)}, bf16[256,256]{1,0:T(8,128)(2,1)S(1)}, u32[]{:S(2)}, u32[]{:S(2)}) collective-permute-start(bf16[256,256]{1,0:T(8,128)(2,1)} %add_some.1.refs_1_), channel_id=1, source_target_pairs={{0,8},{4,12},{8,0},{12,4},{16,24},{20,28},{24,16},{28,20},{1,9},{5... | collective-permute-start | bytes 393224 | tf_op jit(solution)/shard_map/ppermute | solution.py:115
  198.7 9.4 %collective-permute-start.33 = (bf16[3072,256]{1,0:T(8,128)(2,1)}, bf16[3072,256]{1,0:T(8,128)(2,1)}, u32[]{:S(2)}, u32[]{:S(2)}) collective-permute-start(bf16[3072,256]{1,0:T(8,128)(2,1)} %collective-permute-done.32.refs_3_), channel_id=1, source_target_pairs={{0,1},{1,0},{2,3},{3,2},{4,5},{5,4},{6,7},{7,6},{8,9},{9,8},{10,11... | collective-permute-start | bytes 4718600 | tf_op jit(solution)/shard_map/ppermute | solution.py:115
  199.6 21.4 %all-to-all-start.4 = ((bf16[8,128,256]{2,1,0:T(8,128)(2,1)}), bf16[8,128,256]{2,1,0:T(8,128)(2,1)S(1)}, u32[]{:S(2)}, u32[]{:S(2)}) async-start(bf16[8,128,256]{2,1,0:T(8,128)(2,1)} %get-tuple-element.79), calls=%async_computation.4 | async-start | bytes 1048576 | tf_op jit(solution)/shard_map/all_to_all | solution.py:124
  204.8 10.7 %collective-permute-start.22 = (bf16[1024,256]{1,0:T(8,128)(2,1)}, bf16[1024,256]{1,0:T(8,128)(2,1)S(1)}, u32[]{:S(2)}, u32[]{:S(2)}) collective-permute-start(bf16[1024,256]{1,0:T(8,128)(2,1)} %get-tuple-element.63.refs_2_.refs_1_), channel_id=1, source_target_pairs={{0,1},{1,0},{2,3},{3,2},{4,5},{5,4},{6,7},{7,6},{8,9},{9,8},{10,11... | collective-permute-start | bytes 1572872 | tf_op jit(solution)/shard_map/ppermute | solution.py:115
  205.3 16.8 %collective-permute-start.40 = (bf16[256,256]{1,0:T(8,128)(2,1)S(1)}, bf16[256,256]{1,0:T(8,128)(2,1)S(1)}, u32[]{:S(2)}, u32[]{:S(2)}) collective-permute-start(bf16[256,256]{1,0:T(8,128)(2,1)S(1)} %copy-done.25), channel_id=1, source_target_pairs={{0,4},{4,0},{8,12},{12,8},{16,20},{20,16},{24,28},{28,24},{1,5},{5... | collective-permute-start | bytes 393224 | tf_op jit(solution)/shard_map/ppermute | solution.py:115
  206.1 16.0 %collective-permute-start.43 = (bf16[256,256]{1,0:T(8,128)(2,1)S(1)}, bf16[256,256]{1,0:T(8,128)(2,1)S(1)}, u32[]{:S(2)}, u32[]{:S(2)}) collective-permute-start(bf16[256,256]{1,0:T(8,128)(2,1)S(1)} %collective-permute-done.39.refs_15_.refs_7_), channel_id=1, source_target_pairs={{0,4},{4,0},{8,12},{12,8},{16,20},{20,16},{24,28},{28,24},{1,5},{5... | collective-permute-start | bytes 393224 | tf_op jit(solution)/shard_map/ppermute | solution.py:115
  207.3 14.8 %collective-permute-start.42 = (bf16[256,256]{1,0:T(8,128)(2,1)S(1)}, bf16[256,256]{1,0:T(8,128)(2,1)S(1)}, u32[]{:S(2)}, u32[]{:S(2)}) collective-permute-start(bf16[256,256]{1,0:T(8,128)(2,1)S(1)} %collective-permute-done.38.refs_14_.refs_5_), channel_id=1, source_target_pairs={{0,4},{4,0},{8,12},{12,8},{16,20},{20,16},{24,28},{28,24},{1,5},{5... | collective-permute-start | bytes 393224 | tf_op jit(solution)/shard_map/ppermute | solution.py:115
  208.1 8.6 %collective-permute-start.24 = (bf16[1024,256]{1,0:T(8,128)(2,1)}, bf16[1024,256]{1,0:T(8,128)(2,1)S(1)}, u32[]{:S(2)}, u32[]{:S(2)}) collective-permute-start(bf16[1024,256]{1,0:T(8,128)(2,1)} %collective-permute-done.23.refs_3_), channel_id=1, source_target_pairs={{0,1},{1,0},{2,3},{3,2},{4,5},{5,4},{6,7},{7,6},{8,9},{9,8},{10,11... | collective-permute-start | bytes 1572872 | tf_op jit(solution)/shard_map/ppermute | solution.py:115
  215.5 7.9 %collective-permute-start.41 = (bf16[256,256]{1,0:T(8,128)(2,1)S(1)}, bf16[256,256]{1,0:T(8,128)(2,1)S(1)}, u32[]{:S(2)}, u32[]{:S(2)}) collective-permute-start(bf16[256,256]{1,0:T(8,128)(2,1)S(1)} %collective-permute-done.37.refs_13_.refs_3_), channel_id=1, source_target_pairs={{0,4},{4,0},{8,12},{12,8},{16,20},{20,16},{24,28},{28,24},{1,5},{5... | collective-permute-start | bytes 393224 | tf_op jit(solution)/shard_map/ppermute | solution.py:115
  (32 other events, 166.0 us)

commit v5 on v4

--- a/solution.py
+++ b/solution.py
@@ -22,7 +22,7 @@
     lambda: 0.001,
     hidden_slope=5,
     self_half=3,
-    combine=4,
+    combine=1,
     w_back=4,
     rows_back=16,
     add=20,
@@ -132,6 +132,13 @@
     return pl.BlockSpec((block, columns), lambda i: (i, 0))
 
 
+def each_chunk(step, counts, run):
+    first = 0
+    for k, count in enumerate(counts):
+        pl.when((step >= first) & (step < first + count))(functools.partial(run, k))
+        first += count
+
+
 def chunk_spec(block, columns, first, count):
     return pl.BlockSpec((block, columns), lambda i: (jnp.clip(i - first, 0, count - 1), 0))
 
@@ -277,16 +284,16 @@
     lax.fori_loop(1, (depth + 7) // 8, more, 0)
 
 
-def spread(slots, row_dev, near=()):
-    groups, _, slots_node, node_dev = slots.shape
+def spread(slots, first, count, row_dev, near=()):
+    _, _, slots_node, node_dev = slots.shape
     tiles = node_dev // lane_tile
     buckets = row_dev // bucket_rows
     return call(
         spread_kernel,
         "spread",
-        [(slots, pl.BlockSpec((1, 3, slots_node, node_dev), lambda i: (i, 0, 0, 0)))],
-        [(pl.BlockSpec((1, row_dev, node_dev), lambda i: (i, 0, 0)), shape((groups, row_dev, node_dev), bf16))],
-        grid=(groups,),
+        [(slots, pl.BlockSpec((1, 3, slots_node, node_dev), lambda i: (first + i, 0, 0, 0)))],
+        [(pl.BlockSpec((1, row_dev, node_dev), lambda i: (i, 0, 0)), shape((count, row_dev, node_dev), bf16))],
+        grid=(count,),
         scratch=[
             pltpu.VMEM((tiles, 3, slots_node, lane_tile), f32),
             pltpu.VMEM((tiles, buckets, 8, lane_tile), f32),
@@ -331,41 +338,53 @@
     )[0]
 
 
-def pool_kernel(last, views, hidden_ref, *refs):
-    matrix, refs = refs[:views], refs[views:]
-    rows = matrix[0].shape[1]
-    for g in range(matrix[0].shape[0]):
-        total = dot(hidden_ref[:, 0:rows], matrix[0][g], (1, 0))
-        for v in range(1, views):
-            total = total + dot(hidden_ref[:, v * rows : (v + 1) * rows], matrix[v][g], (1, 0))
-        nodes = total.shape[1]
-        at = slice(g * nodes, (g + 1) * nodes)
-        if len(refs) > 1:
-            total = total + refs[0][:, at]
-        if last:
-            refs[-1][at, :] = total.T.astype(bf16)
-        else:
-            refs[-1][:, at] = total
+def pool_kernel(last, parts, counts, *refs):
+    hidden_refs, refs = refs[: len(counts)], refs[len(counts) :]
+    views = sum(counts)
+    matrix, refs = refs[: parts * views], refs[parts * views :]
+    groups, rows, nodes = matrix[0].shape
+    steps = pl.num_programs(0) // parts
+
+    def one_part(p):
+        for g in range(groups):
+            total, v = None, p * views
+            for hidden_ref, count in zip(hidden_refs, counts):
+                for k in range(count):
+                    term = dot(hidden_ref[:, k * rows : (k + 1) * rows], matrix[v][g], (1, 0))
+                    total, v = term if total is None else total + term, v + 1
+            at = slice(g * nodes, (g + 1) * nodes)
+            if len(refs) > 1:
+                total = total + refs[0][:, at]
+            if last:
+                refs[-1][at, :] = total.T.astype(bf16)
+            else:
+                refs[-1][:, at] = total
+
+    each_chunk(pl.program_id(0), [steps] * parts, one_part)
 
 
 def pool(hidden_t, matrix, first, so_far, step_rows, last, near=()):
-    columns, rows = hidden_t.shape
-    groups, _, node_dev = matrix.shape
-    nodes = groups * node_dev
-    views = rows // step_rows
+    columns = hidden_t[0].shape[0]
+    per, _, node_dev = matrix[0].shape
+    parts, counts = len(matrix), [a.shape[1] // step_rows for a in hidden_t]
+    nodes = parts * per * node_dev
+    steps = per // 2
     total_block = pl.BlockSpec((columns, 2 * node_dev), lambda i: (0, i))
-    block = (2, step_rows, node_dev)
-    view = [pl.BlockSpec(block, functools.partial(lambda v, i: (i, v, 0), first // step_rows + v)) for v in range(views)]
-    return call(
-        functools.partial(pool_kernel, last, views),
+    operands = list(hidden_t)
+    for p in range(parts):
+        for v in range(sum(counts)):
+            index = functools.partial(lambda p, v, i: (jnp.clip(i - p * steps, 0, steps - 1), v, 0), p, first // step_rows + v)
+            operands.append((matrix[p], pl.BlockSpec((2, step_rows, node_dev), index)))
+    return call(
+        functools.partial(pool_kernel, last, parts, counts),
         "pool",
-        [hidden_t] + [(matrix, spec) for spec in view] + ([] if so_far is None else [(so_far, total_block)]),
+        operands + ([] if so_far is None else [(so_far, total_block)]),
         [
             (row_blocks(2 * node_dev, columns), shape((nodes, columns), bf16))
             if last
             else (total_block, shape((columns, nodes), f32))
         ],
-        grid=(groups // 2,),
+        grid=(parts * steps,),
         near=near,
     )[0]
 
@@ -593,21 +612,14 @@
     )[0]
 
 
-def each_chunk(step, counts, run):
-    first = 0
-    for k, count in enumerate(counts):
-        pl.when((step >= first) & (step < first + count))(functools.partial(run, k))
-        first += count
-
-
-def rows_back_kernel(chunk_counts, grad_counts, sides, place_ref, *refs):
+def rows_back_kernel(chunk_counts, grad_counts, sides, parts, place_ref, *refs):
     chunks = len(chunk_counts)
-    matrix_ref, pooled_ref, slopes = refs[0], refs[1], refs[2 : 2 + chunks]
-    table = refs[2 + chunks : 2 + chunks + chunks * sides]
-    extra_ref, rest = refs[2 + chunks + chunks * sides], refs[3 + chunks + chunks * sides :]
+    matrix, refs = refs[:parts], refs[parts:]
+    pooled_ref, slopes, table = refs[0], refs[1 : 1 + chunks], refs[1 + chunks : 1 + chunks + chunks * sides]
+    extra_ref, rest = refs[1 + chunks + chunks * sides], refs[2 + chunks + chunks * sides :]
     grad_refs, (q_ref, total_ref, bias_ref, low_ref) = rest[: len(grad_counts)], rest[len(grad_counts) :]
     step = pl.program_id(0)
-    matrix = jnp.concatenate([matrix_ref[g] for g in range(matrix_ref.shape[0])], axis=1)
+    matrix = jnp.concatenate([part[g] for part in matrix for g in range(part.shape[0])], axis=1)
     summed = dot(matrix, pooled_ref[...], (1, 0))
     width = table[0].shape[1]
 
@@ -649,15 +661,18 @@
 
 def rows_back(place, matrix, pooled, slopes, table, extra, grad_rows, near=()):
     sides = len(table[0])
-    groups, row_dev, node_dev = matrix.shape
+    per, row_dev, node_dev = matrix[0].shape
+    groups = per * len(matrix)
     columns, width = pooled.shape[1], table[0][0].shape[1]
     block = min(min(a.shape[0] for a in slopes), step_rows * 2048 // (groups * node_dev))
     by_side = [chunk_specs([part[j] for part in table], block) for j in range(sides)]
     grads = [shape((rows, columns), bf16) for rows in grad_rows]
     return call(
-        functools.partial(rows_back_kernel, [a.shape[0] // block for a in slopes], [r // block for r in grad_rows], sides),
+        functools.partial(rows_back_kernel, [a.shape[0] // block for a in slopes], [r // block for r in grad_rows], sides, len(matrix)),
         "rows_back",
-        [(place, smem), (far(matrix), pl.BlockSpec((groups, block, node_dev), lambda i: (0, i, 0))), pooled]
+        [(place, smem)]
+        + [(far(part), pl.BlockSpec((per, block, node_dev), lambda i: (0, i, 0))) for part in matrix]
+        + [pooled]
         + list(zip(map(far, slopes), chunk_specs(slopes, block)))
         + [(far(table[k][j]), by_side[j][k]) for k in range(len(table)) for j in range(sides)]
         + [far(extra)],
@@ -754,20 +769,20 @@
 
     part_a = [low_a, beside_a, across_a, swap(across_a, "mp", 1)]
     hidden_a = hidden(place, part_a, q_low, q_bias, "value")
-    matrix = spread(slots, row_dev, near=[hidden_a])
-    so_far = pool(hidden_a, matrix, 0, None, unit, False)
+    first = spread(slots, 0, groups // 2, row_dev, near=[hidden_a])
+    across_b = gate(across_b, [first])
     low_c = gate(low_c, [across_b])
     across_c, beside_c = swap(low_c, "mp", 2), swap(low_c, "mp", 1)
-    across_b = gate(across_b, [matrix])
+    matrix = [first, spread(slots, groups // 2, groups // 2, row_dev)]
     part_b = [low_b, beside_b, across_b, swap(across_b, "mp", 1)]
-    hidden_b = hidden(place, part_b, q_low, q_bias, "value", near=[so_far])
-    so_far = pool(hidden_b, matrix, unit, so_far, unit, False)
+    hidden_b = hidden(place, part_b, q_low, q_bias, "value", near=[matrix[1]])
+    so_far = pool([hidden_a, hidden_b], matrix, 0, None, unit, False)
     across_c = gate(across_c, [hidden_b])
     part_c = [low_c, beside_c, across_c, swap(across_c, "mp", 1)]
     parts = [part_a, part_b, part_c]
     hidden_c = hidden(place, part_c, q_low, q_bias, "value", near=[so_far])
-    w_pooled = all_sides(gate(w_pooled, [matrix]))
-    part_sums = pool(hidden_c, matrix, 3 * unit, so_far, unit, True)
+    w_pooled = all_sides(gate(w_pooled, [matrix[1]]))
+    part_sums = pool([hidden_c], matrix, 3 * unit, so_far, unit, True)
     pooled = exchange(part_sums.reshape(groups * sides, few, columns), ("dp", "mp"))
 
     early = self_half(place, part_a, w_self, w_bias, cotangent, near=[part_sums, w_pooled[2]])
@@ -782,12 +797,12 @@
     embedding, even, odd, extra, *grad_self = w_back(
         place, part_a, late, all_sides(pooled), w_self, node_dev, groups
     )
-    q_cut = cut_rows(place, q_low, sides, after=[late[0]])
+    q_cut = cut_rows(place, q_low, sides, after=[slope[0]])
     q_cut = [q_cut[0]] + [swap(q_cut[j], "mp", j) for j in range(1, sides)]
     grad_self = [grad_self[0]] + [swap(grad_self[j], "mp", j) for j in range(1, sides)]
 
     grad_a, grad_b, q_parts = rows_back(place, matrix, grad_pooled, slope, parts, extra, [unit, 3 * unit], near=[q_cut[2]])
-    pairs = add_pairs(even, swap(odd, "dp", 1), after=[grad_a], near=[grad_self[2], grad_self[3]])
+    pairs = add_pairs(even, swap(odd, "dp", 1), after=[grad_a], near=[grad_self[1], grad_self[2], grad_self[3]])
     count = groups // 2
     pairs = [pairs[0]] + [swap(pairs[s], "dp", 2 * s) for s in range(1, count)]
     grad_b = gate(grad_b, [pairs[0]])
@@ -802,7 +817,7 @@
     table_grad = table_back(place, grads, q_cut, grad_self, unit, row_dev, near=[pieces[2], pieces[4], pieces[6]])
     across_a = swap(grad_a, "mp", 2)
     grads = [grad_a, swap(grad_a, "mp", 1), across_a, swap(across_a, "mp", 1)]
-    table_grad = table_back(place, grads, q_cut, grad_self, 0, row_dev, table_grad)
+    table_grad = table_back(place, grads, q_cut, grad_self, 0, row_dev, table_grad, near=[pieces[1]])
     q_grad = widen(exchange(q_pieces, "dp").reshape(-1, columns), after=[table_grad])
     w_grad = collect(place, pieces, after=[table_grad])
     return (

time: 229 us -> 227 us (level)
  waiting for transfers between devices: 57.3 us -> 55 us
    ppermute x44, waiting for transfers between devices: 47 us -> 44.4 us  [swap(): return lax.ppermute(array, axis, [(i, i ^ bits) for i in range(size)])]
    unnamed x94 -> x96, local copies, waits for them, and re-layouts: 4.48 us -> 5.04 us
  transfers between devices with their start and end apart: 49 -> 49, of which waited for: 14 -> 14; matrix products, arithmetic and copies ran while one was open for 0% -> 0% of each run, Pallas kernels for 39% -> 40%
where the time goes in v5:
time: 227 us; the launch traced here: 223 us
  Pallas kernels  98.7 us (43%)
  starting transfers between devices  62.9 us (28%)
  waiting for transfers between devices  55 us (24%)
  local copies, waits for them, and re-layouts  5.04 us (2%)
    pallas_call x26, Pallas kernels, call(): pl.pallas_call(inner, grid=grid, in_specs=specs + [pl.BlockSpec(memory_sp...  98.7 us
    ppermute x44, waiting for transfers between devices, swap(): return lax.ppermute(array, axis, [(i, i ^ bits) for i in range(size)])  44.4 us
    ppermute x44, starting transfers between devices, swap(): return lax.ppermute(array, axis, [(i, i ^ bits) for i in range(size)])  33.5 us
    all_to_all x5, starting transfers between devices, exchange(): return lax.all_to_all(array, axes, split_axis=0, concat_axis=0, tiled=True)  29.4 us
    all_to_all x5, waiting for transfers between devices, exchange(): return lax.all_to_all(array, axes, split_axis=0, concat_axis=0, tiled=True)  10.5 us
    unnamed x96, local copies, waits for them, and re-layouts  5.04 us
  transfers between devices with their start and end apart: 49, of which 14 were waited for; matrix products, arithmetic and copies ran while one was open for 0% of the time, Pallas kernels for 40%

profile of v5, /device:TPU:12, one launch (start us, length us, event | category | flops | bytes accessed | tf_op | source)
XLA Modules:
  0.0 222.9 jit_solution(11446436090689896203)
XLA Ops:
  0.6 2.1 low.3.refs_2_.refs_1_.refs_7_
  2.7 1.5 collective-permute-start.1
  4.2 2.8 %low.4 = (bf16[2048,256]{1,0:T(8,128)(2,1)}, bf16[1024,256]{1,0:T(8,128)(2,1)}) custom-call(f32[4096,256]{1,0:T(8,128)} %refs_1_.2, f32[4096,256]{1,0:T(8,128)} %refs_1_.2, bf16[1024,256]{1,0:T(8,128)(2,1)} %low.3.refs_2_.refs_1_.refs_7_), custom_call_target="tpu_custom_call" | custom-call | flops 1150000 | bytes 3690 | tf_op jit(solution)/shard_map/low/pallas_call | solution.py:82
  7.1 2.5 %slots.1.refs_3_ = s16[8,3,50,256]{3,2,1,0:T(8,128)(2,1)} custom-call(s32[2]{0:T(128)S(1)} %pad_add_fusion.refs_0_, s32[50,256]{1,0:T(8,128)} %bitcast.18, s32[1,256]{1,0:T(1,128)} %bitcast.26, f32[50,256]{1,0:T(8,128)} %bitcast.19, bf16[2048,256]{1,0:T(8,128)(2,1)} %get-tuple-element.46.refs_0_.refs_4_), custom_call_target="tpu_custom_call" | custom-call | flops 1150000 | bytes 3690 | tf_op jit(solution)/shard_map/slots/pallas_call | solution.py:82
  9.6 6.4 %all-to-all-start = ((s16[8,3,50,256]{3,2,1,0:T(8,128)(2,1)}), s16[8,3,50,256]{3,2,1,0:T(8,128)(2,1)S(1)}, u32[]{:S(2)}, u32[]{:S(2)}) async-start(s16[8,3,50,256]{3,2,1,0:T(8,128)(2,1)} %slots.1.refs_3_), calls=%async_computation | async-start | bytes 1376256 | tf_op jit(solution)/shard_map/all_to_all | solution.py:124
  16.6 0.8 copy-done.7
  17.4 1.5 collective-permute-start.3
  19.4 3.8 %low.5 = (bf16[1024,256]{1,0:T(8,128)(2,1)}, bf16[1024,256]{1,0:T(8,128)(2,1)}, bf16[1024,256]{1,0:T(8,128)(2,1)}) custom-call(f32[1024,256]{1,0:T(8,128)} %refs_0_.5, f32[2048,256]{1,0:T(8,128)} %refs_2_.1, f32[2048,256]{1,0:T(8,128)} %refs_2_.1, s16[8,3,50,256]{3,2,1,0:T(8,128)(2,1)} %slots.1.refs_3_), custom_call_target="tpu_custom_call" | custom-call | flops 1150000 | bytes 3690 | tf_op jit(solution)/shard_map/low/pallas_call | solution.py:82
  23.3 2.3 %hidden_value.3.refs_1_.refs_0_ = bf16[256,1024]{1,0:T(8,128)(2,1)S(1)} custom-call(s32[2]{0:T(128)S(1)} %pad_add_fusion.refs_0_, bf16[1024,256]{1,0:T(8,128)(2,1)S(1)} %copy-done.6, bf16[1024,256]{1,0:T(8,128)(2,1)S(1)} %collective-permute-done.refs_2_.refs_8_, bf16[1024,256]{1,0:T(8,128)(2,1)S(1)} %copy-done.8, ...), custom_call_target="tpu_custom_call" | custom-call | flops 1150000 | bytes 3690 | tf_op jit(solution)/shard_map/hidden_value/pallas_call | solution.py:82
  25.6 0.8 copy-done.17
  26.4 0.8 copy-done.18
  27.2 3.2 %all-to-all-done.refs_0_ = s16[8,3,50,256]{3,2,1,0:T(8,128)(2,1)S(1)} async-done(((s16[8,3,50,256]{3,2,1,0:T(8,128)(2,1)}), s16[8,3,50,256]{3,2,1,0:T(8,128)(2,1)S(1)}, u32[]{:S(2)}, u32[]{:S(2)}) %all-to-all-start) | async-done | bytes 614432 | tf_op jit(solution)/shard_map/all_to_all | solution.py:124
  30.4 6.1 %spread.2.refs_1_.refs_2_.refs_3_.refs_4_ = bf16[4,4096,256]{2,1,0:T(8,128)(2,1)S(1)} custom-call(s16[8,3,50,256]{3,2,1,0:T(8,128)(2,1)S(1)} %all-to-all-done.refs_0_, bf16[256,1024]{1,0:T(8,128)(2,1)S(1)} %hidden_value.3.refs_1_.refs_0_), custom_call_target="tpu_custom_call" | custom-call | flops 1150000 | bytes 3690 | tf_op jit(solution)/shard_map/spread/pallas_call | solution.py:82
  36.5 5.0 %collective-permute-done.3.refs_0_ = bf16[2048,256]{1,0:T(8,128)(2,1)S(1)} collective-permute-done((bf16[2048,256]{1,0:T(8,128)(2,1)S(1)}, bf16[2048,256]{1,0:T(8,128)(2,1)S(1)}, u32[]{:S(2)}, u32[]{:S(2)}) %collective-permute-start.3) | collective-permute-done | bytes 1048608 | tf_op jit(solution)/shard_map/ppermute | solution.py:115
  41.5 1.6 collective-permute-start.5
  43.0 6.5 %spread.3.refs_7_.refs_5_.refs_6_.refs_2_.refs_1_ = bf16[4,4096,256]{2,1,0:T(8,128)(2,1)S(1)} custom-call(s16[8,3,50,256]{3,2,1,0:T(8,128)(2,1)S(1)} %all-to-all-done.refs_0_), custom_call_target="tpu_custom_call" | custom-call | flops 1150000 | bytes 3690 | tf_op jit(solution)/shard_map/spread/pallas_call | solution.py:82
  49.8 4.7 %hidden_value.4.refs_1_ = bf16[256,2048]{1,0:T(8,128)(2,1)S(1)} custom-call(s32[2]{0:T(128)S(1)} %pad_add_fusion.refs_0_, bf16[2048,256]{1,0:T(8,128)(2,1)S(1)} %gate.6.refs_1_.refs_11_, bf16[2048,256]{1,0:T(8,128)(2,1)} %collective-permute-done.6.refs_2_.refs_12_, bf16[2048,256]{1,0:T(8,128)(2,1)S(1)} %gate.7.refs_1_.refs_3_.refs_13_, ...), custom_call_target="tpu_custom_call" | custom-call | flops 1150000 | bytes 3690 | tf_op jit(solution)/shard_map/hidden_value/pallas_call | solution.py:82
  54.5 1.2 collective-permute-done.5.refs_0_
  55.8 1.6 collective-permute-start.9
  57.4 5.2 %pool.2.refs_7_.refs_3_ = f32[256,2048]{1,0:T(8,128)S(1)} custom-call(bf16[256,1024]{1,0:T(8,128)(2,1)S(1)} %hidden_value.3.refs_1_.refs_0_, bf16[256,2048]{1,0:T(8,128)(2,1)S(1)} %hidden_value.4.refs_1_, bf16[4,4096,256]{2,1,0:T(8,128)(2,1)S(1)} %spread.2.refs_1_.refs_2_.refs_3_.refs_4_, bf16[4,4096,256]{2,1,0:T(8,128)(2,1)S(1)} %spread.2.refs_1_.refs_2_.refs_3_.refs_4_, ...), custom_call_target="tpu_custom_call" | custom-call | flops 1150000 | bytes 3690 | tf_op jit(solution)/shard_map/pool/pallas_call | solution.py:82
  62.6 2.6 %hidden_value.5.refs_0_ = bf16[256,1024]{1,0:T(8,128)(2,1)S(1)} custom-call(s32[2]{0:T(128)S(1)} %pad_add_fusion.refs_0_, bf16[1024,256]{1,0:T(8,128)(2,1)S(1)} %gate.8.refs_1_.refs_15_, bf16[1024,256]{1,0:T(8,128)(2,1)S(1)} %collective-permute-done.4.refs_2_.refs_16_, bf16[1024,256]{1,0:T(8,128)(2,1)S(1)} %gate.9.refs_3_.refs_17_, ...), custom_call_target="tpu_custom_call" | custom-call | flops 1150000 | bytes 3690 | tf_op jit(solution)/shard_map/hidden_value/pallas_call | solution.py:82
  65.3 3.5 %pool.3.refs_8_ = bf16[2048,256]{1,0:T(8,128)(2,1)} custom-call(bf16[256,1024]{1,0:T(8,128)(2,1)S(1)} %hidden_value.5.refs_0_, bf16[4,4096,256]{2,1,0:T(8,128)(2,1)S(1)} %spread.2.refs_1_.refs_2_.refs_3_.refs_4_, bf16[4,4096,256]{2,1,0:T(8,128)(2,1)S(1)} %spread.3.refs_7_.refs_5_.refs_6_.refs_2_.refs_1_, f32[256,2048]{1,0:T(8,128)S(1)} %pool.2.refs_7_.refs_3_), custom_call_target="tpu_custom_call" | custom-call | flops 1150000 | bytes 3690 | tf_op jit(solution)/shard_map/pool/pallas_call | solution.py:82
  68.8 5.1 %all-to-all-start.1 = ((bf16[32,64,256]{2,1,0:T(8,128)(2,1)}), bf16[32,64,256]{2,1,0:T(8,128)(2,1)S(1)}, u32[]{:S(2)}, u32[]{:S(2)}) async-start(bf16[32,64,256]{2,1,0:T(8,128)(2,1)} %bitcast.6), calls=%async_computation.1 | async-start | bytes 2097152 | tf_op jit(solution)/shard_map/all_to_all | solution.py:124
  74.5 2.5 %self_half.1 = (f32[64,512]{1,0:T(8,128)}, f32[64,512]{1,0:T(8,128)}, f32[64,512]{1,0:T(8,128)}, f32[64,512]{1,0:T(8,128)}) custom-call(s32[2]{0:T(128)S(1)} %pad_add_fusion.refs_0_, bf16[1024,256]{1,0:T(8,128)(2,1)} %low.3.refs_2_.refs_1_.refs_7_, bf16[1024,256]{1,0:T(8,128)(2,1)} %copy-done.17, bf16[1024,256]{1,0:T(8,128)(2,1)} %copy-done.7, ...), custom_call_target="tpu_custom_call" | custom-call | flops 3449999872 | bytes 11070000 | tf_op jit(solution)/shard_map/self_half/pallas_call | solution.py:82
  77.1 1.5 collective-permute-start.11
  78.8 3.5 %hidden_slope.3.refs_9_.refs_2_.refs_4_ = bf16[1024,256]{1,0:T(8,128)(2,1)} custom-call(s32[2]{0:T(128)S(1)} %pad_add_fusion.refs_0_, bf16[1024,256]{1,0:T(8,128)(2,1)} %low.3.refs_2_.refs_1_.refs_7_, bf16[1024,256]{1,0:T(8,128)(2,1)} %copy-done.17, bf16[1024,256]{1,0:T(8,128)(2,1)} %copy-done.7, bf16[1024,256]{1,0:T(8,128)(2,1)} %copy-done.18, ...), custom_call_target="tpu_custom_call" | custom-call | flops 5750000128 | bytes 18450000 | tf_op jit(solution)/shard_map/hidden_slope/pallas_call | solution.py:82
  82.3 3.5 %hidden_slope.5.refs_11_.refs_6_ = bf16[1024,256]{1,0:T(8,128)(2,1)} custom-call(s32[2]{0:T(128)S(1)} %pad_add_fusion.refs_0_, bf16[1024,256]{1,0:T(8,128)(2,1)} %copy-done.10, bf16[1024,256]{1,0:T(8,128)(2,1)} %copy-done.19, bf16[1024,256]{1,0:T(8,128)(2,1)} %copy-done.11, bf16[1024,256]{1,0:T(8,128)(2,1)} %copy-done.20, ...), custom_call_target="tpu_custom_call" | custom-call | flops 5750000128 | bytes 18450000 | tf_op jit(solution)/shard_map/hidden_slope/pallas_call | solution.py:82
  85.8 5.6 %hidden_slope.4.refs_10_.refs_5_ = bf16[2048,256]{1,0:T(8,128)(2,1)} custom-call(s32[2]{0:T(128)S(1)} %pad_add_fusion.refs_0_, bf16[2048,256]{1,0:T(8,128)(2,1)} %copy-done.4, bf16[2048,256]{1,0:T(8,128)(2,1)} %collective-permute-done.6.refs_2_.refs_12_, bf16[2048,256]{1,0:T(8,128)(2,1)} %copy-done.2, bf16[2048,256]{1,0:T(8,128)(2,1)} %copy-done.16, ...), custom_call_target="tpu_custom_call" | custom-call | flops 5750000128 | bytes 18450000 | tf_op jit(solution)/shard_map/hidden_slope/pallas_call | solution.py:82
  91.5 7.4 %all-to-all-done.1 = bf16[32,64,256]{2,1,0:T(8,128)(2,1)S(1)} async-done(((bf16[32,64,256]{2,1,0:T(8,128)(2,1)}), bf16[32,64,256]{2,1,0:T(8,128)(2,1)S(1)}, u32[]{:S(2)}, u32[]{:S(2)}) %all-to-all-start.1) | async-done | bytes 1048608 | tf_op jit(solution)/shard_map/all_to_all | solution.py:124
  98.9 4.0 %combine.1 = (bf16[8,4,64,256]{3,2,1,0:T(8,128)(2,1)}, bf16[64,1024]{1,0:T(8,128)(2,1)}, bf16[80,512]{1,0:T(8,128)(2,1)}, bf16[80,512]{1,0:T(8,128)(2,1)}, bf16[...) custom-call(bf16[8,4,64,256]{3,2,1,0:T(8,128)(2,1)S(1)} %bitcast.15, f32[64,512]{1,0:T(8,128)} %get-tuple-element.50.refs_7_.refs_1_, ...), custom_call_target="tpu_custom_call" | custom-call | flops 1150000000 | bytes 3690000 | tf_op jit(solution)/shard_map/combine/pallas_call | solution.py:82
  103.0 4.9 %all-to-all-start.2 = ((bf16[32,64,256]{2,1,0:T(8,128)(2,1)}), bf16[32,64,256]{2,1,0:T(8,128)(2,1)S(1)}, u32[]{:S(2)}, u32[]{:S(2)}) async-start(bf16[32,64,256]{2,1,0:T(8,128)(2,1)} %bitcast.9), calls=%async_computation.2 | async-start | bytes 2097152 | tf_op jit(solution)/shard_map/all_to_all | solution.py:124
  107.9 1.5 collective-permute-start.19
  109.4 10.4 %collective-permute-done.19.refs_11_ = bf16[64,1024]{1,0:T(8,128)(2,1)S(1)} collective-permute-done((bf16[64,1024]{1,0:T(8,128)(2,1)S(1)}, bf16[64,1024]{1,0:T(8,128)(2,1)S(1)}, u32[]{:S(2)}, u32[]{:S(2)}) %collective-permute-start.19) | collective-permute-done | bytes 131104 | tf_op jit(solution)/shard_map/ppermute | solution.py:115
  120.3 0.9 collective-permute-start.16
  121.7 1.9 cut.1
  123.6 0.9 collective-permute-start.21
  124.5 1.5 collective-permute-done.16.refs_7_
  126.0 1.3 collective-permute-done.17.refs_8_
  127.4 3.1 %w_back.1 = (f32[256,256]{1,0:T(8,128)}, bf16[4,256,256]{2,1,0:T(8,128)(2,1)}, bf16[4,256,256]{2,1,0:T(8,128)(2,1)}, bf16[16,256]{1,0:T(8,128)(2,1)}, bf16[256,2...) custom-call(s32[2]{0:T(128)S(1)} %pad_add_fusion.refs_0_, ...), custom_call_target="tpu_custom_call" | custom-call | flops 4600000000 | bytes 14760000 | tf_op jit(solution)/shard_map/w_back/pallas_call | solution.py:82
  130.4 0.9 collective-permute-start.27
  132.0 0.8 collective-permute-start.29
  133.2 15.2 %rows_back.1 = (bf16[1024,256]{1,0:T(8,128)(2,1)}, bf16[3072,256]{1,0:T(8,128)(2,1)}, bf16[8,144,256]{2,1,0:T(8,128)(2,1)}) custom-call(s32[2]{0:T(128)S(1)} %pad_add_fusion.refs_0_, bf16[4,4096,256]{2,1,0:T(8,128)(2,1)} %copy-done.1, bf16[4,4096,256]{2,1,0:T(8,128)(2,1)} %copy-done, bf16[2048,256]{1,0:T(8,128)(2,1)S(1)} %bitcast.17, ...), custom_call_target="tpu_custom_call" | custom-call | flops 18400000000 | bytes 59040000 | tf_op jit(solution)/shard_map/rows_back/pallas_call | solution.py:82
  148.5 2.0 add_pairs.1
  150.5 0.9 copy-done.21
  151.5 1.4 collective-permute-start.32
  152.8 8.1 %all-to-all-start.3 = ((bf16[8,144,256]{2,1,0:T(8,128)(2,1)}), bf16[8,144,256]{2,1,0:T(8,128)(2,1)S(1)}, u32[]{:S(2)}, u32[]{:S(2)}) async-start(bf16[8,144,256]{2,1,0:T(8,128)(2,1)} %get-tuple-element.78), calls=%async_computation.3 | async-start | bytes 1179648 | tf_op jit(solution)/shard_map/all_to_all | solution.py:124
  161.5 2.4 %collective-permute-start.35 = (bf16[256,256]{1,0:T(8,128)(2,1)S(1)}, bf16[256,256]{1,0:T(8,128)(2,1)S(1)}, u32[]{:S(2)}, u32[]{:S(2)}) collective-permute-start(bf16[256,256]{1,0:T(8,128)(2,1)S(1)} %copy-done.43), channel_id=1, source_target_pairs={{0,16},{4,20},{8,24},{12,28},{16,0},{20,4},{24,8},{28,12},{1,17},{... | collective-permute-start | bytes 393224 | tf_op jit(solution)/shard_map/ppermute | solution.py:115
  164.4 11.2 %collective-permute-done.34.refs_1_ = bf16[256,256]{1,0:T(8,128)(2,1)S(1)} collective-permute-done((bf16[256,256]{1,0:T(8,128)(2,1)S(1)}, bf16[256,256]{1,0:T(8,128)(2,1)S(1)}, u32[]{:S(2)}, u32[]{:S(2)}) %collective-permute-start.34) | collective-permute-done | bytes 131104 | tf_op jit(solution)/shard_map/ppermute | solution.py:115
  175.7 6.3 %collective-permute-done.35.refs_2_ = bf16[256,256]{1,0:T(8,128)(2,1)S(1)} collective-permute-done((bf16[256,256]{1,0:T(8,128)(2,1)S(1)}, bf16[256,256]{1,0:T(8,128)(2,1)S(1)}, u32[]{:S(2)}, u32[]{:S(2)}) %collective-permute-start.35) | collective-permute-done | bytes 131104 | tf_op jit(solution)/shard_map/ppermute | solution.py:115
  182.0 4.6 %collective-permute-done.36.refs_3_ = bf16[256,256]{1,0:T(8,128)(2,1)S(1)} collective-permute-done((bf16[256,256]{1,0:T(8,128)(2,1)S(1)}, bf16[256,256]{1,0:T(8,128)(2,1)S(1)}, u32[]{:S(2)}, u32[]{:S(2)}) %collective-permute-start.36) | collective-permute-done | bytes 131104 | tf_op jit(solution)/shard_map/ppermute | solution.py:115
  187.9 1.6 collective-permute-start.23
  189.6 1.0 collective-permute-done.26.refs_8_
  190.6 5.0 %collective-permute-start.38 = (bf16[256,256]{1,0:T(8,128)(2,1)}, bf16[256,256]{1,0:T(8,128)(2,1)S(1)}, u32[]{:S(2)}, u32[]{:S(2)}) collective-permute-start(bf16[256,256]{1,0:T(8,128)(2,1)} %add_some.1.refs_1_), channel_id=1, source_target_pairs={{0,16},{4,20},{8,24},{12,28},{16,0},{20,4},{24,8},{28,12},{1,17},{... | collective-permute-start | bytes 393224 | tf_op jit(solution)/shard_map/ppermute | solution.py:115
  196.4 0.9 add.3
  197.3 5.0 %all-to-all-start.4 = ((bf16[8,128,256]{2,1,0:T(8,128)(2,1)}), bf16[8,128,256]{2,1,0:T(8,128)(2,1)S(1)}, u32[]{:S(2)}, u32[]{:S(2)}) async-start(bf16[8,128,256]{2,1,0:T(8,128)(2,1)} %get-tuple-element.79), calls=%async_computation.4 | async-start | bytes 1048576 | tf_op jit(solution)/shard_map/all_to_all | solution.py:124
  202.5 0.9 collective-permute-done.37.refs_13_.refs_3_
  204.1 1.3 collective-permute-start.43
  206.2 7.3 %table_back.2.refs_13_ = f32[4096,256]{1,0:T(8,128)} custom-call(s32[2]{0:T(128)S(1)} %pad_add_fusion.refs_0_, bf16[3072,256]{1,0:T(8,128)(2,1)} %copy-done.15, bf16[3072,256]{1,0:T(8,128)(2,1)} %collective-permute-done.31.refs_2_, bf16[3072,256]{1,0:T(8,128)(2,1)} %collective-permute-done.32.refs_3_, bf16[3072,256]{1,0:T(8,128)(2,1)} %collective-permute-done.33.refs_4_, ...), custom_call_target="tpu_custom_call" | custom-call | flops 23000000512 | bytes 73800000 | tf_op jit(solution)/shard_map/table_back/pallas_call | solution.py:82
  213.5 1.3 collective-permute-start.41
  214.9 0.8 copy-done.36
  215.6 0.8 copy-done.37
  216.4 3.5 %table_back.3.refs_1_.refs_9_ = f32[4096,256]{1,0:T(8,128)} custom-call(s32[2]{0:T(128)S(1)} %pad_add_fusion.refs_0_, bf16[1024,256]{1,0:T(8,128)(2,1)} %get-tuple-element.63.refs_2_.refs_1_, bf16[1024,256]{1,0:T(8,128)(2,1)} %copy-done.36, bf16[1024,256]{1,0:T(8,128)(2,1)} %collective-permute-done.23.refs_3_, ...), custom_call_target="tpu_custom_call", output_to_operand_aliasing={{}: (13, {})} | custom-call | flops 23000000512 | bytes 73800000 | tf_op jit(solution)/shard_map/table_back/pallas_call | solution.py:82
  219.9 1.0 widen.1
  220.9 2.0 collect.1
  (163 shorter events, 9.9 us)
Async XLA Ops:
  2.7 13.9 %collective-permute-start.1 = (bf16[1024,256]{1,0:T(8,128)(2,1)}, bf16[1024,256]{1,0:T(8,128)(2,1)S(1)}, u32[]{:S(2)}, u32[]{:S(2)}) collective-permute-start(bf16[1024,256]{1,0:T(8,128)(2,1)} %low.3.refs_2_.refs_1_.refs_7_), channel_id=1, source_target_pairs={{0,2},{1,3},{2,0},{3,1},{4,6},{5,7},{6,4},{7,5},{8,10},{9,11},{10,... | collective-permute-start | bytes 1572872 | tf_op jit(solution)/shard_map/ppermute | solution.py:115
  9.6 20.8 %all-to-all-start = ((s16[8,3,50,256]{3,2,1,0:T(8,128)(2,1)}), s16[8,3,50,256]{3,2,1,0:T(8,128)(2,1)S(1)}, u32[]{:S(2)}, u32[]{:S(2)}) async-start(s16[8,3,50,256]{3,2,1,0:T(8,128)(2,1)} %slots.1.refs_3_), calls=%async_computation | async-start | bytes 1376256 | tf_op jit(solution)/shard_map/all_to_all | solution.py:124
  17.4 32.4 %copy-start.4 = (bf16[2048,256]{1,0:T(8,128)(2,1)}, bf16[2048,256]{1,0:T(8,128)(2,1)S(1)}, u32[]{:S(2)}) copy-start(bf16[2048,256]{1,0:T(8,128)(2,1)S(1)} %gate.6.refs_1_.refs_11_) | copy-start | bytes 3145732
  17.4 24.0 %collective-permute-start.3 = (bf16[2048,256]{1,0:T(8,128)(2,1)S(1)}, bf16[2048,256]{1,0:T(8,128)(2,1)S(1)}, u32[]{:S(2)}, u32[]{:S(2)}) collective-permute-start(bf16[2048,256]{1,0:T(8,128)(2,1)S(1)} %gate.6.refs_1_.refs_11_), channel_id=1, source_target_pairs={{0,2},{1,3},{2,0},{3,1},{4,6},{5,7},{6,4},{7,5},{8,10},{9,11},{10,... | collective-permute-start | bytes 3145736 | tf_op jit(solution)/shard_map/ppermute | solution.py:115
  18.9 4.4 %collective-permute-start = (bf16[1024,256]{1,0:T(8,128)(2,1)S(1)}, bf16[1024,256]{1,0:T(8,128)(2,1)S(1)}, u32[]{:S(2)}, u32[]{:S(2)}) collective-permute-start(bf16[1024,256]{1,0:T(8,128)(2,1)S(1)} %copy-done.5), channel_id=1, source_target_pairs={{0,1},{1,0},{2,3},{3,2},{4,5},{5,4},{6,7},{7,6},{8,9},{9,8},{10,11... | collective-permute-start | bytes 1572872 | tf_op jit(solution)/shard_map/ppermute | solution.py:115
  18.9 4.4 %collective-permute-start.2 = (bf16[1024,256]{1,0:T(8,128)(2,1)}, bf16[1024,256]{1,0:T(8,128)(2,1)S(1)}, u32[]{:S(2)}, u32[]{:S(2)}) collective-permute-start(bf16[1024,256]{1,0:T(8,128)(2,1)} %copy-done.7), channel_id=1, source_target_pairs={{0,1},{1,0},{2,3},{3,2},{4,5},{5,4},{6,7},{7,6},{8,9},{9,8},{10,11... | collective-permute-start | bytes 1572872 | tf_op jit(solution)/shard_map/ppermute | solution.py:115
  23.2 26.5 %collective-permute-start.6 = (bf16[2048,256]{1,0:T(8,128)(2,1)S(1)}, bf16[2048,256]{1,0:T(8,128)(2,1)}, u32[]{:S(2)}, u32[]{:S(2)}) collective-permute-start(bf16[2048,256]{1,0:T(8,128)(2,1)S(1)} %gate.6.refs_1_.refs_11_), channel_id=1, source_target_pairs={{0,1},{1,0},{2,3},{3,2},{4,5},{5,4},{6,7},{7,6},{8,9},{9,8},{10,11... | collective-permute-start | bytes 3145736 | tf_op jit(solution)/shard_map/ppermute | solution.py:115
  36.4 28.8 %copy-start.1 = (bf16[4,4096,256]{2,1,0:T(8,128)(2,1)}, bf16[4,4096,256]{2,1,0:T(8,128)(2,1)S(1)}, u32[]{:S(2)}) copy-start(bf16[4,4096,256]{2,1,0:T(8,128)(2,1)S(1)} %spread.2.refs_1_.refs_2_.refs_3_.refs_4_) | copy-start | bytes 25165828
  41.4 8.3 %collective-permute-start.7 = (bf16[2048,256]{1,0:T(8,128)(2,1)S(1)}, bf16[2048,256]{1,0:T(8,128)(2,1)S(1)}, u32[]{:S(2)}, u32[]{:S(2)}) collective-permute-start(bf16[2048,256]{1,0:T(8,128)(2,1)S(1)} %gate.7.refs_1_.refs_3_.refs_13_), channel_id=1, source_target_pairs={{0,1},{1,0},{2,3},{3,2},{4,5},{5,4},{6,7},{7,6},{8,9},{9,8},{10,11... | collective-permute-start | bytes 3145736 | tf_op jit(solution)/shard_map/ppermute | solution.py:115
  41.5 21.1 %copy-start.10 = (bf16[1024,256]{1,0:T(8,128)(2,1)}, bf16[1024,256]{1,0:T(8,128)(2,1)S(1)}, u32[]{:S(2)}) copy-start(bf16[1024,256]{1,0:T(8,128)(2,1)S(1)} %gate.8.refs_1_.refs_15_) | copy-start | bytes 1572868
  41.5 14.3 %collective-permute-start.5 = (bf16[1024,256]{1,0:T(8,128)(2,1)S(1)}, bf16[1024,256]{1,0:T(8,128)(2,1)S(1)}, u32[]{:S(2)}, u32[]{:S(2)}) collective-permute-start(bf16[1024,256]{1,0:T(8,128)(2,1)S(1)} %gate.8.refs_1_.refs_15_), channel_id=1, source_target_pairs={{0,2},{1,3},{2,0},{3,1},{4,6},{5,7},{6,4},{7,5},{8,10},{9,11},{10,... | collective-permute-start | bytes 1572872 | tf_op jit(solution)/shard_map/ppermute | solution.py:115
  49.5 15.7 %copy-start = (bf16[4,4096,256]{2,1,0:T(8,128)(2,1)}, bf16[4,4096,256]{2,1,0:T(8,128)(2,1)S(1)}, u32[]{:S(2)}) copy-start(bf16[4,4096,256]{2,1,0:T(8,128)(2,1)S(1)} %spread.3.refs_7_.refs_5_.refs_6_.refs_2_.refs_1_) | copy-start | bytes 25165828
  49.5 13.0 %collective-permute-start.4 = (bf16[1024,256]{1,0:T(8,128)(2,1)S(1)}, bf16[1024,256]{1,0:T(8,128)(2,1)S(1)}, u32[]{:S(2)}, u32[]{:S(2)}) collective-permute-start(bf16[1024,256]{1,0:T(8,128)(2,1)S(1)} %gate.8.refs_1_.refs_15_), channel_id=1, source_target_pairs={{0,1},{1,0},{2,3},{3,2},{4,5},{5,4},{6,7},{7,6},{8,9},{9,8},{10,11... | collective-permute-start | bytes 1572872 | tf_op jit(solution)/shard_map/ppermute | solution.py:115
  55.8 6.8 %collective-permute-start.8 = (bf16[1024,256]{1,0:T(8,128)(2,1)S(1)}, bf16[1024,256]{1,0:T(8,128)(2,1)S(1)}, u32[]{:S(2)}, u32[]{:S(2)}) collective-permute-start(bf16[1024,256]{1,0:T(8,128)(2,1)S(1)} %gate.9.refs_3_.refs_17_), channel_id=1, source_target_pairs={{0,1},{1,0},{2,3},{3,2},{4,5},{5,4},{6,7},{7,6},{8,9},{9,8},{10,11... | collective-permute-start | bytes 1572872 | tf_op jit(solution)/shard_map/ppermute | solution.py:115
  55.8 18.1 %copy-start.13 = (bf16[1024,256]{1,0:T(8,128)(2,1)}, bf16[1024,256]{1,0:T(8,128)(2,1)S(1)}, u32[]{:S(2)}) copy-start(bf16[1024,256]{1,0:T(8,128)(2,1)S(1)} %gate.10.refs_5_) | copy-start | bytes 1572868
  55.8 18.3 %collective-permute-start.9 = (bf16[1024,256]{1,0:T(8,128)(2,1)S(1)}, bf16[1024,256]{1,0:T(8,128)(2,1)}, u32[]{:S(2)}, u32[]{:S(2)}) collective-permute-start(bf16[1024,256]{1,0:T(8,128)(2,1)S(1)} %gate.10.refs_5_), channel_id=1, source_target_pairs={{0,2},{1,3},{2,0},{3,1},{4,6},{5,7},{6,4},{7,5},{8,10},{9,11},{10,... | collective-permute-start | bytes 1572872 | tf_op jit(solution)/shard_map/ppermute | solution.py:115
  68.8 30.1 %all-to-all-start.1 = ((bf16[32,64,256]{2,1,0:T(8,128)(2,1)}), bf16[32,64,256]{2,1,0:T(8,128)(2,1)S(1)}, u32[]{:S(2)}, u32[]{:S(2)}) async-start(bf16[32,64,256]{2,1,0:T(8,128)(2,1)} %bitcast.6), calls=%async_computation.1 | async-start | bytes 2097152 | tf_op jit(solution)/shard_map/all_to_all | solution.py:124
  73.9 17.5 %collective-permute-start.13 = (bf16[1024,256]{1,0:T(8,128)(2,1)S(1)}, bf16[1024,256]{1,0:T(8,128)(2,1)S(1)}, u32[]{:S(2)}, u32[]{:S(2)}) collective-permute-start(bf16[1024,256]{1,0:T(8,128)(2,1)S(1)} %gate.10.refs_5_), channel_id=1, source_target_pairs={{0,1},{1,0},{2,3},{3,2},{4,5},{5,4},{6,7},{7,6},{8,9},{9,8},{10,11... | collective-permute-start | bytes 1572872 | tf_op jit(solution)/shard_map/ppermute | solution.py:115
  74.1 17.3 %collective-permute-start.14 = (bf16[1024,256]{1,0:T(8,128)(2,1)}, bf16[1024,256]{1,0:T(8,128)(2,1)S(1)}, u32[]{:S(2)}, u32[]{:S(2)}) collective-permute-start(bf16[1024,256]{1,0:T(8,128)(2,1)} %collective-permute-done.9.refs_9_.refs_7_), channel_id=1, source_target_pairs={{0,1},{1,0},{2,3},{3,2},{4,5},{5,4},{6,7},{7,6},{8,9},{9,8},{10,11... | collective-permute-start | bytes 1572872 | tf_op jit(solution)/shard_map/ppermute | solution.py:115
  77.0 14.5 %collective-permute-start.10 = (f32[64,512]{1,0:T(8,128)}, f32[64,512]{1,0:T(8,128)S(1)}, u32[]{:S(2)}, u32[]{:S(2)}) collective-permute-start(f32[64,512]{1,0:T(8,128)} %get-tuple-element.51), channel_id=1, source_target_pairs={{0,1},{1,0},{2,3},{3,2},{4,5},{5,4},{6,7},{7,6},{8,9},{9,8},{10,11... | collective-permute-start | bytes 393224 | tf_op jit(solution)/shard_map/ppermute | solution.py:115
  77.1 14.3 %collective-permute-start.11 = (f32[64,512]{1,0:T(8,128)}, f32[64,512]{1,0:T(8,128)S(1)}, u32[]{:S(2)}, u32[]{:S(2)}) collective-permute-start(f32[64,512]{1,0:T(8,128)} %get-tuple-element.52), channel_id=1, source_target_pairs={{0,2},{1,3},{2,0},{3,1},{4,6},{5,7},{6,4},{7,5},{8,10},{9,11},{10,... | collective-permute-start | bytes 393224 | tf_op jit(solution)/shard_map/ppermute | solution.py:115
  78.6 12.9 %collective-permute-start.12 = (f32[64,512]{1,0:T(8,128)}, f32[64,512]{1,0:T(8,128)S(1)}, u32[]{:S(2)}, u32[]{:S(2)}) collective-permute-start(f32[64,512]{1,0:T(8,128)} %get-tuple-element.53), channel_id=1, source_target_pairs={{0,3},{1,2},{2,1},{3,0},{4,7},{5,6},{6,5},{7,4},{8,11},{9,10},{10,... | collective-permute-start | bytes 393224 | tf_op jit(solution)/shard_map/ppermute | solution.py:115
  102.9 16.9 %copy-start.47 = (bf16[80,512]{1,0:T(8,128)(2,1)S(1)}, bf16[80,512]{1,0:T(8,128)(2,1)}, u32[]{:S(2)}) copy-start(bf16[80,512]{1,0:T(8,128)(2,1)} %get-tuple-element.55) | copy-start | bytes 245764
  102.9 17.4 %copy-start.46 = (bf16[80,512]{1,0:T(8,128)(2,1)S(1)}, bf16[80,512]{1,0:T(8,128)(2,1)}, u32[]{:S(2)}) copy-start(bf16[80,512]{1,0:T(8,128)(2,1)} %get-tuple-element.56) | copy-start | bytes 245764
  103.0 18.3 %copy-start.45 = (bf16[80,512]{1,0:T(8,128)(2,1)S(1)}, bf16[80,512]{1,0:T(8,128)(2,1)}, u32[]{:S(2)}) copy-start(bf16[80,512]{1,0:T(8,128)(2,1)} %get-tuple-element.57) | copy-start | bytes 245764
  103.0 30.3 %all-to-all-start.2 = ((bf16[32,64,256]{2,1,0:T(8,128)(2,1)}), bf16[32,64,256]{2,1,0:T(8,128)(2,1)S(1)}, u32[]{:S(2)}, u32[]{:S(2)}) async-start(bf16[32,64,256]{2,1,0:T(8,128)(2,1)} %bitcast.9), calls=%async_computation.2 | async-start | bytes 2097152 | tf_op jit(solution)/shard_map/all_to_all | solution.py:124
  107.9 11.9 %collective-permute-start.19 = (bf16[64,1024]{1,0:T(8,128)(2,1)S(1)}, bf16[64,1024]{1,0:T(8,128)(2,1)S(1)}, u32[]{:S(2)}, u32[]{:S(2)}) collective-permute-start(bf16[64,1024]{1,0:T(8,128)(2,1)S(1)} %copy-done.28), channel_id=1, source_target_pairs={{0,2},{1,3},{2,0},{3,1},{4,6},{5,7},{6,4},{7,5},{8,10},{9,11},{10,... | collective-permute-start | bytes 393224 | tf_op jit(solution)/shard_map/ppermute | solution.py:115
  109.4 18.0 %collective-permute-start.18 = (bf16[64,1024]{1,0:T(8,128)(2,1)S(1)}, bf16[64,1024]{1,0:T(8,128)(2,1)S(1)}, u32[]{:S(2)}, u32[]{:S(2)}) collective-permute-start(bf16[64,1024]{1,0:T(8,128)(2,1)S(1)} %copy-done.28), channel_id=1, source_target_pairs={{0,1},{1,0},{2,3},{3,2},{4,5},{5,4},{6,7},{7,6},{8,9},{9,8},{10,11... | collective-permute-start | bytes 393224 | tf_op jit(solution)/shard_map/ppermute | solution.py:115
  119.8 7.6 %collective-permute-start.20 = (bf16[64,1024]{1,0:T(8,128)(2,1)S(1)}, bf16[64,1024]{1,0:T(8,128)(2,1)S(1)}, u32[]{:S(2)}, u32[]{:S(2)}) collective-permute-start(bf16[64,1024]{1,0:T(8,128)(2,1)S(1)} %collective-permute-done.19.refs_11_), channel_id=1, source_target_pairs={{0,1},{1,0},{2,3},{3,2},{4,5},{5,4},{6,7},{7,6},{8,9},{9,8},{10,11... | collective-permute-start | bytes 393224 | tf_op jit(solution)/shard_map/ppermute | solution.py:115
  119.8 3.8 %collective-permute-start.15 = (bf16[80,512]{1,0:T(8,128)(2,1)S(1)}, bf16[80,512]{1,0:T(8,128)(2,1)S(1)}, u32[]{:S(2)}, u32[]{:S(2)}) collective-permute-start(bf16[80,512]{1,0:T(8,128)(2,1)S(1)} %copy-done.47), channel_id=1, source_target_pairs={{0,1},{1,0},{2,3},{3,2},{4,5},{5,4},{6,7},{7,6},{8,9},{9,8},{10,11... | collective-permute-start | bytes 245768 | tf_op jit(solution)/shard_map/ppermute | solution.py:115
  120.3 5.7 %collective-permute-start.16 = (bf16[80,512]{1,0:T(8,128)(2,1)S(1)}, bf16[80,512]{1,0:T(8,128)(2,1)S(1)}, u32[]{:S(2)}, u32[]{:S(2)}) collective-permute-start(bf16[80,512]{1,0:T(8,128)(2,1)S(1)} %copy-done.46), channel_id=1, source_target_pairs={{0,2},{1,3},{2,0},{3,1},{4,6},{5,7},{6,4},{7,5},{8,10},{9,11},{10,... | collective-permute-start | bytes 245768 | tf_op jit(solution)/shard_map/ppermute | solution.py:115
  121.2 6.1 %collective-permute-start.17 = (bf16[80,512]{1,0:T(8,128)(2,1)S(1)}, bf16[80,512]{1,0:T(8,128)(2,1)S(1)}, u32[]{:S(2)}, u32[]{:S(2)}) collective-permute-start(bf16[80,512]{1,0:T(8,128)(2,1)S(1)} %copy-done.45), channel_id=1, source_target_pairs={{0,3},{1,2},{2,1},{3,0},{4,7},{5,6},{6,5},{7,4},{8,11},{9,10},{10,... | collective-permute-start | bytes 245768 | tf_op jit(solution)/shard_map/ppermute | solution.py:115
  123.6 9.6 %collective-permute-start.21 = (bf16[256,256]{1,0:T(8,128)(2,1)}, bf16[256,256]{1,0:T(8,128)(2,1)S(1)}, u32[]{:S(2)}, u32[]{:S(2)}) collective-permute-start(bf16[256,256]{1,0:T(8,128)(2,1)} %get-tuple-element.62), channel_id=1, source_target_pairs={{0,2},{1,3},{2,0},{3,1},{4,6},{5,7},{6,4},{7,5},{8,10},{9,11},{10,... | collective-permute-start | bytes 393224 | tf_op jit(solution)/shard_map/ppermute | solution.py:115
  130.4 18.0 %collective-permute-start.27 = (bf16[256,256]{1,0:T(8,128)(2,1)}, bf16[256,256]{1,0:T(8,128)(2,1)S(1)}, u32[]{:S(2)}, u32[]{:S(2)}) collective-permute-start(bf16[256,256]{1,0:T(8,128)(2,1)} %get-tuple-element.68), channel_id=1, source_target_pairs={{0,1},{1,0},{2,3},{3,2},{4,5},{5,4},{6,7},{7,6},{8,9},{9,8},{10,11... | collective-permute-start | bytes 393224 | tf_op jit(solution)/shard_map/ppermute | solution.py:115
  131.3 17.1 %collective-permute-start.28 = (bf16[256,256]{1,0:T(8,128)(2,1)}, bf16[256,256]{1,0:T(8,128)(2,1)S(1)}, u32[]{:S(2)}, u32[]{:S(2)}) collective-permute-start(bf16[256,256]{1,0:T(8,128)(2,1)} %get-tuple-element.69), channel_id=1, source_target_pairs={{0,2},{1,3},{2,0},{3,1},{4,6},{5,7},{6,4},{7,5},{8,10},{9,11},{10,... | collective-permute-start | bytes 393224 | tf_op jit(solution)/shard_map/ppermute | solution.py:115
  132.0 16.5 %collective-permute-start.29 = (bf16[256,256]{1,0:T(8,128)(2,1)}, bf16[256,256]{1,0:T(8,128)(2,1)S(1)}, u32[]{:S(2)}, u32[]{:S(2)}) collective-permute-start(bf16[256,256]{1,0:T(8,128)(2,1)} %get-tuple-element.70), channel_id=1, source_target_pairs={{0,3},{1,2},{2,1},{3,0},{4,7},{5,6},{6,5},{7,4},{8,11},{9,10},{10,... | collective-permute-start | bytes 393224 | tf_op jit(solution)/shard_map/ppermute | solution.py:115
  132.8 15.7 %collective-permute-start.30 = (bf16[4,256,256]{2,1,0:T(8,128)(2,1)}, bf16[4,256,256]{2,1,0:T(8,128)(2,1)S(1)}, u32[]{:S(2)}, u32[]{:S(2)}) collective-permute-start(bf16[4,256,256]{2,1,0:T(8,128)(2,1)} %get-tuple-element.73), channel_id=1, source_target_pairs={{0,4},{4,0},{8,12},{12,8},{16,20},{20,16},{24,28},{28,24},{1,5},{5... | collective-permute-start | bytes 1572872 | tf_op jit(solution)/shard_map/ppermute | solution.py:115
  133.2 15.2 %copy-start.23 = (bf16[256,256]{1,0:T(8,128)(2,1)}, bf16[256,256]{1,0:T(8,128)(2,1)S(1)}, u32[]{:S(2)}) copy-start(bf16[256,256]{1,0:T(8,128)(2,1)S(1)} %collective-permute-done.21.refs_20_.refs_7_) | copy-start | bytes 393220
  151.4 12.4 %copy-start.42 = (bf16[256,256]{1,0:T(8,128)(2,1)S(1)}, bf16[256,256]{1,0:T(8,128)(2,1)}, u32[]{:S(2)}) copy-start(bf16[256,256]{1,0:T(8,128)(2,1)} %get-tuple-element.77) | copy-start | bytes 393220
  151.4 13.0 %copy-start.39 = (bf16[256,256]{1,0:T(8,128)(2,1)S(1)}, bf16[256,256]{1,0:T(8,128)(2,1)}, u32[]{:S(2)}) copy-start(bf16[256,256]{1,0:T(8,128)(2,1)} %get-tuple-element.65) | copy-start | bytes 393220
  151.4 24.2 %copy-start.38 = (bf16[256,256]{1,0:T(8,128)(2,1)S(1)}, bf16[256,256]{1,0:T(8,128)(2,1)}, u32[]{:S(2)}) copy-start(bf16[256,256]{1,0:T(8,128)(2,1)} %get-tuple-element.66) | copy-start | bytes 393220
  151.4 35.2 %copy-start.22 = (bf16[256,256]{1,0:T(8,128)(2,1)S(1)}, bf16[256,256]{1,0:T(8,128)(2,1)}, u32[]{:S(2)}) copy-start(bf16[256,256]{1,0:T(8,128)(2,1)} %get-tuple-element.74.refs_1_.refs_0_) | copy-start | bytes 393220
  151.5 38.0 %copy-start.15 = (bf16[3072,256]{1,0:T(8,128)(2,1)}, bf16[3072,256]{1,0:T(8,128)(2,1)S(1)}, u32[]{:S(2)}) copy-start(bf16[3072,256]{1,0:T(8,128)(2,1)S(1)} %gate.11.refs_1_) | copy-start | bytes 4718596
  151.5 44.6 %collective-permute-start.32 = (bf16[3072,256]{1,0:T(8,128)(2,1)S(1)}, bf16[3072,256]{1,0:T(8,128)(2,1)}, u32[]{:S(2)}, u32[]{:S(2)}) collective-permute-start(bf16[3072,256]{1,0:T(8,128)(2,1)S(1)} %gate.11.refs_1_), channel_id=1, source_target_pairs={{0,2},{1,3},{2,0},{3,1},{4,6},{5,7},{6,4},{7,5},{8,10},{9,11},{10,... | collective-permute-start | bytes 4718600 | tf_op jit(solution)/shard_map/ppermute | solution.py:115
  152.8 43.5 %all-to-all-start.3 = ((bf16[8,144,256]{2,1,0:T(8,128)(2,1)}), bf16[8,144,256]{2,1,0:T(8,128)(2,1)S(1)}, u32[]{:S(2)}, u32[]{:S(2)}) async-start(bf16[8,144,256]{2,1,0:T(8,128)(2,1)} %get-tuple-element.78), calls=%async_computation.3 | async-start | bytes 1179648 | tf_op jit(solution)/shard_map/all_to_all | solution.py:124
  160.9 14.7 %collective-permute-start.34 = (bf16[256,256]{1,0:T(8,128)(2,1)S(1)}, bf16[256,256]{1,0:T(8,128)(2,1)S(1)}, u32[]{:S(2)}, u32[]{:S(2)}) collective-permute-start(bf16[256,256]{1,0:T(8,128)(2,1)S(1)} %copy-done.44), channel_id=1, source_target_pairs={{0,8},{4,12},{8,0},{12,4},{16,24},{20,28},{24,16},{28,20},{1,9},{5... | collective-permute-start | bytes 393224 | tf_op jit(solution)/shard_map/ppermute | solution.py:115
  161.5 20.5 %collective-permute-start.35 = (bf16[256,256]{1,0:T(8,128)(2,1)S(1)}, bf16[256,256]{1,0:T(8,128)(2,1)S(1)}, u32[]{:S(2)}, u32[]{:S(2)}) collective-permute-start(bf16[256,256]{1,0:T(8,128)(2,1)S(1)} %copy-done.43), channel_id=1, source_target_pairs={{0,16},{4,20},{8,24},{12,28},{16,0},{20,4},{24,8},{28,12},{1,17},{... | collective-permute-start | bytes 393224 | tf_op jit(solution)/shard_map/ppermute | solution.py:115
  163.9 22.8 %collective-permute-start.36 = (bf16[256,256]{1,0:T(8,128)(2,1)S(1)}, bf16[256,256]{1,0:T(8,128)(2,1)S(1)}, u32[]{:S(2)}, u32[]{:S(2)}) collective-permute-start(bf16[256,256]{1,0:T(8,128)(2,1)S(1)} %copy-done.42), channel_id=1, source_target_pairs={{0,24},{4,28},{8,16},{12,20},{16,8},{20,12},{24,0},{28,4},{1,25},{... | collective-permute-start | bytes 393224 | tf_op jit(solution)/shard_map/ppermute | solution.py:115
  164.4 25.1 %collective-permute-start.25 = (bf16[256,256]{1,0:T(8,128)(2,1)S(1)}, bf16[256,256]{1,0:T(8,128)(2,1)S(1)}, u32[]{:S(2)}, u32[]{:S(2)}) collective-permute-start(bf16[256,256]{1,0:T(8,128)(2,1)S(1)} %copy-done.39), channel_id=1, source_target_pairs={{0,1},{1,0},{2,3},{3,2},{4,5},{5,4},{6,7},{7,6},{8,9},{9,8},{10,11... | collective-permute-start | bytes 393224 | tf_op jit(solution)/shard_map/ppermute | solution.py:115
  175.6 15.0 %collective-permute-start.26 = (bf16[256,256]{1,0:T(8,128)(2,1)S(1)}, bf16[256,256]{1,0:T(8,128)(2,1)S(1)}, u32[]{:S(2)}, u32[]{:S(2)}) collective-permute-start(bf16[256,256]{1,0:T(8,128)(2,1)S(1)} %copy-done.38), channel_id=1, source_target_pairs={{0,3},{1,2},{2,1},{3,0},{4,7},{5,6},{6,5},{7,4},{8,11},{9,10},{10,... | collective-permute-start | bytes 393224 | tf_op jit(solution)/shard_map/ppermute | solution.py:115
  187.3 16.0 %copy-start.27 = (bf16[256,256]{1,0:T(8,128)(2,1)S(1)}, bf16[256,256]{1,0:T(8,128)(2,1)}, u32[]{:S(2)}) copy-start(bf16[256,256]{1,0:T(8,128)(2,1)} %add_some.1.refs_1_) | copy-start | bytes 393220
  187.3 8.3 %collective-permute-start.39 = (bf16[256,256]{1,0:T(8,128)(2,1)}, bf16[256,256]{1,0:T(8,128)(2,1)S(1)}, u32[]{:S(2)}, u32[]{:S(2)}) collective-permute-start(bf16[256,256]{1,0:T(8,128)(2,1)} %add_some.1.refs_1_), channel_id=1, source_target_pairs={{0,24},{4,28},{8,16},{12,20},{16,8},{20,12},{24,0},{28,4},{1,25},{... | collective-permute-start | bytes 393224 | tf_op jit(solution)/shard_map/ppermute | solution.py:115
  187.9 16.2 %collective-permute-start.23 = (bf16[1024,256]{1,0:T(8,128)(2,1)S(1)}, bf16[1024,256]{1,0:T(8,128)(2,1)}, u32[]{:S(2)}, u32[]{:S(2)}) collective-permute-start(bf16[1024,256]{1,0:T(8,128)(2,1)S(1)} %copy-done.35), channel_id=1, source_target_pairs={{0,2},{1,3},{2,0},{3,1},{4,6},{5,7},{6,4},{7,5},{8,10},{9,11},{10,... | collective-permute-start | bytes 1572872 | tf_op jit(solution)/shard_map/ppermute | solution.py:115
  189.5 15.9 %collective-permute-start.31 = (bf16[3072,256]{1,0:T(8,128)(2,1)S(1)}, bf16[3072,256]{1,0:T(8,128)(2,1)}, u32[]{:S(2)}, u32[]{:S(2)}) collective-permute-start(bf16[3072,256]{1,0:T(8,128)(2,1)S(1)} %gate.11.refs_1_), channel_id=1, source_target_pairs={{0,1},{1,0},{2,3},{3,2},{4,5},{5,4},{6,7},{7,6},{8,9},{9,8},{10,11... | collective-permute-start | bytes 4718600 | tf_op jit(solution)/shard_map/ppermute | solution.py:115
  190.6 11.8 %collective-permute-start.38 = (bf16[256,256]{1,0:T(8,128)(2,1)}, bf16[256,256]{1,0:T(8,128)(2,1)S(1)}, u32[]{:S(2)}, u32[]{:S(2)}) collective-permute-start(bf16[256,256]{1,0:T(8,128)(2,1)} %add_some.1.refs_1_), channel_id=1, source_target_pairs={{0,16},{4,20},{8,24},{12,28},{16,0},{20,4},{24,8},{28,12},{1,17},{... | collective-permute-start | bytes 393224 | tf_op jit(solution)/shard_map/ppermute | solution.py:115
  195.6 7.7 %collective-permute-start.37 = (bf16[256,256]{1,0:T(8,128)(2,1)}, bf16[256,256]{1,0:T(8,128)(2,1)S(1)}, u32[]{:S(2)}, u32[]{:S(2)}) collective-permute-start(bf16[256,256]{1,0:T(8,128)(2,1)} %add_some.1.refs_1_), channel_id=1, source_target_pairs={{0,8},{4,12},{8,0},{12,4},{16,24},{20,28},{24,16},{28,20},{1,9},{5... | collective-permute-start | bytes 393224 | tf_op jit(solution)/shard_map/ppermute | solution.py:115
  196.1 10.1 %collective-permute-start.33 = (bf16[3072,256]{1,0:T(8,128)(2,1)}, bf16[3072,256]{1,0:T(8,128)(2,1)}, u32[]{:S(2)}, u32[]{:S(2)}) collective-permute-start(bf16[3072,256]{1,0:T(8,128)(2,1)} %collective-permute-done.32.refs_3_), channel_id=1, source_target_pairs={{0,1},{1,0},{2,3},{3,2},{4,5},{5,4},{6,7},{7,6},{8,9},{9,8},{10,11... | collective-permute-start | bytes 4718600 | tf_op jit(solution)/shard_map/ppermute | solution.py:115
  197.3 22.6 %all-to-all-start.4 = ((bf16[8,128,256]{2,1,0:T(8,128)(2,1)}), bf16[8,128,256]{2,1,0:T(8,128)(2,1)S(1)}, u32[]{:S(2)}, u32[]{:S(2)}) async-start(bf16[8,128,256]{2,1,0:T(8,128)(2,1)} %get-tuple-element.79), calls=%async_computation.4 | async-start | bytes 1048576 | tf_op jit(solution)/shard_map/all_to_all | solution.py:124
  202.4 12.5 %collective-permute-start.22 = (bf16[1024,256]{1,0:T(8,128)(2,1)S(1)}, bf16[1024,256]{1,0:T(8,128)(2,1)S(1)}, u32[]{:S(2)}, u32[]{:S(2)}) collective-permute-start(bf16[1024,256]{1,0:T(8,128)(2,1)S(1)} %copy-done.35), channel_id=1, source_target_pairs={{0,1},{1,0},{2,3},{3,2},{4,5},{5,4},{6,7},{7,6},{8,9},{9,8},{10,11... | collective-permute-start | bytes 1572872 | tf_op jit(solution)/shard_map/ppermute | solution.py:115
  203.4 10.1 %collective-permute-start.40 = (bf16[256,256]{1,0:T(8,128)(2,1)S(1)}, bf16[256,256]{1,0:T(8,128)(2,1)S(1)}, u32[]{:S(2)}, u32[]{:S(2)}) collective-permute-start(bf16[256,256]{1,0:T(8,128)(2,1)S(1)} %copy-done.27), channel_id=1, source_target_pairs={{0,4},{4,0},{8,12},{12,8},{16,20},{20,16},{24,28},{28,24},{1,5},{5... | collective-permute-start | bytes 393224 | tf_op jit(solution)/shard_map/ppermute | solution.py:115
  204.1 16.8 %collective-permute-start.43 = (bf16[256,256]{1,0:T(8,128)(2,1)S(1)}, bf16[256,256]{1,0:T(8,128)(2,1)S(1)}, u32[]{:S(2)}, u32[]{:S(2)}) collective-permute-start(bf16[256,256]{1,0:T(8,128)(2,1)S(1)} %collective-permute-done.39.refs_15_.refs_7_), channel_id=1, source_target_pairs={{0,4},{4,0},{8,12},{12,8},{16,20},{20,16},{24,28},{28,24},{1,5},{5... | collective-permute-start | bytes 393224 | tf_op jit(solution)/shard_map/ppermute | solution.py:115
  205.4 15.5 %collective-permute-start.42 = (bf16[256,256]{1,0:T(8,128)(2,1)S(1)}, bf16[256,256]{1,0:T(8,128)(2,1)S(1)}, u32[]{:S(2)}, u32[]{:S(2)}) collective-permute-start(bf16[256,256]{1,0:T(8,128)(2,1)S(1)} %collective-permute-done.38.refs_14_.refs_5_), channel_id=1, source_target_pairs={{0,4},{4,0},{8,12},{12,8},{16,20},{20,16},{24,28},{28,24},{1,5},{5... | collective-permute-start | bytes 393224 | tf_op jit(solution)/shard_map/ppermute | solution.py:115
  206.1 8.7 %collective-permute-start.24 = (bf16[1024,256]{1,0:T(8,128)(2,1)}, bf16[1024,256]{1,0:T(8,128)(2,1)S(1)}, u32[]{:S(2)}, u32[]{:S(2)}) collective-permute-start(bf16[1024,256]{1,0:T(8,128)(2,1)} %collective-permute-done.23.refs_3_), channel_id=1, source_target_pairs={{0,1},{1,0},{2,3},{3,2},{4,5},{5,4},{6,7},{7,6},{8,9},{9,8},{10,11... | collective-permute-start | bytes 1572872 | tf_op jit(solution)/shard_map/ppermute | solution.py:115
  213.5 7.4 %collective-permute-start.41 = (bf16[256,256]{1,0:T(8,128)(2,1)S(1)}, bf16[256,256]{1,0:T(8,128)(2,1)S(1)}, u32[]{:S(2)}, u32[]{:S(2)}) collective-permute-start(bf16[256,256]{1,0:T(8,128)(2,1)S(1)} %collective-permute-done.37.refs_13_.refs_3_), channel_id=1, source_target_pairs={{0,4},{4,0},{8,12},{12,8},{16,20},{20,16},{24,28},{28,24},{1,5},{5... | collective-permute-start | bytes 393224 | tf_op jit(solution)/shard_map/ppermute | solution.py:115
  (33 other events, 167.1 us)

commit v6 on v5

--- a/solution.py
+++ b/solution.py
@@ -535,7 +535,7 @@
 def add_pairs(own, other, after=(), near=()):
     count, rows, columns = own.shape
     return call(
-        add_pairs_kernel, "add_pairs", [far(own), other], [full((rows, columns), bf16, far_shape)] * count, after=after, near=near
+        add_pairs_kernel, "add_pairs", [far(own), other], [full((rows, columns), bf16)] * count, after=after, near=near
     )
 
 
@@ -548,7 +548,7 @@
 
 def add_some(parts, after=()):
     return call(
-        functools.partial(add_some_kernel, len(parts)), "add_some", parts, [full(parts[0].shape, bf16, far_shape)], after=after
+        functools.partial(add_some_kernel, len(parts)), "add_some", parts, [full(parts[0].shape, bf16)], after=after
     )[0]
 
 

time: 227 us -> 225 us (level)
    unnamed x96 -> x86, local copies, waits for them, and re-layouts: 5.04 us -> 4.47 us
where the time goes in v6:
time: 225 us; the launch traced here: 221 us
  Pallas kernels  96.9 us (43%)
  starting transfers between devices  62.7 us (28%)
  waiting for transfers between devices  55.9 us (25%)
  local copies, waits for them, and re-layouts  4.47 us (2%)
    pallas_call x26, Pallas kernels, call(): pl.pallas_call(inner, grid=grid, in_specs=specs + [pl.BlockSpec(memory_sp...  96.8 us
    ppermute x44, waiting for transfers between devices, swap(): return lax.ppermute(array, axis, [(i, i ^ bits) for i in range(size)])  45.3 us
    ppermute x44, starting transfers between devices, swap(): return lax.ppermute(array, axis, [(i, i ^ bits) for i in range(size)])  33.4 us
    all_to_all x5, starting transfers between devices, exchange(): return lax.all_to_all(array, axes, split_axis=0, concat_axis=0, tiled=True)  29.3 us
    all_to_all x5, waiting for transfers between devices, exchange(): return lax.all_to_all(array, axes, split_axis=0, concat_axis=0, tiled=True)  10.6 us
  transfers between devices with their start and end apart: 49, of which 14 were waited for; matrix products, arithmetic and copies ran while one was open for 0% of the time, Pallas kernels for 40%

profile of v6, /device:TPU:12, one launch (start us, length us, event | category | flops | bytes accessed | tf_op | source)
XLA Modules:
  0.0 221.2 jit_solution(11745031575679014761)
XLA Ops:
  0.6 2.1 low.3.refs_2_.refs_1_.refs_7_
  2.7 1.5 collective-permute-start.1
  4.2 2.8 %low.4 = (bf16[2048,256]{1,0:T(8,128)(2,1)}, bf16[1024,256]{1,0:T(8,128)(2,1)}) custom-call(f32[4096,256]{1,0:T(8,128)} %refs_1_.2, f32[4096,256]{1,0:T(8,128)} %refs_1_.2, bf16[1024,256]{1,0:T(8,128)(2,1)} %low.3.refs_2_.refs_1_.refs_7_), custom_call_target="tpu_custom_call" | custom-call | flops 1150000 | bytes 3690 | tf_op jit(solution)/shard_map/low/pallas_call | solution.py:82
  7.1 2.5 %slots.1.refs_3_ = s16[8,3,50,256]{3,2,1,0:T(8,128)(2,1)} custom-call(s32[2]{0:T(128)S(1)} %pad_add_fusion.refs_0_, s32[50,256]{1,0:T(8,128)} %bitcast.18, s32[1,256]{1,0:T(1,128)} %bitcast.26, f32[50,256]{1,0:T(8,128)} %bitcast.19, bf16[2048,256]{1,0:T(8,128)(2,1)} %get-tuple-element.46.refs_0_.refs_4_), custom_call_target="tpu_custom_call" | custom-call | flops 1150000 | bytes 3690 | tf_op jit(solution)/shard_map/slots/pallas_call | solution.py:82
  9.5 6.4 %all-to-all-start = ((s16[8,3,50,256]{3,2,1,0:T(8,128)(2,1)}), s16[8,3,50,256]{3,2,1,0:T(8,128)(2,1)S(1)}, u32[]{:S(2)}, u32[]{:S(2)}) async-start(s16[8,3,50,256]{3,2,1,0:T(8,128)(2,1)} %slots.1.refs_3_), calls=%async_computation | async-start | bytes 1376256 | tf_op jit(solution)/shard_map/all_to_all | solution.py:124
  16.6 0.8 copy-done.7
  17.4 1.5 collective-permute-start.3
  19.4 3.8 %low.5 = (bf16[1024,256]{1,0:T(8,128)(2,1)}, bf16[1024,256]{1,0:T(8,128)(2,1)}, bf16[1024,256]{1,0:T(8,128)(2,1)}) custom-call(f32[1024,256]{1,0:T(8,128)} %refs_0_.5, f32[2048,256]{1,0:T(8,128)} %refs_2_.1, f32[2048,256]{1,0:T(8,128)} %refs_2_.1, s16[8,3,50,256]{3,2,1,0:T(8,128)(2,1)} %slots.1.refs_3_), custom_call_target="tpu_custom_call" | custom-call | flops 1150000 | bytes 3690 | tf_op jit(solution)/shard_map/low/pallas_call | solution.py:82
  23.3 2.3 %hidden_value.3.refs_1_.refs_0_ = bf16[256,1024]{1,0:T(8,128)(2,1)S(1)} custom-call(s32[2]{0:T(128)S(1)} %pad_add_fusion.refs_0_, bf16[1024,256]{1,0:T(8,128)(2,1)S(1)} %copy-done.6, bf16[1024,256]{1,0:T(8,128)(2,1)S(1)} %collective-permute-done.refs_2_.refs_8_, bf16[1024,256]{1,0:T(8,128)(2,1)S(1)} %copy-done.8, ...), custom_call_target="tpu_custom_call" | custom-call | flops 1150000 | bytes 3690 | tf_op jit(solution)/shard_map/hidden_value/pallas_call | solution.py:82
  25.6 0.8 copy-done.17
  26.4 0.8 copy-done.18
  27.2 3.1 %all-to-all-done.refs_0_ = s16[8,3,50,256]{3,2,1,0:T(8,128)(2,1)S(1)} async-done(((s16[8,3,50,256]{3,2,1,0:T(8,128)(2,1)}), s16[8,3,50,256]{3,2,1,0:T(8,128)(2,1)S(1)}, u32[]{:S(2)}, u32[]{:S(2)}) %all-to-all-start) | async-done | bytes 614432 | tf_op jit(solution)/shard_map/all_to_all | solution.py:124
  30.3 6.2 %spread.2.refs_1_.refs_2_.refs_3_.refs_4_ = bf16[4,4096,256]{2,1,0:T(8,128)(2,1)S(1)} custom-call(s16[8,3,50,256]{3,2,1,0:T(8,128)(2,1)S(1)} %all-to-all-done.refs_0_, bf16[256,1024]{1,0:T(8,128)(2,1)S(1)} %hidden_value.3.refs_1_.refs_0_), custom_call_target="tpu_custom_call" | custom-call | flops 1150000 | bytes 3690 | tf_op jit(solution)/shard_map/spread/pallas_call | solution.py:82
  36.6 4.8 %collective-permute-done.3.refs_0_ = bf16[2048,256]{1,0:T(8,128)(2,1)S(1)} collective-permute-done((bf16[2048,256]{1,0:T(8,128)(2,1)S(1)}, bf16[2048,256]{1,0:T(8,128)(2,1)S(1)}, u32[]{:S(2)}, u32[]{:S(2)}) %collective-permute-start.3) | collective-permute-done | bytes 1048608 | tf_op jit(solution)/shard_map/ppermute | solution.py:115
  41.5 1.6 collective-permute-start.5
  43.0 6.1 %spread.3.refs_7_.refs_5_.refs_6_.refs_2_.refs_1_ = bf16[4,4096,256]{2,1,0:T(8,128)(2,1)S(1)} custom-call(s16[8,3,50,256]{3,2,1,0:T(8,128)(2,1)S(1)} %all-to-all-done.refs_0_), custom_call_target="tpu_custom_call" | custom-call | flops 1150000 | bytes 3690 | tf_op jit(solution)/shard_map/spread/pallas_call | solution.py:82
  49.3 4.7 %hidden_value.4.refs_1_ = bf16[256,2048]{1,0:T(8,128)(2,1)S(1)} custom-call(s32[2]{0:T(128)S(1)} %pad_add_fusion.refs_0_, bf16[2048,256]{1,0:T(8,128)(2,1)S(1)} %gate.6.refs_1_.refs_11_, bf16[2048,256]{1,0:T(8,128)(2,1)} %collective-permute-done.6.refs_2_.refs_12_, bf16[2048,256]{1,0:T(8,128)(2,1)S(1)} %gate.7.refs_1_.refs_3_.refs_13_, ...), custom_call_target="tpu_custom_call" | custom-call | flops 1150000 | bytes 3690 | tf_op jit(solution)/shard_map/hidden_value/pallas_call | solution.py:82
  54.1 1.7 collective-permute-done.5.refs_0_
  55.8 1.6 collective-permute-start.9
  57.4 5.1 %pool.2.refs_7_.refs_3_ = f32[256,2048]{1,0:T(8,128)S(1)} custom-call(bf16[256,1024]{1,0:T(8,128)(2,1)S(1)} %hidden_value.3.refs_1_.refs_0_, bf16[256,2048]{1,0:T(8,128)(2,1)S(1)} %hidden_value.4.refs_1_, bf16[4,4096,256]{2,1,0:T(8,128)(2,1)S(1)} %spread.2.refs_1_.refs_2_.refs_3_.refs_4_, bf16[4,4096,256]{2,1,0:T(8,128)(2,1)S(1)} %spread.2.refs_1_.refs_2_.refs_3_.refs_4_, ...), custom_call_target="tpu_custom_call" | custom-call | flops 1150000 | bytes 3690 | tf_op jit(solution)/shard_map/pool/pallas_call | solution.py:82
  62.5 2.6 %hidden_value.5.refs_0_ = bf16[256,1024]{1,0:T(8,128)(2,1)S(1)} custom-call(s32[2]{0:T(128)S(1)} %pad_add_fusion.refs_0_, bf16[1024,256]{1,0:T(8,128)(2,1)S(1)} %gate.8.refs_1_.refs_15_, bf16[1024,256]{1,0:T(8,128)(2,1)S(1)} %collective-permute-done.4.refs_2_.refs_16_, bf16[1024,256]{1,0:T(8,128)(2,1)S(1)} %gate.9.refs_3_.refs_17_, ...), custom_call_target="tpu_custom_call" | custom-call | flops 1150000 | bytes 3690 | tf_op jit(solution)/shard_map/hidden_value/pallas_call | solution.py:82
  65.2 3.5 %pool.3.refs_8_ = bf16[2048,256]{1,0:T(8,128)(2,1)} custom-call(bf16[256,1024]{1,0:T(8,128)(2,1)S(1)} %hidden_value.5.refs_0_, bf16[4,4096,256]{2,1,0:T(8,128)(2,1)S(1)} %spread.2.refs_1_.refs_2_.refs_3_.refs_4_, bf16[4,4096,256]{2,1,0:T(8,128)(2,1)S(1)} %spread.3.refs_7_.refs_5_.refs_6_.refs_2_.refs_1_, f32[256,2048]{1,0:T(8,128)S(1)} %pool.2.refs_7_.refs_3_), custom_call_target="tpu_custom_call" | custom-call | flops 1150000 | bytes 3690 | tf_op jit(solution)/shard_map/pool/pallas_call | solution.py:82
  68.7 5.1 %all-to-all-start.1 = ((bf16[32,64,256]{2,1,0:T(8,128)(2,1)}), bf16[32,64,256]{2,1,0:T(8,128)(2,1)S(1)}, u32[]{:S(2)}, u32[]{:S(2)}) async-start(bf16[32,64,256]{2,1,0:T(8,128)(2,1)} %bitcast.6), calls=%async_computation.1 | async-start | bytes 2097152 | tf_op jit(solution)/shard_map/all_to_all | solution.py:124
  74.4 2.5 %self_half.1 = (f32[64,512]{1,0:T(8,128)}, f32[64,512]{1,0:T(8,128)}, f32[64,512]{1,0:T(8,128)}, f32[64,512]{1,0:T(8,128)}) custom-call(s32[2]{0:T(128)S(1)} %pad_add_fusion.refs_0_, bf16[1024,256]{1,0:T(8,128)(2,1)} %low.3.refs_2_.refs_1_.refs_7_, bf16[1024,256]{1,0:T(8,128)(2,1)} %copy-done.17, bf16[1024,256]{1,0:T(8,128)(2,1)} %copy-done.7, ...), custom_call_target="tpu_custom_call" | custom-call | flops 3449999872 | bytes 11070000 | tf_op jit(solution)/shard_map/self_half/pallas_call | solution.py:82
  77.0 1.5 collective-permute-start.11
  78.7 3.5 %hidden_slope.3.refs_9_.refs_2_.refs_4_ = bf16[1024,256]{1,0:T(8,128)(2,1)} custom-call(s32[2]{0:T(128)S(1)} %pad_add_fusion.refs_0_, bf16[1024,256]{1,0:T(8,128)(2,1)} %low.3.refs_2_.refs_1_.refs_7_, bf16[1024,256]{1,0:T(8,128)(2,1)} %copy-done.17, bf16[1024,256]{1,0:T(8,128)(2,1)} %copy-done.7, bf16[1024,256]{1,0:T(8,128)(2,1)} %copy-done.18, ...), custom_call_target="tpu_custom_call" | custom-call | flops 5750000128 | bytes 18450000 | tf_op jit(solution)/shard_map/hidden_slope/pallas_call | solution.py:82
  82.2 3.5 %hidden_slope.5.refs_11_.refs_6_ = bf16[1024,256]{1,0:T(8,128)(2,1)} custom-call(s32[2]{0:T(128)S(1)} %pad_add_fusion.refs_0_, bf16[1024,256]{1,0:T(8,128)(2,1)} %copy-done.10, bf16[1024,256]{1,0:T(8,128)(2,1)} %copy-done.19, bf16[1024,256]{1,0:T(8,128)(2,1)} %copy-done.11, bf16[1024,256]{1,0:T(8,128)(2,1)} %copy-done.20, ...), custom_call_target="tpu_custom_call" | custom-call | flops 5750000128 | bytes 18450000 | tf_op jit(solution)/shard_map/hidden_slope/pallas_call | solution.py:82
  85.7 5.5 %hidden_slope.4.refs_10_.refs_5_ = bf16[2048,256]{1,0:T(8,128)(2,1)} custom-call(s32[2]{0:T(128)S(1)} %pad_add_fusion.refs_0_, bf16[2048,256]{1,0:T(8,128)(2,1)} %copy-done.4, bf16[2048,256]{1,0:T(8,128)(2,1)} %collective-permute-done.6.refs_2_.refs_12_, bf16[2048,256]{1,0:T(8,128)(2,1)} %copy-done.2, bf16[2048,256]{1,0:T(8,128)(2,1)} %copy-done.16, ...), custom_call_target="tpu_custom_call" | custom-call | flops 5750000128 | bytes 18450000 | tf_op jit(solution)/shard_map/hidden_slope/pallas_call | solution.py:82
  91.3 7.4 %all-to-all-done.1 = bf16[32,64,256]{2,1,0:T(8,128)(2,1)S(1)} async-done(((bf16[32,64,256]{2,1,0:T(8,128)(2,1)}), bf16[32,64,256]{2,1,0:T(8,128)(2,1)S(1)}, u32[]{:S(2)}, u32[]{:S(2)}) %all-to-all-start.1) | async-done | bytes 1048608 | tf_op jit(solution)/shard_map/all_to_all | solution.py:124
  98.8 4.0 %combine.1 = (bf16[8,4,64,256]{3,2,1,0:T(8,128)(2,1)}, bf16[64,1024]{1,0:T(8,128)(2,1)}, bf16[80,512]{1,0:T(8,128)(2,1)}, bf16[80,512]{1,0:T(8,128)(2,1)}, bf16[...) custom-call(bf16[8,4,64,256]{3,2,1,0:T(8,128)(2,1)S(1)} %bitcast.15, f32[64,512]{1,0:T(8,128)} %get-tuple-element.50.refs_7_.refs_1_, ...), custom_call_target="tpu_custom_call" | custom-call | flops 1150000000 | bytes 3690000 | tf_op jit(solution)/shard_map/combine/pallas_call | solution.py:82
  102.9 4.9 %all-to-all-start.2 = ((bf16[32,64,256]{2,1,0:T(8,128)(2,1)}), bf16[32,64,256]{2,1,0:T(8,128)(2,1)S(1)}, u32[]{:S(2)}, u32[]{:S(2)}) async-start(bf16[32,64,256]{2,1,0:T(8,128)(2,1)} %bitcast.9), calls=%async_computation.2 | async-start | bytes 2097152 | tf_op jit(solution)/shard_map/all_to_all | solution.py:124
  107.7 1.5 collective-permute-start.19
  109.3 10.4 %collective-permute-done.19.refs_11_ = bf16[64,1024]{1,0:T(8,128)(2,1)S(1)} collective-permute-done((bf16[64,1024]{1,0:T(8,128)(2,1)S(1)}, bf16[64,1024]{1,0:T(8,128)(2,1)S(1)}, u32[]{:S(2)}, u32[]{:S(2)}) %collective-permute-start.19) | collective-permute-done | bytes 131104 | tf_op jit(solution)/shard_map/ppermute | solution.py:115
  120.2 0.9 collective-permute-start.16
  121.6 1.9 cut.1
  123.5 0.9 collective-permute-start.21
  124.4 1.5 collective-permute-done.16.refs_7_
  125.9 1.3 collective-permute-done.17.refs_8_
  127.3 3.1 %w_back.1 = (f32[256,256]{1,0:T(8,128)}, bf16[4,256,256]{2,1,0:T(8,128)(2,1)}, bf16[4,256,256]{2,1,0:T(8,128)(2,1)}, bf16[16,256]{1,0:T(8,128)(2,1)}, bf16[256,2...) custom-call(s32[2]{0:T(128)S(1)} %pad_add_fusion.refs_0_, ...), custom_call_target="tpu_custom_call" | custom-call | flops 4600000000 | bytes 14760000 | tf_op jit(solution)/shard_map/w_back/pallas_call | solution.py:82
  130.3 0.9 collective-permute-start.27
  133.1 15.1 %rows_back.1 = (bf16[1024,256]{1,0:T(8,128)(2,1)}, bf16[3072,256]{1,0:T(8,128)(2,1)}, bf16[8,144,256]{2,1,0:T(8,128)(2,1)}) custom-call(s32[2]{0:T(128)S(1)} %pad_add_fusion.refs_0_, bf16[4,4096,256]{2,1,0:T(8,128)(2,1)} %copy-done.1, bf16[4,4096,256]{2,1,0:T(8,128)(2,1)} %copy-done, bf16[2048,256]{1,0:T(8,128)(2,1)S(1)} %bitcast.17, ...), custom_call_target="tpu_custom_call" | custom-call | flops 18400000000 | bytes 59040000 | tf_op jit(solution)/shard_map/rows_back/pallas_call | solution.py:82
  148.3 1.3 add_pairs.1
  150.0 1.3 collective-permute-start.32
  151.3 8.0 %all-to-all-start.3 = ((bf16[8,144,256]{2,1,0:T(8,128)(2,1)}), bf16[8,144,256]{2,1,0:T(8,128)(2,1)S(1)}, u32[]{:S(2)}, u32[]{:S(2)}) async-start(bf16[8,144,256]{2,1,0:T(8,128)(2,1)} %get-tuple-element.78), calls=%async_computation.3 | async-start | bytes 1179648 | tf_op jit(solution)/shard_map/all_to_all | solution.py:124
  159.8 2.4 %collective-permute-start.35 = (bf16[256,256]{1,0:T(8,128)(2,1)S(1)}, bf16[256,256]{1,0:T(8,128)(2,1)S(1)}, u32[]{:S(2)}, u32[]{:S(2)}) collective-permute-start(bf16[256,256]{1,0:T(8,128)(2,1)S(1)} %get-tuple-element.76), channel_id=1, source_target_pairs={{0,16},{4,20},{8,24},{12,28},{16,0},{20,4},{24,8},{28,12},{1,17},{... | collective-permute-start | bytes 393224 | tf_op jit(solution)/shard_map/ppermute | solution.py:115
  162.8 11.2 %collective-permute-done.34.refs_1_ = bf16[256,256]{1,0:T(8,128)(2,1)S(1)} collective-permute-done((bf16[256,256]{1,0:T(8,128)(2,1)S(1)}, bf16[256,256]{1,0:T(8,128)(2,1)S(1)}, u32[]{:S(2)}, u32[]{:S(2)}) %collective-permute-start.34) | collective-permute-done | bytes 131104 | tf_op jit(solution)/shard_map/ppermute | solution.py:115
  174.0 6.5 %collective-permute-done.35.refs_2_ = bf16[256,256]{1,0:T(8,128)(2,1)S(1)} collective-permute-done((bf16[256,256]{1,0:T(8,128)(2,1)S(1)}, bf16[256,256]{1,0:T(8,128)(2,1)S(1)}, u32[]{:S(2)}, u32[]{:S(2)}) %collective-permute-start.35) | collective-permute-done | bytes 131104 | tf_op jit(solution)/shard_map/ppermute | solution.py:115
  180.5 4.6 %collective-permute-done.36.refs_3_ = bf16[256,256]{1,0:T(8,128)(2,1)S(1)} collective-permute-done((bf16[256,256]{1,0:T(8,128)(2,1)S(1)}, bf16[256,256]{1,0:T(8,128)(2,1)S(1)}, u32[]{:S(2)}, u32[]{:S(2)}) %collective-permute-start.36) | collective-permute-done | bytes 131104 | tf_op jit(solution)/shard_map/ppermute | solution.py:115
  185.8 1.6 collective-permute-start.23
  187.5 1.6 collective-permute-done.26.refs_8_
  189.1 5.1 %collective-permute-start.38 = (bf16[256,256]{1,0:T(8,128)(2,1)S(1)}, bf16[256,256]{1,0:T(8,128)(2,1)S(1)}, u32[]{:S(2)}, u32[]{:S(2)}) collective-permute-start(bf16[256,256]{1,0:T(8,128)(2,1)S(1)} %add_some.1.refs_1_), channel_id=1, source_target_pairs={{0,16},{4,20},{8,24},{12,28},{16,0},{20,4},{24,8},{28,12},{1,17},{... | collective-permute-start | bytes 393224 | tf_op jit(solution)/shard_map/ppermute | solution.py:115
  194.8 0.9 add.3
  195.7 5.1 %all-to-all-start.4 = ((bf16[8,128,256]{2,1,0:T(8,128)(2,1)}), bf16[8,128,256]{2,1,0:T(8,128)(2,1)S(1)}, u32[]{:S(2)}, u32[]{:S(2)}) async-start(bf16[8,128,256]{2,1,0:T(8,128)(2,1)} %get-tuple-element.79), calls=%async_computation.4 | async-start | bytes 1048576 | tf_op jit(solution)/shard_map/all_to_all | solution.py:124
  200.8 0.8 collective-permute-done.37.refs_13_.refs_3_
  201.5 0.8 collective-permute-start.40
  202.4 1.2 collective-permute-start.43
  203.6 0.8 collective-permute-start.42
  204.4 7.3 %table_back.2.refs_13_ = f32[4096,256]{1,0:T(8,128)} custom-call(s32[2]{0:T(128)S(1)} %pad_add_fusion.refs_0_, bf16[3072,256]{1,0:T(8,128)(2,1)} %copy-done.15, bf16[3072,256]{1,0:T(8,128)(2,1)} %collective-permute-done.31.refs_2_, bf16[3072,256]{1,0:T(8,128)(2,1)} %collective-permute-done.32.refs_3_, bf16[3072,256]{1,0:T(8,128)(2,1)} %collective-permute-done.33.refs_4_, ...), custom_call_target="tpu_custom_call" | custom-call | flops 23000000512 | bytes 73800000 | tf_op jit(solution)/shard_map/table_back/pallas_call | solution.py:82
  211.8 1.3 collective-permute-start.41
  213.0 0.8 copy-done.34
  213.8 0.8 copy-done.35
  214.6 3.5 %table_back.3.refs_1_.refs_9_ = f32[4096,256]{1,0:T(8,128)} custom-call(s32[2]{0:T(128)S(1)} %pad_add_fusion.refs_0_, bf16[1024,256]{1,0:T(8,128)(2,1)} %get-tuple-element.63.refs_2_.refs_1_, bf16[1024,256]{1,0:T(8,128)(2,1)} %copy-done.34, bf16[1024,256]{1,0:T(8,128)(2,1)} %collective-permute-done.23.refs_3_, ...), custom_call_target="tpu_custom_call", output_to_operand_aliasing={{}: (13, {})} | custom-call | flops 23000000512 | bytes 73800000 | tf_op jit(solution)/shard_map/table_back/pallas_call | solution.py:82
  218.1 1.0 widen.1
  219.2 2.0 collect.1
  (153 shorter events, 8.7 us)
Async XLA Ops:
  2.7 13.9 %collective-permute-start.1 = (bf16[1024,256]{1,0:T(8,128)(2,1)}, bf16[1024,256]{1,0:T(8,128)(2,1)S(1)}, u32[]{:S(2)}, u32[]{:S(2)}) collective-permute-start(bf16[1024,256]{1,0:T(8,128)(2,1)} %low.3.refs_2_.refs_1_.refs_7_), channel_id=1, source_target_pairs={{0,2},{1,3},{2,0},{3,1},{4,6},{5,7},{6,4},{7,5},{8,10},{9,11},{10,... | collective-permute-start | bytes 1572872 | tf_op jit(solution)/shard_map/ppermute | solution.py:115
  7.0 9.6 %copy-start.3 = (bf16[2048,256]{1,0:T(8,128)(2,1)S(1)}, bf16[2048,256]{1,0:T(8,128)(2,1)}, u32[]{:S(2)}) copy-start(bf16[2048,256]{1,0:T(8,128)(2,1)} %get-tuple-element.46.refs_0_.refs_4_) | copy-start | bytes 3145732
  9.5 9.4 %copy-start.5 = (bf16[1024,256]{1,0:T(8,128)(2,1)S(1)}, bf16[1024,256]{1,0:T(8,128)(2,1)}, u32[]{:S(2)}) copy-start(bf16[1024,256]{1,0:T(8,128)(2,1)} %low.3.refs_2_.refs_1_.refs_7_) | copy-start | bytes 1572868
  9.5 20.8 %all-to-all-start = ((s16[8,3,50,256]{3,2,1,0:T(8,128)(2,1)}), s16[8,3,50,256]{3,2,1,0:T(8,128)(2,1)S(1)}, u32[]{:S(2)}, u32[]{:S(2)}) async-start(s16[8,3,50,256]{3,2,1,0:T(8,128)(2,1)} %slots.1.refs_3_), calls=%async_computation | async-start | bytes 1376256 | tf_op jit(solution)/shard_map/all_to_all | solution.py:124
  17.4 31.9 %copy-start.4 = (bf16[2048,256]{1,0:T(8,128)(2,1)}, bf16[2048,256]{1,0:T(8,128)(2,1)S(1)}, u32[]{:S(2)}) copy-start(bf16[2048,256]{1,0:T(8,128)(2,1)S(1)} %gate.6.refs_1_.refs_11_) | copy-start | bytes 3145732
  17.4 24.0 %collective-permute-start.3 = (bf16[2048,256]{1,0:T(8,128)(2,1)S(1)}, bf16[2048,256]{1,0:T(8,128)(2,1)S(1)}, u32[]{:S(2)}, u32[]{:S(2)}) collective-permute-start(bf16[2048,256]{1,0:T(8,128)(2,1)S(1)} %gate.6.refs_1_.refs_11_), channel_id=1, source_target_pairs={{0,2},{1,3},{2,0},{3,1},{4,6},{5,7},{6,4},{7,5},{8,10},{9,11},{10,... | collective-permute-start | bytes 3145736 | tf_op jit(solution)/shard_map/ppermute | solution.py:115
  18.9 4.4 %collective-permute-start = (bf16[1024,256]{1,0:T(8,128)(2,1)S(1)}, bf16[1024,256]{1,0:T(8,128)(2,1)S(1)}, u32[]{:S(2)}, u32[]{:S(2)}) collective-permute-start(bf16[1024,256]{1,0:T(8,128)(2,1)S(1)} %copy-done.5), channel_id=1, source_target_pairs={{0,1},{1,0},{2,3},{3,2},{4,5},{5,4},{6,7},{7,6},{8,9},{9,8},{10,11... | collective-permute-start | bytes 1572872 | tf_op jit(solution)/shard_map/ppermute | solution.py:115
  18.9 4.4 %collective-permute-start.2 = (bf16[1024,256]{1,0:T(8,128)(2,1)}, bf16[1024,256]{1,0:T(8,128)(2,1)S(1)}, u32[]{:S(2)}, u32[]{:S(2)}) collective-permute-start(bf16[1024,256]{1,0:T(8,128)(2,1)} %copy-done.7), channel_id=1, source_target_pairs={{0,1},{1,0},{2,3},{3,2},{4,5},{5,4},{6,7},{7,6},{8,9},{9,8},{10,11... | collective-permute-start | bytes 1572872 | tf_op jit(solution)/shard_map/ppermute | solution.py:115
  23.2 26.1 %collective-permute-start.6 = (bf16[2048,256]{1,0:T(8,128)(2,1)S(1)}, bf16[2048,256]{1,0:T(8,128)(2,1)}, u32[]{:S(2)}, u32[]{:S(2)}) collective-permute-start(bf16[2048,256]{1,0:T(8,128)(2,1)S(1)} %gate.6.refs_1_.refs_11_), channel_id=1, source_target_pairs={{0,1},{1,0},{2,3},{3,2},{4,5},{5,4},{6,7},{7,6},{8,9},{9,8},{10,11... | collective-permute-start | bytes 3145736 | tf_op jit(solution)/shard_map/ppermute | solution.py:115
  36.6 28.6 %copy-start.1 = (bf16[4,4096,256]{2,1,0:T(8,128)(2,1)}, bf16[4,4096,256]{2,1,0:T(8,128)(2,1)S(1)}, u32[]{:S(2)}) copy-start(bf16[4,4096,256]{2,1,0:T(8,128)(2,1)S(1)} %spread.2.refs_1_.refs_2_.refs_3_.refs_4_) | copy-start | bytes 25165828
  41.4 7.9 %collective-permute-start.7 = (bf16[2048,256]{1,0:T(8,128)(2,1)S(1)}, bf16[2048,256]{1,0:T(8,128)(2,1)S(1)}, u32[]{:S(2)}, u32[]{:S(2)}) collective-permute-start(bf16[2048,256]{1,0:T(8,128)(2,1)S(1)} %gate.7.refs_1_.refs_3_.refs_13_), channel_id=1, source_target_pairs={{0,1},{1,0},{2,3},{3,2},{4,5},{5,4},{6,7},{7,6},{8,9},{9,8},{10,11... | collective-permute-start | bytes 3145736 | tf_op jit(solution)/shard_map/ppermute | solution.py:115
  41.4 21.0 %copy-start.10 = (bf16[1024,256]{1,0:T(8,128)(2,1)}, bf16[1024,256]{1,0:T(8,128)(2,1)S(1)}, u32[]{:S(2)}) copy-start(bf16[1024,256]{1,0:T(8,128)(2,1)S(1)} %gate.8.refs_1_.refs_15_) | copy-start | bytes 1572868
  41.5 14.3 %collective-permute-start.5 = (bf16[1024,256]{1,0:T(8,128)(2,1)S(1)}, bf16[1024,256]{1,0:T(8,128)(2,1)S(1)}, u32[]{:S(2)}, u32[]{:S(2)}) collective-permute-start(bf16[1024,256]{1,0:T(8,128)(2,1)S(1)} %gate.8.refs_1_.refs_15_), channel_id=1, source_target_pairs={{0,2},{1,3},{2,0},{3,1},{4,6},{5,7},{6,4},{7,5},{8,10},{9,11},{10,... | collective-permute-start | bytes 1572872 | tf_op jit(solution)/shard_map/ppermute | solution.py:115
  49.1 16.1 %copy-start = (bf16[4,4096,256]{2,1,0:T(8,128)(2,1)}, bf16[4,4096,256]{2,1,0:T(8,128)(2,1)S(1)}, u32[]{:S(2)}) copy-start(bf16[4,4096,256]{2,1,0:T(8,128)(2,1)S(1)} %spread.3.refs_7_.refs_5_.refs_6_.refs_2_.refs_1_) | copy-start | bytes 25165828
  49.1 13.4 %collective-permute-start.4 = (bf16[1024,256]{1,0:T(8,128)(2,1)S(1)}, bf16[1024,256]{1,0:T(8,128)(2,1)S(1)}, u32[]{:S(2)}, u32[]{:S(2)}) collective-permute-start(bf16[1024,256]{1,0:T(8,128)(2,1)S(1)} %gate.8.refs_1_.refs_15_), channel_id=1, source_target_pairs={{0,1},{1,0},{2,3},{3,2},{4,5},{5,4},{6,7},{7,6},{8,9},{9,8},{10,11... | collective-permute-start | bytes 1572872 | tf_op jit(solution)/shard_map/ppermute | solution.py:115
  55.8 6.7 %collective-permute-start.8 = (bf16[1024,256]{1,0:T(8,128)(2,1)S(1)}, bf16[1024,256]{1,0:T(8,128)(2,1)S(1)}, u32[]{:S(2)}, u32[]{:S(2)}) collective-permute-start(bf16[1024,256]{1,0:T(8,128)(2,1)S(1)} %gate.9.refs_3_.refs_17_), channel_id=1, source_target_pairs={{0,1},{1,0},{2,3},{3,2},{4,5},{5,4},{6,7},{7,6},{8,9},{9,8},{10,11... | collective-permute-start | bytes 1572872 | tf_op jit(solution)/shard_map/ppermute | solution.py:115
  55.8 18.0 %copy-start.13 = (bf16[1024,256]{1,0:T(8,128)(2,1)}, bf16[1024,256]{1,0:T(8,128)(2,1)S(1)}, u32[]{:S(2)}) copy-start(bf16[1024,256]{1,0:T(8,128)(2,1)S(1)} %gate.10.refs_5_) | copy-start | bytes 1572868
  55.8 18.2 %collective-permute-start.9 = (bf16[1024,256]{1,0:T(8,128)(2,1)S(1)}, bf16[1024,256]{1,0:T(8,128)(2,1)}, u32[]{:S(2)}, u32[]{:S(2)}) collective-permute-start(bf16[1024,256]{1,0:T(8,128)(2,1)S(1)} %gate.10.refs_5_), channel_id=1, source_target_pairs={{0,2},{1,3},{2,0},{3,1},{4,6},{5,7},{6,4},{7,5},{8,10},{9,11},{10,... | collective-permute-start | bytes 1572872 | tf_op jit(solution)/shard_map/ppermute | solution.py:115
  68.7 30.1 %all-to-all-start.1 = ((bf16[32,64,256]{2,1,0:T(8,128)(2,1)}), bf16[32,64,256]{2,1,0:T(8,128)(2,1)S(1)}, u32[]{:S(2)}, u32[]{:S(2)}) async-start(bf16[32,64,256]{2,1,0:T(8,128)(2,1)} %bitcast.6), calls=%async_computation.1 | async-start | bytes 2097152 | tf_op jit(solution)/shard_map/all_to_all | solution.py:124
  73.8 17.5 %collective-permute-start.13 = (bf16[1024,256]{1,0:T(8,128)(2,1)S(1)}, bf16[1024,256]{1,0:T(8,128)(2,1)S(1)}, u32[]{:S(2)}, u32[]{:S(2)}) collective-permute-start(bf16[1024,256]{1,0:T(8,128)(2,1)S(1)} %gate.10.refs_5_), channel_id=1, source_target_pairs={{0,1},{1,0},{2,3},{3,2},{4,5},{5,4},{6,7},{7,6},{8,9},{9,8},{10,11... | collective-permute-start | bytes 1572872 | tf_op jit(solution)/shard_map/ppermute | solution.py:115
  74.0 17.3 %collective-permute-start.14 = (bf16[1024,256]{1,0:T(8,128)(2,1)}, bf16[1024,256]{1,0:T(8,128)(2,1)S(1)}, u32[]{:S(2)}, u32[]{:S(2)}) collective-permute-start(bf16[1024,256]{1,0:T(8,128)(2,1)} %collective-permute-done.9.refs_9_.refs_7_), channel_id=1, source_target_pairs={{0,1},{1,0},{2,3},{3,2},{4,5},{5,4},{6,7},{7,6},{8,9},{9,8},{10,11... | collective-permute-start | bytes 1572872 | tf_op jit(solution)/shard_map/ppermute | solution.py:115
  76.8 14.4 %collective-permute-start.10 = (f32[64,512]{1,0:T(8,128)}, f32[64,512]{1,0:T(8,128)S(1)}, u32[]{:S(2)}, u32[]{:S(2)}) collective-permute-start(f32[64,512]{1,0:T(8,128)} %get-tuple-element.51), channel_id=1, source_target_pairs={{0,1},{1,0},{2,3},{3,2},{4,5},{5,4},{6,7},{7,6},{8,9},{9,8},{10,11... | collective-permute-start | bytes 393224 | tf_op jit(solution)/shard_map/ppermute | solution.py:115
  77.0 14.3 %collective-permute-start.11 = (f32[64,512]{1,0:T(8,128)}, f32[64,512]{1,0:T(8,128)S(1)}, u32[]{:S(2)}, u32[]{:S(2)}) collective-permute-start(f32[64,512]{1,0:T(8,128)} %get-tuple-element.52), channel_id=1, source_target_pairs={{0,2},{1,3},{2,0},{3,1},{4,6},{5,7},{6,4},{7,5},{8,10},{9,11},{10,... | collective-permute-start | bytes 393224 | tf_op jit(solution)/shard_map/ppermute | solution.py:115
  78.5 12.9 %collective-permute-start.12 = (f32[64,512]{1,0:T(8,128)}, f32[64,512]{1,0:T(8,128)S(1)}, u32[]{:S(2)}, u32[]{:S(2)}) collective-permute-start(f32[64,512]{1,0:T(8,128)} %get-tuple-element.53), channel_id=1, source_target_pairs={{0,3},{1,2},{2,1},{3,0},{4,7},{5,6},{6,5},{7,4},{8,11},{9,10},{10,... | collective-permute-start | bytes 393224 | tf_op jit(solution)/shard_map/ppermute | solution.py:115
  102.8 16.9 %copy-start.42 = (bf16[80,512]{1,0:T(8,128)(2,1)S(1)}, bf16[80,512]{1,0:T(8,128)(2,1)}, u32[]{:S(2)}) copy-start(bf16[80,512]{1,0:T(8,128)(2,1)} %get-tuple-element.55) | copy-start | bytes 245764
  102.8 17.4 %copy-start.41 = (bf16[80,512]{1,0:T(8,128)(2,1)S(1)}, bf16[80,512]{1,0:T(8,128)(2,1)}, u32[]{:S(2)}) copy-start(bf16[80,512]{1,0:T(8,128)(2,1)} %get-tuple-element.56) | copy-start | bytes 245764
  102.8 18.3 %copy-start.40 = (bf16[80,512]{1,0:T(8,128)(2,1)S(1)}, bf16[80,512]{1,0:T(8,128)(2,1)}, u32[]{:S(2)}) copy-start(bf16[80,512]{1,0:T(8,128)(2,1)} %get-tuple-element.57) | copy-start | bytes 245764
  102.9 30.2 %all-to-all-start.2 = ((bf16[32,64,256]{2,1,0:T(8,128)(2,1)}), bf16[32,64,256]{2,1,0:T(8,128)(2,1)S(1)}, u32[]{:S(2)}, u32[]{:S(2)}) async-start(bf16[32,64,256]{2,1,0:T(8,128)(2,1)} %bitcast.9), calls=%async_computation.2 | async-start | bytes 2097152 | tf_op jit(solution)/shard_map/all_to_all | solution.py:124
  107.7 11.9 %collective-permute-start.19 = (bf16[64,1024]{1,0:T(8,128)(2,1)S(1)}, bf16[64,1024]{1,0:T(8,128)(2,1)S(1)}, u32[]{:S(2)}, u32[]{:S(2)}) collective-permute-start(bf16[64,1024]{1,0:T(8,128)(2,1)S(1)} %copy-done.27), channel_id=1, source_target_pairs={{0,2},{1,3},{2,0},{3,1},{4,6},{5,7},{6,4},{7,5},{8,10},{9,11},{10,... | collective-permute-start | bytes 393224 | tf_op jit(solution)/shard_map/ppermute | solution.py:115
  109.3 18.0 %collective-permute-start.18 = (bf16[64,1024]{1,0:T(8,128)(2,1)S(1)}, bf16[64,1024]{1,0:T(8,128)(2,1)S(1)}, u32[]{:S(2)}, u32[]{:S(2)}) collective-permute-start(bf16[64,1024]{1,0:T(8,128)(2,1)S(1)} %copy-done.27), channel_id=1, source_target_pairs={{0,1},{1,0},{2,3},{3,2},{4,5},{5,4},{6,7},{7,6},{8,9},{9,8},{10,11... | collective-permute-start | bytes 393224 | tf_op jit(solution)/shard_map/ppermute | solution.py:115
  119.7 7.6 %collective-permute-start.20 = (bf16[64,1024]{1,0:T(8,128)(2,1)S(1)}, bf16[64,1024]{1,0:T(8,128)(2,1)S(1)}, u32[]{:S(2)}, u32[]{:S(2)}) collective-permute-start(bf16[64,1024]{1,0:T(8,128)(2,1)S(1)} %collective-permute-done.19.refs_11_), channel_id=1, source_target_pairs={{0,1},{1,0},{2,3},{3,2},{4,5},{5,4},{6,7},{7,6},{8,9},{9,8},{10,11... | collective-permute-start | bytes 393224 | tf_op jit(solution)/shard_map/ppermute | solution.py:115
  119.7 3.8 %collective-permute-start.15 = (bf16[80,512]{1,0:T(8,128)(2,1)S(1)}, bf16[80,512]{1,0:T(8,128)(2,1)S(1)}, u32[]{:S(2)}, u32[]{:S(2)}) collective-permute-start(bf16[80,512]{1,0:T(8,128)(2,1)S(1)} %copy-done.42), channel_id=1, source_target_pairs={{0,1},{1,0},{2,3},{3,2},{4,5},{5,4},{6,7},{7,6},{8,9},{9,8},{10,11... | collective-permute-start | bytes 245768 | tf_op jit(solution)/shard_map/ppermute | solution.py:115
  120.2 5.7 %collective-permute-start.16 = (bf16[80,512]{1,0:T(8,128)(2,1)S(1)}, bf16[80,512]{1,0:T(8,128)(2,1)S(1)}, u32[]{:S(2)}, u32[]{:S(2)}) collective-permute-start(bf16[80,512]{1,0:T(8,128)(2,1)S(1)} %copy-done.41), channel_id=1, source_target_pairs={{0,2},{1,3},{2,0},{3,1},{4,6},{5,7},{6,4},{7,5},{8,10},{9,11},{10,... | collective-permute-start | bytes 245768 | tf_op jit(solution)/shard_map/ppermute | solution.py:115
  121.1 6.1 %collective-permute-start.17 = (bf16[80,512]{1,0:T(8,128)(2,1)S(1)}, bf16[80,512]{1,0:T(8,128)(2,1)S(1)}, u32[]{:S(2)}, u32[]{:S(2)}) collective-permute-start(bf16[80,512]{1,0:T(8,128)(2,1)S(1)} %copy-done.40), channel_id=1, source_target_pairs={{0,3},{1,2},{2,1},{3,0},{4,7},{5,6},{6,5},{7,4},{8,11},{9,10},{10,... | collective-permute-start | bytes 245768 | tf_op jit(solution)/shard_map/ppermute | solution.py:115
  123.5 9.6 %collective-permute-start.21 = (bf16[256,256]{1,0:T(8,128)(2,1)}, bf16[256,256]{1,0:T(8,128)(2,1)S(1)}, u32[]{:S(2)}, u32[]{:S(2)}) collective-permute-start(bf16[256,256]{1,0:T(8,128)(2,1)} %get-tuple-element.62), channel_id=1, source_target_pairs={{0,2},{1,3},{2,0},{3,1},{4,6},{5,7},{6,4},{7,5},{8,10},{9,11},{10,... | collective-permute-start | bytes 393224 | tf_op jit(solution)/shard_map/ppermute | solution.py:115
  130.3 17.9 %collective-permute-start.27 = (bf16[256,256]{1,0:T(8,128)(2,1)}, bf16[256,256]{1,0:T(8,128)(2,1)S(1)}, u32[]{:S(2)}, u32[]{:S(2)}) collective-permute-start(bf16[256,256]{1,0:T(8,128)(2,1)} %get-tuple-element.68), channel_id=1, source_target_pairs={{0,1},{1,0},{2,3},{3,2},{4,5},{5,4},{6,7},{7,6},{8,9},{9,8},{10,11... | collective-permute-start | bytes 393224 | tf_op jit(solution)/shard_map/ppermute | solution.py:115
  131.2 17.1 %collective-permute-start.28 = (bf16[256,256]{1,0:T(8,128)(2,1)}, bf16[256,256]{1,0:T(8,128)(2,1)S(1)}, u32[]{:S(2)}, u32[]{:S(2)}) collective-permute-start(bf16[256,256]{1,0:T(8,128)(2,1)} %get-tuple-element.69), channel_id=1, source_target_pairs={{0,2},{1,3},{2,0},{3,1},{4,6},{5,7},{6,4},{7,5},{8,10},{9,11},{10,... | collective-permute-start | bytes 393224 | tf_op jit(solution)/shard_map/ppermute | solution.py:115
  131.9 16.4 %collective-permute-start.29 = (bf16[256,256]{1,0:T(8,128)(2,1)}, bf16[256,256]{1,0:T(8,128)(2,1)S(1)}, u32[]{:S(2)}, u32[]{:S(2)}) collective-permute-start(bf16[256,256]{1,0:T(8,128)(2,1)} %get-tuple-element.70), channel_id=1, source_target_pairs={{0,3},{1,2},{2,1},{3,0},{4,7},{5,6},{6,5},{7,4},{8,11},{9,10},{10,... | collective-permute-start | bytes 393224 | tf_op jit(solution)/shard_map/ppermute | solution.py:115
  132.6 15.7 %collective-permute-start.30 = (bf16[4,256,256]{2,1,0:T(8,128)(2,1)}, bf16[4,256,256]{2,1,0:T(8,128)(2,1)S(1)}, u32[]{:S(2)}, u32[]{:S(2)}) collective-permute-start(bf16[4,256,256]{2,1,0:T(8,128)(2,1)} %get-tuple-element.73), channel_id=1, source_target_pairs={{0,4},{4,0},{8,12},{12,8},{16,20},{20,16},{24,28},{28,24},{1,5},{5... | collective-permute-start | bytes 1572872 | tf_op jit(solution)/shard_map/ppermute | solution.py:115
  133.1 15.2 %copy-start.21 = (bf16[256,256]{1,0:T(8,128)(2,1)}, bf16[256,256]{1,0:T(8,128)(2,1)S(1)}, u32[]{:S(2)}) copy-start(bf16[256,256]{1,0:T(8,128)(2,1)S(1)} %collective-permute-done.21.refs_20_.refs_7_) | copy-start | bytes 393220
  150.0 12.8 %copy-start.37 = (bf16[256,256]{1,0:T(8,128)(2,1)S(1)}, bf16[256,256]{1,0:T(8,128)(2,1)}, u32[]{:S(2)}) copy-start(bf16[256,256]{1,0:T(8,128)(2,1)} %get-tuple-element.65) | copy-start | bytes 393220
  150.0 24.0 %copy-start.36 = (bf16[256,256]{1,0:T(8,128)(2,1)S(1)}, bf16[256,256]{1,0:T(8,128)(2,1)}, u32[]{:S(2)}) copy-start(bf16[256,256]{1,0:T(8,128)(2,1)} %get-tuple-element.66) | copy-start | bytes 393220
  150.0 37.4 %copy-start.15 = (bf16[3072,256]{1,0:T(8,128)(2,1)}, bf16[3072,256]{1,0:T(8,128)(2,1)S(1)}, u32[]{:S(2)}) copy-start(bf16[3072,256]{1,0:T(8,128)(2,1)S(1)} %gate.11.refs_1_) | copy-start | bytes 4718596
  150.0 44.6 %collective-permute-start.32 = (bf16[3072,256]{1,0:T(8,128)(2,1)S(1)}, bf16[3072,256]{1,0:T(8,128)(2,1)}, u32[]{:S(2)}, u32[]{:S(2)}) collective-permute-start(bf16[3072,256]{1,0:T(8,128)(2,1)S(1)} %gate.11.refs_1_), channel_id=1, source_target_pairs={{0,2},{1,3},{2,0},{3,1},{4,6},{5,7},{6,4},{7,5},{8,10},{9,11},{10,... | collective-permute-start | bytes 4718600 | tf_op jit(solution)/shard_map/ppermute | solution.py:115
  151.3 43.5 %all-to-all-start.3 = ((bf16[8,144,256]{2,1,0:T(8,128)(2,1)}), bf16[8,144,256]{2,1,0:T(8,128)(2,1)S(1)}, u32[]{:S(2)}, u32[]{:S(2)}) async-start(bf16[8,144,256]{2,1,0:T(8,128)(2,1)} %get-tuple-element.78), calls=%async_computation.3 | async-start | bytes 1179648 | tf_op jit(solution)/shard_map/all_to_all | solution.py:124
  159.3 14.7 %collective-permute-start.34 = (bf16[256,256]{1,0:T(8,128)(2,1)S(1)}, bf16[256,256]{1,0:T(8,128)(2,1)S(1)}, u32[]{:S(2)}, u32[]{:S(2)}) collective-permute-start(bf16[256,256]{1,0:T(8,128)(2,1)S(1)} %get-tuple-element.75), channel_id=1, source_target_pairs={{0,8},{4,12},{8,0},{12,4},{16,24},{20,28},{24,16},{28,20},{1,9},{5... | collective-permute-start | bytes 393224 | tf_op jit(solution)/shard_map/ppermute | solution.py:115
  159.8 20.6 %collective-permute-start.35 = (bf16[256,256]{1,0:T(8,128)(2,1)S(1)}, bf16[256,256]{1,0:T(8,128)(2,1)S(1)}, u32[]{:S(2)}, u32[]{:S(2)}) collective-permute-start(bf16[256,256]{1,0:T(8,128)(2,1)S(1)} %get-tuple-element.76), channel_id=1, source_target_pairs={{0,16},{4,20},{8,24},{12,28},{16,0},{20,4},{24,8},{28,12},{1,17},{... | collective-permute-start | bytes 393224 | tf_op jit(solution)/shard_map/ppermute | solution.py:115
  162.2 22.9 %collective-permute-start.36 = (bf16[256,256]{1,0:T(8,128)(2,1)S(1)}, bf16[256,256]{1,0:T(8,128)(2,1)S(1)}, u32[]{:S(2)}, u32[]{:S(2)}) collective-permute-start(bf16[256,256]{1,0:T(8,128)(2,1)S(1)} %get-tuple-element.77), channel_id=1, source_target_pairs={{0,24},{4,28},{8,16},{12,20},{16,8},{20,12},{24,0},{28,4},{1,25},{... | collective-permute-start | bytes 393224 | tf_op jit(solution)/shard_map/ppermute | solution.py:115
  162.8 24.6 %collective-permute-start.25 = (bf16[256,256]{1,0:T(8,128)(2,1)S(1)}, bf16[256,256]{1,0:T(8,128)(2,1)S(1)}, u32[]{:S(2)}, u32[]{:S(2)}) collective-permute-start(bf16[256,256]{1,0:T(8,128)(2,1)S(1)} %copy-done.37), channel_id=1, source_target_pairs={{0,1},{1,0},{2,3},{3,2},{4,5},{5,4},{6,7},{7,6},{8,9},{9,8},{10,11... | collective-permute-start | bytes 393224 | tf_op jit(solution)/shard_map/ppermute | solution.py:115
  174.0 15.1 %collective-permute-start.26 = (bf16[256,256]{1,0:T(8,128)(2,1)S(1)}, bf16[256,256]{1,0:T(8,128)(2,1)S(1)}, u32[]{:S(2)}, u32[]{:S(2)}) collective-permute-start(bf16[256,256]{1,0:T(8,128)(2,1)S(1)} %copy-done.36), channel_id=1, source_target_pairs={{0,3},{1,2},{2,1},{3,0},{4,7},{5,6},{6,5},{7,4},{8,11},{9,10},{10,... | collective-permute-start | bytes 393224 | tf_op jit(solution)/shard_map/ppermute | solution.py:115
  185.2 9.6 %copy-start.25 = (bf16[256,256]{1,0:T(8,128)(2,1)}, bf16[256,256]{1,0:T(8,128)(2,1)S(1)}, u32[]{:S(2)}) copy-start(bf16[256,256]{1,0:T(8,128)(2,1)S(1)} %add_some.1.refs_1_) | copy-start | bytes 393220
  185.2 9.0 %collective-permute-start.39 = (bf16[256,256]{1,0:T(8,128)(2,1)S(1)}, bf16[256,256]{1,0:T(8,128)(2,1)S(1)}, u32[]{:S(2)}, u32[]{:S(2)}) collective-permute-start(bf16[256,256]{1,0:T(8,128)(2,1)S(1)} %add_some.1.refs_1_), channel_id=1, source_target_pairs={{0,24},{4,28},{8,16},{12,20},{16,8},{20,12},{24,0},{28,4},{1,25},{... | collective-permute-start | bytes 393224 | tf_op jit(solution)/shard_map/ppermute | solution.py:115
  185.8 16.6 %collective-permute-start.23 = (bf16[1024,256]{1,0:T(8,128)(2,1)}, bf16[1024,256]{1,0:T(8,128)(2,1)}, u32[]{:S(2)}, u32[]{:S(2)}) collective-permute-start(bf16[1024,256]{1,0:T(8,128)(2,1)} %get-tuple-element.63.refs_2_.refs_1_), channel_id=1, source_target_pairs={{0,2},{1,3},{2,0},{3,1},{4,6},{5,7},{6,4},{7,5},{8,10},{9,11},{10,... | collective-permute-start | bytes 1572872 | tf_op jit(solution)/shard_map/ppermute | solution.py:115
  187.4 16.2 %collective-permute-start.31 = (bf16[3072,256]{1,0:T(8,128)(2,1)S(1)}, bf16[3072,256]{1,0:T(8,128)(2,1)}, u32[]{:S(2)}, u32[]{:S(2)}) collective-permute-start(bf16[3072,256]{1,0:T(8,128)(2,1)S(1)} %gate.11.refs_1_), channel_id=1, source_target_pairs={{0,1},{1,0},{2,3},{3,2},{4,5},{5,4},{6,7},{7,6},{8,9},{9,8},{10,11... | collective-permute-start | bytes 4718600 | tf_op jit(solution)/shard_map/ppermute | solution.py:115
  189.1 11.7 %collective-permute-start.38 = (bf16[256,256]{1,0:T(8,128)(2,1)S(1)}, bf16[256,256]{1,0:T(8,128)(2,1)S(1)}, u32[]{:S(2)}, u32[]{:S(2)}) collective-permute-start(bf16[256,256]{1,0:T(8,128)(2,1)S(1)} %add_some.1.refs_1_), channel_id=1, source_target_pairs={{0,16},{4,20},{8,24},{12,28},{16,0},{20,4},{24,8},{28,12},{1,17},{... | collective-permute-start | bytes 393224 | tf_op jit(solution)/shard_map/ppermute | solution.py:115
  194.2 7.4 %collective-permute-start.37 = (bf16[256,256]{1,0:T(8,128)(2,1)S(1)}, bf16[256,256]{1,0:T(8,128)(2,1)S(1)}, u32[]{:S(2)}, u32[]{:S(2)}) collective-permute-start(bf16[256,256]{1,0:T(8,128)(2,1)S(1)} %add_some.1.refs_1_), channel_id=1, source_target_pairs={{0,8},{4,12},{8,0},{12,4},{16,24},{20,28},{24,16},{28,20},{1,9},{5... | collective-permute-start | bytes 393224 | tf_op jit(solution)/shard_map/ppermute | solution.py:115
  194.6 9.8 %collective-permute-start.33 = (bf16[3072,256]{1,0:T(8,128)(2,1)}, bf16[3072,256]{1,0:T(8,128)(2,1)}, u32[]{:S(2)}, u32[]{:S(2)}) collective-permute-start(bf16[3072,256]{1,0:T(8,128)(2,1)} %collective-permute-done.32.refs_3_), channel_id=1, source_target_pairs={{0,1},{1,0},{2,3},{3,2},{4,5},{5,4},{6,7},{7,6},{8,9},{9,8},{10,11... | collective-permute-start | bytes 4718600 | tf_op jit(solution)/shard_map/ppermute | solution.py:115
  195.7 22.4 %all-to-all-start.4 = ((bf16[8,128,256]{2,1,0:T(8,128)(2,1)}), bf16[8,128,256]{2,1,0:T(8,128)(2,1)S(1)}, u32[]{:S(2)}, u32[]{:S(2)}) async-start(bf16[8,128,256]{2,1,0:T(8,128)(2,1)} %get-tuple-element.79), calls=%async_computation.4 | async-start | bytes 1048576 | tf_op jit(solution)/shard_map/all_to_all | solution.py:124
  200.7 12.3 %collective-permute-start.22 = (bf16[1024,256]{1,0:T(8,128)(2,1)}, bf16[1024,256]{1,0:T(8,128)(2,1)S(1)}, u32[]{:S(2)}, u32[]{:S(2)}) collective-permute-start(bf16[1024,256]{1,0:T(8,128)(2,1)} %get-tuple-element.63.refs_2_.refs_1_), channel_id=1, source_target_pairs={{0,1},{1,0},{2,3},{3,2},{4,5},{5,4},{6,7},{7,6},{8,9},{9,8},{10,11... | collective-permute-start | bytes 1572872 | tf_op jit(solution)/shard_map/ppermute | solution.py:115
  201.5 10.2 %collective-permute-start.40 = (bf16[256,256]{1,0:T(8,128)(2,1)}, bf16[256,256]{1,0:T(8,128)(2,1)S(1)}, u32[]{:S(2)}, u32[]{:S(2)}) collective-permute-start(bf16[256,256]{1,0:T(8,128)(2,1)} %copy-done.25), channel_id=1, source_target_pairs={{0,4},{4,0},{8,12},{12,8},{16,20},{20,16},{24,28},{28,24},{1,5},{5... | collective-permute-start | bytes 393224 | tf_op jit(solution)/shard_map/ppermute | solution.py:115
  202.4 16.8 %collective-permute-start.43 = (bf16[256,256]{1,0:T(8,128)(2,1)S(1)}, bf16[256,256]{1,0:T(8,128)(2,1)S(1)}, u32[]{:S(2)}, u32[]{:S(2)}) collective-permute-start(bf16[256,256]{1,0:T(8,128)(2,1)S(1)} %collective-permute-done.39.refs_15_.refs_7_), channel_id=1, source_target_pairs={{0,4},{4,0},{8,12},{12,8},{16,20},{20,16},{24,28},{28,24},{1,5},{5... | collective-permute-start | bytes 393224 | tf_op jit(solution)/shard_map/ppermute | solution.py:115
  203.6 15.6 %collective-permute-start.42 = (bf16[256,256]{1,0:T(8,128)(2,1)S(1)}, bf16[256,256]{1,0:T(8,128)(2,1)S(1)}, u32[]{:S(2)}, u32[]{:S(2)}) collective-permute-start(bf16[256,256]{1,0:T(8,128)(2,1)S(1)} %collective-permute-done.38.refs_14_.refs_5_), channel_id=1, source_target_pairs={{0,4},{4,0},{8,12},{12,8},{16,20},{20,16},{24,28},{28,24},{1,5},{5... | collective-permute-start | bytes 393224 | tf_op jit(solution)/shard_map/ppermute | solution.py:115
  204.4 8.6 %collective-permute-start.24 = (bf16[1024,256]{1,0:T(8,128)(2,1)}, bf16[1024,256]{1,0:T(8,128)(2,1)S(1)}, u32[]{:S(2)}, u32[]{:S(2)}) collective-permute-start(bf16[1024,256]{1,0:T(8,128)(2,1)} %collective-permute-done.23.refs_3_), channel_id=1, source_target_pairs={{0,1},{1,0},{2,3},{3,2},{4,5},{5,4},{6,7},{7,6},{8,9},{9,8},{10,11... | collective-permute-start | bytes 1572872 | tf_op jit(solution)/shard_map/ppermute | solution.py:115
  211.8 7.5 %collective-permute-start.41 = (bf16[256,256]{1,0:T(8,128)(2,1)S(1)}, bf16[256,256]{1,0:T(8,128)(2,1)S(1)}, u32[]{:S(2)}, u32[]{:S(2)}) collective-permute-start(bf16[256,256]{1,0:T(8,128)(2,1)S(1)} %collective-permute-done.37.refs_13_.refs_3_), channel_id=1, source_target_pairs={{0,4},{4,0},{8,12},{12,8},{16,20},{20,16},{24,28},{28,24},{1,5},{5... | collective-permute-start | bytes 393224 | tf_op jit(solution)/shard_map/ppermute | solution.py:115
  (28 other events, 115.8 us)
